TPU v7x, 32 devices: a whole 2x2x4 slice. The times are simulated.
32 devices in a mesh: dp: 4 (over y, x), rows: 2 (over core), cols: 4 (over z).
Axes of the slice: x: 2, y: 2, z: 4, core: 2. Of those that a mesh axis runs over, the one named last changes fastest.
Arguments:
- block_input: bfloat16 [1024, 8, 1536], P('cols', 'dp', 'rows'), may hold values from -6 to 6
- block_cotangent: bfloat16 [1024, 8, 1536], P('cols', 'dp', 'rows'), may hold values from -6 to 6
- w_query: bfloat16 [2, 1536, 1536], P(None, 'rows', 'cols'), may hold values from -0.15625 to 0.15625
- w_key: bfloat16 [2, 1536, 768], P(None, 'rows', 'cols'), may hold values from -0.15625 to 0.15625
- w_value: bfloat16 [2, 1536, 768], P(None, 'rows', 'cols'), may hold values from -0.15625 to 0.15625
- w_out: bfloat16 [2, 1536, 1536], P(None, 'cols', 'rows'), may hold values from -1.25 to 1.25
- w_gate: bfloat16 [2, 1536, 4096], P(None, 'rows', 'cols'), may hold values from -0.15625 to 0.15625
- w_up: bfloat16 [2, 1536, 4096], P(None, 'rows', 'cols'), may hold values from -0.15625 to 0.15625
- w_down: bfloat16 [2, 4096, 1536], P(None, 'cols', 'rows'), may hold values from -0.09375 to 0.09375
- norm_gains: float32 [2, 2, 1536], P(None, None, 'rows'), may hold values from 0.5 to 1.5
Outputs:
- activations: float32 [1024, 8, 1536], P('cols', 'dp', 'rows')
- input_grad: float32 [1024, 8, 1536], P('cols', 'dp', 'rows')
- grad_query: float32 [2, 1536, 1536], P(None, 'rows', 'cols')
- grad_key: float32 [2, 1536, 768], P(None, 'rows', 'cols')
- grad_value: float32 [2, 1536, 768], P(None, 'rows', 'cols')
- grad_out: float32 [2, 1536, 1536], P(None, 'cols', 'rows')
- grad_gate: float32 [2, 1536, 4096], P(None, 'rows', 'cols')
- grad_up: float32 [2, 1536, 4096], P(None, 'rows', 'cols')
- grad_down: float32 [2, 4096, 1536], P(None, 'cols', 'rows')
- grad_gains: float32 [2, 2, 1536], P(None, None, 'rows')
All inputs are finite; a program needn't handle non-finite values.
Results may differ from a plain program's by a relative error of at most 0.02.
Values may be sent and summed in bfloat16 or wider, within the bound.
No kernel may reach another device: no remote copies, remote signals or barrier semaphores. Data moves between devices by JAX's collectives and lax.ppermute only.
A program may use at most 256 MiB of HBM per device.

v0:
```python
import jax
import jax.numpy as jnp
from jax import lax
from jax.sharding import PartitionSpec as P

D = 1536
HEAD = 96
LEN = 1024
LAYERS = 2


EPSILON = 1e-05
ROPE_BASE = 100000.0
NEGATIVE = -1e30


def width_total(partial_sum):
    return lax.psum(partial_sum, "rows")


def col_gather(blocks_in):
    return lax.all_gather(blocks_in, "cols", axis=0, tiled=True)


def row_gather(blocks_in):
    return lax.all_gather(blocks_in, "rows", axis=0, tiled=True)


def row_reduce(left_side, right_side, pattern):
    return lax.psum_scatter(
        jnp.einsum(pattern, left_side, right_side, preferred_element_type=jnp.float32),
        "rows",
        scatter_dimension=0,
        tiled=True,
    )


def width_product_total(left_side, local_weight, pattern):
    return row_reduce(left_side, local_weight, pattern)


def column_reduction(left_side, right_side, pattern):
    return lax.psum_scatter(
        jnp.einsum(pattern, left_side, right_side, preferred_element_type=jnp.float32),
        "cols",
        scatter_dimension=0,
        tiled=True,
    )


def rope_tables(positions, head_width):
    indices = jnp.arange(head_width // 2, dtype=jnp.float32)
    inverse = ROPE_BASE ** (-2.0 * indices / head_width)
    angles = positions.astype(jnp.float32)[:, None] * inverse[None, :]
    return (jnp.cos(angles)[:, None, None, :], jnp.sin(angles)[:, None, None, :])


def rotate(vectors, cosine, sine):
    half_width = vectors.shape[-1] // 2
    first_half = vectors[..., :half_width]
    second_half = vectors[..., half_width:]
    return jnp.concatenate(
        [first_half * cosine - second_half * sine, second_half * cosine + first_half * sine],
        axis=-1,
    )


def normalize(hidden_state, gain_row):
    squares = width_total(jnp.sum(hidden_state * hidden_state, axis=-1))
    factor = lax.rsqrt(squares / D + EPSILON)[..., None]
    unit_vals = hidden_state * factor
    return (unit_vals, factor, (unit_vals * gain_row).astype(jnp.bfloat16))


def normalize_back(grad_normed, unit_vals, factor, gain_row):
    grad_unit = grad_normed * gain_row
    inner_dot = width_total(jnp.sum(grad_unit * unit_vals, axis=-1))[..., None]
    grad_gain = jnp.sum(grad_normed * unit_vals, axis=(0, 1))
    return (factor * (grad_unit - unit_vals * inner_dot / D), grad_gain)


def score_block(query_low, key_all, row_pos):
    factor = query_low.shape[-1] ** (-0.5)
    raw_scores = (
        jnp.einsum("qscre,ksce->scrqk", query_low, key_all, preferred_element_type=jnp.float32)
        * factor
    )
    key_pos = jnp.arange(key_all.shape[0], dtype=jnp.int32)
    return jnp.where(row_pos[:, None] >= key_pos[None, :], raw_scores, NEGATIVE)


def attend(query_low, key_all, value_all, row_pos):
    scores = score_block(query_low, key_all, row_pos)
    highest = jnp.max(scores, axis=-1, keepdims=True)
    log_total = highest + jnp.log(jnp.sum(jnp.exp(scores - highest), axis=-1, keepdims=True))
    probs_low = jnp.exp(scores - log_total).astype(jnp.bfloat16)
    attended = jnp.einsum(
        "scrqk,ksce->qscre", probs_low, value_all, preferred_element_type=jnp.float32
    )
    return (attended, log_total)


def weight_grad(gathered_weight, gradient_every_head):
    return jnp.einsum(
        "qxi,qxr->ir", gathered_weight, gradient_every_head, preferred_element_type=jnp.float32
    )


def forward_layer(hidden_state, weights, gains_pair, row_pos):
    w_q_loc, w_k_loc, w_v_loc, output_weight_local, w_g_loc, w_u_loc, down_weight_local = weights
    unit_a, factor_a, normed_a = normalize(hidden_state, gains_pair[0])
    gathered_first_weight = col_gather(normed_a)
    inner_weight = jnp.concatenate([w_q_loc, w_k_loc, w_v_loc], axis=1)
    projected_output = width_product_total(gathered_first_weight, inner_weight, "bjc,ce->bje")
    q_width = w_q_loc.shape[1]
    k_width = w_k_loc.shape[1]
    heads_here = q_width // HEAD
    kv_here = k_width // HEAD
    local_rows, seq_count = (projected_output.shape[0], projected_output.shape[1])
    cosine, sine = rope_tables(row_pos, HEAD)
    query_rot = rotate(
        projected_output[..., :q_width].reshape(local_rows, seq_count, heads_here, HEAD),
        cosine,
        sine,
    )
    key_rot = rotate(
        projected_output[..., q_width : q_width + k_width].reshape(
            local_rows, seq_count, kv_here, HEAD
        ),
        cosine,
        sine,
    )
    query_low = query_rot.astype(jnp.bfloat16).reshape(
        local_rows, seq_count, kv_here, heads_here // kv_here, HEAD
    )
    key_low = key_rot.astype(jnp.bfloat16)
    value_low = (
        projected_output[..., q_width + k_width :]
        .reshape(local_rows, seq_count, kv_here, HEAD)
        .astype(jnp.bfloat16)
    )
    key_all, value_all = (
        lax.all_gather(key_low, "rows", axis=0, tiled=True),
        lax.all_gather(value_low, "rows", axis=0, tiled=True),
    )
    attended, log_total = attend(query_low, key_all, value_all, row_pos)
    attended_every_head = row_gather(
        attended.reshape(local_rows, seq_count, q_width).astype(jnp.bfloat16)
    )
    mixed_output = hidden_state + column_reduction(
        attended_every_head, output_weight_local, "oqx,xr->oqr"
    )
    unit_b, factor_b, normed_b = normalize(mixed_output, gains_pair[1])
    gathered_second_weight = col_gather(normed_b)
    paired_weight = jnp.concatenate([w_g_loc, w_u_loc], axis=1)
    gate_up_product = width_product_total(gathered_second_weight, paired_weight, "bjc,ce->bje")
    ff_here = w_g_loc.shape[1]
    gate_part = gate_up_product[..., :ff_here]
    up_part = gate_up_product[..., ff_here:]
    inner_every_width = row_gather((jax.nn.silu(gate_part) * up_part).astype(jnp.bfloat16))
    layer_result = mixed_output + column_reduction(
        inner_every_width, down_weight_local, "oqx,xr->oqr"
    )
    saved = (
        unit_a,
        factor_a,
        normed_a,
        gathered_first_weight,
        inner_weight,
        query_low,
        key_all,
        value_all,
        log_total,
        attended_every_head,
        unit_b,
        factor_b,
        normed_b,
        gathered_second_weight,
        paired_weight,
        gate_part,
        up_part,
        inner_every_width,
    )
    return (layer_result, saved)


def backward_layer(grad_hidden, weights, gains_pair, row_pos, saved):
    w_q_loc, w_k_loc, w_v_loc, output_weight_local, w_g_loc, w_u_loc, down_weight_local = weights
    (
        unit_a,
        factor_a,
        normed_a,
        gathered_first_weight,
        inner_weight,
        query_low,
        key_all,
        value_all,
        log_total,
        attended_every_head,
        unit_b,
        factor_b,
        normed_b,
        gathered_second_weight,
        paired_weight,
        gate_part,
        up_part,
        inner_every_width,
    ) = saved
    branch_gradient = col_gather(grad_hidden.astype(jnp.bfloat16))
    grad_down_w = jnp.einsum(
        "jbk,jbx->kx", inner_every_width, branch_gradient, preferred_element_type=jnp.float32
    )
    inner_gradient = width_product_total(branch_gradient, down_weight_local, "ukx,nx->ukn")
    sigma = jax.nn.sigmoid(gate_part)
    gate_grad = inner_gradient * up_part * sigma * (1.0 + gate_part * (1.0 - sigma))
    up_grad = inner_gradient * gate_part * sigma
    paired_gradient = row_gather(
        jnp.concatenate([gate_grad, up_grad], axis=-1).astype(jnp.bfloat16)
    )
    grad_pair_w = weight_grad(gathered_second_weight, paired_gradient)
    second_normed_gradient = column_reduction(paired_gradient, paired_weight, "gij,ej->gie")
    back_b, gain_grad_b = normalize_back(second_normed_gradient, unit_b, factor_b, gains_pair[1])
    grad_mixed = grad_hidden + back_b
    branch_gradient = col_gather(grad_mixed.astype(jnp.bfloat16))
    grad_out_w = jnp.einsum(
        "jbk,jbx->kx", attended_every_head, branch_gradient, preferred_element_type=jnp.float32
    )
    attended_output_gradient = width_product_total(
        branch_gradient, output_weight_local, "ukx,nx->ukn"
    )
    grad_low = attended_output_gradient.astype(jnp.bfloat16).reshape(query_low.shape)
    scores = score_block(query_low, key_all, row_pos)
    probs = jnp.exp(scores - log_total)
    prob_grad = jnp.einsum(
        "qscre,ksce->scrqk", grad_low, value_all, preferred_element_type=jnp.float32
    )
    row_delta = jnp.sum(probs * prob_grad, axis=-1, keepdims=True)
    score_grad = (probs * (prob_grad - row_delta)).astype(jnp.bfloat16)
    factor = query_low.shape[-1] ** (-0.5)
    query_grad = (
        jnp.einsum("scrqk,ksce->qscre", score_grad, key_all, preferred_element_type=jnp.float32)
        * factor
    )
    key_grad = (
        jnp.einsum("scrqk,qscre->ksce", score_grad, query_low, preferred_element_type=jnp.float32)
        * factor
    )
    value_grad = jnp.einsum(
        "scrqk,qscre->ksce",
        probs.astype(jnp.bfloat16),
        grad_low,
        preferred_element_type=jnp.float32,
    )
    key_sum, value_sum = (
        lax.psum_scatter(key_grad, "rows", scatter_dimension=0, tiled=True),
        lax.psum_scatter(value_grad, "rows", scatter_dimension=0, tiled=True),
    )
    local_rows, seq_count = (query_low.shape[0], query_low.shape[1])
    cosine, sine = rope_tables(row_pos, HEAD)
    heads_here = query_low.shape[2] * query_low.shape[3]
    query_back = rotate(query_grad.reshape(local_rows, seq_count, heads_here, HEAD), cosine, -sine)
    key_back = rotate(key_sum, cosine, -sine)
    proj_grad = jnp.concatenate(
        [
            query_back.reshape(local_rows, seq_count, -1),
            key_back.reshape(local_rows, seq_count, -1),
            value_sum.reshape(local_rows, seq_count, -1),
        ],
        axis=-1,
    ).astype(jnp.bfloat16)
    projection_every_head = row_gather(proj_grad)
    grad_inner_w = weight_grad(gathered_first_weight, projection_every_head)
    first_normed_gradient = column_reduction(projection_every_head, inner_weight, "gij,ej->gie")
    back_a, gain_grad_a = normalize_back(first_normed_gradient, unit_a, factor_a, gains_pair[0])
    q_width = w_q_loc.shape[1]
    k_width = w_k_loc.shape[1]
    ff_here = w_g_loc.shape[1]
    layer_grads = (
        grad_inner_w[:, :q_width],
        grad_inner_w[:, q_width : q_width + k_width],
        grad_inner_w[:, q_width + k_width :],
        grad_out_w,
        grad_pair_w[:, :ff_here],
        grad_pair_w[:, ff_here:],
        grad_down_w,
        jnp.stack([gain_grad_a, gain_grad_b]),
    )
    return (grad_mixed + back_a, layer_grads)


def shards(
    block_input, block_cotangent, w_query, w_key, w_value, w_out, w_gate, w_up, w_down, norm_gains
):
    row_len = LEN // lax.axis_size("rows")
    row_pos = lax.axis_index("rows") * row_len + jnp.arange(row_len, dtype=jnp.int32)
    hidden_state = block_input.astype(jnp.float32)
    stash = []
    for layer_idx in range(LAYERS):
        weights = (
            w_query[layer_idx],
            w_key[layer_idx],
            w_value[layer_idx],
            w_out[layer_idx],
            w_gate[layer_idx],
            w_up[layer_idx],
            w_down[layer_idx],
        )
        hidden_state, saved = forward_layer(hidden_state, weights, norm_gains[layer_idx], row_pos)
        stash.append(saved)
    grad_hidden = block_cotangent.astype(jnp.float32)
    collected = [None] * LAYERS
    for layer_idx in reversed(range(LAYERS)):
        weights = (
            w_query[layer_idx],
            w_key[layer_idx],
            w_value[layer_idx],
            w_out[layer_idx],
            w_gate[layer_idx],
            w_up[layer_idx],
            w_down[layer_idx],
        )
        grad_hidden, layer_grads = backward_layer(
            grad_hidden, weights, norm_gains[layer_idx], row_pos, stash[layer_idx]
        )
        collected[layer_idx] = layer_grads
    stacked = [jnp.stack([grads_one[member] for grads_one in collected]) for member in range(8)]
    sum_query, sum_key, sum_value, sum_out, sum_gate, sum_up, sum_down = lax.psum(
        (stacked[0], stacked[1], stacked[2], stacked[3], stacked[4], stacked[5], stacked[6]), "dp"
    )
    sum_gains = lax.psum(stacked[7], ("dp", "cols"))
    return (
        hidden_state,
        grad_hidden,
        sum_query,
        sum_key,
        sum_value,
        sum_out,
        sum_gate,
        sum_up,
        sum_down,
        sum_gains,
    )


def solution(mesh):
    in_specs = (
        P("cols", "dp", "rows"),
        P("cols", "dp", "rows"),
        P(None, "rows", "cols"),
        P(None, "rows", "cols"),
        P(None, "rows", "cols"),
        P(None, "cols", "rows"),
        P(None, "rows", "cols"),
        P(None, "rows", "cols"),
        P(None, "cols", "rows"),
        P(None, None, "rows"),
    )
    out_specs = (
        P("cols", "dp", "rows"),
        P("cols", "dp", "rows"),
        P(None, "rows", "cols"),
        P(None, "rows", "cols"),
        P(None, "rows", "cols"),
        P(None, "cols", "rows"),
        P(None, "rows", "cols"),
        P(None, "rows", "cols"),
        P(None, "cols", "rows"),
        P(None, None, "rows"),
    )
    return jax.shard_map(shards, mesh=mesh, in_specs=in_specs, out_specs=out_specs, check_vma=False)
```

profile of v0, /device:TPU:0, one launch (start us, length us, event | category | flops | bytes accessed | tf_op | source)
XLA Modules:
  0.0 2536.5 jit_solution(15543703610103134878)
XLA Ops:
  18.2 63.1 %all-gather.17.cloned.1.call-done = bf16[1024,2,768]{2,0,1:T(8,128)(2,1)} async-done(((bf16[256,2,768]{2,0,1:T(8,128)(2,1)}), bf16[1024,2,768]{2,0,1:T(8,128)(2,1)}) %all-gather.17.cloned.1.call-update) | async-done | bytes 3145744 | tf_op jit(solution)/shard_map/all_gather | solution.py:22
  90.1 11.8 reduce-scatter.21.cloned.1.call-done
  121.5 9.3 exponential_reduce_fusion.1
  142.3 11.1 all-gather.19.cloned.1.call-done
  159.3 112.0 %reduce-scatter.23.cloned.1.call-done = f32[256,2,768]{2,0,1:T(8,128)} async-done(((f32[1024,2,768]{2,0,1:T(8,128)}), f32[256,2,768]{2,0,1:T(8,128)}) %reduce-scatter.23.cloned.1.call-update) | async-done | bytes 1572880 | tf_op jit(solution)/shard_map/reduce_scatter | solution.py:43
  282.7 58.0 %all-gather.21.cloned.1.call-done = bf16[1024,2,768]{2,0,1:T(8,128)(2,1)} async-done(((bf16[256,2,768]{2,0,1:T(8,128)(2,1)}), bf16[1024,2,768]{2,0,1:T(8,128)(2,1)}) %all-gather.21.cloned.1.call-update) | async-done | bytes 3145744 | tf_op jit(solution)/shard_map/all_gather | solution.py:22
  340.7 12.6 fusion.17
  353.4 25.1 reduce-scatter.25.cloned.1.call-done
  384.7 15.0 all-gather.23.cloned.1.call-done
  408.6 112.0 %reduce-scatter.27.cloned.1.call-done = f32[256,2,768]{2,0,1:T(8,128)} async-done(((f32[1024,2,768]{2,0,1:T(8,128)}), f32[256,2,768]{2,0,1:T(8,128)}) %reduce-scatter.27.cloned.1.call-update) | async-done | bytes 1572880 | tf_op jit(solution)/shard_map/reduce_scatter | solution.py:43
  528.9 63.7 %all-gather.25.cloned.1.call-done = bf16[1024,2,768]{2,0,1:T(8,128)(2,1)} async-done(((bf16[256,2,768]{2,0,1:T(8,128)(2,1)}), bf16[1024,2,768]{2,0,1:T(8,128)(2,1)}) %all-gather.25.cloned.1.call-update) | async-done | bytes 3145744 | tf_op jit(solution)/shard_map/all_gather | solution.py:22
  599.9 13.3 reduce-scatter.29.cloned.1.call-done
  634.3 9.2 exponential_reduce_fusion
  643.6 9.1 convolution_convert_fusion
  655.0 11.1 all-gather.27.cloned.1.call-done
  674.1 109.9 %reduce-scatter.31.cloned.1.call-done = f32[256,2,768]{2,0,1:T(8,128)} async-done(((f32[1024,2,768]{2,0,1:T(8,128)}), f32[256,2,768]{2,0,1:T(8,128)}) %reduce-scatter.31.cloned.1.call-update) | async-done | bytes 1572880 | tf_op jit(solution)/shard_map/reduce_scatter | solution.py:43
  792.0 58.3 %all-gather.33.cloned.1.call-done = bf16[1024,2,768]{2,0,1:T(8,128)(2,1)} async-done(((bf16[256,2,768]{2,0,1:T(8,128)(2,1)}), bf16[1024,2,768]{2,0,1:T(8,128)(2,1)}) %all-gather.33.cloned.1.call-update) | async-done | bytes 3145744 | tf_op jit(solution)/shard_map/all_gather | solution.py:22
  850.3 9.2 fusion.28
  859.6 55.0 %all-gather.29.cloned.1.call-done = bf16[1024,2,768]{2,0,1:T(8,128)(2,1)} async-done(((bf16[256,2,768]{2,0,1:T(8,128)(2,1)}), bf16[1024,2,768]{2,0,1:T(8,128)(2,1)}) %all-gather.29.cloned.1.call-update) | async-done | bytes 3145744 | tf_op jit(solution)/shard_map/all_gather | solution.py:22
  914.6 15.0 fusion.15
  932.4 29.7 %reduce-scatter.33.cloned.1.call-done = f32[512,2,2048]{2,0,1:T(8,128)} async-done(((f32[1024,2,2048]{2,0,1:T(8,128)}), f32[512,2,2048]{2,0,1:T(8,128)}) %reduce-scatter.33.cloned.1.call-update) | async-done | bytes 8388624 | tf_op jit(solution)/shard_map/reduce_scatter | solution.py:30
  971.6 21.2 all-gather.35.cloned.1.call-done
  992.8 11.7 fusion.14
  1004.6 112.0 %reduce-scatter.39.cloned.1.call-done = f32[256,2,768]{2,0,1:T(8,128)} async-done(((f32[1024,2,768]{2,0,1:T(8,128)}), f32[256,2,768]{2,0,1:T(8,128)}) %reduce-scatter.39.cloned.1.call-update) | async-done | bytes 1572880 | tf_op jit(solution)/shard_map/reduce_scatter | solution.py:43
  1125.7 63.7 %all-gather.37.cloned.1.call-done = bf16[1024,2,768]{2,0,1:T(8,128)(2,1)} async-done(((bf16[256,2,768]{2,0,1:T(8,128)(2,1)}), bf16[1024,2,768]{2,0,1:T(8,128)(2,1)}) %all-gather.37.cloned.1.call-update) | async-done | bytes 3145744 | tf_op jit(solution)/shard_map/all_gather | solution.py:22
  1194.9 9.7 reduce-scatter.41.cloned.1.call-done
  1207.3 11.5 convolution_bitcast_fusion.7
  1218.9 9.6 fusion.3
  1262.2 12.9 all-gather.39.cloned.1.call-done
  1282.4 9.5 all-gather.31.cloned.1.call-done
  1300.8 105.9 %reduce-scatter.47.cloned.1.call-done = f32[256,2,768]{2,0,1:T(8,128)} async-done(((f32[1024,2,768]{2,0,1:T(8,128)}), f32[256,2,768]{2,0,1:T(8,128)}) %reduce-scatter.47.cloned.1.call-update) | async-done | bytes 1572880 | tf_op jit(solution)/shard_map/reduce_scatter | solution.py:43
  1411.6 109.1 %reduce-scatter.35.cloned.1.call-done = f32[256,2,768]{2,0,1:T(8,128)} async-done(((f32[1024,2,768]{2,0,1:T(8,128)}), f32[256,2,768]{2,0,1:T(8,128)}) %reduce-scatter.35.cloned.1.call-update) | async-done | bytes 1572880 | tf_op jit(solution)/shard_map/reduce_scatter | solution.py:43
  1525.7 63.9 %all-gather.41.cloned.1.call-done = bf16[1024,2,768]{2,0,1:T(8,128)(2,1)} async-done(((bf16[256,2,768]{2,0,1:T(8,128)(2,1)}), bf16[1024,2,768]{2,0,1:T(8,128)(2,1)}) %all-gather.41.cloned.1.call-update) | async-done | bytes 3145744 | tf_op jit(solution)/shard_map/all_gather | solution.py:22
  1589.6 9.2 fusion.32
  1598.8 15.6 reduce-scatter.49.cloned.1.call-done
  1622.8 21.2 all-gather.43.cloned.1.call-done
  1644.0 11.2 fusion.16
  1655.4 112.0 %reduce-scatter.51.cloned.1.call-done = f32[256,2,768]{2,0,1:T(8,128)} async-done(((f32[1024,2,768]{2,0,1:T(8,128)}), f32[256,2,768]{2,0,1:T(8,128)}) %reduce-scatter.51.cloned.1.call-update) | async-done | bytes 1572880 | tf_op jit(solution)/shard_map/reduce_scatter | solution.py:43
  1776.2 64.1 %all-gather.45.cloned.1.call-done = bf16[1024,2,768]{2,0,1:T(8,128)(2,1)} async-done(((bf16[256,2,768]{2,0,1:T(8,128)(2,1)}), bf16[1024,2,768]{2,0,1:T(8,128)(2,1)}) %all-gather.45.cloned.1.call-update) | async-done | bytes 3145744 | tf_op jit(solution)/shard_map/all_gather | solution.py:22
  1846.2 9.3 reduce-scatter.53.cloned.1.call-done
  1857.3 9.3 convolution_bitcast_fusion.6
  1866.7 9.4 fusion
  1905.5 13.3 all-gather.47.cloned.1.call-done
  1932.5 10.6 convolution_bitcast_fusion
  1959.7 9.6 convolution_bitcast_fusion.1
  1993.2 44.9 %reduce-scatter.59.cloned.1.call-done = f32[256,2,768]{2,0,1:T(8,128)} async-done(((f32[1024,2,768]{2,0,1:T(8,128)}), f32[256,2,768]{2,0,1:T(8,128)}) %reduce-scatter.59.cloned.1.call-update) | async-done | bytes 1572880 | tf_op jit(solution)/shard_map/reduce_scatter | solution.py:43
  2046.9 78.0 %psum.127 = f32[2,2,768]{2,1,0:T(2,128)} all-reduce(f32[2,2,768]{2,1,0:T(2,128)S(1)} %pad_maximum_fusion.23), channel_id=1, replica_groups=mesh['dp'=4,'rows'=2,'cols'=4] {'dp','cols'}, use_global_device_ids=true, to_apply=%region_53.54 | all-reduce | flops 3072 | bytes 24576 | tf_op jit(solution)/shard_map/psum | solution.py:330
  2124.9 383.7 %all-reduce.3.cloned.1.call-done = (f32[2,768,384]{1,2,0:T(8,128)}, f32[2,768,192]{1,2,0:T(8,128)}, f32[2,768,192]{1,2,0:T(8,128)}, f32[2,384,768]{2,1,0:T(8,128...) async-done(((f32[2,768,384]{1,2,0:T(8,128)}, f32[2,768,192]{1,2,0:T(8,128)}, f32[2,768,192]{1,2,0:T(8,128)}, f32[2,384,768]{2,1,0:T(8,128)}, ...) | async-done | bytes 25952272 | tf_op jit(solution)/shard_map/psum | solution.py:327
  (416 shorter events, 364.8 us)
Async XLA Ops:
  7.2 74.1 %all-gather.17.cloned.1.call-start = ((), (), s32[]{:S(2)}) async-start(), calls=%async_computation.20 | async-start | bytes 3932160 | tf_op jit(solution)/shard_map/all_gather | solution.py:22
  12.8 262.7 %copy-start.58 = (f32[768]{0:T(1024)}, f32[768]{0:T(1024)S(1)}, u32[]{:S(2)}) copy-start(f32[768]{0:T(1024)S(1)} %get-tuple-element.39) | copy-start | bytes 9220
  12.8 513.1 %copy-start.60 = (f32[768]{0:T(1024)}, f32[768]{0:T(1024)S(1)}, u32[]{:S(2)}) copy-start(f32[768]{0:T(1024)S(1)} %get-tuple-element.41) | copy-start | bytes 9220
  15.1 86.8 %reduce-scatter.21.cloned.1.call-start = ((), (), s32[]{:S(2)}) async-start(), calls=%async_computation.21 | async-start | bytes 9437184 | tf_op jit(solution)/shard_map/reduce_scatter | solution.py:30
  88.6 64.8 %all-gather.19.cloned.1.call-start = ((), (), s32[]{:S(2)}) async-start(), calls=%async_computation.22 | async-start | bytes 2359296 | tf_op jit(solution)/shard_map/all_gather | solution.py:26
  142.2 129.1 %reduce-scatter.23.cloned.1.call-start = ((), (), s32[]{:S(2)}) async-start(), calls=%async_computation.23 | async-start | bytes 7864320 | tf_op jit(solution)/shard_map/reduce_scatter | solution.py:43
  159.3 181.5 %all-gather.21.cloned.1.call-start = ((), (), s32[]{:S(2)}) async-start(), calls=%async_computation.24 | async-start | bytes 3932160 | tf_op jit(solution)/shard_map/all_gather | solution.py:22
  273.0 247.6 %copy-start.2 = (f32[256,2,768]{2,0,1:T(8,128)}, f32[256,2,768]{2,0,1:T(8,128)S(1)}, u32[]{:S(2)}) copy-start(f32[256,2,768]{2,0,1:T(8,128)S(1)} %get-tuple-element.58) | copy-start | bytes 4718596
  276.6 101.8 %reduce-scatter.25.cloned.1.call-start = ((), (), s32[]{:S(2)}) async-start(), calls=%async_computation.25 | async-start | bytes 25165824 | tf_op jit(solution)/shard_map/reduce_scatter | solution.py:30
  353.3 46.4 %all-gather.23.cloned.1.call-start = ((), (), s32[]{:S(2)}) async-start(), calls=%async_computation.26 | async-start | bytes 6291456 | tf_op jit(solution)/shard_map/all_gather | solution.py:26
  384.6 136.0 %reduce-scatter.27.cloned.1.call-start = ((), (), s32[]{:S(2)}) async-start(), calls=%async_computation.27 | async-start | bytes 7864320 | tf_op jit(solution)/shard_map/reduce_scatter | solution.py:43
  408.5 120.0 %copy-start.37 = (bf16[1,768,192]{1,2,0:T(8,128)(2,1)S(1)}, bf16[1,768,192]{1,2,0:T(8,128)(2,1)}, u32[]{:S(2)}) copy-start(bf16[1,768,192]{1,2,0:T(8,128)(2,1)} %get-tuple-element.95) | copy-start | bytes 884740
  408.5 120.1 %copy-start.38 = (bf16[1,768,192]{1,2,0:T(8,128)(2,1)S(1)}, bf16[1,768,192]{1,2,0:T(8,128)(2,1)}, u32[]{:S(2)}) copy-start(bf16[1,768,192]{1,2,0:T(8,128)(2,1)} %get-tuple-element.97) | copy-start | bytes 884740
  408.6 184.0 %all-gather.25.cloned.1.call-start = ((), (), s32[]{:S(2)}) async-start(), calls=%async_computation.28 | async-start | bytes 3932160 | tf_op jit(solution)/shard_map/all_gather | solution.py:22
  528.4 84.7 %reduce-scatter.29.cloned.1.call-start = ((), (), s32[]{:S(2)}) async-start(), calls=%async_computation.29 | async-start | bytes 9437184 | tf_op jit(solution)/shard_map/reduce_scatter | solution.py:30
  599.8 66.2 %all-gather.27.cloned.1.call-start = ((), (), s32[]{:S(2)}) async-start(), calls=%async_computation.30 | async-start | bytes 2359296 | tf_op jit(solution)/shard_map/all_gather | solution.py:26
  643.5 563.8 %copy-start.55 = (f32[2,2,2,512]{3,2,1,0:T(2,128)}, f32[2,2,2,512]{3,2,1,0:T(2,128)S(1)}, u32[]{:S(2)}) copy-start(f32[2,2,2,512]{3,2,1,0:T(2,128)S(1)} %log_add_fusion) | copy-start | bytes 49156
  654.9 129.1 %reduce-scatter.31.cloned.1.call-start = ((), (), s32[]{:S(2)}) async-start(), calls=%async_computation.31 | async-start | bytes 7864320 | tf_op jit(solution)/shard_map/reduce_scatter | solution.py:43
  672.0 178.3 %all-gather.33.cloned.1.call-start = ((), (), s32[]{:S(2)}) async-start(), calls=%async_computation.36 | async-start | bytes 3932160 | tf_op jit(solution)/shard_map/all_gather | solution.py:22
  674.1 240.5 %all-gather.29.cloned.1.call-start = ((), (), s32[]{:S(2)}) async-start(), calls=%async_computation.32 | async-start | bytes 3932160 | tf_op jit(solution)/shard_map/all_gather | solution.py:22
  789.3 332.7 %copy-start.64 = (f32[256,2]{0,1:T(2,128)}, f32[256,2]{0,1:T(2,128)S(1)}, u32[]{:S(2)}) copy-start(f32[256,2]{0,1:T(2,128)S(1)} %add_rsqrt_fusion) | copy-start | bytes 6148
  791.8 140.6 %reduce-scatter.37.cloned.1.call-start = ((), (), s32[]{:S(2)}) async-start(), calls=%async_computation.37 | async-start | bytes 12582912 | tf_op jit(solution)/shard_map/reduce_scatter | solution.py:30
  859.6 102.5 %reduce-scatter.33.cloned.1.call-start = ((), (), s32[]{:S(2)}) async-start(), calls=%async_computation.33 | async-start | bytes 25165824 | tf_op jit(solution)/shard_map/reduce_scatter | solution.py:30
  929.6 63.2 %all-gather.35.cloned.1.call-start = ((), (), s32[]{:S(2)}) async-start(), calls=%async_computation.38 | async-start | bytes 12582912 | tf_op jit(solution)/shard_map/all_gather | solution.py:26
  971.6 145.0 %reduce-scatter.39.cloned.1.call-start = ((), (), s32[]{:S(2)}) async-start(), calls=%async_computation.39 | async-start | bytes 7864320 | tf_op jit(solution)/shard_map/reduce_scatter | solution.py:43
  1004.5 184.8 %all-gather.37.cloned.1.call-start = ((), (), s32[]{:S(2)}) async-start(), calls=%async_computation.40 | async-start | bytes 3932160 | tf_op jit(solution)/shard_map/all_gather | solution.py:22
  1125.2 79.4 %reduce-scatter.41.cloned.1.call-start = ((), (), s32[]{:S(2)}) async-start(), calls=%async_computation.41 | async-start | bytes 4718592 | tf_op jit(solution)/shard_map/reduce_scatter | solution.py:30
  1194.9 57.1 %reduce-scatter.45.cloned.1.call-start = ((), (), s32[]{:S(2)}) async-start(), calls=%async_computation.43 | async-start | bytes 2359296 | tf_op jit(solution)/shard_map/reduce_scatter | solution.py:256
  1218.8 36.9 %reduce-scatter.43.cloned.1.call-start = ((), (), s32[]{:S(2)}) async-start(), calls=%async_computation.42 | async-start | bytes 2359296 | tf_op jit(solution)/shard_map/reduce_scatter | solution.py:255
  1245.4 29.6 %all-gather.39.cloned.1.call-start = ((), (), s32[]{:S(2)}) async-start(), calls=%async_computation.44 | async-start | bytes 4718592 | tf_op jit(solution)/shard_map/all_gather | solution.py:26
  1261.5 30.3 %all-gather.31.cloned.1.call-start = ((), (), s32[]{:S(2)}) async-start(), calls=%async_computation.34 | async-start | bytes 6291456 | tf_op jit(solution)/shard_map/all_gather | solution.py:26
  1262.1 144.6 %reduce-scatter.47.cloned.1.call-start = ((), (), s32[]{:S(2)}) async-start(), calls=%async_computation.45 | async-start | bytes 7864320 | tf_op jit(solution)/shard_map/reduce_scatter | solution.py:43
  1282.4 238.4 %reduce-scatter.35.cloned.1.call-start = ((), (), s32[]{:S(2)}) async-start(), calls=%async_computation.35 | async-start | bytes 7864320 | tf_op jit(solution)/shard_map/reduce_scatter | solution.py:43
  1300.7 220.0 %copy-start.8 = (bf16[256,2,768]{2,1,0:T(2,128)(2,1)S(1)}, bf16[256,2,768]{2,1,0:T(2,128)(2,1)}, u32[]{:S(2)}) copy-start(bf16[256,2,768]{2,1,0:T(2,128)(2,1)} %param.11) | copy-start | bytes 2359300
  1300.7 220.0 %copy-start.57 = (f32[768]{0:T(1024)S(1)}, f32[768]{0:T(1024)}, u32[]{:S(2)}) copy-start(f32[768]{0:T(1024)} %get-tuple-element.38) | copy-start | bytes 9220
  1300.7 220.0 %copy-start.65 = (f32[256,2]{0,1:T(2,128)S(1)}, f32[256,2]{0,1:T(2,128)}, u32[]{:S(2)}) copy-start(f32[256,2]{0,1:T(2,128)} %copy-done.64) | copy-start | bytes 6148
  1300.8 220.0 %copy-start.73 = (f32[256,2]{0,1:T(2,128)S(1)}, f32[256,2]{0,1:T(2,128)}, u32[]{:S(2)}) copy-start(f32[256,2]{0,1:T(2,128)} %copy-done.72) | copy-start | bytes 6148
  1300.8 288.8 %all-gather.41.cloned.1.call-start = ((), (), s32[]{:S(2)}) async-start(), calls=%async_computation.46 | async-start | bytes 3932160 | tf_op jit(solution)/shard_map/all_gather | solution.py:22
  1525.4 89.0 %reduce-scatter.49.cloned.1.call-start = ((), (), s32[]{:S(2)}) async-start(), calls=%async_computation.47 | async-start | bytes 12582912 | tf_op jit(solution)/shard_map/reduce_scatter | solution.py:30
  1598.8 45.3 %all-gather.43.cloned.1.call-start = ((), (), s32[]{:S(2)}) async-start(), calls=%async_computation.48 | async-start | bytes 12582912 | tf_op jit(solution)/shard_map/all_gather | solution.py:26
  1622.8 144.6 %reduce-scatter.51.cloned.1.call-start = ((), (), s32[]{:S(2)}) async-start(), calls=%async_computation.49 | async-start | bytes 7864320 | tf_op jit(solution)/shard_map/reduce_scatter | solution.py:43
  1655.3 185.0 %all-gather.45.cloned.1.call-start = ((), (), s32[]{:S(2)}) async-start(), calls=%async_computation.50 | async-start | bytes 3932160 | tf_op jit(solution)/shard_map/all_gather | solution.py:22
  1776.2 79.3 %reduce-scatter.53.cloned.1.call-start = ((), (), s32[]{:S(2)}) async-start(), calls=%async_computation.51 | async-start | bytes 4718592 | tf_op jit(solution)/shard_map/reduce_scatter | solution.py:30
  1845.7 51.8 %reduce-scatter.57.cloned.1.call-start = ((), (), s32[]{:S(2)}) async-start(), calls=%async_computation.53 | async-start | bytes 2359296 | tf_op jit(solution)/shard_map/reduce_scatter | solution.py:256
  1866.6 35.6 %reduce-scatter.55.cloned.1.call-start = ((), (), s32[]{:S(2)}) async-start(), calls=%async_computation.52 | async-start | bytes 2359296 | tf_op jit(solution)/shard_map/reduce_scatter | solution.py:255
  1891.9 26.9 %all-gather.47.cloned.1.call-start = ((), (), s32[]{:S(2)}) async-start(), calls=%async_computation.54 | async-start | bytes 4718592 | tf_op jit(solution)/shard_map/all_gather | solution.py:26
  1905.3 132.8 %reduce-scatter.59.cloned.1.call-start = ((), (), s32[]{:S(2)}) async-start(), calls=%async_computation.55 | async-start | bytes 7864320 | tf_op jit(solution)/shard_map/reduce_scatter | solution.py:43
  1926.0 582.6 %all-reduce.3.cloned.1.call-start = ((), (), s32[]{:S(2)}) async-start(), calls=%async_computation.56 | async-start | bytes 51904512 | tf_op jit(solution)/shard_map/psum | solution.py:327
  (82 other events, 2131.8 us)
Sparse Core Ops, SparseCore 0:
  15.2 66.0 all-gather.16
  88.7 13.1 reduce-scatter.20
  142.3 10.9 all-gather.18
  159.4 111.9 reduce-scatter.22
  276.7 63.9 all-gather.20
  353.4 24.9 reduce-scatter.24
  384.7 14.9 all-gather.22
  408.7 111.9 reduce-scatter.26
  528.6 63.9 all-gather.24
  600.0 13.1 reduce-scatter.28
  655.1 10.9 all-gather.26
  672.1 111.9 reduce-scatter.30
  786.3 63.9 all-gather.32
  852.4 62.1 all-gather.28
  916.8 15.4 reduce-scatter.36
  934.5 27.5 reduce-scatter.32
  971.7 21.0 all-gather.34
  1004.7 111.9 reduce-scatter.38
  1125.3 63.9 all-gather.36
  1195.0 9.5 reduce-scatter.40
  1218.9 10.1 reduce-scatter.44
  1245.5 10.1 reduce-scatter.42
  1261.7 13.3 all-gather.38
  1277.0 14.8 all-gather.30
  1294.8 111.9 reduce-scatter.46
  1409.4 111.2 reduce-scatter.34
  1525.5 63.9 all-gather.40
  1598.9 15.4 reduce-scatter.48
  1622.9 21.0 all-gather.42
  1655.4 111.9 reduce-scatter.50
  1776.3 63.9 all-gather.44
  1845.8 9.5 reduce-scatter.52
  1866.7 10.1 reduce-scatter.56
  1892.0 10.2 reduce-scatter.54
  1905.4 13.3 all-gather.46
  1926.1 111.9 reduce-scatter.58
  2043.4 465.1 all-reduce.2
where the time goes:
time: 2540 us
  waiting for transfers between devices  1930 us (76%)
  matrix products  269 us (11%)
  other arithmetic  132 us (5%)
  blocking collectives  108 us (4%)
  local copies, waits for them, and re-layouts  78.6 us (3%)
    reduce_scatter x8, waiting for transfers between devices, column_reduction(): lax.psum_scatter(jnp.einsum(pattern, left_side, right_side, preferred_ele...  818 us
    all_gather x8, waiting for transfers between devices, col_gather(): return lax.all_gather(blocks_in, 'cols', axis=0, tiled=True)  490 us
    psum x1, waiting for transfers between devices, shards(): lax.psum((stacked[0], stacked[1], stacked[2], stacked[3], stacked[4], sta...  384 us
    reduce_scatter x8, waiting for transfers between devices, row_reduce(): lax.psum_scatter(jnp.einsum(pattern, left_side, right_side, preferred_ele...  117 us
    all_gather x8, waiting for transfers between devices, row_gather(): return lax.all_gather(blocks_in, 'rows', axis=0, tiled=True)  115 us
    psum x1, blocking collectives, shards(): sum_gains = lax.psum(stacked[7], ('dp', 'cols'))  78 us
    dot_general x8, matrix products, row_reduce(): jnp.einsum(pattern, left_side, right_side, preferred_element_type=jnp.flo...  71.2 us
    dot_general x8, matrix products, column_reduction(): jnp.einsum(pattern, left_side, right_side, preferred_element_type=jnp.flo...  66.9 us
  transfers between devices with their start and end apart: 37, of which 35 were waited for; matrix products, arithmetic and copies ran while one was open for 7% of the time, Pallas kernels for 0%

commit v1 on v0

v1 whole, which is shorter than its diff:
```python
import functools

import jax
import jax.numpy as jnp
from jax import lax
from jax.experimental import pallas as pl
from jax.experimental.pallas import tpu as pltpu
from jax.sharding import PartitionSpec as P

HEAD = 96
LAYERS = 2
CHUNKS = 2
EPSILON = 1e-05
ROPE_BASE = 100000.0
NEGATIVE = -1e30
LOW = jnp.bfloat16
FULL = jnp.float32
NT = (((1,), (1,)), ((), ()))
TN = (((0,), (0,)), ((), ()))
ROOM = 56 * 2**20
SCALE = 30


def hop(value, axis, distance):
    size = lax.axis_size(axis)
    return lax.ppermute(value, axis, [(i, i ^ distance) for i in range(size)])


def flip_hi(value):
    return hop(value, "cols", lax.axis_size("cols") // 2)


def flip_core(value):
    return hop(value, "rows", 1)


def low_bits():
    bits, bit = [], 1
    while bit < lax.axis_size("cols") // 2:
        bits.append(bit)
        bit *= 2
    return bits


def group_pair(part):
    bits = low_bits()
    for bit in bits[:-1]:
        part = add_low(part, hop(part, "cols", bit))
    return (part, hop(part, "cols", bits[-1]))


class Order:
    def __init__(self):
        self.last = ()

    def after(self, values):
        return lax.optimization_barrier((values, self.last))[0] if self.last else values

    def mark(self, value):
        self.last = (value,)
        return value

    def join(self, *values):
        self.last = (*self.last, values)


def add_low(left, right):
    return (left.astype(FULL) + right.astype(FULL)).astype(LOW)


def low_dot(left, right):
    return jnp.dot(left, right, preferred_element_type=FULL)


def dot_nt(left, right):
    return lax.dot_general(left, right, NT, preferred_element_type=FULL)


def dot_tn(left, right):
    return lax.dot_general(left, right, TN, preferred_element_type=FULL)


def whole(shape):
    return pl.BlockSpec(shape, lambda *_: (0,) * len(shape))


def far():
    return pl.BlockSpec(memory_space=pl.ANY)


def cost(flops, size, exps=0):
    return pl.CostEstimate(
        flops=int(flops * SCALE), bytes_accessed=int(size * SCALE), transcendentals=0
    )


def limits():
    return pltpu.CompilerParams(vmem_limit_bytes=ROOM)


class Part:
    def __init__(self, array, layer=None, row=0, rows=None, column=0, columns=None):
        self.array, self.layer, self.row, self.column = array, layer, row, column
        self.shape = (rows or array.shape[-2], columns or array.shape[-1])

    def view(self, ref):
        ref = ref if self.layer is None else ref.at[self.layer]
        return ref.at[pl.ds(self.row, self.shape[0]), pl.ds(self.column, self.shape[1])]

    def scratch(self):
        return pltpu.VMEM(self.shape, LOW)


def copies_of(parts, refs, held, sems):
    return [
        pltpu.make_async_copy(part.view(ref), to, sems.at[i])
        for i, (part, ref, to) in enumerate(zip(parts, refs, held))
    ]


def half_dots(left, first, second):
    half = left.shape[1] // 2
    return low_dot(left[:, :half], first) + low_dot(left[:, half:], second)


def turn(value, cosine, sine):
    width = value.shape[1]
    q_width = cosine.shape[1]
    ahead = pltpu.roll(value, width - HEAD // 2, 1)
    behind = pltpu.roll(value, HEAD // 2, 1)
    column = lax.broadcasted_iota(jnp.int32, value.shape, 1)
    other = jnp.where(lax.rem(column, HEAD) < HEAD // 2, ahead, behind)
    is_key = lax.broadcasted_iota(jnp.int32, cosine.shape, 1) < q_width // 2
    query = value[:, :q_width] * cosine + other[:, :q_width] * sine
    rest = value[:, q_width:] * jnp.where(is_key, cosine, 1.0)
    rest = rest + other[:, q_width:] * jnp.where(is_key, sine, 0.0)
    return (query, rest)


def put_norm(refs, outs):
    hidden_ref, left_ref, right_ref, gain_ref = refs
    sum_ref, factor_ref, normed_ref = outs
    hidden = hidden_ref[...].astype(FULL)
    if left_ref is not None:
        hidden = hidden + left_ref[...].astype(FULL) + right_ref[...].astype(FULL)
    factor = lax.rsqrt(jnp.mean(hidden * hidden, axis=-1, keepdims=True) + EPSILON)
    sum_ref[...] = hidden
    factor_ref[...] = factor
    normed_ref[...] = (hidden * factor * gain_ref[...]).astype(LOW)


def put_norm_back(refs, outs):
    grad_ref, left_ref, right_ref, hidden_ref, factor_ref, gain_ref = refs
    sum_ref, low_ref, gain_out_ref = outs
    grad_normed = left_ref[...].astype(FULL) + right_ref[...].astype(FULL)
    factor = factor_ref[...]
    unit = hidden_ref[...] * factor
    grad_unit = grad_normed * gain_ref[...]
    inner = jnp.mean(grad_unit * unit, axis=-1, keepdims=True)
    grad = grad_ref[...] + factor * (grad_unit - unit * inner)
    sum_ref[...] = grad
    low_ref[...] = grad.astype(LOW)
    gain_out_ref[...] = jnp.sum(grad_normed * unit, axis=0, keepdims=True)


def norm_shapes(rows, wide):
    return [((rows, wide), FULL), ((rows, 1), FULL), ((rows, wide), LOW)]


def norm_back_shapes(rows, wide):
    return [((rows, wide), FULL), ((rows, wide), LOW), ((1, wide), FULL)]


def call(kernel, name, operands, parts, outs, scratch, flops, exps=0, scalars=()):
    size = sum(2 * p.shape[0] * p.shape[1] for p in parts) + sum(
        s[0] * s[1] * (4 if k == FULL else 2) for s, k in outs
    )
    return pl.pallas_call(
        kernel,
        grid_spec=pltpu.PrefetchScalarGridSpec(
            num_scalar_prefetch=len(scalars),
            grid=(1,),
            in_specs=[whole(v.shape) for v in operands] + [far()] * len(parts),
            out_specs=[whole(s) for s, _ in outs],
            scratch_shapes=list(scratch)
            + [p.scratch() for p in parts]
            + [pltpu.SemaphoreType.DMA((max(len(parts), 1),))],
        ),
        out_shape=[jax.ShapeDtypeStruct(s, k) for s, k in outs],
        compiler_params=limits(),
        cost_estimate=cost(flops, size, exps),
        name=name,
    )(*scalars, *operands, *[p.array for p in parts])


def take(refs, *counts):
    out, at = [], 0
    for count in counts:
        out.append(refs[at : at + count])
        at += count
    return out + [refs[at:]]


def project_kernel(parts, first, *refs):
    ins, refs = take(refs, 2 if first else 4)
    (cos_ref, sin_ref), hbm, outs, (q_ref, kv_ref), held, (sems,) = take(
        refs, 2, len(parts), 3, 2, len(parts)
    )
    copies = copies_of(parts, hbm, held, sems)
    for copy in copies:
        copy.start()
    put_norm([ins[0], None, None, ins[1]] if first else ins, outs)
    normed_ref = outs[2]
    q_width = cos_ref.shape[1]
    for side in range(2):
        copies[2 * side].wait()
        copies[2 * side + 1].wait()
        projected = half_dots(normed_ref[...], held[2 * side][...], held[2 * side + 1][...])
        query, rest = turn(projected, cos_ref[...], sin_ref[...])
        here = slice(side * q_width, (side + 1) * q_width)
        q_ref[:, here] = query.astype(LOW)
        kv_ref[:, here] = rest.astype(LOW)


def project(hidden, pair, gain, parts, cosine, sine):
    rows, wide = hidden.shape
    both = 2 * cosine.shape[1]
    return call(
        functools.partial(project_kernel, parts, pair is None),
        "project",
        [hidden, *(pair or ()), gain, cosine, sine],
        parts,
        norm_shapes(rows, wide) + [((rows, both), LOW)] * 2,
        [],
        4 * rows * wide * both,
    )


def score(key, query, kind, core):
    raw = dot_nt(key, query) * HEAD ** (-0.5)
    if kind == "own":
        key_pos = lax.broadcasted_iota(jnp.int32, raw.shape, 0)
        query_pos = lax.broadcasted_iota(jnp.int32, raw.shape, 1)
        raw = jnp.where(query_pos >= key_pos, raw, NEGATIVE)
    if kind == "sib":
        raw = jnp.where(core == 1, raw, NEGATIVE)
    return raw


def kinds_of(chunks):
    return ["all"] * (2 * chunks - 2) + ["own", "sib"]


def attend_kernel(chunks, parts, core_ref, q_ref, *refs):
    kv_refs, refs = refs[: 2 * chunks], refs[2 * chunks :]
    count = len(parts)
    hbm, (att_ref, lse_ref, part_ref) = refs[:count], refs[count : count + 3]
    held, sems = refs[count + 3 : -1], refs[-1]
    copies = copies_of(parts, hbm, held, sems)
    for copy in copies:
        copy.start()
    core = core_ref[0]
    q_width = q_ref.shape[1] // 2
    kv_width = q_width // 2
    heads = q_width // HEAD
    for h in range(2 * heads):
        group = (h // heads) * q_width + (h % heads) // 2 * HEAD
        mine = slice(h * HEAD, (h + 1) * HEAD)
        query = q_ref[:, mine]
        scores = [
            score(ref[:, group : group + HEAD], query, kind, core)
            for ref, kind in zip(kv_refs, kinds_of(chunks))
        ]
        highest = functools.reduce(
            jnp.maximum, [jnp.max(s, axis=0, keepdims=True) for s in scores]
        )
        exps = [jnp.exp(s - highest) for s in scores]
        total = sum(jnp.sum(e, axis=0, keepdims=True) for e in exps)
        share = 1.0 / total
        lse_ref[h : h + 1, :] = highest + jnp.log(total)
        spot = slice(group + kv_width, group + kv_width + HEAD)
        att = sum(dot_tn((e * share).astype(LOW), ref[:, spot]) for e, ref in zip(exps, kv_refs))
        att_ref[:, mine] = att.astype(LOW)
    for copy in copies:
        copy.wait()
    wide = part_ref.shape[1]
    for side in range(2):
        columns = slice(side * wide // 2, (side + 1) * wide // 2)
        total = low_dot(att_ref[:, :q_width], held[side][...])
        total = total + low_dot(att_ref[:, q_width:], held[2 + side][...])
        part_ref[:, columns] = total.astype(LOW)


def attend(core, query, kvs, parts):
    rows, both = query.shape
    heads = both // HEAD
    wide = 2 * parts[0].shape[1]
    chunks = len(kvs) // 2
    shapes = [(rows, both), (heads, rows), (rows, wide)]
    operands = [query] + list(kvs)
    return pl.pallas_call(
        functools.partial(attend_kernel, chunks, parts),
        grid_spec=pltpu.PrefetchScalarGridSpec(
            num_scalar_prefetch=1,
            grid=(1,),
            in_specs=[whole(v.shape) for v in operands] + [far()] * len(parts),
            out_specs=[whole(s) for s in shapes],
            scratch_shapes=[p.scratch() for p in parts] + [pltpu.SemaphoreType.DMA((len(parts),))],
        ),
        out_shape=[
            jax.ShapeDtypeStruct(s, FULL if i == 1 else LOW) for i, s in enumerate(shapes)
        ],
        compiler_params=limits(),
        cost_estimate=cost(
            8 * heads * rows * rows * len(kvs) * 128 + 2 * rows * both * wide,
            2 * both * wide + 4 * rows * wide,
            heads * rows * rows * len(kvs),
        ),
        name="attend",
    )(core, *operands, *[p.array for p in parts])


def attend_back_kernel(chunks, has_held, parts, core_ref, *refs):
    ins, (q_ref, lse_ref), refs = take(refs, 6, 2)
    kv_refs, refs = refs[: 2 * chunks], refs[2 * chunks :]
    held_refs, refs = (refs[:2], refs[2:]) if has_held else (None, refs)
    count = len(parts)
    hbm, outs, (dq_ref,), out_refs, (grad_ref,), held, (sems,) = take(
        refs, count, 3, 1, 2 * chunks, 1, count
    )
    copies = copies_of(parts, hbm, held, sems)
    for copy in copies:
        copy.start()
    put_norm_back(ins, outs)
    g_ref = outs[1]
    core = core_ref[0]
    q_width = q_ref.shape[1] // 2
    kv_width = q_width // 2
    heads = q_width // HEAD
    half = g_ref.shape[1] // 2
    scale = HEAD ** (-0.5)
    for copy in copies:
        copy.wait()
    for side in range(2):
        grad = dot_nt(g_ref[:, :half], held[2 * side][...])
        grad = grad + dot_nt(g_ref[:, half:], held[2 * side + 1][...])
        grad_ref[:, side * q_width : (side + 1) * q_width] = grad.astype(LOW)
    for first in range(0, 2 * heads, 2):
        group = (first // heads) * q_width + (first % heads) // 2 * HEAD
        key_spot = slice(group, group + HEAD)
        value_spot = slice(group + kv_width, group + kv_width + HEAD)
        key_sums, value_sums = [0.0] * len(kv_refs), [0.0] * len(kv_refs)
        for h in (first, first + 1):
            mine = slice(h * HEAD, (h + 1) * HEAD)
            query, grad, lse = q_ref[:, mine], grad_ref[:, mine], lse_ref[h : h + 1, :]
            probs = [
                jnp.exp(score(ref[:, key_spot], query, kind, core) - lse)
                for ref, kind in zip(kv_refs, kinds_of(chunks))
            ]
            prob_grads = [dot_nt(ref[:, value_spot], grad) for ref in kv_refs]
            delta = sum(
                jnp.sum(p * d, axis=0, keepdims=True) for p, d in zip(probs, prob_grads)
            )
            query_grad = 0.0
            for i, (p, d, ref) in enumerate(zip(probs, prob_grads, kv_refs)):
                score_grad = (p * (d - delta)).astype(LOW)
                query_grad = query_grad + dot_tn(score_grad, ref[:, key_spot])
                key_sums[i] = key_sums[i] + low_dot(score_grad, query)
                value_sums[i] = value_sums[i] + low_dot(p.astype(LOW), grad)
            dq_ref[:, mine] = query_grad * scale
        for i, out_ref in enumerate(out_refs):
            for spot, value in ((key_spot, key_sums[i] * scale), (value_spot, value_sums[i])):
                if has_held and i >= 2 * chunks - 2:
                    value = value + held_refs[i - 2 * chunks + 2][:, spot]
                out_ref[:, spot] = value.astype(out_ref.dtype)


def attend_back(core, norm_ins, query, lse, kvs, held, parts):
    rows, both = query.shape
    heads = both // HEAD
    wide = norm_ins[0].shape[1]
    chunks = len(kvs) // 2
    return call(
        functools.partial(attend_back_kernel, chunks, held is not None, parts),
        "attend_back",
        [*norm_ins, query, lse, *kvs, *(held or ())],
        parts,
        norm_back_shapes(rows, wide) + [((rows, both), FULL)] * (2 * chunks + 1),
        [pltpu.VMEM((rows, both), LOW)],
        20 * heads * rows * rows * len(kvs) * 128 + 2 * rows * both * wide,
        heads * rows * rows * len(kvs),
        (core,),
    )


def project_back_kernel(parts, dq_ref, own_ref, came_ref, cos_ref, sin_ref, *refs):
    count = len(parts)
    hbm, (proj_ref, part_ref), held, sems = refs[:count], refs[count : count + 2], refs[count + 2 : -1], refs[-1]
    copies = copies_of(parts, hbm, held, sems)
    for copy in copies:
        copy.start()
    q_width = cos_ref.shape[1]
    half = part_ref.shape[1] // 2
    for side in range(2):
        here = slice(side * q_width, (side + 1) * q_width)
        rest = own_ref[:, here] + came_ref[:, here].astype(FULL)
        flat = jnp.concatenate([dq_ref[:, here], rest], axis=1)
        query, rest = turn(flat, cos_ref[...], -sin_ref[...])
        start = 2 * side * q_width
        proj_ref[:, start : start + q_width] = query.astype(LOW)
        proj_ref[:, start + q_width : start + 2 * q_width] = rest.astype(LOW)
    for copy in copies:
        copy.wait()
    for side in range(2):
        total = dot_nt(proj_ref[:, : 2 * q_width], held[side][...])
        total = total + dot_nt(proj_ref[:, 2 * q_width :], held[2 + side][...])
        part_ref[:, side * half : (side + 1) * half] = total.astype(LOW)


def project_back(dq, own, came, cosine, sine, parts):
    rows, both = dq.shape
    wide = 2 * parts[0].shape[0]
    operands = [dq, own, came, cosine, sine]
    shapes = [(rows, 2 * both), (rows, wide)]
    return pl.pallas_call(
        functools.partial(project_back_kernel, parts),
        in_specs=[whole(v.shape) for v in operands] + [far()] * len(parts),
        out_specs=[whole(s) for s in shapes],
        out_shape=[jax.ShapeDtypeStruct(s, LOW) for s in shapes],
        grid=(1,),
        scratch_shapes=[p.scratch() for p in parts] + [pltpu.SemaphoreType.DMA((len(parts),))],
        compiler_params=limits(),
        cost_estimate=cost(4 * rows * wide * both, 4 * wide * both + 12 * rows * both),
        name="project_back",
    )(*operands, *[p.array for p in parts])


def ff_kernel(parts, *refs):
    ins, hbm, outs, (gate_ref, up_ref, inner_ref, part_ref), held, (sems,) = take(
        refs, 4, len(parts), 3, 4, len(parts)
    )
    copies = copies_of(parts, hbm, held, sems)
    for copy in copies:
        copy.start()
    put_norm(ins, outs)
    tokens = outs[2][...]
    ff = gate_ref.shape[1] // 2
    half = part_ref.shape[1] // 2
    for side in range(2):
        for copy in copies[4 * side : 4 * side + 4]:
            copy.wait()
        g1_ref, g2_ref, u1_ref, u2_ref = held[4 * side : 4 * side + 4]
        here = slice(side * ff, (side + 1) * ff)
        gate = half_dots(tokens, g1_ref[...], g2_ref[...])
        up = half_dots(tokens, u1_ref[...], u2_ref[...])
        gate_ref[:, here] = gate.astype(LOW)
        up_ref[:, here] = up.astype(LOW)
        inner_ref[:, here] = (gate * jax.nn.sigmoid(gate) * up).astype(LOW)
    for copy in copies[8:]:
        copy.wait()
    for side in range(2):
        total = low_dot(inner_ref[:, :ff], held[8 + side][...])
        total = total + dot_nt(inner_ref[:, ff:], held[10 + side][...])
        part_ref[:, side * half : (side + 1) * half] = total.astype(LOW)


def feed_forward(hidden, pair, gain, pair_parts, down_parts):
    rows, wide = hidden.shape
    ff = down_parts[0].shape[0]
    parts = pair_parts + down_parts
    return call(
        functools.partial(ff_kernel, parts),
        "feed_forward",
        [hidden, *pair, gain],
        parts,
        norm_shapes(rows, wide) + [((rows, 2 * ff), LOW)] * 3 + [((rows, wide), LOW)],
        [],
        12 * rows * wide * ff,
        2 * rows * ff,
    )


def ff_back_kernel(parts, first, *refs):
    ins, (gate_ref, up_ref), hbm, refs = take(refs, 1 if first else 6, 2, len(parts))
    outs, (grad_ref, part_ref), held, (sems,) = take(refs, 0 if first else 3, 2, len(parts))
    copies = copies_of(parts, hbm, held, sems)
    for copy in copies:
        copy.start()
    if first:
        x_ref = ins[0]
    else:
        put_norm_back(ins, outs)
        x_ref = outs[1]
    half = x_ref.shape[1] // 2
    ff = gate_ref.shape[1] // 2
    for side in range(2):
        for copy in copies[2 * side : 2 * side + 2]:
            copy.wait()
        here = slice(side * ff, (side + 1) * ff)
        times = low_dot if side else dot_nt
        inner_grad = times(x_ref[:, :half], held[2 * side][...])
        inner_grad = inner_grad + times(x_ref[:, half:], held[2 * side + 1][...])
        gate, up = gate_ref[:, here].astype(FULL), up_ref[:, here].astype(FULL)
        sigma = jax.nn.sigmoid(gate)
        start = 2 * side * ff
        grad_ref[:, start : start + ff] = (
            inner_grad * up * sigma * (1.0 + gate * (1.0 - sigma))
        ).astype(LOW)
        grad_ref[:, start + ff : start + 2 * ff] = (inner_grad * gate * sigma).astype(LOW)
    for copy in copies[4:]:
        copy.wait()
    for side in range(2):
        total = 0.0
        for i in range(4):
            grad = grad_ref[:, i * ff : (i + 1) * ff]
            total = total + dot_nt(grad, held[4 + 2 * i + side][...])
        part_ref[:, side * half : (side + 1) * half] = total.astype(LOW)


def feed_back(norm_ins, gate, up, pair_parts, down_parts):
    rows, wide = norm_ins[0].shape
    ff = down_parts[0].shape[0]
    g, u = (0, 1, 4, 5), (2, 3, 6, 7)
    order = [g[0], g[1], u[0], u[1], g[2], g[3], u[2], u[3]]
    parts = down_parts + [pair_parts[i] for i in order]
    first = len(norm_ins) == 1
    return call(
        functools.partial(ff_back_kernel, parts, first),
        "feed_back",
        [*norm_ins, gate, up],
        parts,
        ([] if first else norm_back_shapes(rows, wide))
        + [((rows, 4 * ff), LOW), ((rows, wide), LOW)],
        [],
        12 * rows * wide * ff,
        2 * rows * ff,
    )


def ff_weights_kernel(chunks, split, *refs):
    xb_refs, bb_refs, dg_refs, in_refs = [refs[i * chunks : (i + 1) * chunks] for i in range(4)]
    first_ref, second_ref, turned_ref = refs[4 * chunks :]
    j = pl.program_id(0)
    rows = xb_refs[0].shape[0]
    half = first_ref.shape[0]

    def take(x_refs):
        for i, ref in enumerate(x_refs):
            turned_ref[:, i * rows : (i + 1) * rows] = ref[...].T

    def work(y_refs):
        grads = jnp.concatenate([ref[...] for ref in y_refs], axis=0)
        second_ref[...] = low_dot(turned_ref[half:, :], grads).astype(LOW)
        first_ref[...] = low_dot(turned_ref[:half, :], grads).astype(LOW)

    @pl.when(j == 0)
    def _():
        take(xb_refs)

    @pl.when(j == split)
    def _():
        take(bb_refs)

    @pl.when(j < split)
    def _():
        work(dg_refs)

    @pl.when(j >= split)
    def _():
        work(in_refs)


def ff_weights(all_b, branch_b, grads, inner):
    chunks = len(all_b)
    rows, wide = all_b[0].shape
    ff = inner[0].shape[1] // 2
    step = min(512, ff)
    n = ff // step
    split = 4 * n
    full = whole((rows, wide))
    grad = pl.BlockSpec((rows, step), lambda j: (0, jnp.minimum(j, split - 1)))
    last = pl.BlockSpec((rows, step), lambda j: (0, jnp.maximum(j - split, 0)))

    def place(j):
        k = j - split
        early = jnp.where(j < 2 * n, j, j + n)
        late = jnp.where(k < n, 2 * n + k, 4 * n + k)
        return (0, jnp.where(j < split, early, late))

    out = pl.BlockSpec((wide // 2, step), place)
    shape = jax.ShapeDtypeStruct((wide // 2, 6 * ff), LOW)
    return pl.pallas_call(
        functools.partial(ff_weights_kernel, chunks, split),
        grid=(6 * n,),
        in_specs=[full] * (2 * chunks) + [grad] * chunks + [last] * chunks,
        out_specs=[out, out],
        scratch_shapes=[pltpu.VMEM((wide, rows * chunks), LOW)],
        out_shape=[shape, shape],
        compiler_params=limits(),
        cost_estimate=cost(12 * chunks * rows * wide * ff, 12 * wide * ff + 8 * chunks * rows * wide),
        name="ff_weights",
    )(*all_b, *branch_b, *grads, *inner)


def in_weights_kernel(chunks, *refs):
    xa_refs, ba_refs, dp_refs, at_refs = [refs[i * chunks : (i + 1) * chunks] for i in range(4)]
    first_ref, second_ref = refs[4 * chunks :]
    width = dp_refs[0].shape[1] // 2
    q_width = at_refs[0].shape[1] // 2
    half = first_ref.shape[0]
    for x_refs, y_refs, size, base in (
        (xa_refs, dp_refs, width, 0),
        (ba_refs, at_refs, q_width, width),
    ):
        turned = jnp.concatenate([ref[...].T for ref in x_refs], axis=1)
        for side in range(2):
            grads = jnp.concatenate(
                [ref[:, side * size : (side + 1) * size] for ref in y_refs], axis=0
            )
            start = side * (width + q_width) + base
            second_ref[:, start : start + size] = low_dot(turned[half:], grads).astype(LOW)
            first_ref[:, start : start + size] = low_dot(turned[:half], grads).astype(LOW)


def in_weights(all_a, branch_a, grads, attended):
    chunks = len(all_a)
    rows, wide = all_a[0].shape
    width = grads[0].shape[1] + attended[0].shape[1]
    operands = list(all_a) + list(branch_a) + list(grads) + list(attended)
    shape = (wide // 2, width)
    return pl.pallas_call(
        functools.partial(in_weights_kernel, chunks),
        grid=(1,),
        in_specs=[whole(v.shape) for v in operands],
        out_specs=[whole(shape)] * 2,
        out_shape=[jax.ShapeDtypeStruct(shape, LOW)] * 2,
        compiler_params=limits(),
        cost_estimate=cost(
            2 * chunks * rows * wide * width, 2 * wide * width + 4 * chunks * rows * wide
        ),
        name="in_weights",
    )(*operands)


def role_sum_kernel(row_ref, side_ref, left_ref, right_ref, *outs):
    step = pl.program_id(0)
    total = (left_ref[...].astype(FULL) + right_ref[...].astype(FULL)).astype(LOW)
    for i, out_ref in enumerate(outs):

        @pl.when(step // 2 == i)
        def _(out_ref=out_ref):
            out_ref[...] = total


def role_sums(place, left, right):
    rows, both = left.shape[0] // 4, left.shape[1]
    width = both // 2
    picks = [pick for role in ROLES for pick in role]
    row = place ^ jnp.array([m for m, _ in picks], jnp.int32)
    side = jnp.array([s for _, s in picks], jnp.int32)
    block = pl.BlockSpec((rows, width), lambda i, r, s: (r[i], s[i]))

    def out(k):
        return pl.BlockSpec((rows, width), lambda i, r, s: (jnp.where(i > 2 * k, 1, 0), 0))

    return pl.pallas_call(
        role_sum_kernel,
        grid_spec=pltpu.PrefetchScalarGridSpec(
            num_scalar_prefetch=2,
            grid=(8,),
            in_specs=[block, block],
            out_specs=[out(k) for k in range(4)],
        ),
        out_shape=[jax.ShapeDtypeStruct((2 * rows, width), LOW)] * 4,
        compiler_params=limits(),
        cost_estimate=cost(0, 12 * rows * both),
        name="role_sums",
    )(row, side, left, right)


def cut_kernel(place_ref, gate_ref, up_ref, down_ref, *refs):
    outs, turned_ref = refs[:3], refs[3]
    turned_ref[...] = down_ref[...].T
    outs[0][...] = gate_ref[...]
    outs[1][...] = up_ref[...]
    rows = outs[2].shape[0]
    start = pl.multiple_of(place_ref[0] * rows, rows)
    outs[2][...] = turned_ref[pl.ds(start, rows), :]


def cut_ff(place, layer, gate, up, down):
    wide, ff = gate.shape[1:]
    rows = wide // lax.axis_size("dp")
    block = pl.BlockSpec((None, rows, ff), lambda i, p: (layer, p[0], 0))
    return pl.pallas_call(
        cut_kernel,
        grid_spec=pltpu.PrefetchScalarGridSpec(
            num_scalar_prefetch=1,
            grid=(1,),
            in_specs=[block, block, pl.BlockSpec((None, ff, wide), lambda i, p: (layer, 0, 0))],
            out_specs=[whole((rows, ff))] * 3,
            scratch_shapes=[pltpu.VMEM((wide, ff), LOW)],
        ),
        out_shape=[jax.ShapeDtypeStruct((rows, ff), LOW)] * 3,
        compiler_params=limits(),
        cost_estimate=cost(0, 4 * wide * ff),
        name="cut_ff",
    )(place, gate, up, down)


def pick_kernel(hi_ref, block_ref, mine_ref, other_ref):
    first, second = block_ref[:, 0, :], block_ref[:, 1, :]
    mine_ref[...] = jnp.where(hi_ref[0] == 0, first, second)
    other_ref[...] = jnp.where(hi_ref[0] == 0, second, first)


def pick(hi, block):
    rows, _, width = block.shape
    return pl.pallas_call(
        pick_kernel,
        grid_spec=pltpu.PrefetchScalarGridSpec(
            num_scalar_prefetch=1,
            grid=(1,),
            in_specs=[whole(block.shape)],
            out_specs=[whole((rows, width))] * 2,
        ),
        out_shape=[jax.ShapeDtypeStruct((rows, width), LOW)] * 2,
        compiler_params=limits(),
        cost_estimate=cost(0, 8 * rows * width),
        name="pick",
    )(hi.astype(jnp.int32).reshape(1), block)


def spread_ff_kernel(spots, place_ref, *refs):
    count = len(spots)
    gate_refs, up_refs, down_refs = [refs[i * count : (i + 1) * count] for i in range(3)]
    outs, held_ref = refs[-4:-1], refs[-1]
    put_parts(place_ref, gate_refs, spots, outs[0].at[0])
    put_parts(place_ref, up_refs, spots, outs[1].at[0])
    put_parts(place_ref, down_refs, spots, held_ref)
    outs[2][0] = held_ref[...].T


def flatten(pieces):
    parts, spots = [], []
    for m, piece in enumerate(pieces):
        piece = piece if isinstance(piece, tuple) else (piece,)
        for i, part in enumerate(piece):
            if not isinstance(part, tuple):
                part = (part, 0, part.shape[0])
            parts.append((part[0], part[1] // part[2], part[2]))
            spots.append((m, i, len(piece)))
    return (parts, spots)


def put_parts(place_ref, refs, spots, out_ref):
    for ref, (m, i, count) in zip(refs, spots):
        rows = ref.shape[0]
        start = pl.multiple_of((place_ref[0] ^ m) * (rows * count) + i * rows, rows)
        out_ref[pl.ds(start, rows), :] = ref[...].astype(FULL)


def spread_ff(place, pieces, layer, earlier):
    pieces, spots = flatten(pieces)
    count = len(pieces)
    rows, wide = pieces[0][2], pieces[0][0].shape[1]
    ff = wide // 3
    step = min(256, ff)
    steps = ff // step
    tall = rows * count

    def block(k, at):
        return pl.BlockSpec((rows, step), lambda j, p: (at, j + k * steps))

    in_specs = [block(k, at) for k in range(3) for _, at, _ in pieces]
    operands = [array for array, _, _ in pieces] * 3
    aliases = {}
    if earlier is not None:
        aliases = {1 + len(operands) + i: i for i in range(3)}
        in_specs += [pl.BlockSpec(memory_space=pl.ANY)] * 3
        operands += list(earlier)

    def kernel(place_ref, *refs):
        refs = refs[: 3 * count] + refs[len(operands) :]
        spread_ff_kernel(spots, place_ref, *refs)

    tall_out = pl.BlockSpec((1, tall, step), lambda j, p: (layer, 0, j))
    flat_out = pl.BlockSpec((1, step, tall), lambda j, p: (layer, j, 0))
    return pl.pallas_call(
        kernel,
        grid_spec=pltpu.PrefetchScalarGridSpec(
            num_scalar_prefetch=1,
            grid=(steps,),
            in_specs=in_specs,
            out_specs=[tall_out, tall_out, flat_out],
            scratch_shapes=[pltpu.VMEM((tall, step), FULL)],
        ),
        out_shape=[
            jax.ShapeDtypeStruct((LAYERS, tall, ff), FULL),
            jax.ShapeDtypeStruct((LAYERS, tall, ff), FULL),
            jax.ShapeDtypeStruct((LAYERS, ff, tall), FULL),
        ],
        input_output_aliases=aliases,
        compiler_params=limits(),
        cost_estimate=cost(0, 18 * tall * ff),
        name="spread_ff",
    )(place, *operands)


def spread_in(place, pieces, layer, earlier, q_width):
    pieces, spots = flatten(pieces)
    count = len(pieces)
    rows, width = pieces[0][2], pieces[0][0].shape[1]
    tall = rows * count
    kv_width = q_width // 2
    operands = [array for array, _, _ in pieces]
    in_specs = [pl.BlockSpec((rows, width), lambda j, p, at=at: (at, 0)) for _, at, _ in pieces]
    aliases = {}
    if earlier is not None:
        aliases = {1 + count + i: i for i in range(4)}
        in_specs = in_specs + [pl.BlockSpec(memory_space=pl.ANY)] * 4
        operands += list(earlier)

    def kernel(place_ref, *refs):
        piece_refs, (q_ref, k_ref, v_ref, o_ref, held_ref) = refs[:count], refs[len(operands) :]
        put_parts(place_ref, piece_refs, spots, held_ref)
        at = 0
        for out_ref, size in ((q_ref, q_width), (k_ref, kv_width), (v_ref, kv_width)):
            out_ref[0] = held_ref[:, at : at + size]
            at += size
        o_ref[0] = held_ref[:, at:].T

    sizes = [(tall, q_width), (tall, kv_width), (tall, kv_width), (q_width, tall)]
    return pl.pallas_call(
        kernel,
        grid_spec=pltpu.PrefetchScalarGridSpec(
            num_scalar_prefetch=1,
            grid=(1,),
            in_specs=in_specs,
            out_specs=[pl.BlockSpec((1,) + s, lambda j, p: (layer, 0, 0)) for s in sizes],
            scratch_shapes=[pltpu.VMEM((tall, width), FULL)],
        ),
        out_shape=[jax.ShapeDtypeStruct((LAYERS,) + s, FULL) for s in sizes],
        input_output_aliases=aliases,
        compiler_params=limits(),
        cost_estimate=cost(0, 6 * tall * width),
        name="spread_in",
    )(place, *operands)


def gather_kernel(count, tops, place_ref, *refs):
    piece_refs, out_ref = refs[:count], refs[count]
    for m, ref in enumerate(piece_refs):
        row, part_row = 0, 0
        for size in tops:
            part = size // count
            start = pl.multiple_of(row + (place_ref[0] ^ m) * part, part)
            out_ref[pl.ds(start, part), :] = ref[part_row : part_row + part, :]
            row += size
            part_row += part


def gather_pieces(place, pieces, tops):
    count = len(pieces)
    shape = (sum(tops), pieces[0].shape[1])
    return pl.pallas_call(
        functools.partial(gather_kernel, count, tops),
        grid_spec=pltpu.PrefetchScalarGridSpec(
            num_scalar_prefetch=1,
            grid=(1,),
            in_specs=[whole(p.shape) for p in pieces],
            out_specs=whole(shape),
        ),
        out_shape=jax.ShapeDtypeStruct(shape, LOW),
        compiler_params=limits(),
        cost_estimate=cost(0, 4 * shape[0] * shape[1]),
        name="gather_pieces",
    )(place, *pieces)


def cut(weight, layer, place):
    rows = weight.shape[1] // lax.axis_size("dp")
    start = (jnp.int32(layer), place * rows, jnp.int32(0))
    return lax.dynamic_slice(weight, start, (1, rows, weight.shape[2]))[0]


class Group:
    def __init__(self, piece, tops, place):
        self.piece, self.tops, self.place = piece, tops, place
        self.count = lax.axis_size("dp")
        self.even = all(size // self.count % 16 == 0 for size in tops)

    def fetch(self, order):
        self.piece = flip_hi(order.after(self.piece))

    def gather(self, order):
        order.join(self.piece)
        piece = order.after(self.piece)
        if len(self.tops) == 1:
            self.first = lax.all_gather(piece, "dp", axis=0, tiled=True)
            return
        pieces = lax.all_gather(piece, "dp", axis=0)
        at, rows = 0, []
        for size in self.tops:
            part = size // self.count
            rows.append(pieces[:, at : at + part].reshape(size, -1))
            at += part
        self.first = jnp.concatenate(rows, axis=0)

    def cross(self, order):
        self.halves = (self.first, flip_core(self.first))

    def spread(self, order):
        order.join(self.piece)
        if self.even:
            piece = order.after(self.piece)
            self.pieces = [piece] + [hop(piece, "dp", m) for m in (1, 2)]
        else:
            self.gather(order)

    def spread_on(self, order):
        if self.even:
            order.join(*self.pieces[1:])
            piece = order.after(self.pieces[0])
            self.pieces += [hop(piece, "dp", m) for m in range(len(self.pieces), self.count)]

    def collect(self, order):
        if self.even:
            spot = self.place.astype(jnp.int32).reshape(1)
            order.join(*self.pieces[1:])
            pieces = [order.after(self.pieces[0])] + self.pieces[1:]
            self.first = gather_pieces(spot, pieces, self.tops)
        order.mark(self.first)
        self.cross(order)

    def done(self, order):
        order.join(self.halves[1])


def in_groups(layer, w_in, w_out, place, packed):
    in_piece, out_piece = cut(w_in, layer, place), cut(w_out, layer, place)
    wide, q_width = w_in.shape[1], w_out.shape[1]
    if packed and w_in.shape[2] == w_out.shape[2]:
        piece = jnp.concatenate([in_piece, out_piece], axis=0)
        return [Group(piece, (wide, q_width), place)]
    return [Group(in_piece, (wide,), place), Group(out_piece, (q_width,), place)]


ROLES = (((1, 0), (3, 0)), ((2, 1), (3, 1)), ((2, 0), (1, 1)), ((0, 0), (0, 1)))


class Sum:
    def __init__(self, parts, place):
        self.first, self.last = parts
        self.place = place
        self.even = lax.axis_size("dp") == 4

    def flip(self, order):
        self.came = flip_core(order.after(self.last))

    def start(self, order):
        if not self.even:
            total = add_low(self.first, self.came)
            width = total.shape[1] // 2
            self.own = lax.psum_scatter(total[:, :width], "dp", scatter_dimension=0, tiled=True)
            self.other = lax.psum_scatter(total[:, width:], "dp", scatter_dimension=0, tiled=True)
            return
        order.join(self.came)
        spot = self.place.astype(jnp.int32).reshape(1)
        roles = role_sums(spot, order.after(self.first), self.came)
        to_x, to_y, self.on, self.keep = order.mark(roles)
        self.from_x, self.from_y = hop(to_x, "dp", 1), hop(to_y, "dp", 2)

    def arrived(self, order):
        if self.even:
            order.join(self.from_x, self.from_y)

    def second(self, order):
        if not self.even:
            return
        rows = self.on.shape[0] // 2
        on, keep, from_x, from_y = order.after((self.on, self.keep, self.from_x, self.from_y))
        to_y = add_low(on[:rows], from_x[rows:])
        to_x = add_low(on[rows:], from_y[rows:])
        self.own = add_low(keep[:rows], from_x[:rows])
        self.other = add_low(keep[rows:], from_y[:rows])
        order.mark((to_x, to_y))
        self.to_own, self.to_other = hop(to_y, "dp", 2), hop(to_x, "dp", 1)

    def third(self, order):
        if self.even:
            order.join(self.to_own)
            other, came = order.after((self.other, self.to_other))
            self.other = order.mark(add_low(other, came))

    def across(self, order):
        self.far = flip_hi(order.after(self.other))

    def fourth(self, order):
        if self.even:
            own, came, far = order.after((self.own, self.to_own, self.far))
            total = (own.astype(FULL) + came.astype(FULL) + far.astype(FULL)).astype(LOW)
        else:
            total = add_low(self.own, self.far)
        self.total = order.mark(total)

    def near(self, order):
        count = lax.axis_size("dp")
        total = order.after(self.total)
        if not self.even:
            self.pieces = [total] + [hop(total, "dp", m) for m in range(1, count)]
            return
        rows = total.shape[0] // 2
        self.mine = (total[:rows], total[rows:])
        self.beside = [hop(self.mine[0], "dp", 1), hop(self.mine[1], "dp", 2)]

    def fifth(self, order):
        if not self.even:
            return
        top, bottom = self.mine
        order.join(*self.beside)
        near_x, near_y = order.after(tuple(self.beside))
        tops = order.mark(jnp.concatenate([top, near_x], axis=0))
        bottoms = order.mark(jnp.concatenate([bottom, near_y], axis=0))
        tops, bottoms = hop(tops, "dp", 2), hop(bottoms, "dp", 1)
        rows = top.shape[0]
        self.pieces = [
            (top, bottom),
            (near_x, (bottoms, 0, rows)),
            ((tops, 0, rows), near_y),
            ((tops, rows, rows), (bottoms, rows, rows)),
        ]

    def done(self, order):
        order.join(*(part for piece in self.pieces if isinstance(piece, tuple) for part in piece))


def rope_tables(positions, width):
    indices = jnp.arange(HEAD // 2, dtype=FULL)
    inverse = ROPE_BASE ** (-2.0 * indices / HEAD)
    angles = positions.astype(FULL)[:, None] * inverse[None, :]
    cosine, sine = jnp.cos(angles), jnp.sin(angles)
    heads = width // HEAD
    return (
        jnp.concatenate([cosine, cosine] * heads, axis=1),
        jnp.concatenate([-sine, sine] * heads, axis=1),
    )


def finish_back(grad, left, right, hidden, factor, gain):
    unit = hidden * factor
    grad_normed = left.astype(FULL) + right.astype(FULL)
    grad_unit = grad_normed * gain
    inner = jnp.mean(grad_unit * unit, axis=-1, keepdims=True)
    return (
        grad + factor * (grad_unit - unit * inner),
        jnp.sum(grad_normed * unit, axis=0, keepdims=True),
    )


class Arrival:
    def __init__(self, block, hi, lo, core):
        self.block, self.hi, self.lo, self.core = block, hi, lo, core

    def pick(self, order):
        self.mine, self.other = order.mark(pick(self.hi, order.after(self.block)))

    def fetch_on(self, order):
        self.far = flip_hi(order.after(self.other))

    def fetch(self, order):
        self.pick(order)
        self.fetch_on(order)

    def share(self, order):
        order.join(self.far)
        mine, far = order.after((self.mine, self.far))
        self.parts = [jnp.where(self.hi == j, mine, far) for j in range(CHUNKS)]
        order.mark(tuple(self.parts))
        self.halves = [None] * CHUNKS
        self.near = [None] * CHUNKS

    def send(self, order, j):
        self.near[j] = hop(order.after(self.parts[j]), "cols", 1)

    def cross(self, order, j):
        lo, core = self.lo, self.core
        order.join(self.near[j])
        part, near = order.after((self.parts[j], self.near[j]))
        if len(low_bits()) == 1:
            at_home = lo == core
            first = jnp.where(at_home, part, near)
            second = jnp.where(at_home, near, part)
        else:
            for bit in low_bits():
                far = near if bit == 1 else hop(part, "cols", bit)
                part = jnp.where(
                    (lo & bit) == 0,
                    jnp.concatenate([part, far], axis=0),
                    jnp.concatenate([far, part], axis=0),
                )
            half = part.shape[0] // 2
            first = lax.dynamic_slice_in_dim(part, core * half, half, 0)
            second = lax.dynamic_slice_in_dim(part, (1 - core) * half, half, 0)
        first, second = order.mark((first, second))
        self.halves[j] = (first, flip_core(second))

    def chunk(self, order, j):
        order.join(self.halves[j][1])
        return order.mark(jnp.concatenate(order.after(self.halves[j]), axis=-1))


def leave(chunks, hi, lo, core, rows):
    parts = []
    for value in chunks:
        width = value.shape[-1] // 2
        first = value[:, :width]
        second = flip_core(value[:, width:].astype(LOW)).astype(FULL)
        both = jnp.where(
            core == 0,
            jnp.concatenate([first, second], axis=0),
            jnp.concatenate([second, first], axis=0),
        )
        parts.append(lax.dynamic_slice_in_dim(both, lo * rows, rows, 0))
    mine = jnp.where(hi == 0, parts[0], parts[1])
    other = flip_hi(jnp.where(hi == 0, parts[1], parts[0]).astype(LOW)).astype(FULL)
    return jnp.where(
        hi == 0, jnp.stack([mine, other], axis=1), jnp.stack([other, mine], axis=1)
    )


def shards(
    block_input, block_cotangent, w_query, w_key, w_value, w_out, w_gate, w_up, w_down, norm_gains
):
    low_count = lax.axis_size("cols") // 2
    core, col, place = lax.axis_index("rows"), lax.axis_index("cols"), lax.axis_index("dp")
    hi, lo = col // low_count, col % low_count
    core_ref = core.astype(jnp.int32).reshape(1)
    block_rows = block_input.shape[0]
    rows = block_rows * low_count
    q_width = w_query.shape[2]
    half = rows // 2
    tables = [
        rope_tables(jnp.arange(half, dtype=jnp.int32) + j * rows + core * half, q_width)
        for j in range(CHUNKS)
    ]
    spot = place.astype(jnp.int32).reshape(1)
    order = Order()
    w_in = jnp.concatenate([w_query, w_key, w_value], axis=2)
    wide = w_in.shape[1]
    ff = w_gate.shape[2]
    a_groups = [in_groups(0, w_in, w_out, place, True), None]
    order.mark([group.piece for group in a_groups[0]])
    for group in a_groups[0]:
        group.fetch(order)
    arrival = Arrival(block_input, hi, lo, core)
    arrival.fetch(order)
    in_own, out_own, gates, ups, own_downs = [
        (v, flip_core(v)) for v in (w_in, w_out, w_gate, w_up, w_down)
    ]
    gains = jnp.concatenate([norm_gains, flip_core(norm_gains)], axis=-1)
    f_groups = []
    for l in range(LAYERS):
        pieces = order.mark(cut_ff(spot, l, order.after(w_gate), w_up, w_down))
        f_groups.append([Group(piece, (wide,), place) for piece in pieces])
        order.join(*((in_own[1], gains) if not l else (out_own[1],)))
    a_groups[1] = in_groups(1, order.after(w_in), w_out, place, True)
    order.mark([group.piece for group in a_groups[1]])
    order.join(gates[1], ups[1])
    for group in a_groups[0]:
        group.spread(order)
    arrival.share(order)
    arrival.send(order, 0)
    f_groups[0][0].fetch(order)
    for group in a_groups[0]:
        group.spread_on(order)
    arrival.cross(order, 0)
    f_groups[0][0].gather(order)
    f_groups[0][1].fetch(order)
    for group in a_groups[0]:
        group.collect(order)
    hidden = [arrival.chunk(order, 0)]
    order.join(own_downs[1])
    arrival.send(order, 1)
    f_groups[0][1].gather(order)
    for group in a_groups[0]:
        group.done(order)

    cotangent = Arrival(block_cotangent, hi, lo, core)
    stash = [[None] * CHUNKS for _ in range(LAYERS)]
    weights = [None] * LAYERS
    pairs = [None] * CHUNKS

    def front(l, j):
        block, factor_a, normed_a, query, mine = order.mark(
            project(order.after(hidden[j]), pairs[j], gains[l, 0:1], ins, *tables[j])
        )
        kvs.extend([mine, flip_core(mine)])
        return (block, factor_a, normed_a, query)

    def middle(l, j, kept):
        order.join(kvs[2 * j + 1])
        attended, lse, part = order.mark(
            attend(core_ref, order.after(kept[3]), kvs[: 2 * j + 2], outs)
        )
        pairs[j] = group_pair(part)
        return (*kept, kvs[: 2 * j + 2], lse, attended)

    def rear(l, j, kept):
        order.join(pairs[j])
        mixed, factor_b, normed_b, gate, up, inner, part = order.mark(
            feed_forward(order.after(kept[0]), pairs[j], gains[l, 1:2], pair_parts, down_parts)
        )
        hidden[j] = mixed
        pairs[j] = group_pair(part) if l + 1 < LAYERS else part
        stash[l][j] = kept + (mixed, factor_b, normed_b, gate, up, inner)

    for l in range(LAYERS):
        more = l + 1 < LAYERS
        halves = [group.halves for group in a_groups[l]]
        if len(halves) == 1:
            ins = [Part(v, None, 0, wide) for v in halves[0]]
            outs = [Part(v, None, wide, w_out.shape[1]) for v in halves[0]]
        else:
            ins, outs = [[Part(v) for v in pair] for pair in halves]
        ins = [Part(v, l) for v in in_own] + ins
        outs = [Part(v, l) for v in out_own] + outs
        kvs, kept = [], [None] * CHUNKS
        first, second, third = f_groups[l]
        if not l:
            kept[0] = front(l, 0)
            third.fetch(order)
            arrival.cross(order, 1)
            kept[0] = middle(l, 0, kept[0])
            third.gather(order)
            hidden.append(arrival.chunk(order, 1))
            kept[1] = front(l, 1)
            first.cross(order)
            for group in a_groups[1]:
                group.fetch(order)
            order.join(pairs[0])
            kept[1] = middle(l, 1, kept[1])
            first.done(order)
            for group in a_groups[1]:
                group.gather(order)
            f_groups[1][0].fetch(order)
            second.cross(order)
            third.cross(order)
        else:
            order.join(pairs[0])
            kept[0] = front(l, 0)
            second.gather(order)
            third.fetch(order)
            order.join(pairs[1])
            kept[1] = front(l, 1)
            kept[0] = middle(l, 0, kept[0])
            third.gather(order)
            cotangent.fetch_on(order)
            first.cross(order)
            kept[1] = middle(l, 1, kept[1])
            first.done(order)
            cotangent.share(order)
            cotangent.send(order, 1)
            second.cross(order)
            third.cross(order)
        second.done(order)
        third.done(order)
        packs = [group.halves for group in f_groups[l]]
        pair_parts = [Part(v, l) for v in (*gates, *ups)] + [
            Part(v) for pack in packs[:2] for v in pack
        ]
        down_parts = [Part(v, l) for v in own_downs] + [Part(v) for v in packs[2]]
        weights[l] = (ins, outs, pair_parts, down_parts)
        rear(l, 0, kept[0])
        if more:
            order.join(pairs[1])
            f_groups[1][0].gather(order)
            f_groups[1][1].fetch(order)
        else:
            cotangent.cross(order, 1)
            cotangent.send(order, 0)
        rear(l, 1, kept[1])
        if more:
            cotangent.pick(order)
            for group in a_groups[1]:
                group.cross(order)
                group.done(order)
    grads = [None] * CHUNKS
    grads[1] = (cotangent.chunk(order, 1),)

    gain_a, gain_b = [0.0] * LAYERS, [0.0] * LAYERS
    sums = {}

    def ff_step(l, j):
        pair_parts, down_parts = weights[l][2:]
        gate, up, inner = stash[l][j][-3:]
        if len(grads[j]) == 1:
            branch_b = order.after(grads[j][0])
            grad_hidden = branch_b.astype(FULL)
            pair_grad, part = order.mark(feed_back((branch_b,), gate, up, pair_parts, down_parts))
        else:
            order.join(*grads[j][1:3])
            grad_hidden, branch_b, gain_part, pair_grad, part = order.mark(
                feed_back(
                    (order.after(grads[j][0]), *grads[j][1:]), gate, up, pair_parts, down_parts
                )
            )
            gain_a[l + 1] = gain_a[l + 1] + gain_part
        mixed, factor_b, normed_b = stash[l][j][7:10]
        grads[j] = (grad_hidden, *group_pair(part), mixed, factor_b, gains[l, 1:2])
        return (normed_b, branch_b, pair_grad, inner)

    def ff_grad(l, kept):
        columns = list(zip(*kept))
        columns[0] = order.after(columns[0])
        sums["ff", l] = Sum(order.mark(ff_weights(*columns)), place)

    def attend_step(l, j, held):
        block, factor_a, normed_a, query, kvs, lse, attended = stash[l][j][:7]
        order.join(*grads[j][1:3])
        grad_mixed, branch_a, gain_part, dq, *dkvs = order.mark(
            attend_back(
                core_ref,
                (order.after(grads[j][0]), *grads[j][1:]),
                query,
                lse,
                kvs,
                held,
                weights[l][1],
            )
        )
        gain_b[l] = gain_b[l] + gain_part
        grads[j] = (grad_mixed, None, None, block, factor_a, gains[l, 0:1])
        send = order.mark(order.after(dkvs[-1]).astype(LOW))
        middle = (dq, dkvs[-2], flip_core(send))
        return (dkvs[:2], middle, (normed_a, branch_a, None, attended))

    def project_step(l, j, middle, kept):
        dq, mine, came = middle
        order.join(came)
        proj_grad, part = order.mark(
            project_back(order.after(dq), mine, came, *tables[j], weights[l][0])
        )
        grads[j] = (grads[j][0], *group_pair(part), *grads[j][3:])
        return kept[:2] + (proj_grad,) + kept[3:]

    def in_grad(l, kept):
        columns = list(zip(*kept))
        columns[0] = order.after(columns[0])
        sums["in", l] = Sum(order.mark(in_weights(*columns)), place)

    l = LAYERS - 1
    kept, mids = [None] * CHUNKS, [None] * CHUNKS
    kept[1] = ff_step(l, 1)
    cotangent.cross(order, 0)
    grads[0] = (cotangent.chunk(order, 0),)
    kept[0] = ff_step(l, 0)
    ff_grad(l, kept)
    sums["ff", l].flip(order)
    held, mids[1], kept[1] = attend_step(l, 1, None)
    sums["ff", l].start(order)
    order.join(mids[1][2])
    _, mids[0], kept[0] = attend_step(l, 0, held)
    kept[1] = project_step(l, 1, mids[1], kept[1])
    kept[0] = project_step(l, 0, mids[0], kept[0])
    in_grad(l, kept)
    l = 0
    kept, mids = [None] * CHUNKS, [None] * CHUNKS
    kept[1] = ff_step(l, 1)
    sums["ff", 1].second(order)
    kept[0] = ff_step(l, 0)
    sums["in", 1].flip(order)
    ff_grad(l, kept)
    sums["ff", 1].third(order)
    sums["ff", 0].flip(order)
    sums["in", 1].start(order)
    held, mids[1], kept[1] = attend_step(l, 1, None)
    order.join(mids[1][2])
    sums["in", 1].arrived(order)
    sums["ff", 0].start(order)
    _, mids[0], kept[0] = attend_step(l, 0, held)
    kept[1] = project_step(l, 1, mids[1], kept[1])
    kept[0] = project_step(l, 0, mids[0], kept[0])
    in_grad(l, kept)
    for g in grads:
        order.join(*g[1:3])
    ends = [finish_back(order.after(g[0]), *g[1:]) for g in grads]
    order.mark(tuple(g for g, _ in ends))
    gain_a[0] = sum(part for _, part in ends)
    sums["ff", 0].second(order)
    sums["ff", 1].across(order)
    sums["in", 0].flip(order)
    sums["in", 1].second(order)
    sums["ff", 0].third(order)
    sums["ff", 0].across(order)
    sums["in", 0].start(order)
    sums["in", 1].third(order)
    sums["ff", 1].fourth(order)
    sums["in", 1].across(order)
    sums["in", 0].second(order)
    sums["ff", 1].near(order)
    sums["in", 0].third(order)
    sums["in", 0].across(order)
    sums["ff", 1].fifth(order)
    sums["in", 1].fourth(order)
    input_grad = order.mark(leave(order.after([g for g, _ in ends]), hi, lo, core, block_rows))
    sums["in", 1].near(order)
    sums["ff", 1].done(order)
    ff_out = order.mark(spread_ff(order.after(spot), sums["ff", 1].pieces, 1, None))
    sums["in", 1].fifth(order)
    sums["ff", 0].fourth(order)
    sums["ff", 0].near(order)
    sums["in", 0].fourth(order)
    sums["in", 1].done(order)
    sums["ff", 0].fifth(order)
    sums["in", 0].near(order)
    in_out = order.mark(spread_in(order.after(spot), sums["in", 1].pieces, 1, None, q_width))
    sums["in", 0].fifth(order)
    tops = [group_pair(part) for part in order.after(pairs)]
    hidden = [
        h + left.astype(FULL) + right.astype(FULL) for h, (left, right) in zip(hidden, tops)
    ]
    activations = leave(hidden, hi, lo, core, block_rows)
    sums["in", 0].done(order)
    in_out = order.mark(spread_in(order.after(spot), sums["in", 0].pieces, 0, in_out, q_width))
    sums["ff", 0].done(order)
    ff_out = spread_ff(order.after(spot), sums["ff", 0].pieces, 0, ff_out)
    gain_grads = [jnp.concatenate([gain_a[l], gain_b[l]], axis=0) for l in range(LAYERS)]

    grad_gains = jnp.stack(gain_grads)
    width = grad_gains.shape[-1] // 2
    grad_gains = grad_gains[..., :width] + flip_core(grad_gains[..., width:])
    grad_gains = grad_gains + flip_hi(grad_gains)
    bit = 1
    while bit < lax.axis_size("dp"):
        grad_gains = grad_gains + hop(grad_gains, "dp", bit)
        bit *= 2
    return (activations, input_grad, *in_out, *ff_out, grad_gains)


def solution(mesh):
    data = P("cols", "dp", "rows")
    tall = P(None, "rows", "cols")
    flat = P(None, "cols", "rows")
    gains = P(None, None, "rows")
    in_specs = (data, data, tall, tall, tall, flat, tall, tall, flat, gains)
    out_specs = (data, data, tall, tall, tall, flat, tall, tall, flat, gains)
    return jax.shard_map(
        shards, mesh=mesh, in_specs=in_specs, out_specs=out_specs, check_vma=False
    )
```

time: 2540 us -> 1040 us (0.41)
  waiting for transfers between devices: 1930 us -> 422 us
  Pallas kernels: 0 us -> 386 us
  matrix products: 269 us -> 0 us
  blocking collectives: 108 us -> 0 us
  starting transfers between devices: 3.52 us -> 91.8 us
  other arithmetic: 132 us -> 73.2 us
  local copies, waits for them, and re-layouts: 78.6 us -> 42.8 us
    reduce_scatter x20 -> x0, waiting for transfers between devices: 940 us -> none  [the longest x8 818 us: column_reduction(): lax.psum_scatter(jnp.einsum(pattern, left_side, right_side, preferred_ele...]
    all_gather x16 -> x7, waiting for transfers between devices: 605 us -> 93.1 us  [the longest x6 90.5 us: gather(): self.first = lax.all_gather(piece, 'dp', axis=0, tiled=True)]
    pallas_call x0 -> x41, Pallas kernels: none -> 386 us  [the longest x16 185 us: call(): pl.pallas_call(kernel, grid_spec=pltpu.PrefetchScalarGridSpec(num_scalar_...]
    psum x1 -> x0, waiting for transfers between devices: 384 us -> none  [shards(): lax.psum((stacked[0], stacked[1], stacked[2], stacked[3], stacked[4], sta...]
    ppermute x0 -> x109, waiting for transfers between devices: none -> 329 us  [hop(): return lax.ppermute(value, axis, [(i, i ^ distance) for i in range(size)])]
    dot_general x36 -> x0, matrix products: 269 us -> none  [the longest x8 71.2 us: row_reduce(): jnp.einsum(pattern, left_side, right_side, preferred_element_type=jnp.flo...]
    psum x9 -> x0, blocking collectives: 98 us -> none  [the longest x1 78 us: shards(): sum_gains = lax.psum(stacked[7], ('dp', 'cols'))]
    ppermute x0 -> x109, starting transfers between devices: none -> 90.5 us  [hop(): return lax.ppermute(value, axis, [(i, i ^ distance) for i in range(size)])]
  transfers between devices with their start and end apart: 37 -> 116, of which waited for: 35 -> 37; matrix products, arithmetic and copies ran while one was open for 7% -> 9% of each run, Pallas kernels for 0% -> 37%
where the time goes in v1:
time: 1040 us; the launch traced here: 1030 us
  waiting for transfers between devices  422 us (41%)
  Pallas kernels  386 us (37%)
  starting transfers between devices  91.8 us (9%)
  other arithmetic  73.2 us (7%)
  local copies, waits for them, and re-layouts  42.8 us (4%)
  between operations  16.1 us (2%)
    ppermute x109, waiting for transfers between devices, hop(): return lax.ppermute(value, axis, [(i, i ^ distance) for i in range(size)])  329 us
    pallas_call x16, Pallas kernels, call(): pl.pallas_call(kernel, grid_spec=pltpu.PrefetchScalarGridSpec(num_scalar_...  185 us
    all_gather x6, waiting for transfers between devices, gather(): self.first = lax.all_gather(piece, 'dp', axis=0, tiled=True)  90.5 us
    ppermute x109, starting transfers between devices, hop(): return lax.ppermute(value, axis, [(i, i ^ distance) for i in range(size)])  90.5 us
    pallas_call x4, Pallas kernels, role_sums(): pl.pallas_call(role_sum_kernel, grid_spec=pltpu.PrefetchScalarGridSpec(nu...  46 us
    pallas_call x2, Pallas kernels, ff_weights(): pl.pallas_call(functools.partial(ff_weights_kernel, chunks, split), grid=...  37.8 us
    pallas_call x4, Pallas kernels, attend(): pl.pallas_call(functools.partial(attend_kernel, chunks, parts), grid_spec...  33.8 us
    pallas_call x4, Pallas kernels, project_back(): pl.pallas_call(functools.partial(project_back_kernel, parts), in_specs=[w...  25.6 us
  transfers between devices with their start and end apart: 116, of which 37 were waited for; matrix products, arithmetic and copies ran while one was open for 9% of the time, Pallas kernels for 37%

profile of v1, /device:TPU:0, one launch (start us, length us, event | category | flops | bytes accessed | tf_op | source)
XLA Modules:
  0.0 1032.5 jit_solution(7204943333667457661)
XLA Ops:
  35.0 28.6 %collective-permute-done.6.refs_0_ = bf16[288,768]{1,0:T(8,128)(2,1)} collective-permute-done((bf16[288,768]{1,0:T(8,128)(2,1)}, bf16[288,768]{1,0:T(8,128)(2,1)}, u32[]{:S(2)}, u32[]{:S(2)}) %collective-permute-start.6) | collective-permute-done | bytes 442400 | tf_op jit(solution)/shard_map/ppermute | solution.py:26
  80.6 16.7 %collective-permute-done.11 = bf16[192,1024]{1,0:T(8,128)(2,1)} collective-permute-done((bf16[192,1024]{1,0:T(8,128)(2,1)}, bf16[192,1024]{1,0:T(8,128)(2,1)}, u32[]{:S(2)}, u32[]{:S(2)}) %collective-permute-start.11) | collective-permute-done | bytes 393248 | tf_op jit(solution)/shard_map/ppermute | solution.py:26
  112.7 7.3 collective-permute-done.14
  141.1 8.9 collective-permute-done.19
  157.9 13.6 %all-gather.11.cloned.1.call-done.refs_10_.refs_18_ = bf16[768,1024]{1,0:T(8,128)(2,1)} async-done(((bf16[192,1024]{1,0:T(8,128)(2,1)}), bf16[768,1024]{1,0:T(8,128)(2,1)}) %all-gather.11.cloned.1.call-update) | async-done | bytes 1572880 | tf_op jit(solution)/shard_map/all_gather | solution.py:900
  171.5 33.4 %all-gather.13.cloned.1.call-done.refs_14_.refs_10_ = bf16[768,1024]{1,0:T(8,128)(2,1)} async-done(((bf16[192,1024]{1,0:T(8,128)(2,1)}), bf16[768,1024]{1,0:T(8,128)(2,1)}) %all-gather.13.cloned.1.call-update) | async-done | bytes 1572880 | tf_op jit(solution)/shard_map/all_gather | solution.py:900
  204.9 9.2 attend.5
  218.5 11.6 %feed_forward.4 = (f32[256,1536]{1,0:T(8,128)}, f32[256,1]{1,0:T(8,128)}, bf16[256,1536]{1,0:T(8,128)(2,1)}, bf16[256,2048]{1,0:T(8,128)(2,1)}, bf16[256,2048]{1...) custom-call(f32[256,1536]{1,0:T(8,128)} %get-tuple-element.375.refs_0_, ...), custom_call_target="tpu_custom_call" | custom-call | flops 144955146240 | bytes 755005440 | tf_op jit(solution)/shard_map/feed_forward/pallas_call | solution.py:178
  230.6 12.6 %collective-permute-done.26.refs_2_ = bf16[256,1536]{1,0:T(8,128)(2,1)} collective-permute-done((bf16[256,1536]{1,0:T(8,128)(2,1)}, bf16[256,1536]{1,0:T(8,128)(2,1)}, u32[]{:S(2)}, u32[]{:S(2)}) %collective-permute-start.26) | collective-permute-done | bytes 786464 | tf_op jit(solution)/shard_map/ppermute | solution.py:26
  252.1 11.5 %feed_forward.5 = (f32[256,1536]{1,0:T(8,128)}, f32[256,1]{1,0:T(8,128)}, bf16[256,1536]{1,0:T(8,128)(2,1)}, bf16[256,2048]{1,0:T(8,128)(2,1)}, bf16[256,2048]{1...) custom-call(f32[256,1536]{1,0:T(8,128)} %get-tuple-element.384.refs_0_, ...), custom_call_target="tpu_custom_call" | custom-call | flops 144955146240 | bytes 755005440 | tf_op jit(solution)/shard_map/feed_forward/pallas_call | solution.py:178
  269.0 7.3 project.6
  278.9 12.5 %collective-permute-done.31.refs_2_ = bf16[256,1536]{1,0:T(8,128)(2,1)S(1)} collective-permute-done((bf16[256,1536]{1,0:T(8,128)(2,1)}, bf16[256,1536]{1,0:T(8,128)(2,1)S(1)}, u32[]{:S(2)}, u32[]{:S(2)}) %collective-permute-start.31) | collective-permute-done | bytes 786464 | tf_op jit(solution)/shard_map/ppermute | solution.py:26
  292.3 6.9 project.7
  300.0 7.7 attend.6
  311.2 10.1 all-gather.17.cloned.1.call-done.refs_10_.refs_13_
  321.3 33.4 %all-gather.19.cloned.1.call-done.refs_14_.refs_5_ = bf16[768,1024]{1,0:T(8,128)(2,1)} async-done(((bf16[192,1024]{1,0:T(8,128)(2,1)}), bf16[768,1024]{1,0:T(8,128)(2,1)}) %all-gather.19.cloned.1.call-update) | async-done | bytes 1572880 | tf_op jit(solution)/shard_map/all_gather | solution.py:900
  354.7 10.2 attend.7
  369.5 11.2 %feed_forward.6 = (f32[256,1536]{1,0:T(8,128)}, f32[256,1]{1,0:T(8,128)}, bf16[256,1536]{1,0:T(8,128)(2,1)}, bf16[256,2048]{1,0:T(8,128)(2,1)}, bf16[256,2048]{1...) custom-call(f32[256,1536]{1,0:T(8,128)} %get-tuple-element.424.refs_0_.refs_3_, ...), custom_call_target="tpu_custom_call" | custom-call | flops 144955146240 | bytes 755005440 | tf_op jit(solution)/shard_map/feed_forward/pallas_call | solution.py:178
  380.7 13.1 %collective-permute-done.40 = bf16[256,768]{1,0:T(8,128)(2,1)} collective-permute-done((bf16[256,768]{1,0:T(8,128)(2,1)}, bf16[256,768]{1,0:T(8,128)(2,1)}, u32[]{:S(2)}, u32[]{:S(2)}) %collective-permute-start.40) | collective-permute-done | bytes 393248 | tf_op jit(solution)/shard_map/ppermute | solution.py:26
  397.4 11.2 %feed_forward.7 = (f32[256,1536]{1,0:T(8,128)}, f32[256,1]{1,0:T(8,128)}, bf16[256,1536]{1,0:T(8,128)(2,1)}, bf16[256,2048]{1,0:T(8,128)(2,1)}, bf16[256,2048]{1...) custom-call(f32[256,1536]{1,0:T(8,128)} %get-tuple-element.435.refs_0_.refs_3_, ...), custom_call_target="tpu_custom_call" | custom-call | flops 144955146240 | bytes 755005440 | tf_op jit(solution)/shard_map/feed_forward/pallas_call | solution.py:178
  410.5 13.6 %feed_back.4 = (bf16[256,4096]{1,0:T(8,128)(2,1)}, bf16[256,1536]{1,0:T(8,128)(2,1)}) custom-call(bf16[256,1536]{1,0:T(8,128)(2,1)} %pad_maximum_fusion.7.refs_0_.refs_3_, bf16[256,2048]{1,0:T(8,128)(2,1)} %get-tuple-element.441.refs_1_, bf16[256,2048]{1,0:T(8,128)(2,1)} %get-tuple-element.442.refs_2_, bf16[2,1024,768]{2,1,0:T(8,128)(2,1)} %refs_8_.3, ...), custom_call_target="tpu_custom_call" | custom-call | flops 144955146240 | bytes 652738560 | tf_op jit(solution)/shard_map/feed_back/pallas_call | solution.py:178
  428.5 13.6 %feed_back.5 = (bf16[256,4096]{1,0:T(8,128)(2,1)}, bf16[256,1536]{1,0:T(8,128)(2,1)}) custom-call(bf16[256,1536]{1,0:T(8,128)(2,1)} %pad_maximum_fusion.8.refs_0_.refs_2_, bf16[256,2048]{1,0:T(8,128)(2,1)} %get-tuple-element.430.refs_1_, bf16[256,2048]{1,0:T(8,128)(2,1)} %get-tuple-element.431.refs_2_, bf16[2,1024,768]{2,1,0:T(8,128)(2,1)} %refs_8_.3, ...), custom_call_target="tpu_custom_call" | custom-call | flops 144955146240 | bytes 652738560 | tf_op jit(solution)/shard_map/feed_back/pallas_call | solution.py:178
  443.7 19.1 %ff_weights.2 = (bf16[768,6144]{1,0:T(8,128)(2,1)}, bf16[768,6144]{1,0:T(8,128)(2,1)}) custom-call(bf16[256,1536]{1,0:T(8,128)(2,1)} %get-tuple-element.454.refs_0_, bf16[256,1536]{1,0:T(8,128)(2,1)} %get-tuple-element.455.refs_1_, bf16[256,1536]{1,0:T(8,128)(2,1)} %pad_maximum_fusion.8.refs_0_.refs_2_, bf16[256,1536]{1,0:T(8,128)(2,1)} %pad_maximum_fusion.7.refs_0_.refs_3_, ...), custom_call_target="tpu_custom_call" | custom-call | flops 289910292480 | bytes 754974720 | tf_op jit(solution)/shard_map/ff_weights/pallas_call | solution.py:592
  462.8 15.8 %attend_back.4 = (f32[256,1536]{1,0:T(8,128)}, bf16[256,1536]{1,0:T(8,128)(2,1)}, f32[1,1536]{1,0:T(1,128)}, f32[256,768]{1,0:T(8,128)}, f32[256,768]{1,0:T(8,12...) custom-call(s32[1]{0:T(128)} %bitcast.7.core_ref, f32[256,1536]{1,0:T(8,128)} %convert_element_type.311.refs_0_, ...), custom_call_target="tpu_custom_call" | custom-call | flops 179180666880 | bytes 259706880 | tf_op jit(solution)/shard_map/attend_back/pallas_call | solution.py:178
  482.3 14.3 %role_sums.4 = (bf16[384,3072]{1,0:T(8,128)(2,1)}, bf16[384,3072]{1,0:T(8,128)(2,1)}, bf16[384,3072]{1,0:T(8,128)(2,1)}, bf16[384,3072]{1,0:T(8,128)(2,1)}) custom-call(s32[8]{0:T(128)} %broadcast_xor_fusion.row_ref, s32[8]{0:T(128)} %constant.69.clone.side_ref, bf16[768,6144]{1,0:T(8,128)(2,1)} %get-tuple-element.469.left_ref, ...), custom_call_target="tpu_custom_call" | custom-call | bytes 424673280 | tf_op jit(solution)/shard_map/role_sums/pallas_call | solution.py:666
  498.7 12.0 %attend_back.5 = (f32[256,1536]{1,0:T(8,128)}, bf16[256,1536]{1,0:T(8,128)(2,1)}, f32[1,1536]{1,0:T(1,128)}, f32[256,768]{1,0:T(8,128)}, f32[256,768]{1,0:T(8,128)}, /*index=5*/f32[256,768]{1,0:T(8,128)}) custom-call(s32[1]{0:T(128)} %bitcast.7.core_ref, f32[256,1536]{1,0:T(8,128)} %convert_element_type.310.refs_0_, ...), custom_call_target="tpu_custom_call" | custom-call | flops 98650030080 | bytes 212520960 | tf_op jit(solution)/shard_map/attend_back/pallas_call | solution.py:178
  527.8 9.6 in_weights.2
  539.2 14.9 %feed_back.6 = (f32[256,1536]{1,0:T(8,128)}, bf16[256,1536]{1,0:T(8,128)(2,1)}, f32[1,1536]{1,0:T(1,128)}, bf16[256,4096]{1,0:T(8,128)(2,1)}, bf16[256,1536]{1,0:T(8,128)(2,1)}) custom-call(f32[256,1536]{1,0:T(8,128)} %get-tuple-element.492.refs_0_, bf16[256,1536]{1,0:T(8,128)(2,1)} %get-tuple-element.484.refs_1_, ...), custom_call_target="tpu_custom_call" | custom-call | flops 144955146240 | bytes 723701760 | tf_op jit(solution)/shard_map/feed_back/pallas_call | solution.py:178
  563.1 14.9 %feed_back.7 = (f32[256,1536]{1,0:T(8,128)}, bf16[256,1536]{1,0:T(8,128)(2,1)}, f32[1,1536]{1,0:T(1,128)}, bf16[256,4096]{1,0:T(8,128)(2,1)}, bf16[256,1536]{1,0:T(8,128)(2,1)}) custom-call(f32[256,1536]{1,0:T(8,128)} %get-tuple-element.501.refs_0_, bf16[256,1536]{1,0:T(8,128)(2,1)} %get-tuple-element.487.refs_1_, ...), custom_call_target="tpu_custom_call" | custom-call | flops 144955146240 | bytes 723701760 | tf_op jit(solution)/shard_map/feed_back/pallas_call | solution.py:178
  579.6 18.8 %ff_weights.3 = (bf16[768,6144]{1,0:T(8,128)(2,1)}, bf16[768,6144]{1,0:T(8,128)(2,1)}) custom-call(bf16[256,1536]{1,0:T(8,128)(2,1)} %get-tuple-element.507.refs_0_, bf16[256,1536]{1,0:T(8,128)(2,1)} %get-tuple-element.508.refs_1_, bf16[256,1536]{1,0:T(8,128)(2,1)} %get-tuple-element.503.refs_2_, bf16[256,1536]{1,0:T(8,128)(2,1)} %get-tuple-element.494.refs_3_, ...), custom_call_target="tpu_custom_call" | custom-call | flops 289910292480 | bytes 754974720 | tf_op jit(solution)/shard_map/ff_weights/pallas_call | solution.py:592
  601.5 8.8 role_sums.5
  612.4 15.9 %attend_back.6 = (f32[256,1536]{1,0:T(8,128)}, bf16[256,1536]{1,0:T(8,128)(2,1)}, f32[1,1536]{1,0:T(1,128)}, f32[256,768]{1,0:T(8,128)}, f32[256,768]{1,0:T(8,12...) custom-call(s32[1]{0:T(128)} %bitcast.7.core_ref, f32[256,1536]{1,0:T(8,128)} %get-tuple-element.520.refs_0_, ...), custom_call_target="tpu_custom_call" | custom-call | flops 179180666880 | bytes 259706880 | tf_op jit(solution)/shard_map/attend_back/pallas_call | solution.py:178
  633.4 14.3 %role_sums.6 = (bf16[384,3072]{1,0:T(8,128)(2,1)}, bf16[384,3072]{1,0:T(8,128)(2,1)}, bf16[384,3072]{1,0:T(8,128)(2,1)}, bf16[384,3072]{1,0:T(8,128)(2,1)}) custom-call(s32[8]{0:T(128)} %broadcast_xor_fusion.row_ref, s32[8]{0:T(128)} %constant.69.clone.side_ref, bf16[768,6144]{1,0:T(8,128)(2,1)} %get-tuple-element.531.left_ref, ...), custom_call_target="tpu_custom_call" | custom-call | bytes 424673280 | tf_op jit(solution)/shard_map/role_sums/pallas_call | solution.py:666
  649.9 11.9 %attend_back.7 = (f32[256,1536]{1,0:T(8,128)}, bf16[256,1536]{1,0:T(8,128)(2,1)}, f32[1,1536]{1,0:T(1,128)}, f32[256,768]{1,0:T(8,128)}, f32[256,768]{1,0:T(8,128)}, /*index=5*/f32[256,768]{1,0:T(8,128)}) custom-call(s32[1]{0:T(128)} %bitcast.7.core_ref, f32[256,1536]{1,0:T(8,128)} %get-tuple-element.536.refs_0_, ...), custom_call_target="tpu_custom_call" | custom-call | flops 98650030080 | bytes 212520960 | tf_op jit(solution)/shard_map/attend_back/pallas_call | solution.py:178
  678.8 9.9 in_weights.3
  690.2 16.3 %collective-permute-done.66 = bf16[256,1536]{1,0:T(8,128)(2,1)S(1)} collective-permute-done((bf16[256,1536]{1,0:T(8,128)(2,1)}, bf16[256,1536]{1,0:T(8,128)(2,1)S(1)}, u32[]{:S(2)}, u32[]{:S(2)}) %collective-permute-start.66) | collective-permute-done | bytes 786464 | tf_op jit(solution)/shard_map/ppermute | solution.py:26
  723.2 21.9 %collective-permute-done.68 = bf16[192,3072]{1,0:T(8,128)(2,1)S(1)} collective-permute-done((bf16[192,3072]{1,0:T(8,128)(2,1)S(1)}, bf16[192,3072]{1,0:T(8,128)(2,1)S(1)}, u32[]{:S(2)}, u32[]{:S(2)}) %collective-permute-start.68) | collective-permute-done | bytes 1179680 | tf_op jit(solution)/shard_map/ppermute | solution.py:26
  749.0 8.6 role_sums.7
  760.9 37.6 %collective-permute-done.73 = bf16[192,3072]{1,0:T(8,128)(2,1)} collective-permute-done((bf16[192,3072]{1,0:T(8,128)(2,1)S(1)}, bf16[192,3072]{1,0:T(8,128)(2,1)}, u32[]{:S(2)}, u32[]{:S(2)}) %collective-permute-start.73) | collective-permute-done | bytes 1179680 | tf_op jit(solution)/shard_map/ppermute | solution.py:26
  806.3 8.8 collective-permute-done.76
  816.6 10.5 %collective-permute-done.81.refs_2_.refs_10_.refs_18_ = bf16[96,3072]{1,0:T(8,128)(2,1)S(1)} collective-permute-done((bf16[96,3072]{1,0:T(8,128)(2,1)S(1)}, bf16[96,3072]{1,0:T(8,128)(2,1)S(1)}, u32[]{:S(2)}, u32[]{:S(2)}) %collective-permute-start.81) | collective-permute-done | bytes 589856 | tf_op jit(solution)/shard_map/ppermute | solution.py:26
  839.9 39.4 %collective-permute-done.85 = bf16[256,768]{1,0:T(8,128)(2,1)S(1)} collective-permute-done((bf16[256,768]{1,0:T(8,128)(2,1)S(1)}, bf16[256,768]{1,0:T(8,128)(2,1)S(1)}, u32[]{:S(2)}, u32[]{:S(2)}) %collective-permute-start.85) | collective-permute-done | bytes 393248 | tf_op jit(solution)/shard_map/ppermute | solution.py:26
  883.8 7.0 spread_ff.2
  892.4 21.8 %collective-permute-done.79 = bf16[192,3072]{1,0:T(8,128)(2,1)} collective-permute-done((bf16[192,3072]{1,0:T(8,128)(2,1)}, bf16[192,3072]{1,0:T(8,128)(2,1)}, u32[]{:S(2)}, u32[]{:S(2)}) %collective-permute-start.79) | collective-permute-done | bytes 1179680 | tf_op jit(solution)/shard_map/ppermute | solution.py:26
  923.7 18.4 %collective-permute-done.93.refs_4_.refs_6_ = bf16[192,1152]{1,0:T(8,128)(2,1)S(1)} collective-permute-done((bf16[192,1152]{1,0:T(8,128)(2,1)S(1)}, bf16[192,1152]{1,0:T(8,128)(2,1)S(1)}, u32[]{:S(2)}, u32[]{:S(2)}) %collective-permute-start.93) | collective-permute-done | bytes 442400 | tf_op jit(solution)/shard_map/ppermute | solution.py:26
  957.7 13.5 %collective-permute-done.98 = bf16[256,1536]{1,0:T(8,128)(2,1)S(1)} collective-permute-done((bf16[256,1536]{1,0:T(8,128)(2,1)}, bf16[256,1536]{1,0:T(8,128)(2,1)S(1)}, u32[]{:S(2)}, u32[]{:S(2)}) %collective-permute-start.98) | collective-permute-done | bytes 786464 | tf_op jit(solution)/shard_map/ppermute | solution.py:26
  972.7 12.4 %collective-permute-done.96 = bf16[256,1536]{1,0:T(8,128)(2,1)S(1)} collective-permute-done((bf16[256,1536]{1,0:T(8,128)(2,1)}, bf16[256,1536]{1,0:T(8,128)(2,1)S(1)}, u32[]{:S(2)}, u32[]{:S(2)}) %collective-permute-start.96) | collective-permute-done | bytes 786464 | tf_op jit(solution)/shard_map/ppermute | solution.py:26
  1015.2 6.7 spread_ff.3
  (533 shorter events, 309.2 us)
Async XLA Ops:
  7.2 150.3 %all-gather.9.cloned.1.call-start = ((), (), s32[]{:S(2)}) async-start(), calls=%async_computation | async-start | bytes 1966080 | tf_op jit(solution)/shard_map/all_gather | solution.py:900
  7.2 56.4 %collective-permute-start.4 = (bf16[2,768,1024]{2,1,0:T(8,128)(2,1)}, bf16[2,768,1024]{2,1,0:T(8,128)(2,1)}, u32[]{:S(2)}, u32[]{:S(2)}) collective-permute-start(bf16[2,768,1024]{2,1,0:T(8,128)(2,1)} %refs_12_.17), channel_id=1, source_target_pairs={{0,4},{4,0},{1,5},{5,1},{2,6},{6,2},{3,7},{7,3},{8,12},{12,8},{9,1... | collective-permute-start | bytes 9437192 | tf_op jit(solution)/shard_map/ppermute | solution.py:26
  7.8 55.9 %collective-permute-start.5 = (bf16[2,768,1024]{2,1,0:T(8,128)(2,1)}, bf16[2,768,1024]{2,1,0:T(8,128)(2,1)}, u32[]{:S(2)}, u32[]{:S(2)}) collective-permute-start(bf16[2,768,1024]{2,1,0:T(8,128)(2,1)} %refs_14_.3), channel_id=1, source_target_pairs={{0,4},{4,0},{1,5},{5,1},{2,6},{6,2},{3,7},{7,3},{8,12},{12,8},{9,1... | collective-permute-start | bytes 9437192 | tf_op jit(solution)/shard_map/ppermute | solution.py:26
  22.5 44.2 %collective-permute-start = (bf16[256,768]{1,0:T(8,128)(2,1)}, bf16[256,768]{1,0:T(8,128)(2,1)}, u32[]{:S(2)}, u32[]{:S(2)}) collective-permute-start(bf16[256,768]{1,0:T(8,128)(2,1)} %get-tuple-element.323), channel_id=1, source_target_pairs={{0,2},{1,3},{2,0},{3,1},{4,6},{5,7},{6,4},{7,5},{8,10},{9,11},{10,... | collective-permute-start | bytes 1179656 | tf_op jit(solution)/shard_map/ppermute | solution.py:26
  26.2 37.4 %collective-permute-start.6 = (bf16[288,768]{1,0:T(8,128)(2,1)}, bf16[288,768]{1,0:T(8,128)(2,1)}, u32[]{:S(2)}, u32[]{:S(2)}) collective-permute-start(bf16[288,768]{1,0:T(8,128)(2,1)} %pad_maximum_fusion.9), channel_id=1, source_target_pairs={{0,2},{1,3},{2,0},{3,1},{4,6},{5,7},{6,4},{7,5},{8,10},{9,11},{10,... | collective-permute-start | bytes 1327112 | tf_op jit(solution)/shard_map/ppermute | solution.py:26
  26.9 83.2 %collective-permute-start.13 = (bf16[2,1024,768]{2,1,0:T(8,128)(2,1)S(1)}, bf16[2,1024,768]{2,1,0:T(8,128)(2,1)}, u32[]{:S(2)}, u32[]{:S(2)}) collective-permute-start(bf16[2,1024,768]{2,1,0:T(8,128)(2,1)S(1)} %copy-done.8), channel_id=1, source_target_pairs={{0,4},{4,0},{1,5},{5,1},{2,6},{6,2},{3,7},{7,3},{8,12},{12,8},{9,1... | collective-permute-start | bytes 9437192 | tf_op jit(solution)/shard_map/ppermute | solution.py:26
  107.9 63.6 %all-gather.11.cloned.1.call-start = ((), (), s32[]{:S(2)}) async-start(), calls=%async_computation.1 | async-start | bytes 1966080 | tf_op jit(solution)/shard_map/all_gather | solution.py:900
  128.5 76.5 %all-gather.13.cloned.1.call-start = ((), (), s32[]{:S(2)}) async-start(), calls=%async_computation.2 | async-start | bytes 1966080 | tf_op jit(solution)/shard_map/all_gather | solution.py:900
  138.1 33.4 %collective-permute-start.20 = (bf16[256,1536]{1,0:T(8,128)(2,1)}, bf16[256,1536]{1,0:T(8,128)(2,1)S(1)}, u32[]{:S(2)}, u32[]{:S(2)}) collective-permute-start(bf16[256,1536]{1,0:T(8,128)(2,1)} %get-tuple-element.358.refs_1_), channel_id=1, source_target_pairs={{0,1},{1,0},{2,3},{3,2},{4,5},{5,4},{6,7},{7,6},{8,9},{9,8},{10,11... | collective-permute-start | bytes 2359304 | tf_op jit(solution)/shard_map/ppermute | solution.py:26
  151.0 97.3 %all-gather.21.cloned.1.call-start = ((), (), s32[]{:S(2)}) async-start(), calls=%async_computation.6 | async-start | bytes 2211840 | tf_op jit(solution)/shard_map/all_gather | solution.py:902
  157.4 58.2 %collective-permute-start.22 = (bf16[768,1024]{1,0:T(8,128)(2,1)}, bf16[768,1024]{1,0:T(8,128)(2,1)S(1)}, u32[]{:S(2)}, u32[]{:S(2)}) collective-permute-start(bf16[768,1024]{1,0:T(8,128)(2,1)} %all-gather.9.cloned.1.call-done.refs_8_.refs_16_), channel_id=1, source_target_pairs={{0,4},{4,0},{1,5},{5,1},{2,6},{6,2},{3,7},{7,3},{8,12},{12,8},{9,1... | collective-permute-start | bytes 4718600 | tf_op jit(solution)/shard_map/ppermute | solution.py:26
  157.9 57.8 %collective-permute-start.23 = (bf16[288,768]{1,0:T(8,128)(2,1)S(1)}, bf16[288,768]{1,0:T(8,128)(2,1)S(1)}, u32[]{:S(2)}, u32[]{:S(2)}) collective-permute-start(bf16[288,768]{1,0:T(8,128)(2,1)S(1)} %copy-done.58), channel_id=1, source_target_pairs={{0,2},{1,3},{2,0},{3,1},{4,6},{5,7},{6,4},{7,5},{8,10},{9,11},{10,... | collective-permute-start | bytes 1327112 | tf_op jit(solution)/shard_map/ppermute | solution.py:26
  171.5 46.9 %collective-permute-start.24 = (bf16[768,1024]{1,0:T(8,128)(2,1)}, bf16[768,1024]{1,0:T(8,128)(2,1)}, u32[]{:S(2)}, u32[]{:S(2)}) collective-permute-start(bf16[768,1024]{1,0:T(8,128)(2,1)} %all-gather.11.cloned.1.call-done.refs_10_.refs_18_), channel_id=1, source_target_pairs={{0,4},{4,0},{1,5},{5,1},{2,6},{6,2},{3,7},{7,3},{8,12},{12,8},{9,1... | collective-permute-start | bytes 4718600 | tf_op jit(solution)/shard_map/ppermute | solution.py:26
  218.2 93.0 %all-gather.15.cloned.1.call-start = ((), (), s32[]{:S(2)}) async-start(), calls=%async_computation.3 | async-start | bytes 1966080 | tf_op jit(solution)/shard_map/all_gather | solution.py:900
  230.1 38.9 %collective-permute-start.29 = (bf16[256,1536]{1,0:T(8,128)(2,1)}, bf16[256,1536]{1,0:T(8,128)(2,1)}, u32[]{:S(2)}, u32[]{:S(2)}) collective-permute-start(bf16[256,1536]{1,0:T(8,128)(2,1)} %get-tuple-element.382.refs_1_), channel_id=1, source_target_pairs={{0,1},{1,0},{2,3},{3,2},{4,5},{5,4},{6,7},{7,6},{8,9},{9,8},{10,11... | collective-permute-start | bytes 2359304 | tf_op jit(solution)/shard_map/ppermute | solution.py:26
  243.3 33.2 %collective-permute-start.30 = (bf16[192,1024]{1,0:T(8,128)(2,1)}, bf16[192,1024]{1,0:T(8,128)(2,1)}, u32[]{:S(2)}, u32[]{:S(2)}) collective-permute-start(bf16[192,1024]{1,0:T(8,128)(2,1)} %get-tuple-element.402), channel_id=1, source_target_pairs={{0,2},{1,3},{2,0},{3,1},{4,6},{5,7},{6,4},{7,5},{8,10},{9,11},{10,... | collective-permute-start | bytes 1179656 | tf_op jit(solution)/shard_map/ppermute | solution.py:26
  245.7 75.6 %all-gather.17.cloned.1.call-start = ((), (), s32[]{:S(2)}) async-start(), calls=%async_computation.4 | async-start | bytes 1966080 | tf_op jit(solution)/shard_map/all_gather | solution.py:900
  291.5 63.3 %all-gather.19.cloned.1.call-start = ((), (), s32[]{:S(2)}) async-start(), calls=%async_computation.5 | async-start | bytes 1966080 | tf_op jit(solution)/shard_map/all_gather | solution.py:900
  308.5 59.6 %collective-permute-start.39 = (bf16[256,1536]{1,0:T(8,128)(2,1)}, bf16[256,1536]{1,0:T(8,128)(2,1)S(1)}, u32[]{:S(2)}, u32[]{:S(2)}) collective-permute-start(bf16[256,1536]{1,0:T(8,128)(2,1)} %get-tuple-element.412.refs_1_), channel_id=1, source_target_pairs={{0,1},{1,0},{2,3},{3,2},{4,5},{5,4},{6,7},{7,6},{8,9},{9,8},{10,11... | collective-permute-start | bytes 2359304 | tf_op jit(solution)/shard_map/ppermute | solution.py:26
  310.2 54.8 %collective-permute-start.34 = (bf16[256,768]{1,0:T(8,128)(2,1)}, bf16[256,768]{1,0:T(8,128)(2,1)S(1)}, u32[]{:S(2)}, u32[]{:S(2)}) collective-permute-start(bf16[256,768]{1,0:T(8,128)(2,1)} %get-tuple-element.414), channel_id=1, source_target_pairs={{0,2},{1,3},{2,0},{3,1},{4,6},{5,7},{6,4},{7,5},{8,10},{9,11},{10,... | collective-permute-start | bytes 1179656 | tf_op jit(solution)/shard_map/ppermute | solution.py:26
  311.2 55.4 %collective-permute-start.36 = (bf16[768,1024]{1,0:T(8,128)(2,1)}, bf16[768,1024]{1,0:T(8,128)(2,1)S(1)}, u32[]{:S(2)}, u32[]{:S(2)}) collective-permute-start(bf16[768,1024]{1,0:T(8,128)(2,1)} %all-gather.15.cloned.1.call-done.refs_8_.refs_11_), channel_id=1, source_target_pairs={{0,4},{4,0},{1,5},{5,1},{2,6},{6,2},{3,7},{7,3},{8,12},{12,8},{9,1... | collective-permute-start | bytes 4718600 | tf_op jit(solution)/shard_map/ppermute | solution.py:26
  321.3 46.8 %collective-permute-start.37 = (bf16[768,1024]{1,0:T(8,128)(2,1)}, bf16[768,1024]{1,0:T(8,128)(2,1)}, u32[]{:S(2)}, u32[]{:S(2)}) collective-permute-start(bf16[768,1024]{1,0:T(8,128)(2,1)} %all-gather.17.cloned.1.call-done.refs_10_.refs_13_), channel_id=1, source_target_pairs={{0,4},{4,0},{1,5},{5,1},{2,6},{6,2},{3,7},{7,3},{8,12},{12,8},{9,1... | collective-permute-start | bytes 4718600 | tf_op jit(solution)/shard_map/ppermute | solution.py:26
  425.6 37.1 %collective-permute-start.45 = (bf16[256,1536]{1,0:T(8,128)(2,1)}, bf16[256,1536]{1,0:T(8,128)(2,1)}, u32[]{:S(2)}, u32[]{:S(2)}) collective-permute-start(bf16[256,1536]{1,0:T(8,128)(2,1)} %get-tuple-element.447.refs_1_), channel_id=1, source_target_pairs={{0,1},{1,0},{2,3},{3,2},{4,5},{5,4},{6,7},{7,6},{8,9},{9,8},{10,11... | collective-permute-start | bytes 2359304 | tf_op jit(solution)/shard_map/ppermute | solution.py:26
  442.1 56.6 %collective-permute-start.48 = (bf16[256,1536]{1,0:T(8,128)(2,1)}, bf16[256,1536]{1,0:T(8,128)(2,1)}, u32[]{:S(2)}, u32[]{:S(2)}) collective-permute-start(bf16[256,1536]{1,0:T(8,128)(2,1)} %get-tuple-element.453.refs_1_), channel_id=1, source_target_pairs={{0,1},{1,0},{2,3},{3,2},{4,5},{5,4},{6,7},{7,6},{8,9},{9,8},{10,11... | collective-permute-start | bytes 2359304 | tf_op jit(solution)/shard_map/ppermute | solution.py:26
  496.6 58.1 %collective-permute-start.49 = (bf16[384,3072]{1,0:T(8,128)(2,1)}, bf16[384,3072]{1,0:T(8,128)(2,1)}, u32[]{:S(2)}, u32[]{:S(2)}) collective-permute-start(bf16[384,3072]{1,0:T(8,128)(2,1)} %get-tuple-element.470), channel_id=1, source_target_pairs={{0,8},{8,0},{16,24},{24,16},{1,9},{9,1},{17,25},{25,17},{2,10},{10... | collective-permute-start | bytes 7077896 | tf_op jit(solution)/shard_map/ppermute | solution.py:26
  498.1 56.6 %collective-permute-start.50 = (bf16[384,3072]{1,0:T(8,128)(2,1)}, bf16[384,3072]{1,0:T(8,128)(2,1)}, u32[]{:S(2)}, u32[]{:S(2)}) collective-permute-start(bf16[384,3072]{1,0:T(8,128)(2,1)} %get-tuple-element.471), channel_id=1, source_target_pairs={{0,16},{8,24},{16,0},{24,8},{1,17},{9,25},{17,1},{25,9},{2,18},{10... | collective-permute-start | bytes 7077896 | tf_op jit(solution)/shard_map/ppermute | solution.py:26
  526.2 36.9 %collective-permute-start.53 = (bf16[256,1536]{1,0:T(8,128)(2,1)}, bf16[256,1536]{1,0:T(8,128)(2,1)}, u32[]{:S(2)}, u32[]{:S(2)}) collective-permute-start(bf16[256,1536]{1,0:T(8,128)(2,1)} %get-tuple-element.487.refs_1_), channel_id=1, source_target_pairs={{0,1},{1,0},{2,3},{3,2},{4,5},{5,4},{6,7},{7,6},{8,9},{9,8},{10,11... | collective-permute-start | bytes 2359304 | tf_op jit(solution)/shard_map/ppermute | solution.py:26
  554.1 58.3 %collective-permute-start.57 = (bf16[256,1536]{1,0:T(8,128)(2,1)}, bf16[256,1536]{1,0:T(8,128)(2,1)}, u32[]{:S(2)}, u32[]{:S(2)}) collective-permute-start(bf16[256,1536]{1,0:T(8,128)(2,1)} %get-tuple-element.497.refs_1_), channel_id=1, source_target_pairs={{0,1},{1,0},{2,3},{3,2},{4,5},{5,4},{6,7},{7,6},{8,9},{9,8},{10,11... | collective-permute-start | bytes 2359304 | tf_op jit(solution)/shard_map/ppermute | solution.py:26
  561.0 37.3 %collective-permute-start.54 = (bf16[192,3072]{1,0:T(8,128)(2,1)}, bf16[192,3072]{1,0:T(8,128)(2,1)}, u32[]{:S(2)}, u32[]{:S(2)}) collective-permute-start(bf16[192,3072]{1,0:T(8,128)(2,1)} %get-tuple-element.666), channel_id=1, source_target_pairs={{0,8},{8,0},{16,24},{24,16},{1,9},{9,1},{17,25},{25,17},{2,10},{10... | collective-permute-start | bytes 3538952 | tf_op jit(solution)/shard_map/ppermute | solution.py:26
  562.5 35.8 %collective-permute-start.55 = (bf16[192,3072]{1,0:T(8,128)(2,1)}, bf16[192,3072]{1,0:T(8,128)(2,1)}, u32[]{:S(2)}, u32[]{:S(2)}) collective-permute-start(bf16[192,3072]{1,0:T(8,128)(2,1)} %get-tuple-element.667), channel_id=1, source_target_pairs={{0,16},{8,24},{16,0},{24,8},{1,17},{9,25},{17,1},{25,9},{2,18},{10... | collective-permute-start | bytes 3538952 | tf_op jit(solution)/shard_map/ppermute | solution.py:26
  578.0 71.9 %collective-permute-start.62 = (bf16[256,1536]{1,0:T(8,128)(2,1)}, bf16[256,1536]{1,0:T(8,128)(2,1)}, u32[]{:S(2)}, u32[]{:S(2)}) collective-permute-start(bf16[256,1536]{1,0:T(8,128)(2,1)} %get-tuple-element.506.refs_1_), channel_id=1, source_target_pairs={{0,1},{1,0},{2,3},{3,2},{4,5},{5,4},{6,7},{7,6},{8,9},{9,8},{10,11... | collective-permute-start | bytes 2359304 | tf_op jit(solution)/shard_map/ppermute | solution.py:26
  647.8 63.8 %collective-permute-start.64 = (bf16[384,3072]{1,0:T(8,128)(2,1)}, bf16[384,3072]{1,0:T(8,128)(2,1)}, u32[]{:S(2)}, u32[]{:S(2)}) collective-permute-start(bf16[384,3072]{1,0:T(8,128)(2,1)} %get-tuple-element.532), channel_id=1, source_target_pairs={{0,8},{8,0},{16,24},{24,16},{1,9},{9,1},{17,25},{25,17},{2,10},{10... | collective-permute-start | bytes 7077896 | tf_op jit(solution)/shard_map/ppermute | solution.py:26
  648.4 63.2 %collective-permute-start.65 = (bf16[384,3072]{1,0:T(8,128)(2,1)}, bf16[384,3072]{1,0:T(8,128)(2,1)}, u32[]{:S(2)}, u32[]{:S(2)}) collective-permute-start(bf16[384,3072]{1,0:T(8,128)(2,1)} %get-tuple-element.533), channel_id=1, source_target_pairs={{0,16},{8,24},{16,0},{24,8},{1,17},{9,25},{17,1},{25,9},{2,18},{10... | collective-permute-start | bytes 7077896 | tf_op jit(solution)/shard_map/ppermute | solution.py:26
  716.3 32.8 %collective-permute-start.70 = (bf16[768,2304]{1,0:T(8,128)(2,1)S(1)}, bf16[768,2304]{1,0:T(8,128)(2,1)}, u32[]{:S(2)}, u32[]{:S(2)}) collective-permute-start(bf16[768,2304]{1,0:T(8,128)(2,1)S(1)} %copy-done.78), channel_id=1, source_target_pairs={{0,4},{4,0},{1,5},{5,1},{2,6},{6,2},{3,7},{7,3},{8,12},{12,8},{9,1... | collective-permute-start | bytes 10616840 | tf_op jit(solution)/shard_map/ppermute | solution.py:26
  721.2 38.4 %collective-permute-start.74 = (bf16[192,1152]{1,0:T(8,128)(2,1)}, bf16[192,1152]{1,0:T(8,128)(2,1)}, u32[]{:S(2)}, u32[]{:S(2)}) collective-permute-start(bf16[192,1152]{1,0:T(8,128)(2,1)} %get-tuple-element.676), channel_id=1, source_target_pairs={{0,8},{8,0},{16,24},{24,16},{1,9},{9,1},{17,25},{25,17},{2,10},{10... | collective-permute-start | bytes 1327112 | tf_op jit(solution)/shard_map/ppermute | solution.py:26
  721.8 37.9 %collective-permute-start.75 = (bf16[192,1152]{1,0:T(8,128)(2,1)}, bf16[192,1152]{1,0:T(8,128)(2,1)S(1)}, u32[]{:S(2)}, u32[]{:S(2)}) collective-permute-start(bf16[192,1152]{1,0:T(8,128)(2,1)} %get-tuple-element.677), channel_id=1, source_target_pairs={{0,16},{8,24},{16,0},{24,8},{1,17},{9,25},{17,1},{25,9},{2,18},{10... | collective-permute-start | bytes 1327112 | tf_op jit(solution)/shard_map/ppermute | solution.py:26
  745.2 53.3 %collective-permute-start.73 = (bf16[192,3072]{1,0:T(8,128)(2,1)S(1)}, bf16[192,3072]{1,0:T(8,128)(2,1)}, u32[]{:S(2)}, u32[]{:S(2)}) collective-permute-start(bf16[192,3072]{1,0:T(8,128)(2,1)S(1)} %copy-done.41), channel_id=1, source_target_pairs={{0,2},{1,3},{2,0},{3,1},{4,6},{5,7},{6,4},{7,5},{8,10},{9,11},{10,... | collective-permute-start | bytes 3538952 | tf_op jit(solution)/shard_map/ppermute | solution.py:26
  757.6 43.3 %collective-permute-start.71 = (bf16[384,1152]{1,0:T(8,128)(2,1)}, bf16[384,1152]{1,0:T(8,128)(2,1)S(1)}, u32[]{:S(2)}, u32[]{:S(2)}) collective-permute-start(bf16[384,1152]{1,0:T(8,128)(2,1)} %get-tuple-element.569), channel_id=1, source_target_pairs={{0,8},{8,0},{16,24},{24,16},{1,9},{9,1},{17,25},{25,17},{2,10},{10... | collective-permute-start | bytes 2654216 | tf_op jit(solution)/shard_map/ppermute | solution.py:26
  758.2 42.7 %collective-permute-start.72 = (bf16[384,1152]{1,0:T(8,128)(2,1)}, bf16[384,1152]{1,0:T(8,128)(2,1)S(1)}, u32[]{:S(2)}, u32[]{:S(2)}) collective-permute-start(bf16[384,1152]{1,0:T(8,128)(2,1)} %get-tuple-element.570), channel_id=1, source_target_pairs={{0,16},{8,24},{16,0},{24,8},{1,17},{9,25},{17,1},{25,9},{2,18},{10... | collective-permute-start | bytes 2654216 | tf_op jit(solution)/shard_map/ppermute | solution.py:26
  834.8 44.6 %collective-permute-start.85 = (bf16[256,768]{1,0:T(8,128)(2,1)S(1)}, bf16[256,768]{1,0:T(8,128)(2,1)S(1)}, u32[]{:S(2)}, u32[]{:S(2)}) collective-permute-start(bf16[256,768]{1,0:T(8,128)(2,1)S(1)} %select_convert_fusion.1), channel_id=1, source_target_pairs={{0,2},{1,3},{2,0},{3,1},{4,6},{5,7},{6,4},{7,5},{8,10},{9,11},{10,... | collective-permute-start | bytes 1179656 | tf_op jit(solution)/shard_map/ppermute | solution.py:26
  834.9 46.8 %collective-permute-start.89 = (bf16[192,3072]{1,0:T(8,128)(2,1)S(1)}, bf16[192,3072]{1,0:T(8,128)(2,1)S(1)}, u32[]{:S(2)}, u32[]{:S(2)}) collective-permute-start(bf16[192,3072]{1,0:T(8,128)(2,1)S(1)} %pad_maximum_fusion.3), channel_id=1, source_target_pairs={{0,16},{8,24},{16,0},{24,8},{1,17},{9,25},{17,1},{25,9},{2,18},{10... | collective-permute-start | bytes 3538952 | tf_op jit(solution)/shard_map/ppermute | solution.py:26
  836.5 45.4 %collective-permute-start.88 = (bf16[192,3072]{1,0:T(8,128)(2,1)S(1)}, bf16[192,3072]{1,0:T(8,128)(2,1)S(1)}, u32[]{:S(2)}, u32[]{:S(2)}) collective-permute-start(bf16[192,3072]{1,0:T(8,128)(2,1)S(1)} %copy-done.42), channel_id=1, source_target_pairs={{0,8},{8,0},{16,24},{24,16},{1,9},{9,1},{17,25},{25,17},{2,10},{10... | collective-permute-start | bytes 3538952 | tf_op jit(solution)/shard_map/ppermute | solution.py:26
  837.4 76.8 %collective-permute-start.79 = (bf16[192,3072]{1,0:T(8,128)(2,1)}, bf16[192,3072]{1,0:T(8,128)(2,1)}, u32[]{:S(2)}, u32[]{:S(2)}) collective-permute-start(bf16[192,3072]{1,0:T(8,128)(2,1)} %add_convert_fusion.4), channel_id=1, source_target_pairs={{0,2},{1,3},{2,0},{3,1},{4,6},{5,7},{6,4},{7,5},{8,10},{9,11},{10,... | collective-permute-start | bytes 3538952 | tf_op jit(solution)/shard_map/ppermute | solution.py:26
  881.8 41.7 %collective-permute-start.78 = (bf16[192,1152]{1,0:T(8,128)(2,1)}, bf16[192,1152]{1,0:T(8,128)(2,1)S(1)}, u32[]{:S(2)}, u32[]{:S(2)}) collective-permute-start(bf16[192,1152]{1,0:T(8,128)(2,1)} %add_convert_fusion.15), channel_id=1, source_target_pairs={{0,2},{1,3},{2,0},{3,1},{4,6},{5,7},{6,4},{7,5},{8,10},{9,11},{10,... | collective-permute-start | bytes 1327112 | tf_op jit(solution)/shard_map/ppermute | solution.py:26
  890.9 51.2 %collective-permute-start.92 = (bf16[192,1152]{1,0:T(8,128)(2,1)S(1)}, bf16[192,1152]{1,0:T(8,128)(2,1)S(1)}, u32[]{:S(2)}, u32[]{:S(2)}) collective-permute-start(bf16[192,1152]{1,0:T(8,128)(2,1)S(1)} %pad_maximum_fusion.11), channel_id=1, source_target_pairs={{0,8},{8,0},{16,24},{24,16},{1,9},{9,1},{17,25},{25,17},{2,10},{10... | collective-permute-start | bytes 1327112 | tf_op jit(solution)/shard_map/ppermute | solution.py:26
  951.5 35.1 %collective-permute-start.106 = (f32[2,2,768]{2,1,0:T(2,128)S(1)}, f32[2,2,768]{2,1,0:T(2,128)S(1)}, u32[]{:S(2)}, u32[]{:S(2)}) collective-permute-start(f32[2,2,768]{2,1,0:T(2,128)S(1)} %fusion.17), channel_id=1, source_target_pairs={{0,2},{1,3},{2,0},{3,1},{4,6},{5,7},{6,4},{7,5},{8,10},{9,11},{10,... | collective-permute-start | bytes 36872 | tf_op jit(solution)/shard_map/ppermute | solution.py:26
  954.5 59.3 %collective-permute-start.103 = (bf16[192,3072]{1,0:T(8,128)(2,1)}, bf16[192,3072]{1,0:T(8,128)(2,1)S(1)}, u32[]{:S(2)}, u32[]{:S(2)}) collective-permute-start(bf16[192,3072]{1,0:T(8,128)(2,1)} %pad_maximum_fusion.4), channel_id=1, source_target_pairs={{0,8},{8,0},{16,24},{24,16},{1,9},{9,1},{17,25},{25,17},{2,10},{10... | collective-permute-start | bytes 3538952 | tf_op jit(solution)/shard_map/ppermute | solution.py:26
  957.1 56.7 %collective-permute-start.104 = (bf16[192,3072]{1,0:T(8,128)(2,1)}, bf16[192,3072]{1,0:T(8,128)(2,1)S(1)}, u32[]{:S(2)}, u32[]{:S(2)}) collective-permute-start(bf16[192,3072]{1,0:T(8,128)(2,1)} %pad_maximum_fusion.5), channel_id=1, source_target_pairs={{0,16},{8,24},{16,0},{24,8},{1,17},{9,25},{17,1},{25,9},{2,18},{10... | collective-permute-start | bytes 3538952 | tf_op jit(solution)/shard_map/ppermute | solution.py:26
  (166 other events, 2556.9 us)
Sparse Core Ops, SparseCore 0:
  108.1 30.5 all-gather.8
  140.5 31.0 all-gather.10
  173.9 30.9 all-gather.12
  218.3 29.9 all-gather.20
  250.0 30.9 all-gather.14
  291.6 29.6 all-gather.16
  323.7 30.9 all-gather.18

commit v2 on v1

--- a/solution.py
+++ b/solution.py
@@ -19,6 +19,7 @@
 TN = (((0,), (0,)), ((), ()))
 ROOM = 56 * 2**20
 SCALE = 30
+AHEAD = 8 * 2**20
 
 
 def hop(value, axis, distance):
@@ -105,17 +106,61 @@
 
     def view(self, ref):
         ref = ref if self.layer is None else ref.at[self.layer]
+        if self.shape == tuple(ref.shape):
+            return ref
         return ref.at[pl.ds(self.row, self.shape[0]), pl.ds(self.column, self.shape[1])]
 
     def scratch(self):
-        return pltpu.VMEM(self.shape, LOW)
-
-
-def copies_of(parts, refs, held, sems):
-    return [
-        pltpu.make_async_copy(part.view(ref), to, sems.at[i])
-        for i, (part, ref, to) in enumerate(zip(parts, refs, held))
-    ]
+        return pltpu.VMEM(self.shape, self.array.dtype)
+
+
+class Stream:
+    def __init__(self, sources, buffers, sems, ahead):
+        self.copies = [
+            pltpu.make_async_copy(source, buffer, sems.at[i])
+            for i, (source, buffer) in enumerate(zip(sources, buffers))
+        ]
+        self.buffers = buffers
+        self.sizes = [
+            b.shape[0] * b.shape[1] * (4 if b.dtype == FULL else 2) for b in buffers
+        ]
+        self.ahead, self.started, self.waited = ahead, 0, 0
+        self.feed()
+
+    def feed(self):
+        while self.started < len(self.copies) and (
+            sum(self.sizes[self.waited : self.started]) < self.ahead
+        ):
+            self.copies[self.started].start()
+            self.started += 1
+
+    def take(self, count):
+        first = self.waited
+        for i in range(first, first + count):
+            if i >= self.started:
+                self.copies[i].start()
+                self.started += 1
+            self.copies[i].wait()
+            self.waited += 1
+        self.feed()
+        return self.buffers[first : first + count]
+
+
+class Results:
+    def __init__(self, buffers, targets, sems):
+        self.buffers, self.targets, self.sems = buffers, targets, sems
+        self.copies = []
+
+    def put(self, index):
+        copy = pltpu.make_async_copy(
+            self.buffers[index], self.targets[index], self.sems.at[index]
+        )
+        copy.start()
+        self.copies.append(copy)
+
+    def finish(self):
+        for copy in self.copies:
+            copy.wait()
 
 
 def half_dots(left, first, second):
@@ -137,30 +182,33 @@
     return (query, rest)
 
 
-def put_norm(refs, outs):
-    hidden_ref, left_ref, right_ref, gain_ref = refs
-    sum_ref, factor_ref, normed_ref = outs
-    hidden = hidden_ref[...].astype(FULL)
-    if left_ref is not None:
-        hidden = hidden + left_ref[...].astype(FULL) + right_ref[...].astype(FULL)
+def put_norm(refs, gain_ref, results, at):
+    sum_ref, factor_ref, normed_ref = results.buffers[at : at + 3]
+    hidden = refs[0][...].astype(FULL)
+    for ref in refs[1:]:
+        hidden = hidden + ref[...].astype(FULL)
     factor = lax.rsqrt(jnp.mean(hidden * hidden, axis=-1, keepdims=True) + EPSILON)
     sum_ref[...] = hidden
     factor_ref[...] = factor
     normed_ref[...] = (hidden * factor * gain_ref[...]).astype(LOW)
-
-
-def put_norm_back(refs, outs):
+    for i in range(3):
+        results.put(at + i)
+
+
+def put_norm_back(refs, results, at):
     grad_ref, left_ref, right_ref, hidden_ref, factor_ref, gain_ref = refs
-    sum_ref, low_ref, gain_out_ref = outs
+    sum_ref, low_ref, gain_out_ref = results.buffers[at : at + 3]
     grad_normed = left_ref[...].astype(FULL) + right_ref[...].astype(FULL)
     factor = factor_ref[...]
     unit = hidden_ref[...] * factor
     grad_unit = grad_normed * gain_ref[...]
     inner = jnp.mean(grad_unit * unit, axis=-1, keepdims=True)
-    grad = grad_ref[...] + factor * (grad_unit - unit * inner)
+    grad = grad_ref[...].astype(FULL) + factor * (grad_unit - unit * inner)
     sum_ref[...] = grad
     low_ref[...] = grad.astype(LOW)
     gain_out_ref[...] = jnp.sum(grad_normed * unit, axis=0, keepdims=True)
+    for i in range(3):
+        results.put(at + i)
 
 
 def norm_shapes(rows, wide):
@@ -171,68 +219,69 @@
     return [((rows, wide), FULL), ((rows, wide), LOW), ((1, wide), FULL)]
 
 
-def call(kernel, name, operands, parts, outs, scratch, flops, exps=0, scalars=()):
-    size = sum(2 * p.shape[0] * p.shape[1] for p in parts) + sum(
-        s[0] * s[1] * (4 if k == FULL else 2) for s, k in outs
-    )
+def call(body, name, inputs, outs, scratch, flops, exps=0, scalars=(), ahead=AHEAD):
+    inputs = [v if isinstance(v, Part) else Part(v) for v in inputs]
+    size = sum(2 * p.shape[0] * p.shape[1] for p in inputs)
+    count, made = len(inputs), len(outs)
+
+    def kernel(*refs):
+        scalar_refs, refs = refs[: len(scalars)], refs[len(scalars) :]
+        sources, targets, refs = refs[:count], refs[count : count + made], refs[count + made :]
+        held, buffers, refs = refs[:count], refs[count : count + made], refs[count + made :]
+        in_sems, out_sems, own = refs[0], refs[1], refs[2:]
+        stream = Stream([p.view(r) for p, r in zip(inputs, sources)], held, in_sems, ahead)
+        results = Results(buffers, targets, out_sems)
+        body(stream, results, *scalar_refs, *own)
+        results.finish()
+
     return pl.pallas_call(
         kernel,
         grid_spec=pltpu.PrefetchScalarGridSpec(
             num_scalar_prefetch=len(scalars),
             grid=(1,),
-            in_specs=[whole(v.shape) for v in operands] + [far()] * len(parts),
-            out_specs=[whole(s) for s, _ in outs],
-            scratch_shapes=list(scratch)
-            + [p.scratch() for p in parts]
-            + [pltpu.SemaphoreType.DMA((max(len(parts), 1),))],
+            in_specs=[far()] * count,
+            out_specs=[far()] * made,
+            scratch_shapes=[p.scratch() for p in inputs]
+            + [pltpu.VMEM(s, k) for s, k in outs]
+            + [pltpu.SemaphoreType.DMA((count,)), pltpu.SemaphoreType.DMA((made,))]
+            + list(scratch),
         ),
         out_shape=[jax.ShapeDtypeStruct(s, k) for s, k in outs],
         compiler_params=limits(),
         cost_estimate=cost(flops, size, exps),
         name=name,
-    )(*scalars, *operands, *[p.array for p in parts])
-
-
-def take(refs, *counts):
-    out, at = [], 0
-    for count in counts:
-        out.append(refs[at : at + count])
-        at += count
-    return out + [refs[at:]]
-
-
-def project_kernel(parts, first, *refs):
-    ins, refs = take(refs, 2 if first else 4)
-    (cos_ref, sin_ref), hbm, outs, (q_ref, kv_ref), held, (sems,) = take(
-        refs, 2, len(parts), 3, 2, len(parts)
-    )
-    copies = copies_of(parts, hbm, held, sems)
-    for copy in copies:
-        copy.start()
-    put_norm([ins[0], None, None, ins[1]] if first else ins, outs)
-    normed_ref = outs[2]
-    q_width = cos_ref.shape[1]
-    for side in range(2):
-        copies[2 * side].wait()
-        copies[2 * side + 1].wait()
-        projected = half_dots(normed_ref[...], held[2 * side][...], held[2 * side + 1][...])
-        query, rest = turn(projected, cos_ref[...], sin_ref[...])
-        here = slice(side * q_width, (side + 1) * q_width)
-        q_ref[:, here] = query.astype(LOW)
-        kv_ref[:, here] = rest.astype(LOW)
+    )(*scalars, *[p.array for p in inputs])
 
 
 def project(hidden, pair, gain, parts, cosine, sine):
     rows, wide = hidden.shape
-    both = 2 * cosine.shape[1]
+    q_width = cosine.shape[1]
+    ins = [hidden, *(pair or ())]
+
+    def body(stream, results):
+        refs = stream.take(len(ins))
+        (gain_ref,) = stream.take(1)
+        put_norm(refs, gain_ref, results, 0)
+        cos_ref, sin_ref = stream.take(2)
+        tokens = results.buffers[2][...]
+        q_ref, kv_ref = results.buffers[3:]
+        for side in range(2):
+            first, second = stream.take(2)
+            projected = half_dots(tokens, first[...], second[...])
+            query, rest = turn(projected, cos_ref[...], sin_ref[...])
+            here = slice(side * q_width, (side + 1) * q_width)
+            q_ref[:, here] = query.astype(LOW)
+            kv_ref[:, here] = rest.astype(LOW)
+        results.put(4)
+        results.put(3)
+
     return call(
-        functools.partial(project_kernel, parts, pair is None),
+        body,
         "project",
-        [hidden, *(pair or ()), gain, cosine, sine],
-        parts,
-        norm_shapes(rows, wide) + [((rows, both), LOW)] * 2,
+        [*ins, gain, cosine, sine, *parts],
+        norm_shapes(rows, wide) + [((rows, 2 * q_width), LOW)] * 2,
         [],
-        4 * rows * wide * both,
+        8 * rows * wide * q_width,
     )
 
 
@@ -251,228 +300,192 @@
     return ["all"] * (2 * chunks - 2) + ["own", "sib"]
 
 
-def attend_kernel(chunks, parts, core_ref, q_ref, *refs):
-    kv_refs, refs = refs[: 2 * chunks], refs[2 * chunks :]
-    count = len(parts)
-    hbm, (att_ref, lse_ref, part_ref) = refs[:count], refs[count : count + 3]
-    held, sems = refs[count + 3 : -1], refs[-1]
-    copies = copies_of(parts, hbm, held, sems)
-    for copy in copies:
-        copy.start()
-    core = core_ref[0]
-    q_width = q_ref.shape[1] // 2
-    kv_width = q_width // 2
-    heads = q_width // HEAD
-    for h in range(2 * heads):
-        group = (h // heads) * q_width + (h % heads) // 2 * HEAD
-        mine = slice(h * HEAD, (h + 1) * HEAD)
-        query = q_ref[:, mine]
-        scores = [
-            score(ref[:, group : group + HEAD], query, kind, core)
-            for ref, kind in zip(kv_refs, kinds_of(chunks))
-        ]
-        highest = functools.reduce(
-            jnp.maximum, [jnp.max(s, axis=0, keepdims=True) for s in scores]
-        )
-        exps = [jnp.exp(s - highest) for s in scores]
-        total = sum(jnp.sum(e, axis=0, keepdims=True) for e in exps)
-        share = 1.0 / total
-        lse_ref[h : h + 1, :] = highest + jnp.log(total)
-        spot = slice(group + kv_width, group + kv_width + HEAD)
-        att = sum(dot_tn((e * share).astype(LOW), ref[:, spot]) for e, ref in zip(exps, kv_refs))
-        att_ref[:, mine] = att.astype(LOW)
-    for copy in copies:
-        copy.wait()
-    wide = part_ref.shape[1]
-    for side in range(2):
-        columns = slice(side * wide // 2, (side + 1) * wide // 2)
-        total = low_dot(att_ref[:, :q_width], held[side][...])
-        total = total + low_dot(att_ref[:, q_width:], held[2 + side][...])
-        part_ref[:, columns] = total.astype(LOW)
-
-
 def attend(core, query, kvs, parts):
     rows, both = query.shape
-    heads = both // HEAD
     wide = 2 * parts[0].shape[1]
     chunks = len(kvs) // 2
-    shapes = [(rows, both), (heads, rows), (rows, wide)]
-    operands = [query] + list(kvs)
-    return pl.pallas_call(
-        functools.partial(attend_kernel, chunks, parts),
-        grid_spec=pltpu.PrefetchScalarGridSpec(
-            num_scalar_prefetch=1,
-            grid=(1,),
-            in_specs=[whole(v.shape) for v in operands] + [far()] * len(parts),
-            out_specs=[whole(s) for s in shapes],
-            scratch_shapes=[p.scratch() for p in parts] + [pltpu.SemaphoreType.DMA((len(parts),))],
-        ),
-        out_shape=[
-            jax.ShapeDtypeStruct(s, FULL if i == 1 else LOW) for i, s in enumerate(shapes)
-        ],
-        compiler_params=limits(),
-        cost_estimate=cost(
-            8 * heads * rows * rows * len(kvs) * 128 + 2 * rows * both * wide,
-            2 * both * wide + 4 * rows * wide,
-            heads * rows * rows * len(kvs),
-        ),
-        name="attend",
-    )(core, *operands, *[p.array for p in parts])
-
-
-def attend_back_kernel(chunks, has_held, parts, core_ref, *refs):
-    ins, (q_ref, lse_ref), refs = take(refs, 6, 2)
-    kv_refs, refs = refs[: 2 * chunks], refs[2 * chunks :]
-    held_refs, refs = (refs[:2], refs[2:]) if has_held else (None, refs)
-    count = len(parts)
-    hbm, outs, (dq_ref,), out_refs, (grad_ref,), held, (sems,) = take(
-        refs, count, 3, 1, 2 * chunks, 1, count
-    )
-    copies = copies_of(parts, hbm, held, sems)
-    for copy in copies:
-        copy.start()
-    put_norm_back(ins, outs)
-    g_ref = outs[1]
-    core = core_ref[0]
-    q_width = q_ref.shape[1] // 2
+    q_width, heads = both // 2, both // 2 // HEAD
     kv_width = q_width // 2
-    heads = q_width // HEAD
-    half = g_ref.shape[1] // 2
-    scale = HEAD ** (-0.5)
-    for copy in copies:
-        copy.wait()
-    for side in range(2):
-        grad = dot_nt(g_ref[:, :half], held[2 * side][...])
-        grad = grad + dot_nt(g_ref[:, half:], held[2 * side + 1][...])
-        grad_ref[:, side * q_width : (side + 1) * q_width] = grad.astype(LOW)
-    for first in range(0, 2 * heads, 2):
-        group = (first // heads) * q_width + (first % heads) // 2 * HEAD
-        key_spot = slice(group, group + HEAD)
-        value_spot = slice(group + kv_width, group + kv_width + HEAD)
-        key_sums, value_sums = [0.0] * len(kv_refs), [0.0] * len(kv_refs)
-        for h in (first, first + 1):
+
+    def body(stream, results, core_ref):
+        (q_ref,), kv_refs = stream.take(1), stream.take(2 * chunks)
+        att_ref, lse_ref, part_ref = results.buffers
+        side_core = core_ref[0]
+        for h in range(2 * heads):
+            group = (h // heads) * q_width + (h % heads) // 2 * HEAD
             mine = slice(h * HEAD, (h + 1) * HEAD)
-            query, grad, lse = q_ref[:, mine], grad_ref[:, mine], lse_ref[h : h + 1, :]
-            probs = [
-                jnp.exp(score(ref[:, key_spot], query, kind, core) - lse)
+            query = q_ref[:, mine]
+            scores = [
+                score(ref[:, group : group + HEAD], query, kind, side_core)
                 for ref, kind in zip(kv_refs, kinds_of(chunks))
             ]
-            prob_grads = [dot_nt(ref[:, value_spot], grad) for ref in kv_refs]
-            delta = sum(
-                jnp.sum(p * d, axis=0, keepdims=True) for p, d in zip(probs, prob_grads)
+            highest = functools.reduce(
+                jnp.maximum, [jnp.max(s, axis=0, keepdims=True) for s in scores]
             )
-            query_grad = 0.0
-            for i, (p, d, ref) in enumerate(zip(probs, prob_grads, kv_refs)):
-                score_grad = (p * (d - delta)).astype(LOW)
-                query_grad = query_grad + dot_tn(score_grad, ref[:, key_spot])
-                key_sums[i] = key_sums[i] + low_dot(score_grad, query)
-                value_sums[i] = value_sums[i] + low_dot(p.astype(LOW), grad)
-            dq_ref[:, mine] = query_grad * scale
-        for i, out_ref in enumerate(out_refs):
-            for spot, value in ((key_spot, key_sums[i] * scale), (value_spot, value_sums[i])):
-                if has_held and i >= 2 * chunks - 2:
-                    value = value + held_refs[i - 2 * chunks + 2][:, spot]
-                out_ref[:, spot] = value.astype(out_ref.dtype)
+            exps = [jnp.exp(s - highest) for s in scores]
+            total = sum(jnp.sum(e, axis=0, keepdims=True) for e in exps)
+            share = 1.0 / total
+            lse_ref[h : h + 1, :] = highest + jnp.log(total)
+            spot = slice(group + kv_width, group + kv_width + HEAD)
+            att = sum(
+                dot_tn((e * share).astype(LOW), ref[:, spot]) for e, ref in zip(exps, kv_refs)
+            )
+            att_ref[:, mine] = att.astype(LOW)
+        results.put(0)
+        results.put(1)
+        weights = stream.take(4)
+        for side in range(2):
+            columns = slice(side * wide // 2, (side + 1) * wide // 2)
+            total = low_dot(att_ref[:, :q_width], weights[side][...])
+            total = total + low_dot(att_ref[:, q_width:], weights[2 + side][...])
+            part_ref[:, columns] = total.astype(LOW)
+        results.put(2)
+
+    return call(
+        body,
+        "attend",
+        [query, *kvs, *parts],
+        [((rows, both), LOW), ((2 * heads, rows), FULL), ((rows, wide), LOW)],
+        [],
+        16 * heads * rows * rows * len(kvs) * 128 + 2 * rows * both * wide,
+        2 * heads * rows * rows * len(kvs),
+        (core,),
+    )
 
 
 def attend_back(core, norm_ins, query, lse, kvs, held, parts):
     rows, both = query.shape
-    heads = both // HEAD
     wide = norm_ins[0].shape[1]
     chunks = len(kvs) // 2
+    q_width, heads = both // 2, both // 2 // HEAD
+    kv_width = q_width // 2
+    half = wide // 2
+    scale = HEAD ** (-0.5)
+
+    def body(stream, results, core_ref, grad_ref):
+        put_norm_back(stream.take(6), results, 0)
+        g_ref = results.buffers[1]
+        side_core = core_ref[0]
+        for side in range(2):
+            first, second = stream.take(2)
+            grad = dot_nt(g_ref[:, :half], first[...])
+            grad = grad + dot_nt(g_ref[:, half:], second[...])
+            grad_ref[:, side * q_width : (side + 1) * q_width] = grad.astype(LOW)
+        (q_ref,), (lse_ref,), kv_refs = stream.take(1), stream.take(1), stream.take(2 * chunks)
+        held_refs = stream.take(2) if held is not None else None
+        dq_ref, out_refs = results.buffers[3], results.buffers[4:]
+        for first in range(0, 2 * heads, 2):
+            group = (first // heads) * q_width + (first % heads) // 2 * HEAD
+            key_spot = slice(group, group + HEAD)
+            value_spot = slice(group + kv_width, group + kv_width + HEAD)
+            key_sums, value_sums = [0.0] * len(kv_refs), [0.0] * len(kv_refs)
+            for h in (first, first + 1):
+                mine = slice(h * HEAD, (h + 1) * HEAD)
+                query, grad, lse = q_ref[:, mine], grad_ref[:, mine], lse_ref[h : h + 1, :]
+                probs = [
+                    jnp.exp(score(ref[:, key_spot], query, kind, side_core) - lse)
+                    for ref, kind in zip(kv_refs, kinds_of(chunks))
+                ]
+                prob_grads = [dot_nt(ref[:, value_spot], grad) for ref in kv_refs]
+                delta = sum(
+                    jnp.sum(p * d, axis=0, keepdims=True) for p, d in zip(probs, prob_grads)
+                )
+                query_grad = 0.0
+                for i, (p, d, ref) in enumerate(zip(probs, prob_grads, kv_refs)):
+                    score_grad = (p * (d - delta)).astype(LOW)
+                    query_grad = query_grad + dot_tn(score_grad, ref[:, key_spot])
+                    key_sums[i] = key_sums[i] + low_dot(score_grad, query)
+                    value_sums[i] = value_sums[i] + low_dot(p.astype(LOW), grad)
+                dq_ref[:, mine] = query_grad * scale
+            for i, out_ref in enumerate(out_refs):
+                for spot, value in ((key_spot, key_sums[i] * scale), (value_spot, value_sums[i])):
+                    if held is not None and i >= 2 * chunks - 2:
+                        value = value + held_refs[i - 2 * chunks + 2][:, spot]
+                    out_ref[:, spot] = value.astype(out_ref.dtype)
+        for i in range(3, 4 + 2 * chunks):
+            results.put(i)
+
+    kinds = [FULL] * (2 * chunks) + [LOW]
     return call(
-        functools.partial(attend_back_kernel, chunks, held is not None, parts),
+        body,
         "attend_back",
-        [*norm_ins, query, lse, *kvs, *(held or ())],
-        parts,
-        norm_back_shapes(rows, wide) + [((rows, both), FULL)] * (2 * chunks + 1),
+        [*norm_ins, *parts, query, lse, *kvs, *(held or ())],
+        norm_back_shapes(rows, wide) + [((rows, both), k) for k in kinds],
         [pltpu.VMEM((rows, both), LOW)],
-        20 * heads * rows * rows * len(kvs) * 128 + 2 * rows * both * wide,
-        heads * rows * rows * len(kvs),
+        40 * heads * rows * rows * len(kvs) * 128 + 2 * rows * both * wide,
+        2 * heads * rows * rows * len(kvs),
         (core,),
     )
-
-
-def project_back_kernel(parts, dq_ref, own_ref, came_ref, cos_ref, sin_ref, *refs):
-    count = len(parts)
-    hbm, (proj_ref, part_ref), held, sems = refs[:count], refs[count : count + 2], refs[count + 2 : -1], refs[-1]
-    copies = copies_of(parts, hbm, held, sems)
-    for copy in copies:
-        copy.start()
-    q_width = cos_ref.shape[1]
-    half = part_ref.shape[1] // 2
-    for side in range(2):
-        here = slice(side * q_width, (side + 1) * q_width)
-        rest = own_ref[:, here] + came_ref[:, here].astype(FULL)
-        flat = jnp.concatenate([dq_ref[:, here], rest], axis=1)
-        query, rest = turn(flat, cos_ref[...], -sin_ref[...])
-        start = 2 * side * q_width
-        proj_ref[:, start : start + q_width] = query.astype(LOW)
-        proj_ref[:, start + q_width : start + 2 * q_width] = rest.astype(LOW)
-    for copy in copies:
-        copy.wait()
-    for side in range(2):
-        total = dot_nt(proj_ref[:, : 2 * q_width], held[side][...])
-        total = total + dot_nt(proj_ref[:, 2 * q_width :], held[2 + side][...])
-        part_ref[:, side * half : (side + 1) * half] = total.astype(LOW)
 
 
 def project_back(dq, own, came, cosine, sine, parts):
     rows, both = dq.shape
     wide = 2 * parts[0].shape[0]
-    operands = [dq, own, came, cosine, sine]
-    shapes = [(rows, 2 * both), (rows, wide)]
-    return pl.pallas_call(
-        functools.partial(project_back_kernel, parts),
-        in_specs=[whole(v.shape) for v in operands] + [far()] * len(parts),
-        out_specs=[whole(s) for s in shapes],
-        out_shape=[jax.ShapeDtypeStruct(s, LOW) for s in shapes],
-        grid=(1,),
-        scratch_shapes=[p.scratch() for p in parts] + [pltpu.SemaphoreType.DMA((len(parts),))],
-        compiler_params=limits(),
-        cost_estimate=cost(4 * rows * wide * both, 4 * wide * both + 12 * rows * both),
-        name="project_back",
-    )(*operands, *[p.array for p in parts])
-
-
-def ff_kernel(parts, *refs):
-    ins, hbm, outs, (gate_ref, up_ref, inner_ref, part_ref), held, (sems,) = take(
-        refs, 4, len(parts), 3, 4, len(parts)
+    q_width, half = both // 2, wide // 2
+
+    def body(stream, results):
+        cos_ref, sin_ref, dq_ref, own_ref, came_ref = stream.take(5)
+        proj_ref, part_ref = results.buffers
+        for side in range(2):
+            here = slice(side * q_width, (side + 1) * q_width)
+            rest = own_ref[:, here] + came_ref[:, here].astype(FULL)
+            flat = jnp.concatenate([dq_ref[:, here], rest], axis=1)
+            query, rest = turn(flat, cos_ref[...], -sin_ref[...])
+            start = 2 * side * q_width
+            proj_ref[:, start : start + q_width] = query.astype(LOW)
+            proj_ref[:, start + q_width : start + 2 * q_width] = rest.astype(LOW)
+        results.put(0)
+        for side in range(2):
+            own_w, other_w = stream.take(2)
+            total = dot_nt(proj_ref[:, : 2 * q_width], own_w[...])
+            total = total + dot_nt(proj_ref[:, 2 * q_width :], other_w[...])
+            part_ref[:, side * half : (side + 1) * half] = total.astype(LOW)
+        results.put(1)
+
+    return call(
+        body,
+        "project_back",
+        [cosine, sine, dq, own, came, parts[0], parts[2], parts[1], parts[3]],
+        [((rows, 2 * both), LOW), ((rows, wide), LOW)],
+        [],
+        4 * rows * wide * both,
     )
-    copies = copies_of(parts, hbm, held, sems)
-    for copy in copies:
-        copy.start()
-    put_norm(ins, outs)
-    tokens = outs[2][...]
-    ff = gate_ref.shape[1] // 2
-    half = part_ref.shape[1] // 2
-    for side in range(2):
-        for copy in copies[4 * side : 4 * side + 4]:
-            copy.wait()
-        g1_ref, g2_ref, u1_ref, u2_ref = held[4 * side : 4 * side + 4]
-        here = slice(side * ff, (side + 1) * ff)
-        gate = half_dots(tokens, g1_ref[...], g2_ref[...])
-        up = half_dots(tokens, u1_ref[...], u2_ref[...])
-        gate_ref[:, here] = gate.astype(LOW)
-        up_ref[:, here] = up.astype(LOW)
-        inner_ref[:, here] = (gate * jax.nn.sigmoid(gate) * up).astype(LOW)
-    for copy in copies[8:]:
-        copy.wait()
-    for side in range(2):
-        total = low_dot(inner_ref[:, :ff], held[8 + side][...])
-        total = total + dot_nt(inner_ref[:, ff:], held[10 + side][...])
-        part_ref[:, side * half : (side + 1) * half] = total.astype(LOW)
 
 
 def feed_forward(hidden, pair, gain, pair_parts, down_parts):
     rows, wide = hidden.shape
     ff = down_parts[0].shape[0]
-    parts = pair_parts + down_parts
+    half = wide // 2
+
+    def body(stream, results):
+        refs = stream.take(3)
+        (gain_ref,) = stream.take(1)
+        put_norm(refs, gain_ref, results, 0)
+        tokens = results.buffers[2][...]
+        gate_ref, up_ref, inner_ref, part_ref = results.buffers[3:]
+        for side in range(2):
+            here = slice(side * ff, (side + 1) * ff)
+            first, second = stream.take(2)
+            gate = half_dots(tokens, first[...], second[...])
+            gate_ref[:, here] = gate.astype(LOW)
+            gate = gate * jax.nn.sigmoid(gate)
+            first, second = stream.take(2)
+            up = half_dots(tokens, first[...], second[...])
+            up_ref[:, here] = up.astype(LOW)
+            inner_ref[:, here] = (gate * up).astype(LOW)
+        for i in range(3, 6):
+            results.put(i)
+        for side in range(2):
+            own, other = stream.take(2)
+            total = low_dot(inner_ref[:, :ff], own[...])
+            total = total + dot_nt(inner_ref[:, ff:], other[...])
+            part_ref[:, side * half : (side + 1) * half] = total.astype(LOW)
+        results.put(6)
+
     return call(
-        functools.partial(ff_kernel, parts),
+        body,
         "feed_forward",
-        [hidden, *pair, gain],
-        parts,
+        [hidden, *pair, gain, *pair_parts, *[down_parts[i] for i in (0, 2, 1, 3)]],
         norm_shapes(rows, wide) + [((rows, 2 * ff), LOW)] * 3 + [((rows, wide), LOW)],
         [],
         12 * rows * wide * ff,
@@ -480,56 +493,51 @@
     )
 
 
-def ff_back_kernel(parts, first, *refs):
-    ins, (gate_ref, up_ref), hbm, refs = take(refs, 1 if first else 6, 2, len(parts))
-    outs, (grad_ref, part_ref), held, (sems,) = take(refs, 0 if first else 3, 2, len(parts))
-    copies = copies_of(parts, hbm, held, sems)
-    for copy in copies:
-        copy.start()
-    if first:
-        x_ref = ins[0]
-    else:
-        put_norm_back(ins, outs)
-        x_ref = outs[1]
-    half = x_ref.shape[1] // 2
-    ff = gate_ref.shape[1] // 2
-    for side in range(2):
-        for copy in copies[2 * side : 2 * side + 2]:
-            copy.wait()
-        here = slice(side * ff, (side + 1) * ff)
-        times = low_dot if side else dot_nt
-        inner_grad = times(x_ref[:, :half], held[2 * side][...])
-        inner_grad = inner_grad + times(x_ref[:, half:], held[2 * side + 1][...])
-        gate, up = gate_ref[:, here].astype(FULL), up_ref[:, here].astype(FULL)
-        sigma = jax.nn.sigmoid(gate)
-        start = 2 * side * ff
-        grad_ref[:, start : start + ff] = (
-            inner_grad * up * sigma * (1.0 + gate * (1.0 - sigma))
-        ).astype(LOW)
-        grad_ref[:, start + ff : start + 2 * ff] = (inner_grad * gate * sigma).astype(LOW)
-    for copy in copies[4:]:
-        copy.wait()
-    for side in range(2):
-        total = 0.0
-        for i in range(4):
-            grad = grad_ref[:, i * ff : (i + 1) * ff]
-            total = total + dot_nt(grad, held[4 + 2 * i + side][...])
-        part_ref[:, side * half : (side + 1) * half] = total.astype(LOW)
-
-
 def feed_back(norm_ins, gate, up, pair_parts, down_parts):
     rows, wide = norm_ins[0].shape
     ff = down_parts[0].shape[0]
-    g, u = (0, 1, 4, 5), (2, 3, 6, 7)
-    order = [g[0], g[1], u[0], u[1], g[2], g[3], u[2], u[3]]
-    parts = down_parts + [pair_parts[i] for i in order]
-    first = len(norm_ins) == 1
+    half = wide // 2
+    first_layer = len(norm_ins) == 1
+    order = (0, 2, 4, 6, 1, 3, 5, 7)
+    base = 0 if first_layer else 3
+
+    def body(stream, results):
+        ins = stream.take(len(norm_ins))
+        if first_layer:
+            x_ref = ins[0]
+        else:
+            put_norm_back(ins, results, 0)
+            x_ref = results.buffers[1]
+        grad_ref, part_ref = results.buffers[base:]
+        gate_ref, up_ref = stream.take(2)
+        for side in range(2):
+            here = slice(side * ff, (side + 1) * ff)
+            first, second = stream.take(2)
+            times = low_dot if side else dot_nt
+            inner_grad = times(x_ref[:, :half], first[...])
+            inner_grad = inner_grad + times(x_ref[:, half:], second[...])
+            gate, up = gate_ref[:, here].astype(FULL), up_ref[:, here].astype(FULL)
+            sigma = jax.nn.sigmoid(gate)
+            grad_sigma = inner_grad * sigma
+            start = 2 * side * ff
+            grad_ref[:, start : start + ff] = (
+                grad_sigma * up * (1.0 + gate * (1.0 - sigma))
+            ).astype(LOW)
+            grad_ref[:, start + ff : start + 2 * ff] = (grad_sigma * gate).astype(LOW)
+        results.put(base)
+        for side in range(2):
+            total = 0.0
+            for i in range(4):
+                (weight,) = stream.take(1)
+                total = total + dot_nt(grad_ref[:, i * ff : (i + 1) * ff], weight[...])
+            part_ref[:, side * half : (side + 1) * half] = total.astype(LOW)
+        results.put(base + 1)
+
     return call(
-        functools.partial(ff_back_kernel, parts, first),
+        body,
         "feed_back",
-        [*norm_ins, gate, up],
-        parts,
-        ([] if first else norm_back_shapes(rows, wide))
+        [*norm_ins, gate, up, *down_parts, *[pair_parts[i] for i in order]],
+        ([] if first_layer else norm_back_shapes(rows, wide))
         + [((rows, 4 * ff), LOW), ((rows, wide), LOW)],
         [],
         12 * rows * wide * ff,
@@ -708,6 +716,34 @@
     )(place, gate, up, down)
 
 
+def cut_in_kernel(place_ref, q_ref, k_ref, v_ref, o_ref, out_ref):
+    rows, q_width = q_ref.shape
+    kv_width = k_ref.shape[1]
+    out_ref[:rows, :q_width] = q_ref[...]
+    out_ref[:rows, q_width : q_width + kv_width] = k_ref[...]
+    out_ref[:rows, q_width + kv_width :] = v_ref[...]
+    out_ref[rows:, :] = o_ref[...]
+
+
+def cut_in(place, layer, query, key, value, out):
+    count = lax.axis_size("dp")
+    blocks = [(v.shape[1] // count, v.shape[2]) for v in (query, key, value, out)]
+    shape = (blocks[0][0] + blocks[3][0], blocks[3][1])
+    return pl.pallas_call(
+        cut_in_kernel,
+        grid_spec=pltpu.PrefetchScalarGridSpec(
+            num_scalar_prefetch=1,
+            grid=(1,),
+            in_specs=[pl.BlockSpec((None,) + b, lambda i, p: (layer, p[0], 0)) for b in blocks],
+            out_specs=whole(shape),
+        ),
+        out_shape=jax.ShapeDtypeStruct(shape, LOW),
+        compiler_params=limits(),
+        cost_estimate=cost(0, 4 * shape[0] * shape[1]),
+        name="cut_in",
+    )(place, query, key, value, out)
+
+
 def pick_kernel(hi_ref, block_ref, mine_ref, other_ref):
     first, second = block_ref[:, 0, :], block_ref[:, 1, :]
     mine_ref[...] = jnp.where(hi_ref[0] == 0, first, second)
@@ -756,7 +792,9 @@
 def put_parts(place_ref, refs, spots, out_ref):
     for ref, (m, i, count) in zip(refs, spots):
         rows = ref.shape[0]
-        start = pl.multiple_of((place_ref[0] ^ m) * (rows * count) + i * rows, rows)
+        start = 0
+        if len(spots) > 1:
+            start = pl.multiple_of((place_ref[0] ^ m) * (rows * count) + i * rows, rows)
         out_ref[pl.ds(start, rows), :] = ref[...].astype(FULL)
 
 
@@ -907,14 +945,15 @@
             at += part
         self.first = jnp.concatenate(rows, axis=0)
 
-    def cross(self, order):
-        self.halves = (self.first, flip_core(self.first))
-
-    def spread(self, order):
+    def cross(self, order, gated=False):
+        first = order.after(self.first) if gated else self.first
+        self.halves = (first, flip_core(first))
+
+    def spread(self, order, near=(1, 2)):
         order.join(self.piece)
         if self.even:
             piece = order.after(self.piece)
-            self.pieces = [piece] + [hop(piece, "dp", m) for m in (1, 2)]
+            self.pieces = [piece] + [hop(piece, "dp", m) for m in near]
         else:
             self.gather(order)
 
@@ -931,49 +970,46 @@
             pieces = [order.after(self.pieces[0])] + self.pieces[1:]
             self.first = gather_pieces(spot, pieces, self.tops)
         order.mark(self.first)
-        self.cross(order)
+        self.halves = (self.first, flip_core(self.first))
 
     def done(self, order):
         order.join(self.halves[1])
 
 
-def in_groups(layer, w_in, w_out, place, packed):
-    in_piece, out_piece = cut(w_in, layer, place), cut(w_out, layer, place)
-    wide, q_width = w_in.shape[1], w_out.shape[1]
-    if packed and w_in.shape[2] == w_out.shape[2]:
-        piece = jnp.concatenate([in_piece, out_piece], axis=0)
+def in_groups(layer, w_query, w_key, w_value, w_out, place):
+    wide, q_width = w_query.shape[1:]
+    width = q_width + 2 * w_key.shape[2]
+    count = lax.axis_size("dp")
+    if width == w_out.shape[2] and q_width // count % 16 == 0:
+        spot = place.astype(jnp.int32).reshape(1)
+        piece = cut_in(spot, layer, w_query, w_key, w_value, w_out)
         return [Group(piece, (wide, q_width), place)]
-    return [Group(in_piece, (wide,), place), Group(out_piece, (q_width,), place)]
+    piece = jnp.concatenate([cut(v, layer, place) for v in (w_query, w_key, w_value)], axis=1)
+    return [Group(piece, (wide,), place), Group(cut(w_out, layer, place), (q_width,), place)]
 
 
 ROLES = (((1, 0), (3, 0)), ((2, 1), (3, 1)), ((2, 0), (1, 1)), ((0, 0), (0, 1)))
 
 
 class Sum:
-    def __init__(self, parts, place):
+    def __init__(self, parts, place, by_hops):
         self.first, self.last = parts
         self.place = place
-        self.even = lax.axis_size("dp") == 4
+        self.even = by_hops and lax.axis_size("dp") == 4
 
     def flip(self, order):
         self.came = flip_core(order.after(self.last))
 
     def start(self, order):
+        order.join(self.came)
         if not self.even:
-            total = add_low(self.first, self.came)
-            width = total.shape[1] // 2
-            self.own = lax.psum_scatter(total[:, :width], "dp", scatter_dimension=0, tiled=True)
-            self.other = lax.psum_scatter(total[:, width:], "dp", scatter_dimension=0, tiled=True)
+            total = order.mark(add_low(order.after(self.first), self.came))
+            self.both = lax.psum_scatter(total, "dp", scatter_dimension=0, tiled=True)
             return
-        order.join(self.came)
         spot = self.place.astype(jnp.int32).reshape(1)
         roles = role_sums(spot, order.after(self.first), self.came)
         to_x, to_y, self.on, self.keep = order.mark(roles)
         self.from_x, self.from_y = hop(to_x, "dp", 1), hop(to_y, "dp", 2)
-
-    def arrived(self, order):
-        if self.even:
-            order.join(self.from_x, self.from_y)
 
     def second(self, order):
         if not self.even:
@@ -988,28 +1024,38 @@
         self.to_own, self.to_other = hop(to_y, "dp", 2), hop(to_x, "dp", 1)
 
     def third(self, order):
-        if self.even:
-            order.join(self.to_own)
-            other, came = order.after((self.other, self.to_other))
-            self.other = order.mark(add_low(other, came))
+        if not self.even:
+            both = order.after(self.both)
+            width = both.shape[1] // 2
+            self.own, self.other = order.mark((both[:, :width], both[:, width:]))
+            return
+        order.join(self.to_own)
+        other, came = order.after((self.other, self.to_other))
+        self.other = order.mark(add_low(other, came))
 
     def across(self, order):
         self.far = flip_hi(order.after(self.other))
 
     def fourth(self, order):
+        own, far = order.after((self.own, self.far))
+        total = own.astype(FULL) + far.astype(FULL)
         if self.even:
-            own, came, far = order.after((self.own, self.to_own, self.far))
-            total = (own.astype(FULL) + came.astype(FULL) + far.astype(FULL)).astype(LOW)
-        else:
-            total = add_low(self.own, self.far)
-        self.total = order.mark(total)
+            total = total + order.after(self.to_own).astype(FULL)
+        self.total = order.mark(total.astype(LOW))
+
+    def gather(self, order):
+        total = order.after(self.total)
+        self.pieces = [lax.all_gather(total, "dp", axis=0, tiled=True)]
+
+    def straight(self, order):
+        total = order.after(self.total)
+        self.pieces = [total] + [hop(total, "dp", m) for m in range(1, lax.axis_size("dp"))]
 
     def near(self, order):
-        count = lax.axis_size("dp")
+        if not self.even:
+            self.gather(order)
+            return
         total = order.after(self.total)
-        if not self.even:
-            self.pieces = [total] + [hop(total, "dp", m) for m in range(1, count)]
-            return
         rows = total.shape[0] // 2
         self.mine = (total[:rows], total[rows:])
         self.beside = [hop(self.mine[0], "dp", 1), hop(self.mine[1], "dp", 2)]
@@ -1110,23 +1156,46 @@
         return order.mark(jnp.concatenate(order.after(self.halves[j]), axis=-1))
 
 
-def leave(chunks, hi, lo, core, rows):
-    parts = []
-    for value in chunks:
-        width = value.shape[-1] // 2
-        first = value[:, :width]
-        second = flip_core(value[:, width:].astype(LOW)).astype(FULL)
-        both = jnp.where(
-            core == 0,
-            jnp.concatenate([first, second], axis=0),
-            jnp.concatenate([second, first], axis=0),
-        )
-        parts.append(lax.dynamic_slice_in_dim(both, lo * rows, rows, 0))
-    mine = jnp.where(hi == 0, parts[0], parts[1])
-    other = flip_hi(jnp.where(hi == 0, parts[1], parts[0]).astype(LOW)).astype(FULL)
-    return jnp.where(
-        hi == 0, jnp.stack([mine, other], axis=1), jnp.stack([other, mine], axis=1)
-    )
+class Departure:
+    def __init__(self, results, hi, lo, core, rows):
+        self.results, self.hi, self.lo, self.core, self.rows = results, hi, lo, core, rows
+
+    def cross(self, order):
+        flat = order.after([chunk for chunks in self.results for chunk in chunks])
+        half = flat[0].shape[1] // 2
+        self.firsts = [chunk[:, :half] for chunk in flat]
+        send = jnp.concatenate([chunk[:, half:].astype(LOW) for chunk in flat], axis=0)
+        self.came = flip_core(order.mark(send))
+
+    def away(self, order):
+        came = order.after(self.came)
+        size = self.firsts[0].shape[0]
+        parts = []
+        for i, first in enumerate(self.firsts):
+            second = came[i * size : (i + 1) * size].astype(FULL)
+            both = jnp.where(
+                self.core == 0,
+                jnp.concatenate([first, second], axis=0),
+                jnp.concatenate([second, first], axis=0),
+            )
+            parts.append(lax.dynamic_slice_in_dim(both, self.lo * self.rows, self.rows, 0))
+        pairs = list(zip(parts[0::2], parts[1::2]))
+        self.mine = [jnp.where(self.hi == 0, a, b) for a, b in pairs]
+        others = [jnp.where(self.hi == 0, b, a).astype(LOW) for a, b in pairs]
+        self.mine, send = order.mark((self.mine, jnp.concatenate(others, axis=0)))
+        self.far = flip_hi(send)
+
+    def done(self, order):
+        far = order.after(self.far)
+        out = []
+        for i, mine in enumerate(self.mine):
+            other = far[i * self.rows : (i + 1) * self.rows].astype(FULL)
+            out.append(
+                jnp.where(
+                    self.hi == 0, jnp.stack([mine, other], axis=1), jnp.stack([other, mine], axis=1)
+                )
+            )
+        return out
 
 
 def shards(
@@ -1149,12 +1218,12 @@
     w_in = jnp.concatenate([w_query, w_key, w_value], axis=2)
     wide = w_in.shape[1]
     ff = w_gate.shape[2]
-    a_groups = [in_groups(0, w_in, w_out, place, True), None]
+    arrival = Arrival(block_input, hi, lo, core)
+    arrival.fetch(order)
+    a_groups = [in_groups(0, order.after(w_query), w_key, w_value, w_out, place), None]
     order.mark([group.piece for group in a_groups[0]])
     for group in a_groups[0]:
         group.fetch(order)
-    arrival = Arrival(block_input, hi, lo, core)
-    arrival.fetch(order)
     in_own, out_own, gates, ups, own_downs = [
         (v, flip_core(v)) for v in (w_in, w_out, w_gate, w_up, w_down)
     ]
@@ -1164,12 +1233,14 @@
         pieces = order.mark(cut_ff(spot, l, order.after(w_gate), w_up, w_down))
         f_groups.append([Group(piece, (wide,), place) for piece in pieces])
         order.join(*((in_own[1], gains) if not l else (out_own[1],)))
-    a_groups[1] = in_groups(1, order.after(w_in), w_out, place, True)
+    a_groups[1] = in_groups(1, order.after(w_query), w_key, w_value, w_out, place)
     order.mark([group.piece for group in a_groups[1]])
     order.join(gates[1], ups[1])
+    cotangent = Arrival(block_cotangent, hi, lo, core)
+    cotangent.pick(order)
+    arrival.share(order)
     for group in a_groups[0]:
         group.spread(order)
-    arrival.share(order)
     arrival.send(order, 0)
     f_groups[0][0].fetch(order)
     for group in a_groups[0]:
@@ -1186,7 +1257,6 @@
     for group in a_groups[0]:
         group.done(order)
 
-    cotangent = Arrival(block_cotangent, hi, lo, core)
     stash = [[None] * CHUNKS for _ in range(LAYERS)]
     weights = [None] * LAYERS
     pairs = [None] * CHUNKS
@@ -1228,24 +1298,22 @@
         kvs, kept = [], [None] * CHUNKS
         first, second, third = f_groups[l]
         if not l:
+            third.fetch(order)
             kept[0] = front(l, 0)
-            third.fetch(order)
             arrival.cross(order, 1)
-            kept[0] = middle(l, 0, kept[0])
-            third.gather(order)
             hidden.append(arrival.chunk(order, 1))
             kept[1] = front(l, 1)
-            first.cross(order)
+            kept[0] = middle(l, 0, kept[0])
+            kept[1] = middle(l, 1, kept[1])
+            third.spread(order, range(1, lax.axis_size("dp")))
+            order.join(pairs[0])
             for group in a_groups[1]:
                 group.fetch(order)
-            order.join(pairs[0])
-            kept[1] = middle(l, 1, kept[1])
+            order.join(pairs[1])
+            first.cross(order)
+            third.collect(order)
+            second.cross(order)
             first.done(order)
-            for group in a_groups[1]:
-                group.gather(order)
-            f_groups[1][0].fetch(order)
-            second.cross(order)
-            third.cross(order)
         else:
             order.join(pairs[0])
             kept[0] = front(l, 0)
@@ -1254,15 +1322,14 @@
             order.join(pairs[1])
             kept[1] = front(l, 1)
             kept[0] = middle(l, 0, kept[0])
-            third.gather(order)
+            third.spread(order, range(1, lax.axis_size("dp")))
             cotangent.fetch_on(order)
-            first.cross(order)
             kept[1] = middle(l, 1, kept[1])
+            order.join(pairs[0])
+            first.cross(order, True)
+            third.collect(order)
+            second.cross(order)
             first.done(order)
-            cotangent.share(order)
-            cotangent.send(order, 1)
-            second.cross(order)
-            third.cross(order)
         second.done(order)
         third.done(order)
         packs = [group.halves for group in f_groups[l]]
@@ -1273,17 +1340,23 @@
         weights[l] = (ins, outs, pair_parts, down_parts)
         rear(l, 0, kept[0])
         if more:
-            order.join(pairs[1])
+            for group in a_groups[1]:
+                group.gather(order)
+            f_groups[1][0].fetch(order)
+        else:
+            cotangent.share(order)
+            cotangent.send(order, 1)
+            cotangent.send(order, 0)
+        order.join(pairs[1])
+        rear(l, 1, kept[1])
+        if not more:
+            cotangent.cross(order, 1)
+        if more:
             f_groups[1][0].gather(order)
             f_groups[1][1].fetch(order)
-        else:
-            cotangent.cross(order, 1)
-            cotangent.send(order, 0)
-        rear(l, 1, kept[1])
-        if more:
-            cotangent.pick(order)
+            order.join(pairs[0])
             for group in a_groups[1]:
-                group.cross(order)
+                group.cross(order, True)
                 group.done(order)
     grads = [None] * CHUNKS
     grads[1] = (cotangent.chunk(order, 1),)
@@ -1313,7 +1386,7 @@
     def ff_grad(l, kept):
         columns = list(zip(*kept))
         columns[0] = order.after(columns[0])
-        sums["ff", l] = Sum(order.mark(ff_weights(*columns)), place)
+        sums["ff", l] = Sum(order.mark(ff_weights(*columns)), place, l == 0)
 
     def attend_step(l, j, held):
         block, factor_a, normed_a, query, kvs, lse, attended = stash[l][j][:7]
@@ -1331,8 +1404,7 @@
         )
         gain_b[l] = gain_b[l] + gain_part
         grads[j] = (grad_mixed, None, None, block, factor_a, gains[l, 0:1])
-        send = order.mark(order.after(dkvs[-1]).astype(LOW))
-        middle = (dq, dkvs[-2], flip_core(send))
+        middle = (dq, dkvs[-2], flip_core(dkvs[-1]))
         return (dkvs[:2], middle, (normed_a, branch_a, None, attended))
 
     def project_step(l, j, middle, kept):
@@ -1347,7 +1419,7 @@
     def in_grad(l, kept):
         columns = list(zip(*kept))
         columns[0] = order.after(columns[0])
-        sums["in", l] = Sum(order.mark(in_weights(*columns)), place)
+        sums["in", l] = Sum(order.mark(in_weights(*columns)), place, l == 0)
 
     l = LAYERS - 1
     kept, mids = [None] * CHUNKS, [None] * CHUNKS
@@ -1367,74 +1439,74 @@
     l = 0
     kept, mids = [None] * CHUNKS, [None] * CHUNKS
     kept[1] = ff_step(l, 1)
-    sums["ff", 1].second(order)
     kept[0] = ff_step(l, 0)
     sums["in", 1].flip(order)
     ff_grad(l, kept)
     sums["ff", 1].third(order)
+    sums["ff", 1].across(order)
+    sums["in", 1].start(order)
     sums["ff", 0].flip(order)
-    sums["in", 1].start(order)
     held, mids[1], kept[1] = attend_step(l, 1, None)
-    order.join(mids[1][2])
-    sums["in", 1].arrived(order)
     sums["ff", 0].start(order)
     _, mids[0], kept[0] = attend_step(l, 0, held)
     kept[1] = project_step(l, 1, mids[1], kept[1])
     kept[0] = project_step(l, 0, mids[0], kept[0])
+    sums["ff", 1].fourth(order)
+    sums["ff", 1].gather(order)
+    sums["in", 1].third(order)
     in_grad(l, kept)
-    for g in grads:
+    for g in reversed(grads):
         order.join(*g[1:3])
     ends = [finish_back(order.after(g[0]), *g[1:]) for g in grads]
     order.mark(tuple(g for g, _ in ends))
     gain_a[0] = sum(part for _, part in ends)
+    tops = [group_pair(part) for part in order.after(pairs)]
+    gain_grads = [jnp.concatenate([gain_a[l], gain_b[l]], axis=0) for l in range(LAYERS)]
+    grad_gains = order.after(jnp.stack(gain_grads))
+    width = grad_gains.shape[-1] // 2
+    gains_came = flip_core(grad_gains[..., width:])
     sums["ff", 0].second(order)
-    sums["ff", 1].across(order)
     sums["in", 0].flip(order)
-    sums["in", 1].second(order)
+    sums["in", 1].across(order)
+    grad_gains = order.mark(grad_gains[..., :width] + order.after(gains_came))
+    gains_came = flip_hi(grad_gains)
+    sums["in", 0].start(order)
+    sums["in", 1].fourth(order)
+    grad_gains = order.mark(grad_gains + order.after(gains_came))
+    order.join(tops)
     sums["ff", 0].third(order)
     sums["ff", 0].across(order)
-    sums["in", 0].start(order)
-    sums["in", 1].third(order)
-    sums["ff", 1].fourth(order)
-    sums["in", 1].across(order)
+    sums["in", 1].gather(order)
+    hidden = [
+        h + left.astype(FULL) + right.astype(FULL)
+        for h, (left, right) in order.after(list(zip(hidden, tops)))
+    ]
+    results = Departure((hidden, [g for g, _ in ends]), hi, lo, core, block_rows)
+    results.cross(order)
+    gains_came = hop(grad_gains, "dp", 1)
     sums["in", 0].second(order)
-    sums["ff", 1].near(order)
-    sums["in", 0].third(order)
-    sums["in", 0].across(order)
-    sums["ff", 1].fifth(order)
-    sums["in", 1].fourth(order)
-    input_grad = order.mark(leave(order.after([g for g, _ in ends]), hi, lo, core, block_rows))
-    sums["in", 1].near(order)
-    sums["ff", 1].done(order)
-    ff_out = order.mark(spread_ff(order.after(spot), sums["ff", 1].pieces, 1, None))
-    sums["in", 1].fifth(order)
     sums["ff", 0].fourth(order)
     sums["ff", 0].near(order)
+    sums["in", 0].third(order)
+    sums["ff", 0].fifth(order)
+    sums["in", 0].across(order)
+    results.away(order)
+    grad_gains = order.mark(grad_gains + order.after(gains_came))
+    bit = 2
+    while bit < lax.axis_size("dp"):
+        gains_came = hop(grad_gains, "dp", bit)
+        if 2 * bit < lax.axis_size("dp"):
+            grad_gains = order.mark(grad_gains + order.after(gains_came))
+        bit *= 2
+    ff_out = order.mark(spread_ff(order.after(spot), sums["ff", 1].pieces, 1, None))
     sums["in", 0].fourth(order)
-    sums["in", 1].done(order)
-    sums["ff", 0].fifth(order)
-    sums["in", 0].near(order)
+    sums["in", 0].straight(order)
     in_out = order.mark(spread_in(order.after(spot), sums["in", 1].pieces, 1, None, q_width))
-    sums["in", 0].fifth(order)
-    tops = [group_pair(part) for part in order.after(pairs)]
-    hidden = [
-        h + left.astype(FULL) + right.astype(FULL) for h, (left, right) in zip(hidden, tops)
-    ]
-    activations = leave(hidden, hi, lo, core, block_rows)
-    sums["in", 0].done(order)
-    in_out = order.mark(spread_in(order.after(spot), sums["in", 0].pieces, 0, in_out, q_width))
+    activations, input_grad = order.mark(results.done(order))
     sums["ff", 0].done(order)
-    ff_out = spread_ff(order.after(spot), sums["ff", 0].pieces, 0, ff_out)
-    gain_grads = [jnp.concatenate([gain_a[l], gain_b[l]], axis=0) for l in range(LAYERS)]
-
-    grad_gains = jnp.stack(gain_grads)
-    width = grad_gains.shape[-1] // 2
-    grad_gains = grad_gains[..., :width] + flip_core(grad_gains[..., width:])
-    grad_gains = grad_gains + flip_hi(grad_gains)
-    bit = 1
-    while bit < lax.axis_size("dp"):
-        grad_gains = grad_gains + hop(grad_gains, "dp", bit)
-        bit *= 2
+    ff_out = order.mark(spread_ff(order.after(spot), sums["ff", 0].pieces, 0, ff_out))
+    in_out = spread_in(order.after(spot), sums["in", 0].pieces, 0, in_out, q_width)
+    grad_gains = grad_gains + gains_came
     return (activations, input_grad, *in_out, *ff_out, grad_gains)
 
 

time: 1040 us -> 899 us (0.86)
  waiting for transfers between devices: 422 us -> 305 us
  Pallas kernels: 386 us -> 363 us
    all_gather x6 -> x4, waiting for transfers between devices: 90.5 us -> 11 us  [gather(): self.first = lax.all_gather(piece, 'dp', axis=0, tiled=True)]
    ppermute x109 -> x94, waiting for transfers between devices: 329 us -> 271 us  [hop(): return lax.ppermute(value, axis, [(i, i ^ distance) for i in range(size)])]
    pallas_call x8 -> x2, Pallas kernels: 59.4 us -> 3.91 us  [cut_in(): pl.pallas_call(cut_in_kernel, grid_spec=pltpu.PrefetchScalarGridSpec(num_...]
    pallas_call x16 -> x24, Pallas kernels: 185 us -> 236 us  [call(): pl.pallas_call(kernel, grid_spec=pltpu.PrefetchScalarGridSpec(num_scalar_...]
    pallas_call x4 -> x2, Pallas kernels: 46 us -> 23.6 us  [role_sums(): pl.pallas_call(role_sum_kernel, grid_spec=pltpu.PrefetchScalarGridSpec(nu...]
    all_gather x1, waiting for transfers between devices: 2.57 us -> 19.9 us  [gather(): pieces = lax.all_gather(piece, 'dp', axis=0)]
    convert_element_type x8 -> x6, other arithmetic: 20.9 us -> 28.1 us  [add_low(): return (left.astype(FULL) + right.astype(FULL)).astype(LOW)]
    unnamed x200 -> x202, local copies, waits for them, and re-layouts: 25.4 us -> 30.4 us
  transfers between devices with their start and end apart: 116 -> 103, of which waited for: 37 -> 38; matrix products, arithmetic and copies ran while one was open for 9% -> 10% of each run, Pallas kernels for 37% -> 40%
where the time goes in v2:
time: 899 us; the launch traced here: 889 us
  Pallas kernels  363 us (40%)
  waiting for transfers between devices  305 us (34%)
  starting transfers between devices  87.6 us (10%)
  other arithmetic  71 us (8%)
  local copies, waits for them, and re-layouts  46 us (5%)
  between operations  15.8 us (2%)
    ppermute x94, waiting for transfers between devices, hop(): return lax.ppermute(value, axis, [(i, i ^ distance) for i in range(size)])  271 us
    pallas_call x24, Pallas kernels, call(): pl.pallas_call(kernel, grid_spec=pltpu.PrefetchScalarGridSpec(num_scalar_...  236 us
    ppermute x94, starting transfers between devices, hop(): return lax.ppermute(value, axis, [(i, i ^ distance) for i in range(size)])  85.8 us
    pallas_call x2, Pallas kernels, ff_weights(): pl.pallas_call(functools.partial(ff_weights_kernel, chunks, split), grid=...  37.6 us
    unnamed x202, local copies, waits for them, and re-layouts  30.4 us
    convert_element_type x6, other arithmetic, add_low(): return (left.astype(FULL) + right.astype(FULL)).astype(LOW)  28.1 us
    pallas_call x2, Pallas kernels, role_sums(): pl.pallas_call(role_sum_kernel, grid_spec=pltpu.PrefetchScalarGridSpec(nu...  23.6 us
    all_gather x1, waiting for transfers between devices, gather(): pieces = lax.all_gather(piece, 'dp', axis=0)  19.9 us
  transfers between devices with their start and end apart: 103, of which 38 were waited for; matrix products, arithmetic and copies ran while one was open for 10% of the time, Pallas kernels for 40%

profile of v2, /device:TPU:0, one launch (start us, length us, event | category | flops | bytes accessed | tf_op | source)
XLA Modules:
  0.0 889.0 jit_solution(5885102243392524722)
XLA Ops:
  39.9 9.4 %collective-permute-done = bf16[256,768]{1,0:T(8,128)(2,1)S(1)} collective-permute-done((bf16[256,768]{1,0:T(8,128)(2,1)}, bf16[256,768]{1,0:T(8,128)(2,1)S(1)}, u32[]{:S(2)}, u32[]{:S(2)}) %collective-permute-start) | collective-permute-done | bytes 393248 | tf_op jit(solution)/shard_map/ppermute | solution.py:27
  49.3 9.1 %collective-permute-done.6.refs_0_ = bf16[288,768]{1,0:T(8,128)(2,1)S(1)} collective-permute-done((bf16[288,768]{1,0:T(8,128)(2,1)S(1)}, bf16[288,768]{1,0:T(8,128)(2,1)S(1)}, u32[]{:S(2)}, u32[]{:S(2)}) %collective-permute-start.6) | collective-permute-done | bytes 442400 | tf_op jit(solution)/shard_map/ppermute | solution.py:27
  62.2 8.1 collective-permute-done.8.refs_1_
  74.6 17.0 %collective-permute-done.11 = bf16[192,1024]{1,0:T(8,128)(2,1)S(1)} collective-permute-done((bf16[192,1024]{1,0:T(8,128)(2,1)}, bf16[192,1024]{1,0:T(8,128)(2,1)S(1)}, u32[]{:S(2)}, u32[]{:S(2)}) %collective-permute-start.11) | collective-permute-done | bytes 393248 | tf_op jit(solution)/shard_map/ppermute | solution.py:27
  102.5 12.7 %collective-permute-done.14 = bf16[192,1024]{1,0:T(8,128)(2,1)S(1)} collective-permute-done((bf16[192,1024]{1,0:T(8,128)(2,1)}, bf16[192,1024]{1,0:T(8,128)(2,1)S(1)}, u32[]{:S(2)}, u32[]{:S(2)}) %collective-permute-start.14) | collective-permute-done | bytes 393248 | tf_op jit(solution)/shard_map/ppermute | solution.py:27
  115.1 6.0 project.4
  131.9 6.7 attend.4
  142.6 9.5 %attend.5 = (bf16[256,768]{1,0:T(8,128)(2,1)}, f32[8,256]{1,0:T(8,128)}, bf16[256,1536]{1,0:T(8,128)(2,1)}) custom-call(s32[1]{0:T(128)} %bitcast.3.refs_0_, bf16[256,768]{1,0:T(8,128)(2,1)} %get-tuple-element.358.refs_1_.refs_11_, bf16[256,768]{1,0:T(8,128)(2,1)} %get-tuple-element.344.refs_2_.refs_13_, bf16[256,768]{1,0:T(8,128)(2,1)} %copy-done.87, ...), custom_call_target="tpu_custom_call" | custom-call | flops 82543902720 | bytes 129761280 | tf_op jit(solution)/shard_map/attend/pallas_call | solution.py:237
  161.8 10.9 %all-gather.11.cloned.1.call-done.refs_10_.refs_15_ = bf16[768,1024]{1,0:T(8,128)(2,1)} async-done(((bf16[192,1024]{1,0:T(8,128)(2,1)}), bf16[768,1024]{1,0:T(8,128)(2,1)}) %all-gather.11.cloned.1.call-update) | async-done | bytes 1572880 | tf_op jit(solution)/shard_map/all_gather | solution.py:938
  173.2 7.7 collective-permute-done.25.refs_3_
  189.7 11.4 %feed_forward.4 = (f32[256,1536]{1,0:T(8,128)}, f32[256,1]{1,0:T(8,128)}, bf16[256,1536]{1,0:T(8,128)(2,1)}, bf16[256,2048]{1,0:T(8,128)(2,1)}, bf16[256,2048]{1...) custom-call(f32[256,1536]{1,0:T(8,128)} %get-tuple-element.366.refs_0_, ...), custom_call_target="tpu_custom_call" | custom-call | flops 144955146240 | bytes 637102080 | tf_op jit(solution)/shard_map/feed_forward/pallas_call | solution.py:237
  208.2 12.4 %feed_forward.5 = (f32[256,1536]{1,0:T(8,128)}, f32[256,1]{1,0:T(8,128)}, bf16[256,1536]{1,0:T(8,128)(2,1)}, bf16[256,2048]{1,0:T(8,128)(2,1)}, bf16[256,2048]{1...) custom-call(f32[256,1536]{1,0:T(8,128)} %get-tuple-element.375.refs_0_, ...), custom_call_target="tpu_custom_call" | custom-call | flops 144955146240 | bytes 637102080 | tf_op jit(solution)/shard_map/feed_forward/pallas_call | solution.py:237
  220.6 19.9 %all-gather.21.cloned.1.call-done = bf16[1152,768]{1,0:T(8,128)(2,1)} async-done(((bf16[288,768]{1,0:T(8,128)(2,1)}), bf16[1152,768]{1,0:T(8,128)(2,1)}) %all-gather.21.cloned.1.call-update) | async-done | bytes 1769488 | tf_op jit(solution)/shard_map/all_gather | solution.py:940
  248.2 6.6 project.6
  255.0 16.1 %collective-permute-done.33 = bf16[192,1024]{1,0:T(8,128)(2,1)S(1)} collective-permute-done((bf16[192,1024]{1,0:T(8,128)(2,1)}, bf16[192,1024]{1,0:T(8,128)(2,1)S(1)}, u32[]{:S(2)}, u32[]{:S(2)}) %collective-permute-start.33) | collective-permute-done | bytes 393248 | tf_op jit(solution)/shard_map/ppermute | solution.py:27
  274.4 6.6 project.7
  282.2 6.7 attend.6
  295.6 9.2 %attend.7 = (bf16[256,768]{1,0:T(8,128)(2,1)}, f32[8,256]{1,0:T(8,128)}, bf16[256,1536]{1,0:T(8,128)(2,1)}) custom-call(s32[1]{0:T(128)} %bitcast.3.refs_0_, bf16[256,768]{1,0:T(8,128)(2,1)} %get-tuple-element.405.refs_1_.refs_11_, bf16[256,768]{1,0:T(8,128)(2,1)} %get-tuple-element.391.refs_2_.refs_13_, bf16[256,768]{1,0:T(8,128)(2,1)} %copy-done.90, ...), custom_call_target="tpu_custom_call" | custom-call | flops 82543902720 | bytes 129761280 | tf_op jit(solution)/shard_map/attend/pallas_call | solution.py:237
  310.1 10.4 %collective-permute-done.41.refs_3_ = bf16[192,1024]{1,0:T(8,128)(2,1)S(1)} collective-permute-done((bf16[192,1024]{1,0:T(8,128)(2,1)S(1)}, bf16[192,1024]{1,0:T(8,128)(2,1)S(1)}, u32[]{:S(2)}, u32[]{:S(2)}) %collective-permute-start.41) | collective-permute-done | bytes 393248 | tf_op jit(solution)/shard_map/ppermute | solution.py:27
  331.0 11.5 %feed_forward.6 = (f32[256,1536]{1,0:T(8,128)}, f32[256,1]{1,0:T(8,128)}, bf16[256,1536]{1,0:T(8,128)(2,1)}, bf16[256,2048]{1,0:T(8,128)(2,1)}, bf16[256,2048]{1...) custom-call(f32[256,1536]{1,0:T(8,128)} %get-tuple-element.413.refs_0_.refs_3_, ...), custom_call_target="tpu_custom_call" | custom-call | flops 144955146240 | bytes 637102080 | tf_op jit(solution)/shard_map/feed_forward/pallas_call | solution.py:237
  342.5 9.0 %collective-permute-done.45 = bf16[256,768]{1,0:T(8,128)(2,1)} collective-permute-done((bf16[256,768]{1,0:T(8,128)(2,1)}, bf16[256,768]{1,0:T(8,128)(2,1)}, u32[]{:S(2)}, u32[]{:S(2)}) %collective-permute-start.45) | collective-permute-done | bytes 393248 | tf_op jit(solution)/shard_map/ppermute | solution.py:27
  356.8 11.5 %feed_forward.7 = (f32[256,1536]{1,0:T(8,128)}, f32[256,1]{1,0:T(8,128)}, bf16[256,1536]{1,0:T(8,128)(2,1)}, bf16[256,2048]{1,0:T(8,128)(2,1)}, bf16[256,2048]{1...) custom-call(f32[256,1536]{1,0:T(8,128)} %get-tuple-element.424.refs_0_.refs_3_, ...), custom_call_target="tpu_custom_call" | custom-call | flops 144955146240 | bytes 637102080 | tf_op jit(solution)/shard_map/feed_forward/pallas_call | solution.py:237
  372.2 13.4 %feed_back.4 = (bf16[256,4096]{1,0:T(8,128)(2,1)}, bf16[256,1536]{1,0:T(8,128)(2,1)}) custom-call(bf16[256,1536]{1,0:T(8,128)(2,1)} %pad_maximum_fusion.6.refs_0_.refs_3_, bf16[256,2048]{1,0:T(8,128)(2,1)} %get-tuple-element.431.refs_1_, bf16[256,2048]{1,0:T(8,128)(2,1)} %get-tuple-element.432.refs_2_, bf16[2,1024,768]{2,1,0:T(8,128)(2,1)} %refs_8_.7, ...), custom_call_target="tpu_custom_call" | custom-call | flops 144955146240 | bytes 652738560 | tf_op jit(solution)/shard_map/feed_back/pallas_call | solution.py:237
  391.7 13.2 %feed_back.5 = (bf16[256,4096]{1,0:T(8,128)(2,1)}, bf16[256,1536]{1,0:T(8,128)(2,1)}) custom-call(bf16[256,1536]{1,0:T(8,128)(2,1)} %pad_maximum_fusion.7.refs_0_.refs_2_, bf16[256,2048]{1,0:T(8,128)(2,1)} %get-tuple-element.419.refs_1_, bf16[256,2048]{1,0:T(8,128)(2,1)} %get-tuple-element.420.refs_2_, bf16[2,1024,768]{2,1,0:T(8,128)(2,1)} %refs_8_.7, ...), custom_call_target="tpu_custom_call" | custom-call | flops 144955146240 | bytes 652738560 | tf_op jit(solution)/shard_map/feed_back/pallas_call | solution.py:237
  406.7 18.9 %ff_weights.2 = (bf16[768,6144]{1,0:T(8,128)(2,1)}, bf16[768,6144]{1,0:T(8,128)(2,1)}) custom-call(bf16[256,1536]{1,0:T(8,128)(2,1)} %get-tuple-element.446.refs_0_, bf16[256,1536]{1,0:T(8,128)(2,1)} %get-tuple-element.447.refs_1_, bf16[256,1536]{1,0:T(8,128)(2,1)} %pad_maximum_fusion.7.refs_0_.refs_2_, bf16[256,1536]{1,0:T(8,128)(2,1)} %pad_maximum_fusion.6.refs_0_.refs_3_, ...), custom_call_target="tpu_custom_call" | custom-call | flops 289910292480 | bytes 754974720 | tf_op jit(solution)/shard_map/ff_weights/pallas_call | solution.py:600
  426.9 14.5 %attend_back.4 = (f32[256,1536]{1,0:T(8,128)}, bf16[256,1536]{1,0:T(8,128)(2,1)}, f32[1,1536]{1,0:T(1,128)}, f32[256,768]{1,0:T(8,128)}, f32[256,768]{1,0:T(8,12...) custom-call(s32[1]{0:T(128)} %bitcast.3.refs_0_, ...), custom_call_target="tpu_custom_call" | custom-call | flops 179180666880 | bytes 224363520 | tf_op jit(solution)/shard_map/attend_back/pallas_call | solution.py:237
  442.0 12.3 %add_convert_fusion = bf16[768,6144]{1,0:T(8,128)(2,1)} fusion(bf16[768,6144]{1,0:T(8,128)(2,1)} %collective-permute-done.52, bf16[768,6144]{1,0:T(8,128)(2,1)} %get-tuple-element.460), kind=kLoop, calls=%fused_computation | loop fusion | flops 18874368 | bytes 28311552 | tf_op jit(solution)/shard_map/convert_element_type | solution.py:69
  454.8 11.6 %attend_back.5 = (f32[256,1536]{1,0:T(8,128)}, bf16[256,1536]{1,0:T(8,128)(2,1)}, f32[1,1536]{1,0:T(1,128)}, f32[256,768]{1,0:T(8,128)}, f32[256,768]{1,0:T(8,128)}, /*index=5*/bf16[256,768]{1,0:T(8,128)(2,1)}) custom-call(s32[1]{0:T(128)} %bitcast.3.refs_0_, f32[256,1536]{1,0:T(8,128)} %convert_element_type.220.refs_1_, ...), custom_call_target="tpu_custom_call" | custom-call | flops 98650030080 | bytes 224363520 | tf_op jit(solution)/shard_map/attend_back/pallas_call | solution.py:237
  481.3 9.6 %in_weights.2 = (bf16[768,2304]{1,0:T(8,128)(2,1)}, bf16[768,2304]{1,0:T(8,128)(2,1)}) custom-call(bf16[256,1536]{1,0:T(8,128)(2,1)} %get-tuple-element.474.refs_0_, bf16[256,1536]{1,0:T(8,128)(2,1)} %get-tuple-element.475.refs_1_, bf16[256,1536]{1,0:T(8,128)(2,1)} %get-tuple-element.464.refs_2_, bf16[256,1536]{1,0:T(8,128)(2,1)} %get-tuple-element.452.refs_3_, ...), custom_call_target="tpu_custom_call" | custom-call | flops 108716359680 | bytes 306708480 | tf_op jit(solution)/shard_map/in_weights/pallas_call | solution.py:639
  493.1 15.1 %feed_back.6 = (f32[256,1536]{1,0:T(8,128)}, bf16[256,1536]{1,0:T(8,128)(2,1)}, f32[1,1536]{1,0:T(1,128)}, bf16[256,4096]{1,0:T(8,128)(2,1)}, bf16[256,1536]{1,0:T(8,128)(2,1)}) custom-call(f32[256,1536]{1,0:T(8,128)} %get-tuple-element.478.refs_0_, bf16[256,1536]{1,0:T(8,128)(2,1)} %get-tuple-element.470.refs_1_, ...), custom_call_target="tpu_custom_call" | custom-call | flops 144955146240 | bytes 723624960 | tf_op jit(solution)/shard_map/feed_back/pallas_call | solution.py:237
  509.8 15.0 %feed_back.7 = (f32[256,1536]{1,0:T(8,128)}, bf16[256,1536]{1,0:T(8,128)(2,1)}, f32[1,1536]{1,0:T(1,128)}, bf16[256,4096]{1,0:T(8,128)(2,1)}, bf16[256,1536]{1,0:T(8,128)(2,1)}) custom-call(f32[256,1536]{1,0:T(8,128)} %get-tuple-element.484.refs_0_, bf16[256,1536]{1,0:T(8,128)(2,1)} %get-tuple-element.473.refs_1_, ...), custom_call_target="tpu_custom_call" | custom-call | flops 144955146240 | bytes 723624960 | tf_op jit(solution)/shard_map/feed_back/pallas_call | solution.py:237
  525.4 18.7 %ff_weights.3 = (bf16[768,6144]{1,0:T(8,128)(2,1)}, bf16[768,6144]{1,0:T(8,128)(2,1)}) custom-call(bf16[256,1536]{1,0:T(8,128)(2,1)} %get-tuple-element.490.refs_0_, bf16[256,1536]{1,0:T(8,128)(2,1)} %get-tuple-element.491.refs_1_, bf16[256,1536]{1,0:T(8,128)(2,1)} %get-tuple-element.486.refs_2_, bf16[256,1536]{1,0:T(8,128)(2,1)} %get-tuple-element.480.refs_3_, ...), custom_call_target="tpu_custom_call" | custom-call | flops 289910292480 | bytes 754974720 | tf_op jit(solution)/shard_map/ff_weights/pallas_call | solution.py:600
  555.5 14.6 %attend_back.6 = (f32[256,1536]{1,0:T(8,128)}, bf16[256,1536]{1,0:T(8,128)(2,1)}, f32[1,1536]{1,0:T(1,128)}, f32[256,768]{1,0:T(8,128)}, f32[256,768]{1,0:T(8,12...) custom-call(s32[1]{0:T(128)} %bitcast.3.refs_0_, f32[256,1536]{1,0:T(8,128)} %get-tuple-element.497.refs_1_, ...), custom_call_target="tpu_custom_call" | custom-call | flops 179180666880 | bytes 224363520 | tf_op jit(solution)/shard_map/attend_back/pallas_call | solution.py:237
  573.0 14.6 %role_sums.2 = (bf16[384,3072]{1,0:T(8,128)(2,1)}, bf16[384,3072]{1,0:T(8,128)(2,1)}, bf16[384,3072]{1,0:T(8,128)(2,1)}, bf16[384,3072]{1,0:T(8,128)(2,1)}) custom-call(s32[8]{0:T(128)} %broadcast_xor_fusion.row_ref, s32[8]{0:T(128)} %constant.62.clone.side_ref, bf16[768,6144]{1,0:T(8,128)(2,1)} %get-tuple-element.507.left_ref, ...), custom_call_target="tpu_custom_call" | custom-call | bytes 424673280 | tf_op jit(solution)/shard_map/role_sums/pallas_call | solution.py:674
  589.7 10.8 %attend_back.7 = (f32[256,1536]{1,0:T(8,128)}, bf16[256,1536]{1,0:T(8,128)(2,1)}, f32[1,1536]{1,0:T(1,128)}, f32[256,768]{1,0:T(8,128)}, f32[256,768]{1,0:T(8,128)}, /*index=5*/bf16[256,768]{1,0:T(8,128)(2,1)}) custom-call(s32[1]{0:T(128)} %bitcast.3.refs_0_, f32[256,1536]{1,0:T(8,128)} %get-tuple-element.512.refs_1_, ...), custom_call_target="tpu_custom_call" | custom-call | flops 98650030080 | bytes 224363520 | tf_op jit(solution)/shard_map/attend_back/pallas_call | solution.py:237
  601.4 5.9 project_back.6
  616.1 9.1 %collective-permute-done.62 = bf16[192,3072]{1,0:T(8,128)(2,1)} collective-permute-done((bf16[192,3072]{1,0:T(8,128)(2,1)}, bf16[192,3072]{1,0:T(8,128)(2,1)}, u32[]{:S(2)}, u32[]{:S(2)}) %collective-permute-start.62) | collective-permute-done | bytes 1179680 | tf_op jit(solution)/shard_map/ppermute | solution.py:27
  630.1 9.7 %in_weights.3 = (bf16[768,2304]{1,0:T(8,128)(2,1)}, bf16[768,2304]{1,0:T(8,128)(2,1)}) custom-call(bf16[256,1536]{1,0:T(8,128)(2,1)} %get-tuple-element.529.refs_0_, bf16[256,1536]{1,0:T(8,128)(2,1)} %get-tuple-element.530.refs_1_, bf16[256,1536]{1,0:T(8,128)(2,1)} %get-tuple-element.516.refs_2_, bf16[256,1536]{1,0:T(8,128)(2,1)} %get-tuple-element.499.refs_3_, ...), custom_call_target="tpu_custom_call" | custom-call | flops 108716359680 | bytes 306708480 | tf_op jit(solution)/shard_map/in_weights/pallas_call | solution.py:639
  642.0 16.7 %collective-permute-done.66 = bf16[256,1536]{1,0:T(8,128)(2,1)S(1)} collective-permute-done((bf16[256,1536]{1,0:T(8,128)(2,1)}, bf16[256,1536]{1,0:T(8,128)(2,1)S(1)}, u32[]{:S(2)}, u32[]{:S(2)}) %collective-permute-start.66) | collective-permute-done | bytes 786464 | tf_op jit(solution)/shard_map/ppermute | solution.py:27
  677.8 9.0 %role_sums.3 = (bf16[384,1152]{1,0:T(8,128)(2,1)}, bf16[384,1152]{1,0:T(8,128)(2,1)}, bf16[384,1152]{1,0:T(8,128)(2,1)}, bf16[384,1152]{1,0:T(8,128)(2,1)}) custom-call(s32[8]{0:T(128)} %broadcast_xor_fusion.row_ref, s32[8]{0:T(128)} %constant.62.clone.side_ref, bf16[768,2304]{1,0:T(8,128)(2,1)} %get-tuple-element.545.left_ref, ...), custom_call_target="tpu_custom_call" | custom-call | bytes 159252480 | tf_op jit(solution)/shard_map/role_sums/pallas_call | solution.py:674
  686.7 7.8 collective-permute-done.74
  695.5 21.7 %collective-permute-done.73 = f32[2,2,768]{2,1,0:T(2,128)S(1)} collective-permute-done((f32[2,2,768]{2,1,0:T(2,128)S(1)}, f32[2,2,768]{2,1,0:T(2,128)S(1)}, u32[]{:S(2)}, u32[]{:S(2)}) %collective-permute-start.73) | collective-permute-done | bytes 12320 | tf_op jit(solution)/shard_map/ppermute | solution.py:27
  731.7 26.4 %collective-permute-done.79 = bf16[384,1152]{1,0:T(8,128)(2,1)S(1)} collective-permute-done((bf16[384,1152]{1,0:T(8,128)(2,1)}, bf16[384,1152]{1,0:T(8,128)(2,1)S(1)}, u32[]{:S(2)}, u32[]{:S(2)}) %collective-permute-start.79) | collective-permute-done | bytes 884768 | tf_op jit(solution)/shard_map/ppermute | solution.py:27
  761.6 15.5 %collective-permute-done.78 = bf16[192,3072]{1,0:T(8,128)(2,1)S(1)} collective-permute-done((bf16[192,3072]{1,0:T(8,128)(2,1)S(1)}, bf16[192,3072]{1,0:T(8,128)(2,1)S(1)}, u32[]{:S(2)}, u32[]{:S(2)}) %collective-permute-start.78) | collective-permute-done | bytes 1179680 | tf_op jit(solution)/shard_map/ppermute | solution.py:27
  786.6 6.4 collective-permute-done.81.refs_2_.refs_10_.refs_18_
  807.7 32.5 %collective-permute-done.87 = f32[2,2,768]{2,1,0:T(2,128)S(1)} collective-permute-done((f32[2,2,768]{2,1,0:T(2,128)S(1)}, f32[2,2,768]{2,1,0:T(2,128)S(1)}, u32[]{:S(2)}, u32[]{:S(2)}) %collective-permute-start.87) | collective-permute-done | bytes 12320 | tf_op jit(solution)/shard_map/ppermute | solution.py:27
  841.4 6.5 spread_ff.2
  866.0 6.7 spread_ff.3
  (494 shorter events, 288.4 us)
Async XLA Ops:
  7.2 148.7 %all-gather.9.cloned.1.call-start = ((), (), s32[]{:S(2)}) async-start(), calls=%async_computation.2 | async-start | bytes 1966080 | tf_op jit(solution)/shard_map/all_gather | solution.py:938
  7.2 28.8 %collective-permute-start.4 = (bf16[2,768,1024]{2,1,0:T(8,128)(2,1)}, bf16[2,768,1024]{2,1,0:T(8,128)(2,1)}, u32[]{:S(2)}, u32[]{:S(2)}) collective-permute-start(bf16[2,768,1024]{2,1,0:T(8,128)(2,1)} %refs_12_.11), channel_id=1, source_target_pairs={{0,4},{4,0},{1,5},{5,1},{2,6},{6,2},{3,7},{7,3},{8,12},{12,8},{9,1... | collective-permute-start | bytes 9437192 | tf_op jit(solution)/shard_map/ppermute | solution.py:27
  7.8 28.3 %collective-permute-start.5 = (bf16[2,768,1024]{2,1,0:T(8,128)(2,1)}, bf16[2,768,1024]{2,1,0:T(8,128)(2,1)}, u32[]{:S(2)}, u32[]{:S(2)}) collective-permute-start(bf16[2,768,1024]{2,1,0:T(8,128)(2,1)} %refs_13_.3), channel_id=1, source_target_pairs={{0,4},{4,0},{1,5},{5,1},{2,6},{6,2},{3,7},{7,3},{8,12},{12,8},{9,1... | collective-permute-start | bytes 9437192 | tf_op jit(solution)/shard_map/ppermute | solution.py:27
  17.5 31.8 %collective-permute-start = (bf16[256,768]{1,0:T(8,128)(2,1)}, bf16[256,768]{1,0:T(8,128)(2,1)S(1)}, u32[]{:S(2)}, u32[]{:S(2)}) collective-permute-start(bf16[256,768]{1,0:T(8,128)(2,1)} %get-tuple-element.310), channel_id=1, source_target_pairs={{0,2},{1,3},{2,0},{3,1},{4,6},{5,7},{6,4},{7,5},{8,10},{9,11},{10,... | collective-permute-start | bytes 1179656 | tf_op jit(solution)/shard_map/ppermute | solution.py:27
  21.2 79.4 %collective-permute-start.13 = (bf16[2,1024,768]{2,1,0:T(8,128)(2,1)}, bf16[2,1024,768]{2,1,0:T(8,128)(2,1)}, u32[]{:S(2)}, u32[]{:S(2)}) collective-permute-start(bf16[2,1024,768]{2,1,0:T(8,128)(2,1)} %refs_8_.7), channel_id=1, source_target_pairs={{0,4},{4,0},{1,5},{5,1},{2,6},{6,2},{3,7},{7,3},{8,12},{12,8},{9,1... | collective-permute-start | bytes 9437192 | tf_op jit(solution)/shard_map/ppermute | solution.py:27
  27.3 31.1 %collective-permute-start.6 = (bf16[288,768]{1,0:T(8,128)(2,1)S(1)}, bf16[288,768]{1,0:T(8,128)(2,1)S(1)}, u32[]{:S(2)}, u32[]{:S(2)}) collective-permute-start(bf16[288,768]{1,0:T(8,128)(2,1)S(1)} %copy-done.43), channel_id=1, source_target_pairs={{0,2},{1,3},{2,0},{3,1},{4,6},{5,7},{6,4},{7,5},{8,10},{9,11},{10,... | collective-permute-start | bytes 1327112 | tf_op jit(solution)/shard_map/ppermute | solution.py:27
  100.3 72.5 %all-gather.11.cloned.1.call-start = ((), (), s32[]{:S(2)}) async-start(), calls=%async_computation.3 | async-start | bytes 1966080 | tf_op jit(solution)/shard_map/all_gather | solution.py:938
  123.5 116.9 %all-gather.21.cloned.1.call-start = ((), (), s32[]{:S(2)}) async-start(), calls=%async_computation.10 | async-start | bytes 2211840 | tf_op jit(solution)/shard_map/all_gather | solution.py:940
  124.2 28.2 %collective-permute-start.16 = (bf16[192,1024]{1,0:T(8,128)(2,1)}, bf16[192,1024]{1,0:T(8,128)(2,1)}, u32[]{:S(2)}, u32[]{:S(2)}) collective-permute-start(bf16[192,1024]{1,0:T(8,128)(2,1)} %get-tuple-element.339), channel_id=1, source_target_pairs={{0,2},{1,3},{2,0},{3,1},{4,6},{5,7},{6,4},{7,5},{8,10},{9,11},{10,... | collective-permute-start | bytes 1179656 | tf_op jit(solution)/shard_map/ppermute | solution.py:27
  152.2 28.7 %collective-permute-start.22 = (bf16[256,1536]{1,0:T(8,128)(2,1)}, bf16[256,1536]{1,0:T(8,128)(2,1)S(1)}, u32[]{:S(2)}, u32[]{:S(2)}) collective-permute-start(bf16[256,1536]{1,0:T(8,128)(2,1)} %get-tuple-element.361.refs_1_), channel_id=1, source_target_pairs={{0,1},{1,0},{2,3},{3,2},{4,5},{5,4},{6,7},{7,6},{8,9},{9,8},{10,11... | collective-permute-start | bytes 2359304 | tf_op jit(solution)/shard_map/ppermute | solution.py:27
  154.3 26.6 %collective-permute-start.25 = (bf16[192,1024]{1,0:T(8,128)(2,1)}, bf16[192,1024]{1,0:T(8,128)(2,1)S(1)}, u32[]{:S(2)}, u32[]{:S(2)}) collective-permute-start(bf16[192,1024]{1,0:T(8,128)(2,1)} %collective-permute-done.16.refs_0_), channel_id=1, source_target_pairs={{0,24},{8,16},{16,8},{24,0},{1,25},{9,17},{17,9},{25,1},{2,26},{10... | collective-permute-start | bytes 1179656 | tf_op jit(solution)/shard_map/ppermute | solution.py:27
  161.8 25.8 %collective-permute-start.26 = (bf16[768,1024]{1,0:T(8,128)(2,1)}, bf16[768,1024]{1,0:T(8,128)(2,1)S(1)}, u32[]{:S(2)}, u32[]{:S(2)}) collective-permute-start(bf16[768,1024]{1,0:T(8,128)(2,1)} %all-gather.9.cloned.1.call-done.refs_8_.refs_14_), channel_id=1, source_target_pairs={{0,4},{4,0},{1,5},{5,1},{2,6},{6,2},{3,7},{7,3},{8,12},{12,8},{9,1... | collective-permute-start | bytes 4718600 | tf_op jit(solution)/shard_map/ppermute | solution.py:27
  201.1 41.9 %collective-permute-start.31 = (bf16[256,1536]{1,0:T(8,128)(2,1)}, bf16[256,1536]{1,0:T(8,128)(2,1)}, u32[]{:S(2)}, u32[]{:S(2)}) collective-permute-start(bf16[256,1536]{1,0:T(8,128)(2,1)} %get-tuple-element.373.refs_1_), channel_id=1, source_target_pairs={{0,1},{1,0},{2,3},{3,2},{4,5},{5,4},{6,7},{7,6},{8,9},{9,8},{10,11... | collective-permute-start | bytes 2359304 | tf_op jit(solution)/shard_map/ppermute | solution.py:27
  208.0 35.1 %collective-permute-start.30 = (bf16[192,1024]{1,0:T(8,128)(2,1)}, bf16[192,1024]{1,0:T(8,128)(2,1)}, u32[]{:S(2)}, u32[]{:S(2)}) collective-permute-start(bf16[192,1024]{1,0:T(8,128)(2,1)} %get-tuple-element.383), channel_id=1, source_target_pairs={{0,2},{1,3},{2,0},{3,1},{4,6},{5,7},{6,4},{7,5},{8,10},{9,11},{10,... | collective-permute-start | bytes 1179656 | tf_op jit(solution)/shard_map/ppermute | solution.py:27
  208.0 96.8 %all-gather.13.cloned.1.call-start = ((), (), s32[]{:S(2)}) async-start(), calls=%async_computation.4 | async-start | bytes 1966080 | tf_op jit(solution)/shard_map/all_gather | solution.py:938
  244.2 27.8 %collective-permute-start.35 = (bf16[256,1536]{1,0:T(8,128)(2,1)S(1)}, bf16[256,1536]{1,0:T(8,128)(2,1)}, u32[]{:S(2)}, u32[]{:S(2)}) collective-permute-start(bf16[256,1536]{1,0:T(8,128)(2,1)S(1)} %copy-done.85), channel_id=1, source_target_pairs={{0,1},{1,0},{2,3},{3,2},{4,5},{5,4},{6,7},{7,6},{8,9},{9,8},{10,11... | collective-permute-start | bytes 2359304 | tf_op jit(solution)/shard_map/ppermute | solution.py:27
  248.2 75.8 %all-gather.15.cloned.1.call-start = ((), (), s32[]{:S(2)}) async-start(), calls=%async_computation.5 | async-start | bytes 1966080 | tf_op jit(solution)/shard_map/all_gather | solution.py:938
  254.9 26.5 %collective-permute-start.36 = (bf16[256,768]{1,0:T(8,128)(2,1)}, bf16[256,768]{1,0:T(8,128)(2,1)S(1)}, u32[]{:S(2)}, u32[]{:S(2)}) collective-permute-start(bf16[256,768]{1,0:T(8,128)(2,1)} %get-tuple-element.391.refs_2_.refs_13_), channel_id=1, source_target_pairs={{0,4},{4,0},{1,5},{5,1},{2,6},{6,2},{3,7},{7,3},{8,12},{12,8},{9,1... | collective-permute-start | bytes 1179656 | tf_op jit(solution)/shard_map/ppermute | solution.py:27
  281.1 265.7 %reduce-scatter.3.cloned.1.call-start = ((), (), s32[]{:S(2)}) async-start(), calls=%async_computation.6 | async-start | bytes 11796480 | tf_op jit(solution)/shard_map/reduce_scatter | solution.py:1007
  293.4 27.2 %collective-permute-start.41 = (bf16[192,1024]{1,0:T(8,128)(2,1)S(1)}, bf16[192,1024]{1,0:T(8,128)(2,1)S(1)}, u32[]{:S(2)}, u32[]{:S(2)}) collective-permute-start(bf16[192,1024]{1,0:T(8,128)(2,1)S(1)} %collective-permute-done.34.refs_0_), channel_id=1, source_target_pairs={{0,24},{8,16},{16,8},{24,0},{1,25},{9,17},{17,9},{25,1},{2,26},{10... | collective-permute-start | bytes 1179656 | tf_op jit(solution)/shard_map/ppermute | solution.py:27
  324.5 32.4 %collective-permute-start.46 = (bf16[256,1536]{1,0:T(8,128)(2,1)}, bf16[256,1536]{1,0:T(8,128)(2,1)}, u32[]{:S(2)}, u32[]{:S(2)}) collective-permute-start(bf16[256,1536]{1,0:T(8,128)(2,1)} %get-tuple-element.408.refs_1_), channel_id=1, source_target_pairs={{0,1},{1,0},{2,3},{3,2},{4,5},{5,4},{6,7},{7,6},{8,9},{9,8},{10,11... | collective-permute-start | bytes 2359304 | tf_op jit(solution)/shard_map/ppermute | solution.py:27
  389.1 37.8 %collective-permute-start.51 = (bf16[256,1536]{1,0:T(8,128)(2,1)}, bf16[256,1536]{1,0:T(8,128)(2,1)}, u32[]{:S(2)}, u32[]{:S(2)}) collective-permute-start(bf16[256,1536]{1,0:T(8,128)(2,1)} %get-tuple-element.439.refs_2_), channel_id=1, source_target_pairs={{0,1},{1,0},{2,3},{3,2},{4,5},{5,4},{6,7},{7,6},{8,9},{9,8},{10,11... | collective-permute-start | bytes 2359304 | tf_op jit(solution)/shard_map/ppermute | solution.py:27
  405.0 49.9 %collective-permute-start.54 = (bf16[256,1536]{1,0:T(8,128)(2,1)}, bf16[256,1536]{1,0:T(8,128)(2,1)}, u32[]{:S(2)}, u32[]{:S(2)}) collective-permute-start(bf16[256,1536]{1,0:T(8,128)(2,1)} %get-tuple-element.445.refs_2_), channel_id=1, source_target_pairs={{0,1},{1,0},{2,3},{3,2},{4,5},{5,4},{6,7},{7,6},{8,9},{9,8},{10,11... | collective-permute-start | bytes 2359304 | tf_op jit(solution)/shard_map/ppermute | solution.py:27
  454.4 173.5 %reduce-scatter.5.cloned.1.call-start = ((), (), s32[]{:S(2)}) async-start(), calls=%async_computation.7 | async-start | bytes 4423680 | tf_op jit(solution)/shard_map/reduce_scatter | solution.py:1007
  479.0 30.8 %collective-permute-start.57 = (bf16[256,1536]{1,0:T(8,128)(2,1)}, bf16[256,1536]{1,0:T(8,128)(2,1)}, u32[]{:S(2)}, u32[]{:S(2)}) collective-permute-start(bf16[256,1536]{1,0:T(8,128)(2,1)} %get-tuple-element.473.refs_1_), channel_id=1, source_target_pairs={{0,1},{1,0},{2,3},{3,2},{4,5},{5,4},{6,7},{7,6},{8,9},{9,8},{10,11... | collective-permute-start | bytes 2359304 | tf_op jit(solution)/shard_map/ppermute | solution.py:27
  508.2 47.4 %collective-permute-start.59 = (bf16[256,1536]{1,0:T(8,128)(2,1)}, bf16[256,1536]{1,0:T(8,128)(2,1)}, u32[]{:S(2)}, u32[]{:S(2)}) collective-permute-start(bf16[256,1536]{1,0:T(8,128)(2,1)} %get-tuple-element.483.refs_2_), channel_id=1, source_target_pairs={{0,1},{1,0},{2,3},{3,2},{4,5},{5,4},{6,7},{7,6},{8,9},{9,8},{10,11... | collective-permute-start | bytes 2359304 | tf_op jit(solution)/shard_map/ppermute | solution.py:27
  524.8 65.0 %collective-permute-start.61 = (bf16[256,1536]{1,0:T(8,128)(2,1)}, bf16[256,1536]{1,0:T(8,128)(2,1)}, u32[]{:S(2)}, u32[]{:S(2)}) collective-permute-start(bf16[256,1536]{1,0:T(8,128)(2,1)} %get-tuple-element.489.refs_2_), channel_id=1, source_target_pairs={{0,1},{1,0},{2,3},{3,2},{4,5},{5,4},{6,7},{7,6},{8,9},{9,8},{10,11... | collective-permute-start | bytes 2359304 | tf_op jit(solution)/shard_map/ppermute | solution.py:27
  555.0 286.4 %all-gather.17.cloned.1.call-start = ((), (), s32[]{:S(2)}) async-start(), calls=%async_computation.8 | async-start | bytes 5898240 | tf_op jit(solution)/shard_map/all_gather | solution.py:1048
  570.1 30.5 %collective-permute-start.63 = (bf16[256,768]{1,0:T(8,128)(2,1)}, bf16[256,768]{1,0:T(8,128)(2,1)S(1)}, u32[]{:S(2)}, u32[]{:S(2)}) collective-permute-start(bf16[256,768]{1,0:T(8,128)(2,1)} %get-tuple-element.505), channel_id=1, source_target_pairs={{0,4},{4,0},{1,5},{5,1},{2,6},{6,2},{3,7},{7,3},{8,12},{12,8},{9,1... | collective-permute-start | bytes 1179656 | tf_op jit(solution)/shard_map/ppermute | solution.py:27
  570.6 54.5 %collective-permute-start.62 = (bf16[192,3072]{1,0:T(8,128)(2,1)}, bf16[192,3072]{1,0:T(8,128)(2,1)}, u32[]{:S(2)}, u32[]{:S(2)}) collective-permute-start(bf16[192,3072]{1,0:T(8,128)(2,1)} %get-tuple-element.514), channel_id=1, source_target_pairs={{0,2},{1,3},{2,0},{3,1},{4,6},{5,7},{6,4},{7,5},{8,10},{9,11},{10,... | collective-permute-start | bytes 3538952 | tf_op jit(solution)/shard_map/ppermute | solution.py:27
  587.6 76.2 %collective-permute-start.69 = (bf16[384,3072]{1,0:T(8,128)(2,1)}, bf16[384,3072]{1,0:T(8,128)(2,1)}, u32[]{:S(2)}, u32[]{:S(2)}) collective-permute-start(bf16[384,3072]{1,0:T(8,128)(2,1)} %get-tuple-element.508), channel_id=1, source_target_pairs={{0,8},{8,0},{16,24},{24,16},{1,9},{9,1},{17,25},{25,17},{2,10},{10... | collective-permute-start | bytes 7077896 | tf_op jit(solution)/shard_map/ppermute | solution.py:27
  589.0 74.8 %collective-permute-start.70 = (bf16[384,3072]{1,0:T(8,128)(2,1)}, bf16[384,3072]{1,0:T(8,128)(2,1)}, u32[]{:S(2)}, u32[]{:S(2)}) collective-permute-start(bf16[384,3072]{1,0:T(8,128)(2,1)} %get-tuple-element.509), channel_id=1, source_target_pairs={{0,16},{8,24},{16,0},{24,8},{1,17},{9,25},{17,1},{25,9},{2,18},{10... | collective-permute-start | bytes 7077896 | tf_op jit(solution)/shard_map/ppermute | solution.py:27
  607.3 34.7 %collective-permute-start.65 = (bf16[256,1536]{1,0:T(8,128)(2,1)}, bf16[256,1536]{1,0:T(8,128)(2,1)}, u32[]{:S(2)}, u32[]{:S(2)}) collective-permute-start(bf16[256,1536]{1,0:T(8,128)(2,1)} %get-tuple-element.522), channel_id=1, source_target_pairs={{0,1},{1,0},{2,3},{3,2},{4,5},{5,4},{6,7},{7,6},{8,9},{9,8},{10,11... | collective-permute-start | bytes 2359304 | tf_op jit(solution)/shard_map/ppermute | solution.py:27
  615.5 43.2 %collective-permute-start.66 = (bf16[256,1536]{1,0:T(8,128)(2,1)}, bf16[256,1536]{1,0:T(8,128)(2,1)S(1)}, u32[]{:S(2)}, u32[]{:S(2)}) collective-permute-start(bf16[256,1536]{1,0:T(8,128)(2,1)} %get-tuple-element.525), channel_id=1, source_target_pairs={{0,1},{1,0},{2,3},{3,2},{4,5},{5,4},{6,7},{7,6},{8,9},{9,8},{10,11... | collective-permute-start | bytes 2359304 | tf_op jit(solution)/shard_map/ppermute | solution.py:27
  669.6 182.9 %all-gather.19.cloned.1.call-start = ((), (), s32[]{:S(2)}) async-start(), calls=%async_computation.9 | async-start | bytes 2211840 | tf_op jit(solution)/shard_map/all_gather | solution.py:1048
  669.8 51.6 %collective-permute-start.71 = (bf16[192,3072]{1,0:T(8,128)(2,1)}, bf16[192,3072]{1,0:T(8,128)(2,1)}, u32[]{:S(2)}, u32[]{:S(2)}) collective-permute-start(bf16[192,3072]{1,0:T(8,128)(2,1)} %get-tuple-element.638), channel_id=1, source_target_pairs={{0,8},{8,0},{16,24},{24,16},{1,9},{9,1},{17,25},{25,17},{2,10},{10... | collective-permute-start | bytes 3538952 | tf_op jit(solution)/shard_map/ppermute | solution.py:27
  671.2 50.2 %collective-permute-start.76 = (bf16[192,3072]{1,0:T(8,128)(2,1)}, bf16[192,3072]{1,0:T(8,128)(2,1)}, u32[]{:S(2)}, u32[]{:S(2)}) collective-permute-start(bf16[192,3072]{1,0:T(8,128)(2,1)} %get-tuple-element.639), channel_id=1, source_target_pairs={{0,16},{8,24},{16,0},{24,8},{1,17},{9,25},{17,1},{25,9},{2,18},{10... | collective-permute-start | bytes 3538952 | tf_op jit(solution)/shard_map/ppermute | solution.py:27
  675.7 42.8 %collective-permute-start.67 = (bf16[256,1536]{1,0:T(8,128)(2,1)}, bf16[256,1536]{1,0:T(8,128)(2,1)}, u32[]{:S(2)}, u32[]{:S(2)}) collective-permute-start(bf16[256,1536]{1,0:T(8,128)(2,1)} %get-tuple-element.556), channel_id=1, source_target_pairs={{0,1},{1,0},{2,3},{3,2},{4,5},{5,4},{6,7},{7,6},{8,9},{9,8},{10,11... | collective-permute-start | bytes 2359304 | tf_op jit(solution)/shard_map/ppermute | solution.py:27
  677.1 44.3 %collective-permute-start.68 = (bf16[256,1536]{1,0:T(8,128)(2,1)}, bf16[256,1536]{1,0:T(8,128)(2,1)}, u32[]{:S(2)}, u32[]{:S(2)}) collective-permute-start(bf16[256,1536]{1,0:T(8,128)(2,1)} %get-tuple-element.559), channel_id=1, source_target_pairs={{0,1},{1,0},{2,3},{3,2},{4,5},{5,4},{6,7},{7,6},{8,9},{9,8},{10,11... | collective-permute-start | bytes 2359304 | tf_op jit(solution)/shard_map/ppermute | solution.py:27
  717.2 40.9 %collective-permute-start.79 = (bf16[384,1152]{1,0:T(8,128)(2,1)}, bf16[384,1152]{1,0:T(8,128)(2,1)S(1)}, u32[]{:S(2)}, u32[]{:S(2)}) collective-permute-start(bf16[384,1152]{1,0:T(8,128)(2,1)} %get-tuple-element.546), channel_id=1, source_target_pairs={{0,8},{8,0},{16,24},{24,16},{1,9},{9,1},{17,25},{25,17},{2,10},{10... | collective-permute-start | bytes 2654216 | tf_op jit(solution)/shard_map/ppermute | solution.py:27
  718.5 39.7 %collective-permute-start.80 = (bf16[384,1152]{1,0:T(8,128)(2,1)}, bf16[384,1152]{1,0:T(8,128)(2,1)S(1)}, u32[]{:S(2)}, u32[]{:S(2)}) collective-permute-start(bf16[384,1152]{1,0:T(8,128)(2,1)} %get-tuple-element.547), channel_id=1, source_target_pairs={{0,16},{8,24},{16,0},{24,8},{1,17},{9,25},{17,1},{25,9},{2,18},{10... | collective-permute-start | bytes 2654216 | tf_op jit(solution)/shard_map/ppermute | solution.py:27
  723.7 53.4 %collective-permute-start.78 = (bf16[192,3072]{1,0:T(8,128)(2,1)S(1)}, bf16[192,3072]{1,0:T(8,128)(2,1)S(1)}, u32[]{:S(2)}, u32[]{:S(2)}) collective-permute-start(bf16[192,3072]{1,0:T(8,128)(2,1)S(1)} %add_convert_fusion.4), channel_id=1, source_target_pairs={{0,2},{1,3},{2,0},{3,1},{4,6},{5,7},{6,4},{7,5},{8,10},{9,11},{10,... | collective-permute-start | bytes 3538952 | tf_op jit(solution)/shard_map/ppermute | solution.py:27
  731.7 63.5 %collective-permute-start.77 = (bf16[1024,768]{1,0:T(8,128)(2,1)}, bf16[1024,768]{1,0:T(8,128)(2,1)}, u32[]{:S(2)}, u32[]{:S(2)}) collective-permute-start(bf16[1024,768]{1,0:T(8,128)(2,1)} %pad_maximum_fusion.2), channel_id=1, source_target_pairs={{0,4},{4,0},{1,5},{5,1},{2,6},{6,2},{3,7},{7,3},{8,12},{12,8},{9,1... | collective-permute-start | bytes 4718600 | tf_op jit(solution)/shard_map/ppermute | solution.py:27
  795.2 53.2 %collective-permute-start.86 = (bf16[192,1152]{1,0:T(8,128)(2,1)}, bf16[192,1152]{1,0:T(8,128)(2,1)}, u32[]{:S(2)}, u32[]{:S(2)}) collective-permute-start(bf16[192,1152]{1,0:T(8,128)(2,1)} %add_convert_fusion.11), channel_id=1, source_target_pairs={{0,2},{1,3},{2,0},{3,1},{4,6},{5,7},{6,4},{7,5},{8,10},{9,11},{10,... | collective-permute-start | bytes 1327112 | tf_op jit(solution)/shard_map/ppermute | solution.py:27
  801.0 55.3 %collective-permute-start.85 = (bf16[512,768]{1,0:T(8,128)(2,1)}, bf16[512,768]{1,0:T(8,128)(2,1)}, u32[]{:S(2)}, u32[]{:S(2)}) collective-permute-start(bf16[512,768]{1,0:T(8,128)(2,1)} %pad_maximum_fusion.8), channel_id=1, source_target_pairs={{0,2},{1,3},{2,0},{3,1},{4,6},{5,7},{6,4},{7,5},{8,10},{9,11},{10,... | collective-permute-start | bytes 2359304 | tf_op jit(solution)/shard_map/ppermute | solution.py:27
  804.9 59.1 %collective-permute-start.89 = (bf16[192,3072]{1,0:T(8,128)(2,1)}, bf16[192,3072]{1,0:T(8,128)(2,1)S(1)}, u32[]{:S(2)}, u32[]{:S(2)}) collective-permute-start(bf16[192,3072]{1,0:T(8,128)(2,1)} %pad_maximum_fusion.4), channel_id=1, source_target_pairs={{0,16},{8,24},{16,0},{24,8},{1,17},{9,25},{17,1},{25,9},{2,18},{10... | collective-permute-start | bytes 3538952 | tf_op jit(solution)/shard_map/ppermute | solution.py:27
  805.6 58.3 %collective-permute-start.88 = (bf16[192,3072]{1,0:T(8,128)(2,1)}, bf16[192,3072]{1,0:T(8,128)(2,1)S(1)}, u32[]{:S(2)}, u32[]{:S(2)}) collective-permute-start(bf16[192,3072]{1,0:T(8,128)(2,1)} %pad_maximum_fusion.3), channel_id=1, source_target_pairs={{0,8},{8,0},{16,24},{24,16},{1,9},{9,1},{17,25},{25,17},{2,10},{10... | collective-permute-start | bytes 3538952 | tf_op jit(solution)/shard_map/ppermute | solution.py:27
  806.9 33.3 %collective-permute-start.87 = (f32[2,2,768]{2,1,0:T(2,128)S(1)}, f32[2,2,768]{2,1,0:T(2,128)S(1)}, u32[]{:S(2)}, u32[]{:S(2)}) collective-permute-start(f32[2,2,768]{2,1,0:T(2,128)S(1)} %add.179), channel_id=1, source_target_pairs={{0,8},{8,0},{16,24},{24,16},{1,9},{9,1},{17,25},{25,17},{2,10},{10... | collective-permute-start | bytes 36872 | tf_op jit(solution)/shard_map/ppermute | solution.py:27
  (154 other events, 1745.3 us)
Sparse Core Ops, SparseCore 0:
  100.4 30.4 all-gather.8
  133.3 39.3 all-gather.10
  208.1 32.2 all-gather.20
  248.3 28.1 all-gather.12
  281.3 39.7 all-gather.14
  454.5 92.2 reduce-scatter.2
  555.1 56.5 reduce-scatter.4
  669.7 88.8 all-gather.16
  784.6 41.8 all-gather.18

commit v3 on v2

--- a/solution.py
+++ b/solution.py
@@ -48,6 +48,18 @@
     for bit in bits[:-1]:
         part = add_low(part, hop(part, "cols", bit))
     return (part, hop(part, "cols", bits[-1]))
+
+
+def last_pair(part):
+    cols, bits = lax.axis_size("cols"), low_bits()
+    if len(bits) != 1:
+        return group_pair(part)
+    pairs = []
+    for core in range(2):
+        for col in range(cols):
+            if col % 2 != core:
+                pairs.append((core * cols + col, core * cols + (col ^ 1)))
+    return (part, lax.ppermute(part, ("rows", "cols"), pairs))
 
 
 class Order:
@@ -285,15 +297,17 @@
     )
 
 
-def score(key, query, kind, core):
+def score(key, query, kind):
     raw = dot_nt(key, query) * HEAD ** (-0.5)
     if kind == "own":
         key_pos = lax.broadcasted_iota(jnp.int32, raw.shape, 0)
         query_pos = lax.broadcasted_iota(jnp.int32, raw.shape, 1)
         raw = jnp.where(query_pos >= key_pos, raw, NEGATIVE)
-    if kind == "sib":
-        raw = jnp.where(core == 1, raw, NEGATIVE)
     return raw
+
+
+def offsets_of(chunks, core):
+    return [0.0] * (2 * chunks - 1) + [jnp.where(core == 1, 0.0, -NEGATIVE)]
 
 
 def kinds_of(chunks):
@@ -310,19 +324,20 @@
     def body(stream, results, core_ref):
         (q_ref,), kv_refs = stream.take(1), stream.take(2 * chunks)
         att_ref, lse_ref, part_ref = results.buffers
-        side_core = core_ref[0]
+        offsets = offsets_of(chunks, core_ref[0])
         for h in range(2 * heads):
             group = (h // heads) * q_width + (h % heads) // 2 * HEAD
             mine = slice(h * HEAD, (h + 1) * HEAD)
             query = q_ref[:, mine]
             scores = [
-                score(ref[:, group : group + HEAD], query, kind, side_core)
+                score(ref[:, group : group + HEAD], query, kind)
                 for ref, kind in zip(kv_refs, kinds_of(chunks))
             ]
             highest = functools.reduce(
-                jnp.maximum, [jnp.max(s, axis=0, keepdims=True) for s in scores]
+                jnp.maximum,
+                [jnp.max(s, axis=0, keepdims=True) - o for s, o in zip(scores, offsets)],
             )
-            exps = [jnp.exp(s - highest) for s in scores]
+            exps = [jnp.exp(s - (highest + o)) for s, o in zip(scores, offsets)]
             total = sum(jnp.sum(e, axis=0, keepdims=True) for e in exps)
             share = 1.0 / total
             lse_ref[h : h + 1, :] = highest + jnp.log(total)
@@ -365,7 +380,7 @@
     def body(stream, results, core_ref, grad_ref):
         put_norm_back(stream.take(6), results, 0)
         g_ref = results.buffers[1]
-        side_core = core_ref[0]
+        offsets = offsets_of(chunks, core_ref[0])
         for side in range(2):
             first, second = stream.take(2)
             grad = dot_nt(g_ref[:, :half], first[...])
@@ -383,8 +398,8 @@
                 mine = slice(h * HEAD, (h + 1) * HEAD)
                 query, grad, lse = q_ref[:, mine], grad_ref[:, mine], lse_ref[h : h + 1, :]
                 probs = [
-                    jnp.exp(score(ref[:, key_spot], query, kind, side_core) - lse)
-                    for ref, kind in zip(kv_refs, kinds_of(chunks))
+                    jnp.exp(score(ref[:, key_spot], query, kind) - (lse + o))
+                    for ref, kind, o in zip(kv_refs, kinds_of(chunks), offsets)
                 ]
                 prob_grads = [dot_nt(ref[:, value_spot], grad) for ref in kv_refs]
                 delta = sum(
@@ -558,8 +573,9 @@
 
     def work(y_refs):
         grads = jnp.concatenate([ref[...] for ref in y_refs], axis=0)
-        second_ref[...] = low_dot(turned_ref[half:, :], grads).astype(LOW)
-        first_ref[...] = low_dot(turned_ref[:half, :], grads).astype(LOW)
+        total = low_dot(turned_ref[...], grads)
+        first_ref[...] = total[:half].astype(LOW)
+        second_ref[...] = total[half:].astype(LOW)
 
     @pl.when(j == 0)
     def _():
@@ -582,7 +598,7 @@
     chunks = len(all_b)
     rows, wide = all_b[0].shape
     ff = inner[0].shape[1] // 2
-    step = min(512, ff)
+    step = min(1024, ff)
     n = ff // step
     split = 4 * n
     full = whole((rows, wide))
@@ -626,8 +642,9 @@
                 [ref[:, side * size : (side + 1) * size] for ref in y_refs], axis=0
             )
             start = side * (width + q_width) + base
-            second_ref[:, start : start + size] = low_dot(turned[half:], grads).astype(LOW)
-            first_ref[:, start : start + size] = low_dot(turned[:half], grads).astype(LOW)
+            total = low_dot(turned, grads)
+            first_ref[:, start : start + size] = total[:half].astype(LOW)
+            second_ref[:, start : start + size] = total[half:].astype(LOW)
 
 
 def in_weights(all_a, branch_a, grads, attended):
@@ -652,7 +669,7 @@
 
 def role_sum_kernel(row_ref, side_ref, left_ref, right_ref, *outs):
     step = pl.program_id(0)
-    total = (left_ref[...].astype(FULL) + right_ref[...].astype(FULL)).astype(LOW)
+    total = left_ref[...] + right_ref[...]
     for i, out_ref in enumerate(outs):
 
         @pl.when(step // 2 == i)
@@ -1311,7 +1328,12 @@
                 group.fetch(order)
             order.join(pairs[1])
             first.cross(order)
+            for group in a_groups[1]:
+                order.join(group.piece)
             third.collect(order)
+            for group in a_groups[1]:
+                group.gather(order)
+            f_groups[1][0].fetch(order)
             second.cross(order)
             first.done(order)
         else:
@@ -1339,11 +1361,7 @@
         down_parts = [Part(v, l) for v in own_downs] + [Part(v) for v in packs[2]]
         weights[l] = (ins, outs, pair_parts, down_parts)
         rear(l, 0, kept[0])
-        if more:
-            for group in a_groups[1]:
-                group.gather(order)
-            f_groups[1][0].fetch(order)
-        else:
+        if not more:
             cotangent.share(order)
             cotangent.send(order, 1)
             cotangent.send(order, 0)
@@ -1413,7 +1431,8 @@
         proj_grad, part = order.mark(
             project_back(order.after(dq), mine, came, *tables[j], weights[l][0])
         )
-        grads[j] = (grads[j][0], *group_pair(part), *grads[j][3:])
+        pair = group_pair(part) if l else last_pair(part)
+        grads[j] = (grads[j][0], *pair, *grads[j][3:])
         return kept[:2] + (proj_grad,) + kept[3:]
 
     def in_grad(l, kept):
@@ -1451,16 +1470,19 @@
     _, mids[0], kept[0] = attend_step(l, 0, held)
     kept[1] = project_step(l, 1, mids[1], kept[1])
     kept[0] = project_step(l, 0, mids[0], kept[0])
+    sums["in", 1].third(order)
+    in_grad(l, kept)
     sums["ff", 1].fourth(order)
     sums["ff", 1].gather(order)
-    sums["in", 1].third(order)
-    in_grad(l, kept)
     for g in reversed(grads):
         order.join(*g[1:3])
     ends = [finish_back(order.after(g[0]), *g[1:]) for g in grads]
     order.mark(tuple(g for g, _ in ends))
     gain_a[0] = sum(part for _, part in ends)
-    tops = [group_pair(part) for part in order.after(pairs)]
+    if len(low_bits()) == 1:
+        gain_a[0] = jnp.where(lo == core, gain_a[0], 0.0)
+        gain_a[0] = gain_a[0] + hop(gain_a[0], "cols", 1)
+    tops = [last_pair(part) for part in order.after(pairs)]
     gain_grads = [jnp.concatenate([gain_a[l], gain_b[l]], axis=0) for l in range(LAYERS)]
     grad_gains = order.after(jnp.stack(gain_grads))
     width = grad_gains.shape[-1] // 2
@@ -1474,39 +1496,38 @@
     sums["in", 1].fourth(order)
     grad_gains = order.mark(grad_gains + order.after(gains_came))
     order.join(tops)
-    sums["ff", 0].third(order)
-    sums["ff", 0].across(order)
-    sums["in", 1].gather(order)
     hidden = [
         h + left.astype(FULL) + right.astype(FULL)
         for h, (left, right) in order.after(list(zip(hidden, tops)))
     ]
     results = Departure((hidden, [g for g, _ in ends]), hi, lo, core, block_rows)
     results.cross(order)
-    gains_came = hop(grad_gains, "dp", 1)
+    sums["ff", 0].third(order)
+    sums["ff", 0].across(order)
+    gains_came = hop(order.after(grad_gains), "dp", 1)
+    sums["in", 1].gather(order)
     sums["in", 0].second(order)
     sums["ff", 0].fourth(order)
     sums["ff", 0].near(order)
     sums["in", 0].third(order)
-    sums["ff", 0].fifth(order)
     sums["in", 0].across(order)
-    results.away(order)
-    grad_gains = order.mark(grad_gains + order.after(gains_came))
-    bit = 2
+    ff_out = order.mark(spread_ff(order.after(spot), sums["ff", 1].pieces, 1, None))
+    bit = 1
     while bit < lax.axis_size("dp"):
-        gains_came = hop(grad_gains, "dp", bit)
-        if 2 * bit < lax.axis_size("dp"):
-            grad_gains = order.mark(grad_gains + order.after(gains_came))
+        grad_gains = order.mark(grad_gains + order.after(gains_came))
         bit *= 2
-    ff_out = order.mark(spread_ff(order.after(spot), sums["ff", 1].pieces, 1, None))
-    sums["in", 0].fourth(order)
-    sums["in", 0].straight(order)
+        if bit < lax.axis_size("dp"):
+            gains_came = hop(grad_gains, "dp", bit)
+        if bit == 2:
+            sums["ff", 0].fifth(order)
+            sums["in", 0].fourth(order)
+            sums["in", 0].straight(order)
+            results.away(order)
     in_out = order.mark(spread_in(order.after(spot), sums["in", 1].pieces, 1, None, q_width))
-    activations, input_grad = order.mark(results.done(order))
     sums["ff", 0].done(order)
     ff_out = order.mark(spread_ff(order.after(spot), sums["ff", 0].pieces, 0, ff_out))
-    in_out = spread_in(order.after(spot), sums["in", 0].pieces, 0, in_out, q_width)
-    grad_gains = grad_gains + gains_came
+    in_out = order.mark(spread_in(order.after(spot), sums["in", 0].pieces, 0, in_out, q_width))
+    activations, input_grad = results.done(order)
     return (activations, input_grad, *in_out, *ff_out, grad_gains)
 
 

time: 899 us -> 863 us (0.960)
  waiting for transfers between devices: 305 us -> 248 us
  starting transfers between devices: 87.6 us -> 103 us
    ppermute x94 -> x91, waiting for transfers between devices: 271 us -> 219 us  [hop(): return lax.ppermute(value, axis, [(i, i ^ distance) for i in range(size)])]
    ppermute x0 -> x4, waiting for transfers between devices: none -> 19.1 us  [last_pair(): return (part, lax.ppermute(part, ('rows', 'cols'), pairs))]
    all_gather x1, waiting for transfers between devices: 19.9 us -> 4.18 us  [gather(): pieces = lax.all_gather(piece, 'dp', axis=0)]
    all_gather x4, waiting for transfers between devices: 11 us -> 0.03 us  [gather(): self.first = lax.all_gather(piece, 'dp', axis=0, tiled=True)]
    ppermute x94 -> x91, starting transfers between devices: 85.8 us -> 95.1 us  [hop(): return lax.ppermute(value, axis, [(i, i ^ distance) for i in range(size)])]
    unnamed x202 -> x182, local copies, waits for them, and re-layouts: 30.4 us -> 27.4 us
  transfers between devices with their start and end apart: 103 -> 104, of which waited for: 38 -> 38; matrix products, arithmetic and copies ran while one was open for 10% -> 11% of each run, Pallas kernels for 40% -> 43%
where the time goes in v3:
time: 863 us; the launch traced here: 854 us
  Pallas kernels  367 us (43%)
  waiting for transfers between devices  248 us (29%)
  starting transfers between devices  103 us (12%)
  other arithmetic  74.7 us (9%)
  local copies, waits for them, and re-layouts  46.1 us (5%)
  between operations  15.8 us (2%)
    pallas_call x24, Pallas kernels, call(): pl.pallas_call(kernel, grid_spec=pltpu.PrefetchScalarGridSpec(num_scalar_...  244 us
    ppermute x91, waiting for transfers between devices, hop(): return lax.ppermute(value, axis, [(i, i ^ distance) for i in range(size)])  219 us
    ppermute x91, starting transfers between devices, hop(): return lax.ppermute(value, axis, [(i, i ^ distance) for i in range(size)])  95.1 us
    pallas_call x2, Pallas kernels, ff_weights(): pl.pallas_call(functools.partial(ff_weights_kernel, chunks, split), grid=...  34 us
    unnamed x182, local copies, waits for them, and re-layouts  27.4 us
    convert_element_type x6, other arithmetic, add_low(): return (left.astype(FULL) + right.astype(FULL)).astype(LOW)  26.3 us
    pallas_call x2, Pallas kernels, role_sums(): pl.pallas_call(role_sum_kernel, grid_spec=pltpu.PrefetchScalarGridSpec(nu...  21.3 us
    pallas_call x2, Pallas kernels, in_weights(): pl.pallas_call(functools.partial(in_weights_kernel, chunks), grid=(1,), i...  19.7 us
  transfers between devices with their start and end apart: 104, of which 38 were waited for; matrix products, arithmetic and copies ran while one was open for 11% of the time, Pallas kernels for 43%

profile of v3, /device:TPU:0, one launch (start us, length us, event | category | flops | bytes accessed | tf_op | source)
XLA Modules:
  0.0 854.2 jit_solution(371467394730913621)
XLA Ops:
  40.0 9.3 %collective-permute-done = bf16[256,768]{1,0:T(8,128)(2,1)S(1)} collective-permute-done((bf16[256,768]{1,0:T(8,128)(2,1)}, bf16[256,768]{1,0:T(8,128)(2,1)S(1)}, u32[]{:S(2)}, u32[]{:S(2)}) %collective-permute-start) | collective-permute-done | bytes 393248 | tf_op jit(solution)/shard_map/ppermute | solution.py:27
  49.3 9.1 %collective-permute-done.6.refs_0_ = bf16[288,768]{1,0:T(8,128)(2,1)S(1)} collective-permute-done((bf16[288,768]{1,0:T(8,128)(2,1)S(1)}, bf16[288,768]{1,0:T(8,128)(2,1)S(1)}, u32[]{:S(2)}, u32[]{:S(2)}) %collective-permute-start.6) | collective-permute-done | bytes 442400 | tf_op jit(solution)/shard_map/ppermute | solution.py:27
  62.2 8.1 collective-permute-done.8.refs_1_
  74.6 17.0 %collective-permute-done.11 = bf16[192,1024]{1,0:T(8,128)(2,1)S(1)} collective-permute-done((bf16[192,1024]{1,0:T(8,128)(2,1)}, bf16[192,1024]{1,0:T(8,128)(2,1)S(1)}, u32[]{:S(2)}, u32[]{:S(2)}) %collective-permute-start.11) | collective-permute-done | bytes 393248 | tf_op jit(solution)/shard_map/ppermute | solution.py:27
  102.5 12.6 %collective-permute-done.14 = bf16[192,1024]{1,0:T(8,128)(2,1)S(1)} collective-permute-done((bf16[192,1024]{1,0:T(8,128)(2,1)}, bf16[192,1024]{1,0:T(8,128)(2,1)S(1)}, u32[]{:S(2)}, u32[]{:S(2)}) %collective-permute-start.14) | collective-permute-done | bytes 393248 | tf_op jit(solution)/shard_map/ppermute | solution.py:27
  115.1 6.0 project.4
  131.9 6.8 attend.4
  142.7 18.7 %attend.5 = (bf16[256,768]{1,0:T(8,128)(2,1)}, f32[8,256]{1,0:T(8,128)}, bf16[256,1536]{1,0:T(8,128)(2,1)}) custom-call(s32[1]{0:T(128)} %bitcast.3.refs_0_, bf16[256,768]{1,0:T(8,128)(2,1)} %get-tuple-element.360.refs_1_.refs_11_, bf16[256,768]{1,0:T(8,128)(2,1)} %get-tuple-element.346.refs_2_.refs_13_, bf16[256,768]{1,0:T(8,128)(2,1)} %copy-done.77, ...), custom_call_target="tpu_custom_call" | custom-call | flops 82543902720 | bytes 129761280 | tf_op jit(solution)/shard_map/attend/pallas_call | solution.py:249
  167.7 8.8 %collective-permute-done.24.refs_1_ = bf16[192,1024]{1,0:T(8,128)(2,1)S(1)} collective-permute-done((bf16[192,1024]{1,0:T(8,128)(2,1)}, bf16[192,1024]{1,0:T(8,128)(2,1)S(1)}, u32[]{:S(2)}, u32[]{:S(2)}) %collective-permute-start.24) | collective-permute-done | bytes 393248 | tf_op jit(solution)/shard_map/ppermute | solution.py:27
  176.5 8.2 collective-permute-done.25.refs_2_
  184.7 6.2 collective-permute-done.22.refs_2_
  199.2 11.7 %feed_forward.4 = (f32[256,1536]{1,0:T(8,128)}, f32[256,1]{1,0:T(8,128)}, bf16[256,1536]{1,0:T(8,128)(2,1)}, bf16[256,2048]{1,0:T(8,128)(2,1)}, bf16[256,2048]{1...) custom-call(f32[256,1536]{1,0:T(8,128)} %get-tuple-element.369.refs_0_, ...), custom_call_target="tpu_custom_call" | custom-call | flops 144955146240 | bytes 637102080 | tf_op jit(solution)/shard_map/feed_forward/pallas_call | solution.py:249
  210.9 11.5 %feed_forward.5 = (f32[256,1536]{1,0:T(8,128)}, f32[256,1]{1,0:T(8,128)}, bf16[256,1536]{1,0:T(8,128)(2,1)}, bf16[256,2048]{1,0:T(8,128)(2,1)}, bf16[256,2048]{1...) custom-call(f32[256,1536]{1,0:T(8,128)} %get-tuple-element.377.refs_0_, ...), custom_call_target="tpu_custom_call" | custom-call | flops 144955146240 | bytes 637102080 | tf_op jit(solution)/shard_map/feed_forward/pallas_call | solution.py:249
  235.3 6.6 project.6
  242.1 15.7 %collective-permute-done.33 = bf16[192,1024]{1,0:T(8,128)(2,1)S(1)} collective-permute-done((bf16[192,1024]{1,0:T(8,128)(2,1)}, bf16[192,1024]{1,0:T(8,128)(2,1)S(1)}, u32[]{:S(2)}, u32[]{:S(2)}) %collective-permute-start.33) | collective-permute-done | bytes 393248 | tf_op jit(solution)/shard_map/ppermute | solution.py:27
  261.1 6.6 project.7
  268.7 6.8 attend.6
  284.3 9.2 %attend.7 = (bf16[256,768]{1,0:T(8,128)(2,1)}, f32[8,256]{1,0:T(8,128)}, bf16[256,1536]{1,0:T(8,128)(2,1)}) custom-call(s32[1]{0:T(128)} %bitcast.3.refs_0_, bf16[256,768]{1,0:T(8,128)(2,1)} %get-tuple-element.407.refs_1_.refs_11_, bf16[256,768]{1,0:T(8,128)(2,1)} %get-tuple-element.393.refs_2_.refs_13_, bf16[256,768]{1,0:T(8,128)(2,1)} %copy-done.80, ...), custom_call_target="tpu_custom_call" | custom-call | flops 82543902720 | bytes 129761280 | tf_op jit(solution)/shard_map/attend/pallas_call | solution.py:249
  298.9 9.4 %collective-permute-done.41.refs_3_ = bf16[192,1024]{1,0:T(8,128)(2,1)S(1)} collective-permute-done((bf16[192,1024]{1,0:T(8,128)(2,1)S(1)}, bf16[192,1024]{1,0:T(8,128)(2,1)S(1)}, u32[]{:S(2)}, u32[]{:S(2)}) %collective-permute-start.41) | collective-permute-done | bytes 393248 | tf_op jit(solution)/shard_map/ppermute | solution.py:27
  318.7 11.5 %feed_forward.6 = (f32[256,1536]{1,0:T(8,128)}, f32[256,1]{1,0:T(8,128)}, bf16[256,1536]{1,0:T(8,128)(2,1)}, bf16[256,2048]{1,0:T(8,128)(2,1)}, bf16[256,2048]{1...) custom-call(f32[256,1536]{1,0:T(8,128)} %get-tuple-element.415.refs_0_.refs_3_, ...), custom_call_target="tpu_custom_call" | custom-call | flops 144955146240 | bytes 637102080 | tf_op jit(solution)/shard_map/feed_forward/pallas_call | solution.py:249
  330.2 8.1 collective-permute-done.45
  343.7 11.5 %feed_forward.7 = (f32[256,1536]{1,0:T(8,128)}, f32[256,1]{1,0:T(8,128)}, bf16[256,1536]{1,0:T(8,128)(2,1)}, bf16[256,2048]{1,0:T(8,128)(2,1)}, bf16[256,2048]{1...) custom-call(f32[256,1536]{1,0:T(8,128)} %get-tuple-element.426.refs_0_.refs_3_, ...), custom_call_target="tpu_custom_call" | custom-call | flops 144955146240 | bytes 637102080 | tf_op jit(solution)/shard_map/feed_forward/pallas_call | solution.py:249
  359.0 13.6 %feed_back.4 = (bf16[256,4096]{1,0:T(8,128)(2,1)}, bf16[256,1536]{1,0:T(8,128)(2,1)}) custom-call(bf16[256,1536]{1,0:T(8,128)(2,1)} %pad_maximum_fusion.6.refs_0_.refs_3_, bf16[256,2048]{1,0:T(8,128)(2,1)} %get-tuple-element.433.refs_1_, bf16[256,2048]{1,0:T(8,128)(2,1)} %get-tuple-element.434.refs_2_, bf16[2,1024,768]{2,1,0:T(8,128)(2,1)} %refs_8_.7, ...), custom_call_target="tpu_custom_call" | custom-call | flops 144955146240 | bytes 652738560 | tf_op jit(solution)/shard_map/feed_back/pallas_call | solution.py:249
  378.8 13.3 %feed_back.5 = (bf16[256,4096]{1,0:T(8,128)(2,1)}, bf16[256,1536]{1,0:T(8,128)(2,1)}) custom-call(bf16[256,1536]{1,0:T(8,128)(2,1)} %pad_maximum_fusion.7.refs_0_.refs_2_, bf16[256,2048]{1,0:T(8,128)(2,1)} %get-tuple-element.421.refs_1_, bf16[256,2048]{1,0:T(8,128)(2,1)} %get-tuple-element.422.refs_2_, bf16[2,1024,768]{2,1,0:T(8,128)(2,1)} %refs_8_.7, ...), custom_call_target="tpu_custom_call" | custom-call | flops 144955146240 | bytes 652738560 | tf_op jit(solution)/shard_map/feed_back/pallas_call | solution.py:249
  393.8 16.9 %ff_weights.2 = (bf16[768,6144]{1,0:T(8,128)(2,1)}, bf16[768,6144]{1,0:T(8,128)(2,1)}) custom-call(bf16[256,1536]{1,0:T(8,128)(2,1)} %get-tuple-element.448.refs_0_, bf16[256,1536]{1,0:T(8,128)(2,1)} %get-tuple-element.449.refs_1_, bf16[256,1536]{1,0:T(8,128)(2,1)} %pad_maximum_fusion.7.refs_0_.refs_2_, bf16[256,1536]{1,0:T(8,128)(2,1)} %pad_maximum_fusion.6.refs_0_.refs_3_, ...), custom_call_target="tpu_custom_call" | custom-call | flops 289910292480 | bytes 754974720 | tf_op jit(solution)/shard_map/ff_weights/pallas_call | solution.py:616
  412.0 14.5 %attend_back.4 = (f32[256,1536]{1,0:T(8,128)}, bf16[256,1536]{1,0:T(8,128)(2,1)}, f32[1,1536]{1,0:T(1,128)}, f32[256,768]{1,0:T(8,128)}, f32[256,768]{1,0:T(8,12...) custom-call(s32[1]{0:T(128)} %bitcast.3.refs_0_, ...), custom_call_target="tpu_custom_call" | custom-call | flops 179180666880 | bytes 224363520 | tf_op jit(solution)/shard_map/attend_back/pallas_call | solution.py:249
  427.1 12.3 %add_convert_fusion = bf16[768,6144]{1,0:T(8,128)(2,1)} fusion(bf16[768,6144]{1,0:T(8,128)(2,1)} %collective-permute-done.52, bf16[768,6144]{1,0:T(8,128)(2,1)} %get-tuple-element.462), kind=kLoop, calls=%fused_computation | loop fusion | flops 18874368 | bytes 28311552 | tf_op jit(solution)/shard_map/convert_element_type | solution.py:81
  439.9 10.9 %attend_back.5 = (f32[256,1536]{1,0:T(8,128)}, bf16[256,1536]{1,0:T(8,128)(2,1)}, f32[1,1536]{1,0:T(1,128)}, f32[256,768]{1,0:T(8,128)}, f32[256,768]{1,0:T(8,128)}, /*index=5*/bf16[256,768]{1,0:T(8,128)(2,1)}) custom-call(s32[1]{0:T(128)} %bitcast.3.refs_0_, f32[256,1536]{1,0:T(8,128)} %convert_element_type.220.refs_1_, ...), custom_call_target="tpu_custom_call" | custom-call | flops 98650030080 | bytes 224363520 | tf_op jit(solution)/shard_map/attend_back/pallas_call | solution.py:249
  450.9 5.9 project_back.4
  465.6 10.1 %in_weights.2 = (bf16[768,2304]{1,0:T(8,128)(2,1)}, bf16[768,2304]{1,0:T(8,128)(2,1)}) custom-call(bf16[256,1536]{1,0:T(8,128)(2,1)} %get-tuple-element.476.refs_0_, bf16[256,1536]{1,0:T(8,128)(2,1)} %get-tuple-element.477.refs_1_, bf16[256,1536]{1,0:T(8,128)(2,1)} %get-tuple-element.466.refs_2_, bf16[256,1536]{1,0:T(8,128)(2,1)} %get-tuple-element.454.refs_3_, ...), custom_call_target="tpu_custom_call" | custom-call | flops 108716359680 | bytes 306708480 | tf_op jit(solution)/shard_map/in_weights/pallas_call | solution.py:656
  477.6 15.1 %feed_back.6 = (f32[256,1536]{1,0:T(8,128)}, bf16[256,1536]{1,0:T(8,128)(2,1)}, f32[1,1536]{1,0:T(1,128)}, bf16[256,4096]{1,0:T(8,128)(2,1)}, bf16[256,1536]{1,0:T(8,128)(2,1)}) custom-call(f32[256,1536]{1,0:T(8,128)} %get-tuple-element.480.refs_0_, bf16[256,1536]{1,0:T(8,128)(2,1)} %get-tuple-element.472.refs_1_, ...), custom_call_target="tpu_custom_call" | custom-call | flops 144955146240 | bytes 723624960 | tf_op jit(solution)/shard_map/feed_back/pallas_call | solution.py:249
  493.9 15.0 %feed_back.7 = (f32[256,1536]{1,0:T(8,128)}, bf16[256,1536]{1,0:T(8,128)(2,1)}, f32[1,1536]{1,0:T(1,128)}, bf16[256,4096]{1,0:T(8,128)(2,1)}, bf16[256,1536]{1,0:T(8,128)(2,1)}) custom-call(f32[256,1536]{1,0:T(8,128)} %get-tuple-element.486.refs_0_, bf16[256,1536]{1,0:T(8,128)(2,1)} %get-tuple-element.475.refs_1_, ...), custom_call_target="tpu_custom_call" | custom-call | flops 144955146240 | bytes 723624960 | tf_op jit(solution)/shard_map/feed_back/pallas_call | solution.py:249
  509.9 17.1 %ff_weights.3 = (bf16[768,6144]{1,0:T(8,128)(2,1)}, bf16[768,6144]{1,0:T(8,128)(2,1)}) custom-call(bf16[256,1536]{1,0:T(8,128)(2,1)} %get-tuple-element.492.refs_0_, bf16[256,1536]{1,0:T(8,128)(2,1)} %get-tuple-element.493.refs_1_, bf16[256,1536]{1,0:T(8,128)(2,1)} %get-tuple-element.488.refs_2_, bf16[256,1536]{1,0:T(8,128)(2,1)} %get-tuple-element.482.refs_3_, ...), custom_call_target="tpu_custom_call" | custom-call | flops 289910292480 | bytes 754974720 | tf_op jit(solution)/shard_map/ff_weights/pallas_call | solution.py:616
  541.5 14.5 %attend_back.6 = (f32[256,1536]{1,0:T(8,128)}, bf16[256,1536]{1,0:T(8,128)(2,1)}, f32[1,1536]{1,0:T(1,128)}, f32[256,768]{1,0:T(8,128)}, f32[256,768]{1,0:T(8,12...) custom-call(s32[1]{0:T(128)} %bitcast.3.refs_0_, f32[256,1536]{1,0:T(8,128)} %get-tuple-element.499.refs_1_, ...), custom_call_target="tpu_custom_call" | custom-call | flops 179180666880 | bytes 224363520 | tf_op jit(solution)/shard_map/attend_back/pallas_call | solution.py:249
  559.0 13.1 %role_sums.2 = (bf16[384,3072]{1,0:T(8,128)(2,1)}, bf16[384,3072]{1,0:T(8,128)(2,1)}, bf16[384,3072]{1,0:T(8,128)(2,1)}, bf16[384,3072]{1,0:T(8,128)(2,1)}) custom-call(s32[8]{0:T(128)} %broadcast_xor_fusion.row_ref, s32[8]{0:T(128)} %constant.62.clone.side_ref, bf16[768,6144]{1,0:T(8,128)(2,1)} %get-tuple-element.509.left_ref, ...), custom_call_target="tpu_custom_call" | custom-call | bytes 424673280 | tf_op jit(solution)/shard_map/role_sums/pallas_call | solution.py:691
  574.2 11.3 %attend_back.7 = (f32[256,1536]{1,0:T(8,128)}, bf16[256,1536]{1,0:T(8,128)(2,1)}, f32[1,1536]{1,0:T(1,128)}, f32[256,768]{1,0:T(8,128)}, f32[256,768]{1,0:T(8,128)}, /*index=5*/bf16[256,768]{1,0:T(8,128)(2,1)}) custom-call(s32[1]{0:T(128)} %bitcast.3.refs_0_, f32[256,1536]{1,0:T(8,128)} %get-tuple-element.514.refs_1_, ...), custom_call_target="tpu_custom_call" | custom-call | flops 98650030080 | bytes 224363520 | tf_op jit(solution)/shard_map/attend_back/pallas_call | solution.py:249
  603.7 9.7 %in_weights.3 = (bf16[768,2304]{1,0:T(8,128)(2,1)}, bf16[768,2304]{1,0:T(8,128)(2,1)}) custom-call(bf16[256,1536]{1,0:T(8,128)(2,1)} %get-tuple-element.529.refs_0_, bf16[256,1536]{1,0:T(8,128)(2,1)} %get-tuple-element.530.refs_1_, bf16[256,1536]{1,0:T(8,128)(2,1)} %get-tuple-element.518.refs_2_, bf16[256,1536]{1,0:T(8,128)(2,1)} %get-tuple-element.501.refs_3_, ...), custom_call_target="tpu_custom_call" | custom-call | flops 108716359680 | bytes 306708480 | tf_op jit(solution)/shard_map/in_weights/pallas_call | solution.py:656
  619.5 8.4 collective-permute-done.66
  654.3 8.2 role_sums.3
  668.8 7.5 collective-permute-done.68
  684.8 12.2 %collective-permute-done.79 = bf16[192,3072]{1,0:T(8,128)(2,1)} collective-permute-done((bf16[192,3072]{1,0:T(8,128)(2,1)}, bf16[192,3072]{1,0:T(8,128)(2,1)}, u32[]{:S(2)}, u32[]{:S(2)}) %collective-permute-start.79) | collective-permute-done | bytes 1179680 | tf_op jit(solution)/shard_map/ppermute | solution.py:27
  701.3 31.4 %collective-permute-done.77 = bf16[384,1152]{1,0:T(8,128)(2,1)S(1)} collective-permute-done((bf16[384,1152]{1,0:T(8,128)(2,1)}, bf16[384,1152]{1,0:T(8,128)(2,1)S(1)}, u32[]{:S(2)}, u32[]{:S(2)}) %collective-permute-start.77) | collective-permute-done | bytes 884768 | tf_op jit(solution)/shard_map/ppermute | solution.py:27
  740.2 16.6 %collective-permute-start.76 = (bf16[1024,768]{1,0:T(8,128)(2,1)}, bf16[1024,768]{1,0:T(8,128)(2,1)}, u32[]{:S(2)}, u32[]{:S(2)}) collective-permute-start(bf16[1024,768]{1,0:T(8,128)(2,1)} %pad_maximum_fusion.2), channel_id=1, source_target_pairs={{0,4},{4,0},{1,5},{5,1},{2,6},{6,2},{3,7},{7,3},{8,12},{12,8},{9,1... | collective-permute-start | bytes 4718600 | tf_op jit(solution)/shard_map/ppermute | solution.py:27
  762.9 6.5 spread_ff.2
  771.8 14.2 %collective-permute-done.84 = bf16[192,1152]{1,0:T(8,128)(2,1)} collective-permute-done((bf16[192,1152]{1,0:T(8,128)(2,1)}, bf16[192,1152]{1,0:T(8,128)(2,1)}, u32[]{:S(2)}, u32[]{:S(2)}) %collective-permute-start.84) | collective-permute-done | bytes 442400 | tf_op jit(solution)/shard_map/ppermute | solution.py:27
  795.4 15.0 %collective-permute-done.89 = f32[2,2,768]{2,1,0:T(2,128)S(1)} collective-permute-done((f32[2,2,768]{2,1,0:T(2,128)S(1)}, f32[2,2,768]{2,1,0:T(2,128)S(1)}, u32[]{:S(2)}, u32[]{:S(2)}) %collective-permute-start.89) | collective-permute-done | bytes 12320 | tf_op jit(solution)/shard_map/ppermute | solution.py:27
  818.8 7.0 spread_ff.3
  825.8 6.2 collective-permute-done.93.refs_2_
  (477 shorter events, 292.5 us)
Async XLA Ops:
  7.2 160.5 %all-gather.9.cloned.1.call-start = ((), (), s32[]{:S(2)}) async-start(), calls=%async_computation.2 | async-start | bytes 1966080 | tf_op jit(solution)/shard_map/all_gather | solution.py:955
  7.2 28.9 %collective-permute-start.4 = (bf16[2,768,1024]{2,1,0:T(8,128)(2,1)}, bf16[2,768,1024]{2,1,0:T(8,128)(2,1)}, u32[]{:S(2)}, u32[]{:S(2)}) collective-permute-start(bf16[2,768,1024]{2,1,0:T(8,128)(2,1)} %refs_12_.11), channel_id=1, source_target_pairs={{0,4},{4,0},{1,5},{5,1},{2,6},{6,2},{3,7},{7,3},{8,12},{12,8},{9,1... | collective-permute-start | bytes 9437192 | tf_op jit(solution)/shard_map/ppermute | solution.py:27
  7.8 28.4 %collective-permute-start.5 = (bf16[2,768,1024]{2,1,0:T(8,128)(2,1)}, bf16[2,768,1024]{2,1,0:T(8,128)(2,1)}, u32[]{:S(2)}, u32[]{:S(2)}) collective-permute-start(bf16[2,768,1024]{2,1,0:T(8,128)(2,1)} %refs_13_.3), channel_id=1, source_target_pairs={{0,4},{4,0},{1,5},{5,1},{2,6},{6,2},{3,7},{7,3},{8,12},{12,8},{9,1... | collective-permute-start | bytes 9437192 | tf_op jit(solution)/shard_map/ppermute | solution.py:27
  17.5 31.8 %collective-permute-start = (bf16[256,768]{1,0:T(8,128)(2,1)}, bf16[256,768]{1,0:T(8,128)(2,1)S(1)}, u32[]{:S(2)}, u32[]{:S(2)}) collective-permute-start(bf16[256,768]{1,0:T(8,128)(2,1)} %get-tuple-element.312), channel_id=1, source_target_pairs={{0,2},{1,3},{2,0},{3,1},{4,6},{5,7},{6,4},{7,5},{8,10},{9,11},{10,... | collective-permute-start | bytes 1179656 | tf_op jit(solution)/shard_map/ppermute | solution.py:27
  21.2 79.5 %collective-permute-start.13 = (bf16[2,1024,768]{2,1,0:T(8,128)(2,1)}, bf16[2,1024,768]{2,1,0:T(8,128)(2,1)}, u32[]{:S(2)}, u32[]{:S(2)}) collective-permute-start(bf16[2,1024,768]{2,1,0:T(8,128)(2,1)} %refs_8_.7), channel_id=1, source_target_pairs={{0,4},{4,0},{1,5},{5,1},{2,6},{6,2},{3,7},{7,3},{8,12},{12,8},{9,1... | collective-permute-start | bytes 9437192 | tf_op jit(solution)/shard_map/ppermute | solution.py:27
  27.3 31.1 %collective-permute-start.6 = (bf16[288,768]{1,0:T(8,128)(2,1)S(1)}, bf16[288,768]{1,0:T(8,128)(2,1)S(1)}, u32[]{:S(2)}, u32[]{:S(2)}) collective-permute-start(bf16[288,768]{1,0:T(8,128)(2,1)S(1)} %copy-done.40), channel_id=1, source_target_pairs={{0,2},{1,3},{2,0},{3,1},{4,6},{5,7},{6,4},{7,5},{8,10},{9,11},{10,... | collective-permute-start | bytes 1327112 | tf_op jit(solution)/shard_map/ppermute | solution.py:27
  100.3 76.2 %all-gather.11.cloned.1.call-start = ((), (), s32[]{:S(2)}) async-start(), calls=%async_computation.3 | async-start | bytes 1966080 | tf_op jit(solution)/shard_map/all_gather | solution.py:955
  123.6 103.1 %all-gather.21.cloned.1.call-start = ((), (), s32[]{:S(2)}) async-start(), calls=%async_computation.10 | async-start | bytes 2211840 | tf_op jit(solution)/shard_map/all_gather | solution.py:957
  124.2 37.5 %collective-permute-start.16 = (bf16[192,1024]{1,0:T(8,128)(2,1)}, bf16[192,1024]{1,0:T(8,128)(2,1)}, u32[]{:S(2)}, u32[]{:S(2)}) collective-permute-start(bf16[192,1024]{1,0:T(8,128)(2,1)} %get-tuple-element.341), channel_id=1, source_target_pairs={{0,2},{1,3},{2,0},{3,1},{4,6},{5,7},{6,4},{7,5},{8,10},{9,11},{10,... | collective-permute-start | bytes 1179656 | tf_op jit(solution)/shard_map/ppermute | solution.py:27
  161.5 29.4 %collective-permute-start.22 = (bf16[256,1536]{1,0:T(8,128)(2,1)}, bf16[256,1536]{1,0:T(8,128)(2,1)S(1)}, u32[]{:S(2)}, u32[]{:S(2)}) collective-permute-start(bf16[256,1536]{1,0:T(8,128)(2,1)} %get-tuple-element.363.refs_1_), channel_id=1, source_target_pairs={{0,1},{1,0},{2,3},{3,2},{4,5},{5,4},{6,7},{7,6},{8,9},{9,8},{10,11... | collective-permute-start | bytes 2359304 | tf_op jit(solution)/shard_map/ppermute | solution.py:27
  162.5 28.3 %collective-permute-start.23 = (bf16[288,768]{1,0:T(8,128)(2,1)S(1)}, bf16[288,768]{1,0:T(8,128)(2,1)S(1)}, u32[]{:S(2)}, u32[]{:S(2)}) collective-permute-start(bf16[288,768]{1,0:T(8,128)(2,1)S(1)} %copy-done.39), channel_id=1, source_target_pairs={{0,2},{1,3},{2,0},{3,1},{4,6},{5,7},{6,4},{7,5},{8,10},{9,11},{10,... | collective-permute-start | bytes 1327112 | tf_op jit(solution)/shard_map/ppermute | solution.py:27
  194.4 34.9 %collective-permute-start.30 = (bf16[192,1024]{1,0:T(8,128)(2,1)}, bf16[192,1024]{1,0:T(8,128)(2,1)}, u32[]{:S(2)}, u32[]{:S(2)}) collective-permute-start(bf16[192,1024]{1,0:T(8,128)(2,1)} %get-tuple-element.385), channel_id=1, source_target_pairs={{0,2},{1,3},{2,0},{3,1},{4,6},{5,7},{6,4},{7,5},{8,10},{9,11},{10,... | collective-permute-start | bytes 1179656 | tf_op jit(solution)/shard_map/ppermute | solution.py:27
  194.9 98.6 %all-gather.13.cloned.1.call-start = ((), (), s32[]{:S(2)}) async-start(), calls=%async_computation.4 | async-start | bytes 1966080 | tf_op jit(solution)/shard_map/all_gather | solution.py:955
  231.5 28.5 %collective-permute-start.35 = (bf16[256,1536]{1,0:T(8,128)(2,1)S(1)}, bf16[256,1536]{1,0:T(8,128)(2,1)}, u32[]{:S(2)}, u32[]{:S(2)}) collective-permute-start(bf16[256,1536]{1,0:T(8,128)(2,1)S(1)} %copy-done.75), channel_id=1, source_target_pairs={{0,1},{1,0},{2,3},{3,2},{4,5},{5,4},{6,7},{7,6},{8,9},{9,8},{10,11... | collective-permute-start | bytes 2359304 | tf_op jit(solution)/shard_map/ppermute | solution.py:27
  234.4 77.3 %all-gather.15.cloned.1.call-start = ((), (), s32[]{:S(2)}) async-start(), calls=%async_computation.5 | async-start | bytes 1966080 | tf_op jit(solution)/shard_map/all_gather | solution.py:955
  241.9 26.0 %collective-permute-start.36 = (bf16[256,768]{1,0:T(8,128)(2,1)}, bf16[256,768]{1,0:T(8,128)(2,1)S(1)}, u32[]{:S(2)}, u32[]{:S(2)}) collective-permute-start(bf16[256,768]{1,0:T(8,128)(2,1)} %get-tuple-element.393.refs_2_.refs_13_), channel_id=1, source_target_pairs={{0,4},{4,0},{1,5},{5,1},{2,6},{6,2},{3,7},{7,3},{8,12},{12,8},{9,1... | collective-permute-start | bytes 1179656 | tf_op jit(solution)/shard_map/ppermute | solution.py:27
  267.8 265.0 %reduce-scatter.3.cloned.1.call-start = ((), (), s32[]{:S(2)}) async-start(), calls=%async_computation.6 | async-start | bytes 11796480 | tf_op jit(solution)/shard_map/reduce_scatter | solution.py:1024
  281.9 26.4 %collective-permute-start.41 = (bf16[192,1024]{1,0:T(8,128)(2,1)S(1)}, bf16[192,1024]{1,0:T(8,128)(2,1)S(1)}, u32[]{:S(2)}, u32[]{:S(2)}) collective-permute-start(bf16[192,1024]{1,0:T(8,128)(2,1)S(1)} %collective-permute-done.34.refs_0_), channel_id=1, source_target_pairs={{0,24},{8,16},{16,8},{24,0},{1,25},{9,17},{17,9},{25,1},{2,26},{10... | collective-permute-start | bytes 1179656 | tf_op jit(solution)/shard_map/ppermute | solution.py:27
  312.1 31.5 %collective-permute-start.46 = (bf16[256,1536]{1,0:T(8,128)(2,1)}, bf16[256,1536]{1,0:T(8,128)(2,1)}, u32[]{:S(2)}, u32[]{:S(2)}) collective-permute-start(bf16[256,1536]{1,0:T(8,128)(2,1)} %get-tuple-element.410.refs_1_), channel_id=1, source_target_pairs={{0,1},{1,0},{2,3},{3,2},{4,5},{5,4},{6,7},{7,6},{8,9},{9,8},{10,11... | collective-permute-start | bytes 2359304 | tf_op jit(solution)/shard_map/ppermute | solution.py:27
  376.1 35.9 %collective-permute-start.51 = (bf16[256,1536]{1,0:T(8,128)(2,1)}, bf16[256,1536]{1,0:T(8,128)(2,1)}, u32[]{:S(2)}, u32[]{:S(2)}) collective-permute-start(bf16[256,1536]{1,0:T(8,128)(2,1)} %get-tuple-element.441.refs_2_), channel_id=1, source_target_pairs={{0,1},{1,0},{2,3},{3,2},{4,5},{5,4},{6,7},{7,6},{8,9},{9,8},{10,11... | collective-permute-start | bytes 2359304 | tf_op jit(solution)/shard_map/ppermute | solution.py:27
  392.1 47.8 %collective-permute-start.54 = (bf16[256,1536]{1,0:T(8,128)(2,1)}, bf16[256,1536]{1,0:T(8,128)(2,1)}, u32[]{:S(2)}, u32[]{:S(2)}) collective-permute-start(bf16[256,1536]{1,0:T(8,128)(2,1)} %get-tuple-element.447.refs_2_), channel_id=1, source_target_pairs={{0,1},{1,0},{2,3},{3,2},{4,5},{5,4},{6,7},{7,6},{8,9},{9,8},{10,11... | collective-permute-start | bytes 2359304 | tf_op jit(solution)/shard_map/ppermute | solution.py:27
  439.5 162.1 %reduce-scatter.5.cloned.1.call-start = ((), (), s32[]{:S(2)}) async-start(), calls=%async_computation.7 | async-start | bytes 4423680 | tf_op jit(solution)/shard_map/reduce_scatter | solution.py:1024
  463.8 30.1 %collective-permute-start.57 = (bf16[256,1536]{1,0:T(8,128)(2,1)}, bf16[256,1536]{1,0:T(8,128)(2,1)}, u32[]{:S(2)}, u32[]{:S(2)}) collective-permute-start(bf16[256,1536]{1,0:T(8,128)(2,1)} %get-tuple-element.475.refs_1_), channel_id=1, source_target_pairs={{0,1},{1,0},{2,3},{3,2},{4,5},{5,4},{6,7},{7,6},{8,9},{9,8},{10,11... | collective-permute-start | bytes 2359304 | tf_op jit(solution)/shard_map/ppermute | solution.py:27
  492.7 48.8 %collective-permute-start.59 = (bf16[256,1536]{1,0:T(8,128)(2,1)}, bf16[256,1536]{1,0:T(8,128)(2,1)}, u32[]{:S(2)}, u32[]{:S(2)}) collective-permute-start(bf16[256,1536]{1,0:T(8,128)(2,1)} %get-tuple-element.485.refs_2_), channel_id=1, source_target_pairs={{0,1},{1,0},{2,3},{3,2},{4,5},{5,4},{6,7},{7,6},{8,9},{9,8},{10,11... | collective-permute-start | bytes 2359304 | tf_op jit(solution)/shard_map/ppermute | solution.py:27
  508.9 65.3 %collective-permute-start.61 = (bf16[256,1536]{1,0:T(8,128)(2,1)}, bf16[256,1536]{1,0:T(8,128)(2,1)}, u32[]{:S(2)}, u32[]{:S(2)}) collective-permute-start(bf16[256,1536]{1,0:T(8,128)(2,1)} %get-tuple-element.491.refs_2_), channel_id=1, source_target_pairs={{0,1},{1,0},{2,3},{3,2},{4,5},{5,4},{6,7},{7,6},{8,9},{9,8},{10,11... | collective-permute-start | bytes 2359304 | tf_op jit(solution)/shard_map/ppermute | solution.py:27
  509.9 26.3 %collective-permute-start.58 = (bf16[768,2304]{1,0:T(8,128)(2,1)}, bf16[768,2304]{1,0:T(8,128)(2,1)}, u32[]{:S(2)}, u32[]{:S(2)}) collective-permute-start(bf16[768,2304]{1,0:T(8,128)(2,1)} %get-tuple-element.497), channel_id=1, source_target_pairs={{0,4},{4,0},{1,5},{5,1},{2,6},{6,2},{3,7},{7,3},{8,12},{12,8},{9,1... | collective-permute-start | bytes 10616840 | tf_op jit(solution)/shard_map/ppermute | solution.py:27
  541.0 221.9 %all-gather.17.cloned.1.call-start = ((), (), s32[]{:S(2)}) async-start(), calls=%async_computation.8 | async-start | bytes 5898240 | tf_op jit(solution)/shard_map/all_gather | solution.py:1065
  556.0 29.5 %collective-permute-start.63 = (bf16[256,768]{1,0:T(8,128)(2,1)}, bf16[256,768]{1,0:T(8,128)(2,1)S(1)}, u32[]{:S(2)}, u32[]{:S(2)}) collective-permute-start(bf16[256,768]{1,0:T(8,128)(2,1)} %get-tuple-element.507), channel_id=1, source_target_pairs={{0,4},{4,0},{1,5},{5,1},{2,6},{6,2},{3,7},{7,3},{8,12},{12,8},{9,1... | collective-permute-start | bytes 1179656 | tf_op jit(solution)/shard_map/ppermute | solution.py:27
  556.6 56.8 %collective-permute-start.62 = (bf16[192,3072]{1,0:T(8,128)(2,1)}, bf16[192,3072]{1,0:T(8,128)(2,1)}, u32[]{:S(2)}, u32[]{:S(2)}) collective-permute-start(bf16[192,3072]{1,0:T(8,128)(2,1)} %get-tuple-element.516), channel_id=1, source_target_pairs={{0,2},{1,3},{2,0},{3,1},{4,6},{5,7},{6,4},{7,5},{8,10},{9,11},{10,... | collective-permute-start | bytes 3538952 | tf_op jit(solution)/shard_map/ppermute | solution.py:27
  572.1 63.3 %collective-permute-start.71 = (bf16[384,3072]{1,0:T(8,128)(2,1)}, bf16[384,3072]{1,0:T(8,128)(2,1)}, u32[]{:S(2)}, u32[]{:S(2)}) collective-permute-start(bf16[384,3072]{1,0:T(8,128)(2,1)} %get-tuple-element.510), channel_id=1, source_target_pairs={{0,8},{8,0},{16,24},{24,16},{1,9},{9,1},{17,25},{25,17},{2,10},{10... | collective-permute-start | bytes 7077896 | tf_op jit(solution)/shard_map/ppermute | solution.py:27
  573.5 62.4 %collective-permute-start.72 = (bf16[384,3072]{1,0:T(8,128)(2,1)}, bf16[384,3072]{1,0:T(8,128)(2,1)}, u32[]{:S(2)}, u32[]{:S(2)}) collective-permute-start(bf16[384,3072]{1,0:T(8,128)(2,1)} %get-tuple-element.511), channel_id=1, source_target_pairs={{0,16},{8,24},{16,0},{24,8},{1,17},{9,25},{17,1},{25,9},{2,18},{10... | collective-permute-start | bytes 7077896 | tf_op jit(solution)/shard_map/ppermute | solution.py:27
  592.1 27.3 %collective-permute-start.65 = (bf16[256,1536]{1,0:T(8,128)(2,1)}, bf16[256,1536]{1,0:T(8,128)(2,1)}, u32[]{:S(2)}, u32[]{:S(2)}) collective-permute-start(bf16[256,1536]{1,0:T(8,128)(2,1)} %get-tuple-element.524), channel_id=1, source_target_pairs={{1,0},{3,2},{4,5},{6,7},{9,8},{11,10},{12,13},{14,15},{17,16},{19,... | collective-permute-start | bytes 2359304 | tf_op jit(solution)/shard_map/ppermute | solution.py:62
  600.0 27.9 %collective-permute-start.66 = (bf16[256,1536]{1,0:T(8,128)(2,1)}, bf16[256,1536]{1,0:T(8,128)(2,1)}, u32[]{:S(2)}, u32[]{:S(2)}) collective-permute-start(bf16[256,1536]{1,0:T(8,128)(2,1)} %get-tuple-element.527), channel_id=1, source_target_pairs={{1,0},{3,2},{4,5},{6,7},{9,8},{11,10},{12,13},{14,15},{17,16},{19,... | collective-permute-start | bytes 2359304 | tf_op jit(solution)/shard_map/ppermute | solution.py:62
  640.1 173.9 %all-gather.19.cloned.1.call-start = ((), (), s32[]{:S(2)}) async-start(), calls=%async_computation.9 | async-start | bytes 2211840 | tf_op jit(solution)/shard_map/all_gather | solution.py:1065
  645.2 31.1 %collective-permute-start.68 = (bf16[256,1536]{1,0:T(8,128)(2,1)}, bf16[256,1536]{1,0:T(8,128)(2,1)}, u32[]{:S(2)}, u32[]{:S(2)}) collective-permute-start(bf16[256,1536]{1,0:T(8,128)(2,1)} %get-tuple-element.558), channel_id=1, source_target_pairs={{1,0},{3,2},{4,5},{6,7},{9,8},{11,10},{12,13},{14,15},{17,16},{19,... | collective-permute-start | bytes 2359304 | tf_op jit(solution)/shard_map/ppermute | solution.py:62
  651.7 45.3 %collective-permute-start.79 = (bf16[192,3072]{1,0:T(8,128)(2,1)}, bf16[192,3072]{1,0:T(8,128)(2,1)}, u32[]{:S(2)}, u32[]{:S(2)}) collective-permute-start(bf16[192,3072]{1,0:T(8,128)(2,1)} %get-tuple-element.642), channel_id=1, source_target_pairs={{0,8},{8,0},{16,24},{24,16},{1,9},{9,1},{17,25},{25,17},{2,10},{10... | collective-permute-start | bytes 3538952 | tf_op jit(solution)/shard_map/ppermute | solution.py:27
  664.5 32.5 %collective-permute-start.80 = (bf16[192,3072]{1,0:T(8,128)(2,1)S(1)}, bf16[192,3072]{1,0:T(8,128)(2,1)}, u32[]{:S(2)}, u32[]{:S(2)}) collective-permute-start(bf16[192,3072]{1,0:T(8,128)(2,1)S(1)} %get-tuple-element.643), channel_id=1, source_target_pairs={{0,16},{8,24},{16,0},{24,8},{1,17},{9,25},{17,1},{25,9},{2,18},{10... | collective-permute-start | bytes 3538952 | tf_op jit(solution)/shard_map/ppermute | solution.py:27
  665.9 66.8 %collective-permute-start.77 = (bf16[384,1152]{1,0:T(8,128)(2,1)}, bf16[384,1152]{1,0:T(8,128)(2,1)S(1)}, u32[]{:S(2)}, u32[]{:S(2)}) collective-permute-start(bf16[384,1152]{1,0:T(8,128)(2,1)} %get-tuple-element.547), channel_id=1, source_target_pairs={{0,8},{8,0},{16,24},{24,16},{1,9},{9,1},{17,25},{25,17},{2,10},{10... | collective-permute-start | bytes 2654216 | tf_op jit(solution)/shard_map/ppermute | solution.py:27
  668.1 64.6 %collective-permute-start.78 = (bf16[384,1152]{1,0:T(8,128)(2,1)}, bf16[384,1152]{1,0:T(8,128)(2,1)S(1)}, u32[]{:S(2)}, u32[]{:S(2)}) collective-permute-start(bf16[384,1152]{1,0:T(8,128)(2,1)} %get-tuple-element.548), channel_id=1, source_target_pairs={{0,16},{8,24},{16,0},{24,8},{1,17},{9,25},{17,1},{25,9},{2,18},{10... | collective-permute-start | bytes 2654216 | tf_op jit(solution)/shard_map/ppermute | solution.py:27
  698.8 37.3 %collective-permute-start.82 = (bf16[192,3072]{1,0:T(8,128)(2,1)S(1)}, bf16[192,3072]{1,0:T(8,128)(2,1)S(1)}, u32[]{:S(2)}, u32[]{:S(2)}) collective-permute-start(bf16[192,3072]{1,0:T(8,128)(2,1)S(1)} %add_convert_fusion.4), channel_id=1, source_target_pairs={{0,2},{1,3},{2,0},{3,1},{4,6},{5,7},{6,4},{7,5},{8,10},{9,11},{10,... | collective-permute-start | bytes 3538952 | tf_op jit(solution)/shard_map/ppermute | solution.py:27
  734.4 26.6 %collective-permute-start.83 = (bf16[192,1152]{1,0:T(8,128)(2,1)}, bf16[192,1152]{1,0:T(8,128)(2,1)}, u32[]{:S(2)}, u32[]{:S(2)}) collective-permute-start(bf16[192,1152]{1,0:T(8,128)(2,1)} %get-tuple-element.655), channel_id=1, source_target_pairs={{0,16},{8,24},{16,0},{24,8},{1,17},{9,25},{17,1},{25,9},{2,18},{10... | collective-permute-start | bytes 1327112 | tf_op jit(solution)/shard_map/ppermute | solution.py:27
  738.1 31.4 %collective-permute-start.85 = (bf16[96,3072]{1,0:T(8,128)(2,1)S(1)}, bf16[96,3072]{1,0:T(8,128)(2,1)S(1)}, u32[]{:S(2)}, u32[]{:S(2)}) collective-permute-start(bf16[96,3072]{1,0:T(8,128)(2,1)S(1)} %get-tuple-element.651.refs_0_.refs_8_.refs_16_), channel_id=1, source_target_pairs={{0,8},{8,0},{16,24},{24,16},{1,9},{9,1},{17,25},{25,17},{2,10},{10... | collective-permute-start | bytes 1769480 | tf_op jit(solution)/shard_map/ppermute | solution.py:27
  739.6 29.9 %collective-permute-start.86 = (bf16[96,3072]{1,0:T(8,128)(2,1)S(1)}, bf16[96,3072]{1,0:T(8,128)(2,1)S(1)}, u32[]{:S(2)}, u32[]{:S(2)}) collective-permute-start(bf16[96,3072]{1,0:T(8,128)(2,1)S(1)} %get-tuple-element.650.refs_1_.refs_9_.refs_17_), channel_id=1, source_target_pairs={{0,16},{8,24},{16,0},{24,8},{1,17},{9,25},{17,1},{25,9},{2,18},{10... | collective-permute-start | bytes 1769480 | tf_op jit(solution)/shard_map/ppermute | solution.py:27
  740.2 47.2 %collective-permute-start.76 = (bf16[1024,768]{1,0:T(8,128)(2,1)}, bf16[1024,768]{1,0:T(8,128)(2,1)}, u32[]{:S(2)}, u32[]{:S(2)}) collective-permute-start(bf16[1024,768]{1,0:T(8,128)(2,1)} %pad_maximum_fusion.2), channel_id=1, source_target_pairs={{0,4},{4,0},{1,5},{5,1},{2,6},{6,2},{3,7},{7,3},{8,12},{12,8},{9,1... | collective-permute-start | bytes 4718600 | tf_op jit(solution)/shard_map/ppermute | solution.py:27
  769.6 41.1 %collective-permute-start.91 = (bf16[192,3072]{1,0:T(8,128)(2,1)S(1)}, bf16[192,3072]{1,0:T(8,128)(2,1)S(1)}, u32[]{:S(2)}, u32[]{:S(2)}) collective-permute-start(bf16[192,3072]{1,0:T(8,128)(2,1)S(1)} %pad_maximum_fusion.4), channel_id=1, source_target_pairs={{0,16},{8,24},{16,0},{24,8},{1,17},{9,25},{17,1},{25,9},{2,18},{10... | collective-permute-start | bytes 3538952 | tf_op jit(solution)/shard_map/ppermute | solution.py:27
  771.5 46.3 %collective-permute-start.90 = (bf16[192,3072]{1,0:T(8,128)(2,1)}, bf16[192,3072]{1,0:T(8,128)(2,1)S(1)}, u32[]{:S(2)}, u32[]{:S(2)}) collective-permute-start(bf16[192,3072]{1,0:T(8,128)(2,1)} %pad_maximum_fusion.3), channel_id=1, source_target_pairs={{0,8},{8,0},{16,24},{24,16},{1,9},{9,1},{17,25},{25,17},{2,10},{10... | collective-permute-start | bytes 3538952 | tf_op jit(solution)/shard_map/ppermute | solution.py:27
  794.5 46.0 %collective-permute-start.88 = (bf16[512,768]{1,0:T(8,128)(2,1)}, bf16[512,768]{1,0:T(8,128)(2,1)}, u32[]{:S(2)}, u32[]{:S(2)}) collective-permute-start(bf16[512,768]{1,0:T(8,128)(2,1)} %pad_maximum_fusion.8), channel_id=1, source_target_pairs={{0,2},{1,3},{2,0},{3,1},{4,6},{5,7},{6,4},{7,5},{8,10},{9,11},{10,... | collective-permute-start | bytes 2359304 | tf_op jit(solution)/shard_map/ppermute | solution.py:27
  795.2 30.5 %collective-permute-start.92 = (bf16[192,1152]{1,0:T(8,128)(2,1)S(1)}, bf16[192,1152]{1,0:T(8,128)(2,1)S(1)}, u32[]{:S(2)}, u32[]{:S(2)}) collective-permute-start(bf16[192,1152]{1,0:T(8,128)(2,1)S(1)} %add_convert_fusion.9.refs_0_), channel_id=1, source_target_pairs={{0,8},{8,0},{16,24},{24,16},{1,9},{9,1},{17,25},{25,17},{2,10},{10... | collective-permute-start | bytes 1327112 | tf_op jit(solution)/shard_map/ppermute | solution.py:27
  (145 other events, 1515.1 us)
Sparse Core Ops, SparseCore 0:
  100.4 30.4 all-gather.8
  133.4 30.9 all-gather.10
  195.1 31.5 all-gather.20
  234.5 29.0 all-gather.12
  268.0 41.1 all-gather.14
  439.6 93.2 reduce-scatter.2
  541.1 56.7 reduce-scatter.4
  640.2 91.0 all-gather.16
  759.5 47.1 all-gather.18

commit v4 on v3

--- a/solution.py
+++ b/solution.py
@@ -1347,7 +1347,7 @@
             third.spread(order, range(1, lax.axis_size("dp")))
             cotangent.fetch_on(order)
             kept[1] = middle(l, 1, kept[1])
-            order.join(pairs[0])
+            order.join(pairs[0], cotangent.far)
             first.cross(order, True)
             third.collect(order)
             second.cross(order)
@@ -1482,7 +1482,6 @@
     if len(low_bits()) == 1:
         gain_a[0] = jnp.where(lo == core, gain_a[0], 0.0)
         gain_a[0] = gain_a[0] + hop(gain_a[0], "cols", 1)
-    tops = [last_pair(part) for part in order.after(pairs)]
     gain_grads = [jnp.concatenate([gain_a[l], gain_b[l]], axis=0) for l in range(LAYERS)]
     grad_gains = order.after(jnp.stack(gain_grads))
     width = grad_gains.shape[-1] // 2
@@ -1495,6 +1494,11 @@
     sums["in", 0].start(order)
     sums["in", 1].fourth(order)
     grad_gains = order.mark(grad_gains + order.after(gains_came))
+    sums["ff", 0].third(order)
+    sums["ff", 0].across(order)
+    tops = [last_pair(part) for part in order.after(pairs)]
+    sums["in", 1].gather(order)
+    sums["in", 0].second(order)
     order.join(tops)
     hidden = [
         h + left.astype(FULL) + right.astype(FULL)
@@ -1502,11 +1506,7 @@
     ]
     results = Departure((hidden, [g for g, _ in ends]), hi, lo, core, block_rows)
     results.cross(order)
-    sums["ff", 0].third(order)
-    sums["ff", 0].across(order)
     gains_came = hop(order.after(grad_gains), "dp", 1)
-    sums["in", 1].gather(order)
-    sums["in", 0].second(order)
     sums["ff", 0].fourth(order)
     sums["ff", 0].near(order)
     sums["in", 0].third(order)

time: 863 us -> 843 us (0.977)
  starting transfers between devices: 103 us -> 82.8 us
    ppermute x91, starting transfers between devices: 95.1 us -> 75.1 us  [hop(): return lax.ppermute(value, axis, [(i, i ^ distance) for i in range(size)])]
    ppermute x91, waiting for transfers between devices: 219 us -> 229 us  [hop(): return lax.ppermute(value, axis, [(i, i ^ distance) for i in range(size)])]
    unnamed x182 -> x190, local copies, waits for them, and re-layouts: 27.4 us -> 26.9 us
  transfers between devices with their start and end apart: 104 -> 104, of which waited for: 38 -> 43; matrix products, arithmetic and copies ran while one was open for 11% -> 11% of each run, Pallas kernels for 43% -> 44%
where the time goes in v4:
time: 843 us; the launch traced here: 834 us
  Pallas kernels  366 us (43%)
  waiting for transfers between devices  252 us (30%)
  starting transfers between devices  82.8 us (10%)
  other arithmetic  71.6 us (8%)
  local copies, waits for them, and re-layouts  45.5 us (5%)
  between operations  15.7 us (2%)
    pallas_call x24, Pallas kernels, call(): pl.pallas_call(kernel, grid_spec=pltpu.PrefetchScalarGridSpec(num_scalar_...  245 us
    ppermute x91, waiting for transfers between devices, hop(): return lax.ppermute(value, axis, [(i, i ^ distance) for i in range(size)])  229 us
    ppermute x91, starting transfers between devices, hop(): return lax.ppermute(value, axis, [(i, i ^ distance) for i in range(size)])  75.1 us
    pallas_call x2, Pallas kernels, ff_weights(): pl.pallas_call(functools.partial(ff_weights_kernel, chunks, split), grid=...  33.9 us
    convert_element_type x6, other arithmetic, add_low(): return (left.astype(FULL) + right.astype(FULL)).astype(LOW)  27.8 us
    unnamed x190, local copies, waits for them, and re-layouts  26.9 us
    pallas_call x2, Pallas kernels, role_sums(): pl.pallas_call(role_sum_kernel, grid_spec=pltpu.PrefetchScalarGridSpec(nu...  21.3 us
    pallas_call x2, Pallas kernels, in_weights(): pl.pallas_call(functools.partial(in_weights_kernel, chunks), grid=(1,), i...  19.6 us
  transfers between devices with their start and end apart: 104, of which 43 were waited for; matrix products, arithmetic and copies ran while one was open for 11% of the time, Pallas kernels for 44%

profile of v4, /device:TPU:0, one launch (start us, length us, event | category | flops | bytes accessed | tf_op | source)
XLA Modules:
  0.0 833.6 jit_solution(1290838000224035018)
XLA Ops:
  39.8 9.5 %collective-permute-done = bf16[256,768]{1,0:T(8,128)(2,1)S(1)} collective-permute-done((bf16[256,768]{1,0:T(8,128)(2,1)}, bf16[256,768]{1,0:T(8,128)(2,1)S(1)}, u32[]{:S(2)}, u32[]{:S(2)}) %collective-permute-start) | collective-permute-done | bytes 393248 | tf_op jit(solution)/shard_map/ppermute | solution.py:27
  49.3 9.1 %collective-permute-done.6.refs_0_ = bf16[288,768]{1,0:T(8,128)(2,1)S(1)} collective-permute-done((bf16[288,768]{1,0:T(8,128)(2,1)S(1)}, bf16[288,768]{1,0:T(8,128)(2,1)S(1)}, u32[]{:S(2)}, u32[]{:S(2)}) %collective-permute-start.6) | collective-permute-done | bytes 442400 | tf_op jit(solution)/shard_map/ppermute | solution.py:27
  62.2 8.1 collective-permute-done.8.refs_1_
  74.6 17.0 %collective-permute-done.11 = bf16[192,1024]{1,0:T(8,128)(2,1)S(1)} collective-permute-done((bf16[192,1024]{1,0:T(8,128)(2,1)}, bf16[192,1024]{1,0:T(8,128)(2,1)S(1)}, u32[]{:S(2)}, u32[]{:S(2)}) %collective-permute-start.11) | collective-permute-done | bytes 393248 | tf_op jit(solution)/shard_map/ppermute | solution.py:27
  102.5 12.6 %collective-permute-done.14 = bf16[192,1024]{1,0:T(8,128)(2,1)S(1)} collective-permute-done((bf16[192,1024]{1,0:T(8,128)(2,1)}, bf16[192,1024]{1,0:T(8,128)(2,1)S(1)}, u32[]{:S(2)}, u32[]{:S(2)}) %collective-permute-start.14) | collective-permute-done | bytes 393248 | tf_op jit(solution)/shard_map/ppermute | solution.py:27
  115.1 6.0 project.4
  125.1 5.9 project.5
  131.9 6.8 attend.4
  142.7 18.7 %attend.5 = (bf16[256,768]{1,0:T(8,128)(2,1)}, f32[8,256]{1,0:T(8,128)}, bf16[256,1536]{1,0:T(8,128)(2,1)}) custom-call(s32[1]{0:T(128)} %bitcast.3.refs_0_, bf16[256,768]{1,0:T(8,128)(2,1)} %get-tuple-element.360.refs_1_.refs_11_, bf16[256,768]{1,0:T(8,128)(2,1)} %get-tuple-element.346.refs_2_.refs_13_, bf16[256,768]{1,0:T(8,128)(2,1)} %copy-done.81, ...), custom_call_target="tpu_custom_call" | custom-call | flops 82543902720 | bytes 129761280 | tf_op jit(solution)/shard_map/attend/pallas_call | solution.py:249
  167.7 8.7 %collective-permute-done.24.refs_1_ = bf16[192,1024]{1,0:T(8,128)(2,1)S(1)} collective-permute-done((bf16[192,1024]{1,0:T(8,128)(2,1)}, bf16[192,1024]{1,0:T(8,128)(2,1)S(1)}, u32[]{:S(2)}, u32[]{:S(2)}) %collective-permute-start.24) | collective-permute-done | bytes 393248 | tf_op jit(solution)/shard_map/ppermute | solution.py:27
  176.4 8.2 collective-permute-done.25.refs_2_
  184.6 6.2 collective-permute-done.22.refs_2_
  199.1 11.7 %feed_forward.4 = (f32[256,1536]{1,0:T(8,128)}, f32[256,1]{1,0:T(8,128)}, bf16[256,1536]{1,0:T(8,128)(2,1)}, bf16[256,2048]{1,0:T(8,128)(2,1)}, bf16[256,2048]{1...) custom-call(f32[256,1536]{1,0:T(8,128)} %get-tuple-element.369.refs_0_, ...), custom_call_target="tpu_custom_call" | custom-call | flops 144955146240 | bytes 637102080 | tf_op jit(solution)/shard_map/feed_forward/pallas_call | solution.py:249
  210.9 11.5 %feed_forward.5 = (f32[256,1536]{1,0:T(8,128)}, f32[256,1]{1,0:T(8,128)}, bf16[256,1536]{1,0:T(8,128)(2,1)}, bf16[256,2048]{1,0:T(8,128)(2,1)}, bf16[256,2048]{1...) custom-call(f32[256,1536]{1,0:T(8,128)} %get-tuple-element.377.refs_0_, ...), custom_call_target="tpu_custom_call" | custom-call | flops 144955146240 | bytes 637102080 | tf_op jit(solution)/shard_map/feed_forward/pallas_call | solution.py:249
  235.2 6.6 project.6
  242.1 15.6 %collective-permute-done.33 = bf16[192,1024]{1,0:T(8,128)(2,1)S(1)} collective-permute-done((bf16[192,1024]{1,0:T(8,128)(2,1)}, bf16[192,1024]{1,0:T(8,128)(2,1)S(1)}, u32[]{:S(2)}, u32[]{:S(2)}) %collective-permute-start.33) | collective-permute-done | bytes 393248 | tf_op jit(solution)/shard_map/ppermute | solution.py:27
  261.0 6.6 project.7
  268.6 6.9 attend.6
  283.5 9.2 %attend.7 = (bf16[256,768]{1,0:T(8,128)(2,1)}, f32[8,256]{1,0:T(8,128)}, bf16[256,1536]{1,0:T(8,128)(2,1)}) custom-call(s32[1]{0:T(128)} %bitcast.3.refs_0_, bf16[256,768]{1,0:T(8,128)(2,1)} %get-tuple-element.407.refs_1_.refs_11_, bf16[256,768]{1,0:T(8,128)(2,1)} %get-tuple-element.393.refs_2_.refs_13_, bf16[256,768]{1,0:T(8,128)(2,1)} %copy-done.85, ...), custom_call_target="tpu_custom_call" | custom-call | flops 82543902720 | bytes 129761280 | tf_op jit(solution)/shard_map/attend/pallas_call | solution.py:249
  292.8 10.5 %collective-permute-done.39 = bf16[256,768]{1,0:T(8,128)(2,1)S(1)} collective-permute-done((bf16[256,768]{1,0:T(8,128)(2,1)S(1)}, bf16[256,768]{1,0:T(8,128)(2,1)S(1)}, u32[]{:S(2)}, u32[]{:S(2)}) %collective-permute-start.39) | collective-permute-done | bytes 393248 | tf_op jit(solution)/shard_map/ppermute | solution.py:27
  318.6 11.6 %feed_forward.6 = (f32[256,1536]{1,0:T(8,128)}, f32[256,1]{1,0:T(8,128)}, bf16[256,1536]{1,0:T(8,128)(2,1)}, bf16[256,2048]{1,0:T(8,128)(2,1)}, bf16[256,2048]{1...) custom-call(f32[256,1536]{1,0:T(8,128)} %get-tuple-element.416.refs_0_.refs_3_, ...), custom_call_target="tpu_custom_call" | custom-call | flops 144955146240 | bytes 637102080 | tf_op jit(solution)/shard_map/feed_forward/pallas_call | solution.py:249
  331.9 11.5 %feed_forward.7 = (f32[256,1536]{1,0:T(8,128)}, f32[256,1]{1,0:T(8,128)}, bf16[256,1536]{1,0:T(8,128)(2,1)}, bf16[256,2048]{1,0:T(8,128)(2,1)}, bf16[256,2048]{1...) custom-call(f32[256,1536]{1,0:T(8,128)} %get-tuple-element.426.refs_0_.refs_3_, ...), custom_call_target="tpu_custom_call" | custom-call | flops 144955146240 | bytes 637102080 | tf_op jit(solution)/shard_map/feed_forward/pallas_call | solution.py:249
  347.3 13.6 %feed_back.4 = (bf16[256,4096]{1,0:T(8,128)(2,1)}, bf16[256,1536]{1,0:T(8,128)(2,1)}) custom-call(bf16[256,1536]{1,0:T(8,128)(2,1)} %pad_maximum_fusion.6.refs_0_.refs_3_, bf16[256,2048]{1,0:T(8,128)(2,1)} %get-tuple-element.433.refs_1_, bf16[256,2048]{1,0:T(8,128)(2,1)} %get-tuple-element.434.refs_2_, bf16[2,1024,768]{2,1,0:T(8,128)(2,1)} %refs_8_.7, ...), custom_call_target="tpu_custom_call" | custom-call | flops 144955146240 | bytes 652738560 | tf_op jit(solution)/shard_map/feed_back/pallas_call | solution.py:249
  367.9 13.2 %feed_back.5 = (bf16[256,4096]{1,0:T(8,128)(2,1)}, bf16[256,1536]{1,0:T(8,128)(2,1)}) custom-call(bf16[256,1536]{1,0:T(8,128)(2,1)} %pad_maximum_fusion.7.refs_0_.refs_2_, bf16[256,2048]{1,0:T(8,128)(2,1)} %get-tuple-element.421.refs_1_, bf16[256,2048]{1,0:T(8,128)(2,1)} %get-tuple-element.422.refs_2_, bf16[2,1024,768]{2,1,0:T(8,128)(2,1)} %refs_8_.7, ...), custom_call_target="tpu_custom_call" | custom-call | flops 144955146240 | bytes 652738560 | tf_op jit(solution)/shard_map/feed_back/pallas_call | solution.py:249
  382.0 16.9 %ff_weights.2 = (bf16[768,6144]{1,0:T(8,128)(2,1)}, bf16[768,6144]{1,0:T(8,128)(2,1)}) custom-call(bf16[256,1536]{1,0:T(8,128)(2,1)} %get-tuple-element.448.refs_0_, bf16[256,1536]{1,0:T(8,128)(2,1)} %get-tuple-element.449.refs_1_, bf16[256,1536]{1,0:T(8,128)(2,1)} %pad_maximum_fusion.7.refs_0_.refs_2_, bf16[256,1536]{1,0:T(8,128)(2,1)} %pad_maximum_fusion.6.refs_0_.refs_3_, ...), custom_call_target="tpu_custom_call" | custom-call | flops 289910292480 | bytes 754974720 | tf_op jit(solution)/shard_map/ff_weights/pallas_call | solution.py:616
  400.2 14.5 %attend_back.4 = (f32[256,1536]{1,0:T(8,128)}, bf16[256,1536]{1,0:T(8,128)(2,1)}, f32[1,1536]{1,0:T(1,128)}, f32[256,768]{1,0:T(8,128)}, f32[256,768]{1,0:T(8,12...) custom-call(s32[1]{0:T(128)} %bitcast.3.refs_0_, ...), custom_call_target="tpu_custom_call" | custom-call | flops 179180666880 | bytes 224363520 | tf_op jit(solution)/shard_map/attend_back/pallas_call | solution.py:249
  415.3 12.3 %add_convert_fusion = bf16[768,6144]{1,0:T(8,128)(2,1)} fusion(bf16[768,6144]{1,0:T(8,128)(2,1)} %collective-permute-done.52, bf16[768,6144]{1,0:T(8,128)(2,1)} %get-tuple-element.462), kind=kLoop, calls=%fused_computation | loop fusion | flops 18874368 | bytes 28311552 | tf_op jit(solution)/shard_map/convert_element_type | solution.py:81
  428.2 10.9 %attend_back.5 = (f32[256,1536]{1,0:T(8,128)}, bf16[256,1536]{1,0:T(8,128)(2,1)}, f32[1,1536]{1,0:T(1,128)}, f32[256,768]{1,0:T(8,128)}, f32[256,768]{1,0:T(8,128)}, /*index=5*/bf16[256,768]{1,0:T(8,128)(2,1)}) custom-call(s32[1]{0:T(128)} %bitcast.3.refs_0_, f32[256,1536]{1,0:T(8,128)} %convert_element_type.220.refs_1_, ...), custom_call_target="tpu_custom_call" | custom-call | flops 98650030080 | bytes 224363520 | tf_op jit(solution)/shard_map/attend_back/pallas_call | solution.py:249
  439.1 6.1 project_back.4
  454.0 10.0 %in_weights.2 = (bf16[768,2304]{1,0:T(8,128)(2,1)}, bf16[768,2304]{1,0:T(8,128)(2,1)}) custom-call(bf16[256,1536]{1,0:T(8,128)(2,1)} %get-tuple-element.476.refs_0_, bf16[256,1536]{1,0:T(8,128)(2,1)} %get-tuple-element.477.refs_1_, bf16[256,1536]{1,0:T(8,128)(2,1)} %get-tuple-element.466.refs_2_, bf16[256,1536]{1,0:T(8,128)(2,1)} %get-tuple-element.454.refs_3_, ...), custom_call_target="tpu_custom_call" | custom-call | flops 108716359680 | bytes 306708480 | tf_op jit(solution)/shard_map/in_weights/pallas_call | solution.py:656
  466.0 15.2 %feed_back.6 = (f32[256,1536]{1,0:T(8,128)}, bf16[256,1536]{1,0:T(8,128)(2,1)}, f32[1,1536]{1,0:T(1,128)}, bf16[256,4096]{1,0:T(8,128)(2,1)}, bf16[256,1536]{1,0:T(8,128)(2,1)}) custom-call(f32[256,1536]{1,0:T(8,128)} %get-tuple-element.480.refs_0_, bf16[256,1536]{1,0:T(8,128)(2,1)} %get-tuple-element.472.refs_1_, ...), custom_call_target="tpu_custom_call" | custom-call | flops 144955146240 | bytes 723624960 | tf_op jit(solution)/shard_map/feed_back/pallas_call | solution.py:249
  482.5 15.0 %feed_back.7 = (f32[256,1536]{1,0:T(8,128)}, bf16[256,1536]{1,0:T(8,128)(2,1)}, f32[1,1536]{1,0:T(1,128)}, bf16[256,4096]{1,0:T(8,128)(2,1)}, bf16[256,1536]{1,0:T(8,128)(2,1)}) custom-call(f32[256,1536]{1,0:T(8,128)} %get-tuple-element.486.refs_0_, bf16[256,1536]{1,0:T(8,128)(2,1)} %get-tuple-element.475.refs_1_, ...), custom_call_target="tpu_custom_call" | custom-call | flops 144955146240 | bytes 723624960 | tf_op jit(solution)/shard_map/feed_back/pallas_call | solution.py:249
  498.6 17.0 %ff_weights.3 = (bf16[768,6144]{1,0:T(8,128)(2,1)}, bf16[768,6144]{1,0:T(8,128)(2,1)}) custom-call(bf16[256,1536]{1,0:T(8,128)(2,1)} %get-tuple-element.492.refs_0_, bf16[256,1536]{1,0:T(8,128)(2,1)} %get-tuple-element.493.refs_1_, bf16[256,1536]{1,0:T(8,128)(2,1)} %get-tuple-element.488.refs_2_, bf16[256,1536]{1,0:T(8,128)(2,1)} %get-tuple-element.482.refs_3_, ...), custom_call_target="tpu_custom_call" | custom-call | flops 289910292480 | bytes 754974720 | tf_op jit(solution)/shard_map/ff_weights/pallas_call | solution.py:616
  515.6 6.2 reduce-scatter.3.cloned.1.call-done
  530.5 14.5 %attend_back.6 = (f32[256,1536]{1,0:T(8,128)}, bf16[256,1536]{1,0:T(8,128)(2,1)}, f32[1,1536]{1,0:T(1,128)}, f32[256,768]{1,0:T(8,128)}, f32[256,768]{1,0:T(8,12...) custom-call(s32[1]{0:T(128)} %bitcast.3.refs_0_, f32[256,1536]{1,0:T(8,128)} %get-tuple-element.499.refs_1_, ...), custom_call_target="tpu_custom_call" | custom-call | flops 179180666880 | bytes 224363520 | tf_op jit(solution)/shard_map/attend_back/pallas_call | solution.py:249
  548.0 13.1 %role_sums.2 = (bf16[384,3072]{1,0:T(8,128)(2,1)}, bf16[384,3072]{1,0:T(8,128)(2,1)}, bf16[384,3072]{1,0:T(8,128)(2,1)}, bf16[384,3072]{1,0:T(8,128)(2,1)}) custom-call(s32[8]{0:T(128)} %broadcast_xor_fusion.row_ref, s32[8]{0:T(128)} %constant.62.clone.side_ref, bf16[768,6144]{1,0:T(8,128)(2,1)} %get-tuple-element.509.left_ref, ...), custom_call_target="tpu_custom_call" | custom-call | bytes 424673280 | tf_op jit(solution)/shard_map/role_sums/pallas_call | solution.py:691
  563.1 11.3 %attend_back.7 = (f32[256,1536]{1,0:T(8,128)}, bf16[256,1536]{1,0:T(8,128)(2,1)}, f32[1,1536]{1,0:T(1,128)}, f32[256,768]{1,0:T(8,128)}, f32[256,768]{1,0:T(8,128)}, /*index=5*/bf16[256,768]{1,0:T(8,128)(2,1)}) custom-call(s32[1]{0:T(128)} %bitcast.3.refs_0_, f32[256,1536]{1,0:T(8,128)} %get-tuple-element.514.refs_1_, ...), custom_call_target="tpu_custom_call" | custom-call | flops 98650030080 | bytes 224363520 | tf_op jit(solution)/shard_map/attend_back/pallas_call | solution.py:249
  575.3 5.8 project_back.6
  592.6 9.7 %in_weights.3 = (bf16[768,2304]{1,0:T(8,128)(2,1)}, bf16[768,2304]{1,0:T(8,128)(2,1)}) custom-call(bf16[256,1536]{1,0:T(8,128)(2,1)} %get-tuple-element.529.refs_0_, bf16[256,1536]{1,0:T(8,128)(2,1)} %get-tuple-element.530.refs_1_, bf16[256,1536]{1,0:T(8,128)(2,1)} %get-tuple-element.518.refs_2_, bf16[256,1536]{1,0:T(8,128)(2,1)} %get-tuple-element.501.refs_3_, ...), custom_call_target="tpu_custom_call" | custom-call | flops 108716359680 | bytes 306708480 | tf_op jit(solution)/shard_map/in_weights/pallas_call | solution.py:656
  608.4 8.4 %collective-permute-done.68 = bf16[256,1536]{1,0:T(8,128)(2,1)} collective-permute-done((bf16[256,1536]{1,0:T(8,128)(2,1)}, bf16[256,1536]{1,0:T(8,128)(2,1)}, u32[]{:S(2)}, u32[]{:S(2)}) %collective-permute-start.68) | collective-permute-done | bytes 786464 | tf_op jit(solution)/shard_map/ppermute | solution.py:62
  640.7 8.1 role_sums.3
  649.9 8.4 %collective-permute-done.73 = bf16[192,1152]{1,0:T(8,128)(2,1)S(1)} collective-permute-done((bf16[192,1152]{1,0:T(8,128)(2,1)}, bf16[192,1152]{1,0:T(8,128)(2,1)S(1)}, u32[]{:S(2)}, u32[]{:S(2)}) %collective-permute-start.73) | collective-permute-done | bytes 442400 | tf_op jit(solution)/shard_map/ppermute | solution.py:27
  660.9 18.3 %collective-permute-done.69 = bf16[192,3072]{1,0:T(8,128)(2,1)} collective-permute-done((bf16[192,3072]{1,0:T(8,128)(2,1)}, bf16[192,3072]{1,0:T(8,128)(2,1)}, u32[]{:S(2)}, u32[]{:S(2)}) %collective-permute-start.69) | collective-permute-done | bytes 1179680 | tf_op jit(solution)/shard_map/ppermute | solution.py:27
  687.0 28.4 %collective-permute-done.78 = bf16[384,1152]{1,0:T(8,128)(2,1)} collective-permute-done((bf16[384,1152]{1,0:T(8,128)(2,1)}, bf16[384,1152]{1,0:T(8,128)(2,1)}, u32[]{:S(2)}, u32[]{:S(2)}) %collective-permute-start.78) | collective-permute-done | bytes 884768 | tf_op jit(solution)/shard_map/ppermute | solution.py:27
  726.6 6.4 collective-permute-done.82
  743.7 6.4 spread_ff.2
  775.3 15.8 %collective-permute-done.89 = f32[2,2,768]{2,1,0:T(2,128)S(1)} collective-permute-done((f32[2,2,768]{2,1,0:T(2,128)S(1)}, f32[2,2,768]{2,1,0:T(2,128)S(1)}, u32[]{:S(2)}, u32[]{:S(2)}) %collective-permute-start.89) | collective-permute-done | bytes 12320 | tf_op jit(solution)/shard_map/ppermute | solution.py:27
  799.9 6.7 spread_ff.3
  (485 shorter events, 287.0 us)
Async XLA Ops:
  7.2 160.5 %all-gather.9.cloned.1.call-start = ((), (), s32[]{:S(2)}) async-start(), calls=%async_computation.2 | async-start | bytes 1966080 | tf_op jit(solution)/shard_map/all_gather | solution.py:955
  7.2 28.8 %collective-permute-start.4 = (bf16[2,768,1024]{2,1,0:T(8,128)(2,1)}, bf16[2,768,1024]{2,1,0:T(8,128)(2,1)}, u32[]{:S(2)}, u32[]{:S(2)}) collective-permute-start(bf16[2,768,1024]{2,1,0:T(8,128)(2,1)} %refs_12_.11), channel_id=1, source_target_pairs={{0,4},{4,0},{1,5},{5,1},{2,6},{6,2},{3,7},{7,3},{8,12},{12,8},{9,1... | collective-permute-start | bytes 9437192 | tf_op jit(solution)/shard_map/ppermute | solution.py:27
  7.8 28.2 %collective-permute-start.5 = (bf16[2,768,1024]{2,1,0:T(8,128)(2,1)}, bf16[2,768,1024]{2,1,0:T(8,128)(2,1)}, u32[]{:S(2)}, u32[]{:S(2)}) collective-permute-start(bf16[2,768,1024]{2,1,0:T(8,128)(2,1)} %refs_13_.3), channel_id=1, source_target_pairs={{0,4},{4,0},{1,5},{5,1},{2,6},{6,2},{3,7},{7,3},{8,12},{12,8},{9,1... | collective-permute-start | bytes 9437192 | tf_op jit(solution)/shard_map/ppermute | solution.py:27
  17.5 31.8 %collective-permute-start = (bf16[256,768]{1,0:T(8,128)(2,1)}, bf16[256,768]{1,0:T(8,128)(2,1)S(1)}, u32[]{:S(2)}, u32[]{:S(2)}) collective-permute-start(bf16[256,768]{1,0:T(8,128)(2,1)} %get-tuple-element.312), channel_id=1, source_target_pairs={{0,2},{1,3},{2,0},{3,1},{4,6},{5,7},{6,4},{7,5},{8,10},{9,11},{10,... | collective-permute-start | bytes 1179656 | tf_op jit(solution)/shard_map/ppermute | solution.py:27
  21.2 79.5 %collective-permute-start.13 = (bf16[2,1024,768]{2,1,0:T(8,128)(2,1)}, bf16[2,1024,768]{2,1,0:T(8,128)(2,1)}, u32[]{:S(2)}, u32[]{:S(2)}) collective-permute-start(bf16[2,1024,768]{2,1,0:T(8,128)(2,1)} %refs_8_.7), channel_id=1, source_target_pairs={{0,4},{4,0},{1,5},{5,1},{2,6},{6,2},{3,7},{7,3},{8,12},{12,8},{9,1... | collective-permute-start | bytes 9437192 | tf_op jit(solution)/shard_map/ppermute | solution.py:27
  27.3 31.1 %collective-permute-start.6 = (bf16[288,768]{1,0:T(8,128)(2,1)S(1)}, bf16[288,768]{1,0:T(8,128)(2,1)S(1)}, u32[]{:S(2)}, u32[]{:S(2)}) collective-permute-start(bf16[288,768]{1,0:T(8,128)(2,1)S(1)} %copy-done.42), channel_id=1, source_target_pairs={{0,2},{1,3},{2,0},{3,1},{4,6},{5,7},{6,4},{7,5},{8,10},{9,11},{10,... | collective-permute-start | bytes 1327112 | tf_op jit(solution)/shard_map/ppermute | solution.py:27
  100.3 76.1 %all-gather.11.cloned.1.call-start = ((), (), s32[]{:S(2)}) async-start(), calls=%async_computation.3 | async-start | bytes 1966080 | tf_op jit(solution)/shard_map/all_gather | solution.py:955
  123.5 103.1 %all-gather.21.cloned.1.call-start = ((), (), s32[]{:S(2)}) async-start(), calls=%async_computation.10 | async-start | bytes 2211840 | tf_op jit(solution)/shard_map/all_gather | solution.py:957
  124.1 37.5 %collective-permute-start.16 = (bf16[192,1024]{1,0:T(8,128)(2,1)}, bf16[192,1024]{1,0:T(8,128)(2,1)}, u32[]{:S(2)}, u32[]{:S(2)}) collective-permute-start(bf16[192,1024]{1,0:T(8,128)(2,1)} %get-tuple-element.341), channel_id=1, source_target_pairs={{0,2},{1,3},{2,0},{3,1},{4,6},{5,7},{6,4},{7,5},{8,10},{9,11},{10,... | collective-permute-start | bytes 1179656 | tf_op jit(solution)/shard_map/ppermute | solution.py:27
  161.4 29.4 %collective-permute-start.22 = (bf16[256,1536]{1,0:T(8,128)(2,1)}, bf16[256,1536]{1,0:T(8,128)(2,1)S(1)}, u32[]{:S(2)}, u32[]{:S(2)}) collective-permute-start(bf16[256,1536]{1,0:T(8,128)(2,1)} %get-tuple-element.363.refs_1_), channel_id=1, source_target_pairs={{0,1},{1,0},{2,3},{3,2},{4,5},{5,4},{6,7},{7,6},{8,9},{9,8},{10,11... | collective-permute-start | bytes 2359304 | tf_op jit(solution)/shard_map/ppermute | solution.py:27
  162.5 28.3 %collective-permute-start.23 = (bf16[288,768]{1,0:T(8,128)(2,1)S(1)}, bf16[288,768]{1,0:T(8,128)(2,1)S(1)}, u32[]{:S(2)}, u32[]{:S(2)}) collective-permute-start(bf16[288,768]{1,0:T(8,128)(2,1)S(1)} %copy-done.41), channel_id=1, source_target_pairs={{0,2},{1,3},{2,0},{3,1},{4,6},{5,7},{6,4},{7,5},{8,10},{9,11},{10,... | collective-permute-start | bytes 1327112 | tf_op jit(solution)/shard_map/ppermute | solution.py:27
  194.3 34.9 %collective-permute-start.30 = (bf16[192,1024]{1,0:T(8,128)(2,1)}, bf16[192,1024]{1,0:T(8,128)(2,1)}, u32[]{:S(2)}, u32[]{:S(2)}) collective-permute-start(bf16[192,1024]{1,0:T(8,128)(2,1)} %get-tuple-element.385), channel_id=1, source_target_pairs={{0,2},{1,3},{2,0},{3,1},{4,6},{5,7},{6,4},{7,5},{8,10},{9,11},{10,... | collective-permute-start | bytes 1179656 | tf_op jit(solution)/shard_map/ppermute | solution.py:27
  194.9 97.9 %all-gather.13.cloned.1.call-start = ((), (), s32[]{:S(2)}) async-start(), calls=%async_computation.4 | async-start | bytes 1966080 | tf_op jit(solution)/shard_map/all_gather | solution.py:955
  231.4 28.5 %collective-permute-start.35 = (bf16[256,1536]{1,0:T(8,128)(2,1)S(1)}, bf16[256,1536]{1,0:T(8,128)(2,1)}, u32[]{:S(2)}, u32[]{:S(2)}) collective-permute-start(bf16[256,1536]{1,0:T(8,128)(2,1)S(1)} %copy-done.79), channel_id=1, source_target_pairs={{0,1},{1,0},{2,3},{3,2},{4,5},{5,4},{6,7},{7,6},{8,9},{9,8},{10,11... | collective-permute-start | bytes 2359304 | tf_op jit(solution)/shard_map/ppermute | solution.py:27
  231.9 25.8 %collective-permute-start.33 = (bf16[192,1024]{1,0:T(8,128)(2,1)}, bf16[192,1024]{1,0:T(8,128)(2,1)S(1)}, u32[]{:S(2)}, u32[]{:S(2)}) collective-permute-start(bf16[192,1024]{1,0:T(8,128)(2,1)} %get-tuple-element.394), channel_id=1, source_target_pairs={{0,2},{1,3},{2,0},{3,1},{4,6},{5,7},{6,4},{7,5},{8,10},{9,11},{10,... | collective-permute-start | bytes 1179656 | tf_op jit(solution)/shard_map/ppermute | solution.py:27
  234.3 77.3 %all-gather.15.cloned.1.call-start = ((), (), s32[]{:S(2)}) async-start(), calls=%async_computation.5 | async-start | bytes 1966080 | tf_op jit(solution)/shard_map/all_gather | solution.py:955
  241.9 26.0 %collective-permute-start.36 = (bf16[256,768]{1,0:T(8,128)(2,1)}, bf16[256,768]{1,0:T(8,128)(2,1)S(1)}, u32[]{:S(2)}, u32[]{:S(2)}) collective-permute-start(bf16[256,768]{1,0:T(8,128)(2,1)} %get-tuple-element.393.refs_2_.refs_13_), channel_id=1, source_target_pairs={{0,4},{4,0},{1,5},{5,1},{2,6},{6,2},{3,7},{7,3},{8,12},{12,8},{9,1... | collective-permute-start | bytes 1179656 | tf_op jit(solution)/shard_map/ppermute | solution.py:27
  267.8 254.0 %reduce-scatter.3.cloned.1.call-start = ((), (), s32[]{:S(2)}) async-start(), calls=%async_computation.6 | async-start | bytes 11796480 | tf_op jit(solution)/shard_map/reduce_scatter | solution.py:1024
  275.5 29.7 %collective-permute-start.38 = (bf16[256,1536]{1,0:T(8,128)(2,1)}, bf16[256,1536]{1,0:T(8,128)(2,1)S(1)}, u32[]{:S(2)}, u32[]{:S(2)}) collective-permute-start(bf16[256,1536]{1,0:T(8,128)(2,1)} %get-tuple-element.405.refs_1_), channel_id=1, source_target_pairs={{0,1},{1,0},{2,3},{3,2},{4,5},{5,4},{6,7},{7,6},{8,9},{9,8},{10,11... | collective-permute-start | bytes 2359304 | tf_op jit(solution)/shard_map/ppermute | solution.py:27
  280.0 26.2 %collective-permute-start.40 = (bf16[192,1024]{1,0:T(8,128)(2,1)S(1)}, bf16[192,1024]{1,0:T(8,128)(2,1)S(1)}, u32[]{:S(2)}, u32[]{:S(2)}) collective-permute-start(bf16[192,1024]{1,0:T(8,128)(2,1)S(1)} %collective-permute-done.34.refs_0_), channel_id=1, source_target_pairs={{0,8},{8,0},{16,24},{24,16},{1,9},{9,1},{17,25},{25,17},{2,10},{10... | collective-permute-start | bytes 1179656 | tf_op jit(solution)/shard_map/ppermute | solution.py:27
  281.8 26.4 %collective-permute-start.42 = (bf16[192,1024]{1,0:T(8,128)(2,1)S(1)}, bf16[192,1024]{1,0:T(8,128)(2,1)S(1)}, u32[]{:S(2)}, u32[]{:S(2)}) collective-permute-start(bf16[192,1024]{1,0:T(8,128)(2,1)S(1)} %collective-permute-done.34.refs_0_), channel_id=1, source_target_pairs={{0,24},{8,16},{16,8},{24,0},{1,25},{9,17},{17,9},{25,1},{2,26},{10... | collective-permute-start | bytes 1179656 | tf_op jit(solution)/shard_map/ppermute | solution.py:27
  364.4 35.9 %collective-permute-start.51 = (bf16[256,1536]{1,0:T(8,128)(2,1)}, bf16[256,1536]{1,0:T(8,128)(2,1)}, u32[]{:S(2)}, u32[]{:S(2)}) collective-permute-start(bf16[256,1536]{1,0:T(8,128)(2,1)} %get-tuple-element.441.refs_2_), channel_id=1, source_target_pairs={{0,1},{1,0},{2,3},{3,2},{4,5},{5,4},{6,7},{7,6},{8,9},{9,8},{10,11... | collective-permute-start | bytes 2359304 | tf_op jit(solution)/shard_map/ppermute | solution.py:27
  381.2 47.0 %collective-permute-start.54 = (bf16[256,1536]{1,0:T(8,128)(2,1)}, bf16[256,1536]{1,0:T(8,128)(2,1)}, u32[]{:S(2)}, u32[]{:S(2)}) collective-permute-start(bf16[256,1536]{1,0:T(8,128)(2,1)} %get-tuple-element.447.refs_2_), channel_id=1, source_target_pairs={{0,1},{1,0},{2,3},{3,2},{4,5},{5,4},{6,7},{7,6},{8,9},{9,8},{10,11... | collective-permute-start | bytes 2359304 | tf_op jit(solution)/shard_map/ppermute | solution.py:27
  427.7 162.8 %reduce-scatter.5.cloned.1.call-start = ((), (), s32[]{:S(2)}) async-start(), calls=%async_computation.7 | async-start | bytes 4423680 | tf_op jit(solution)/shard_map/reduce_scatter | solution.py:1024
  453.0 29.5 %collective-permute-start.57 = (bf16[256,1536]{1,0:T(8,128)(2,1)}, bf16[256,1536]{1,0:T(8,128)(2,1)}, u32[]{:S(2)}, u32[]{:S(2)}) collective-permute-start(bf16[256,1536]{1,0:T(8,128)(2,1)} %get-tuple-element.475.refs_1_), channel_id=1, source_target_pairs={{0,1},{1,0},{2,3},{3,2},{4,5},{5,4},{6,7},{7,6},{8,9},{9,8},{10,11... | collective-permute-start | bytes 2359304 | tf_op jit(solution)/shard_map/ppermute | solution.py:27
  481.2 49.3 %collective-permute-start.59 = (bf16[256,1536]{1,0:T(8,128)(2,1)}, bf16[256,1536]{1,0:T(8,128)(2,1)}, u32[]{:S(2)}, u32[]{:S(2)}) collective-permute-start(bf16[256,1536]{1,0:T(8,128)(2,1)} %get-tuple-element.485.refs_2_), channel_id=1, source_target_pairs={{0,1},{1,0},{2,3},{3,2},{4,5},{5,4},{6,7},{7,6},{8,9},{9,8},{10,11... | collective-permute-start | bytes 2359304 | tf_op jit(solution)/shard_map/ppermute | solution.py:27
  497.5 65.7 %collective-permute-start.63 = (bf16[256,1536]{1,0:T(8,128)(2,1)}, bf16[256,1536]{1,0:T(8,128)(2,1)}, u32[]{:S(2)}, u32[]{:S(2)}) collective-permute-start(bf16[256,1536]{1,0:T(8,128)(2,1)} %get-tuple-element.491.refs_2_), channel_id=1, source_target_pairs={{0,1},{1,0},{2,3},{3,2},{4,5},{5,4},{6,7},{7,6},{8,9},{9,8},{10,11... | collective-permute-start | bytes 2359304 | tf_op jit(solution)/shard_map/ppermute | solution.py:27
  498.6 26.6 %collective-permute-start.58 = (bf16[768,2304]{1,0:T(8,128)(2,1)}, bf16[768,2304]{1,0:T(8,128)(2,1)}, u32[]{:S(2)}, u32[]{:S(2)}) collective-permute-start(bf16[768,2304]{1,0:T(8,128)(2,1)} %get-tuple-element.497), channel_id=1, source_target_pairs={{0,4},{4,0},{1,5},{5,1},{2,6},{6,2},{3,7},{7,3},{8,12},{12,8},{9,1... | collective-permute-start | bytes 10616840 | tf_op jit(solution)/shard_map/ppermute | solution.py:27
  530.0 213.7 %all-gather.17.cloned.1.call-start = ((), (), s32[]{:S(2)}) async-start(), calls=%async_computation.8 | async-start | bytes 5898240 | tf_op jit(solution)/shard_map/all_gather | solution.py:1065
  545.0 29.5 %collective-permute-start.65 = (bf16[256,768]{1,0:T(8,128)(2,1)}, bf16[256,768]{1,0:T(8,128)(2,1)S(1)}, u32[]{:S(2)}, u32[]{:S(2)}) collective-permute-start(bf16[256,768]{1,0:T(8,128)(2,1)} %get-tuple-element.507), channel_id=1, source_target_pairs={{0,4},{4,0},{1,5},{5,1},{2,6},{6,2},{3,7},{7,3},{8,12},{12,8},{9,1... | collective-permute-start | bytes 1179656 | tf_op jit(solution)/shard_map/ppermute | solution.py:27
  545.5 56.7 %collective-permute-start.64 = (bf16[192,3072]{1,0:T(8,128)(2,1)}, bf16[192,3072]{1,0:T(8,128)(2,1)}, u32[]{:S(2)}, u32[]{:S(2)}) collective-permute-start(bf16[192,3072]{1,0:T(8,128)(2,1)} %get-tuple-element.516), channel_id=1, source_target_pairs={{0,2},{1,3},{2,0},{3,1},{4,6},{5,7},{6,4},{7,5},{8,10},{9,11},{10,... | collective-permute-start | bytes 3538952 | tf_op jit(solution)/shard_map/ppermute | solution.py:27
  561.1 63.3 %collective-permute-start.61 = (bf16[384,3072]{1,0:T(8,128)(2,1)}, bf16[384,3072]{1,0:T(8,128)(2,1)}, u32[]{:S(2)}, u32[]{:S(2)}) collective-permute-start(bf16[384,3072]{1,0:T(8,128)(2,1)} %get-tuple-element.512), channel_id=1, source_target_pairs={{0,8},{8,0},{16,24},{24,16},{1,9},{9,1},{17,25},{25,17},{2,10},{10... | collective-permute-start | bytes 7077896 | tf_op jit(solution)/shard_map/ppermute | solution.py:27
  562.5 62.4 %collective-permute-start.62 = (bf16[384,3072]{1,0:T(8,128)(2,1)}, bf16[384,3072]{1,0:T(8,128)(2,1)}, u32[]{:S(2)}, u32[]{:S(2)}) collective-permute-start(bf16[384,3072]{1,0:T(8,128)(2,1)} %get-tuple-element.513), channel_id=1, source_target_pairs={{0,16},{8,24},{16,0},{24,8},{1,17},{9,25},{17,1},{25,9},{2,18},{10... | collective-permute-start | bytes 7077896 | tf_op jit(solution)/shard_map/ppermute | solution.py:27
  581.1 27.3 %collective-permute-start.67 = (bf16[256,1536]{1,0:T(8,128)(2,1)}, bf16[256,1536]{1,0:T(8,128)(2,1)}, u32[]{:S(2)}, u32[]{:S(2)}) collective-permute-start(bf16[256,1536]{1,0:T(8,128)(2,1)} %get-tuple-element.524), channel_id=1, source_target_pairs={{1,0},{3,2},{4,5},{6,7},{9,8},{11,10},{12,13},{14,15},{17,16},{19,... | collective-permute-start | bytes 2359304 | tf_op jit(solution)/shard_map/ppermute | solution.py:62
  588.9 27.9 %collective-permute-start.68 = (bf16[256,1536]{1,0:T(8,128)(2,1)}, bf16[256,1536]{1,0:T(8,128)(2,1)}, u32[]{:S(2)}, u32[]{:S(2)}) collective-permute-start(bf16[256,1536]{1,0:T(8,128)(2,1)} %get-tuple-element.527), channel_id=1, source_target_pairs={{1,0},{3,2},{4,5},{6,7},{9,8},{11,10},{12,13},{14,15},{17,16},{19,... | collective-permute-start | bytes 2359304 | tf_op jit(solution)/shard_map/ppermute | solution.py:62
  629.1 166.0 %all-gather.19.cloned.1.call-start = ((), (), s32[]{:S(2)}) async-start(), calls=%async_computation.9 | async-start | bytes 2211840 | tf_op jit(solution)/shard_map/all_gather | solution.py:1065
  634.3 44.8 %collective-permute-start.69 = (bf16[192,3072]{1,0:T(8,128)(2,1)}, bf16[192,3072]{1,0:T(8,128)(2,1)}, u32[]{:S(2)}, u32[]{:S(2)}) collective-permute-start(bf16[192,3072]{1,0:T(8,128)(2,1)} %get-tuple-element.642), channel_id=1, source_target_pairs={{0,8},{8,0},{16,24},{24,16},{1,9},{9,1},{17,25},{25,17},{2,10},{10... | collective-permute-start | bytes 3538952 | tf_op jit(solution)/shard_map/ppermute | solution.py:27
  635.3 45.2 %collective-permute-start.75 = (bf16[192,3072]{1,0:T(8,128)(2,1)S(1)}, bf16[192,3072]{1,0:T(8,128)(2,1)}, u32[]{:S(2)}, u32[]{:S(2)}) collective-permute-start(bf16[192,3072]{1,0:T(8,128)(2,1)S(1)} %get-tuple-element.643), channel_id=1, source_target_pairs={{0,16},{8,24},{16,0},{24,8},{1,17},{9,25},{17,1},{25,9},{2,18},{10... | collective-permute-start | bytes 3538952 | tf_op jit(solution)/shard_map/ppermute | solution.py:27
  648.9 66.5 %collective-permute-start.78 = (bf16[384,1152]{1,0:T(8,128)(2,1)}, bf16[384,1152]{1,0:T(8,128)(2,1)}, u32[]{:S(2)}, u32[]{:S(2)}) collective-permute-start(bf16[384,1152]{1,0:T(8,128)(2,1)} %get-tuple-element.546), channel_id=1, source_target_pairs={{0,8},{8,0},{16,24},{24,16},{1,9},{9,1},{17,25},{25,17},{2,10},{10... | collective-permute-start | bytes 2654216 | tf_op jit(solution)/shard_map/ppermute | solution.py:27
  658.3 58.2 %collective-permute-start.79 = (bf16[384,1152]{1,0:T(8,128)(2,1)}, bf16[384,1152]{1,0:T(8,128)(2,1)}, u32[]{:S(2)}, u32[]{:S(2)}) collective-permute-start(bf16[384,1152]{1,0:T(8,128)(2,1)} %get-tuple-element.547), channel_id=1, source_target_pairs={{0,16},{8,24},{16,0},{24,8},{1,17},{9,25},{17,1},{25,9},{2,18},{10... | collective-permute-start | bytes 2654216 | tf_op jit(solution)/shard_map/ppermute | solution.py:27
  682.4 38.9 %collective-permute-start.76 = (bf16[256,1536]{1,0:T(8,128)(2,1)S(1)}, bf16[256,1536]{1,0:T(8,128)(2,1)S(1)}, u32[]{:S(2)}, u32[]{:S(2)}) collective-permute-start(bf16[256,1536]{1,0:T(8,128)(2,1)S(1)} %copy-done.38), channel_id=1, source_target_pairs={{1,0},{3,2},{4,5},{6,7},{9,8},{11,10},{12,13},{14,15},{17,16},{19,... | collective-permute-start | bytes 2359304 | tf_op jit(solution)/shard_map/ppermute | solution.py:62
  683.8 37.9 %collective-permute-start.77 = (bf16[256,1536]{1,0:T(8,128)(2,1)S(1)}, bf16[256,1536]{1,0:T(8,128)(2,1)S(1)}, u32[]{:S(2)}, u32[]{:S(2)}) collective-permute-start(bf16[256,1536]{1,0:T(8,128)(2,1)S(1)} %copy-done.39), channel_id=1, source_target_pairs={{1,0},{3,2},{4,5},{6,7},{9,8},{11,10},{12,13},{14,15},{17,16},{19,... | collective-permute-start | bytes 2359304 | tf_op jit(solution)/shard_map/ppermute | solution.py:62
  685.4 47.6 %collective-permute-start.82 = (bf16[192,3072]{1,0:T(8,128)(2,1)S(1)}, bf16[192,3072]{1,0:T(8,128)(2,1)S(1)}, u32[]{:S(2)}, u32[]{:S(2)}) collective-permute-start(bf16[192,3072]{1,0:T(8,128)(2,1)S(1)} %add_convert_fusion.4), channel_id=1, source_target_pairs={{0,2},{1,3},{2,0},{3,1},{4,6},{5,7},{6,4},{7,5},{8,10},{9,11},{10,... | collective-permute-start | bytes 3538952 | tf_op jit(solution)/shard_map/ppermute | solution.py:27
  737.1 29.0 %collective-permute-start.80 = (bf16[1024,768]{1,0:T(8,128)(2,1)}, bf16[1024,768]{1,0:T(8,128)(2,1)}, u32[]{:S(2)}, u32[]{:S(2)}) collective-permute-start(bf16[1024,768]{1,0:T(8,128)(2,1)} %pad_maximum_fusion.2), channel_id=1, source_target_pairs={{0,4},{4,0},{1,5},{5,1},{2,6},{6,2},{3,7},{7,3},{8,12},{12,8},{9,1... | collective-permute-start | bytes 4718600 | tf_op jit(solution)/shard_map/ppermute | solution.py:27
  755.6 36.3 %collective-permute-start.91 = (bf16[192,3072]{1,0:T(8,128)(2,1)S(1)}, bf16[192,3072]{1,0:T(8,128)(2,1)S(1)}, u32[]{:S(2)}, u32[]{:S(2)}) collective-permute-start(bf16[192,3072]{1,0:T(8,128)(2,1)S(1)} %pad_maximum_fusion.4), channel_id=1, source_target_pairs={{0,16},{8,24},{16,0},{24,8},{1,17},{9,25},{17,1},{25,9},{2,18},{10... | collective-permute-start | bytes 3538952 | tf_op jit(solution)/shard_map/ppermute | solution.py:27
  757.6 41.2 %collective-permute-start.90 = (bf16[192,3072]{1,0:T(8,128)(2,1)}, bf16[192,3072]{1,0:T(8,128)(2,1)S(1)}, u32[]{:S(2)}, u32[]{:S(2)}) collective-permute-start(bf16[192,3072]{1,0:T(8,128)(2,1)} %pad_maximum_fusion.3), channel_id=1, source_target_pairs={{0,8},{8,0},{16,24},{24,16},{1,9},{9,1},{17,25},{25,17},{2,10},{10... | collective-permute-start | bytes 3538952 | tf_op jit(solution)/shard_map/ppermute | solution.py:27
  773.2 46.8 %collective-permute-start.88 = (bf16[512,768]{1,0:T(8,128)(2,1)}, bf16[512,768]{1,0:T(8,128)(2,1)}, u32[]{:S(2)}, u32[]{:S(2)}) collective-permute-start(bf16[512,768]{1,0:T(8,128)(2,1)} %pad_maximum_fusion.8), channel_id=1, source_target_pairs={{0,2},{1,3},{2,0},{3,1},{4,6},{5,7},{6,4},{7,5},{8,10},{9,11},{10,... | collective-permute-start | bytes 2359304 | tf_op jit(solution)/shard_map/ppermute | solution.py:27
  774.2 32.4 %collective-permute-start.92 = (bf16[192,1152]{1,0:T(8,128)(2,1)S(1)}, bf16[192,1152]{1,0:T(8,128)(2,1)S(1)}, u32[]{:S(2)}, u32[]{:S(2)}) collective-permute-start(bf16[192,1152]{1,0:T(8,128)(2,1)S(1)} %add_convert_fusion.9.refs_0_), channel_id=1, source_target_pairs={{0,8},{8,0},{16,24},{24,16},{1,9},{9,1},{17,25},{25,17},{2,10},{10... | collective-permute-start | bytes 1327112 | tf_op jit(solution)/shard_map/ppermute | solution.py:27
  (149 other events, 1501.1 us)
Sparse Core Ops, SparseCore 0:
  100.4 30.4 all-gather.8
  133.4 30.9 all-gather.10
  195.0 31.5 all-gather.20
  234.4 29.0 all-gather.12
  267.9 41.1 all-gather.14
  427.8 93.9 reduce-scatter.2
  530.1 56.7 reduce-scatter.4
  629.2 91.1 all-gather.16
  737.2 41.4 all-gather.18

commit v5 on v4

--- a/solution.py
+++ b/solution.py
@@ -1513,20 +1513,20 @@
     sums["in", 0].across(order)
     ff_out = order.mark(spread_ff(order.after(spot), sums["ff", 1].pieces, 1, None))
     bit = 1
-    while bit < lax.axis_size("dp"):
+    while 2 * bit < lax.axis_size("dp"):
         grad_gains = order.mark(grad_gains + order.after(gains_came))
         bit *= 2
-        if bit < lax.axis_size("dp"):
-            gains_came = hop(grad_gains, "dp", bit)
+        gains_came = hop(grad_gains, "dp", bit)
         if bit == 2:
             sums["ff", 0].fifth(order)
-            sums["in", 0].fourth(order)
-            sums["in", 0].straight(order)
-            results.away(order)
+    sums["in", 0].fourth(order)
+    sums["in", 0].straight(order)
+    results.away(order)
     in_out = order.mark(spread_in(order.after(spot), sums["in", 1].pieces, 1, None, q_width))
     sums["ff", 0].done(order)
     ff_out = order.mark(spread_ff(order.after(spot), sums["ff", 0].pieces, 0, ff_out))
     in_out = order.mark(spread_in(order.after(spot), sums["in", 0].pieces, 0, in_out, q_width))
+    grad_gains = grad_gains + order.after(gains_came)
     activations, input_grad = results.done(order)
     return (activations, input_grad, *in_out, *ff_out, grad_gains)
 

time: 843 us -> 843 us (level)
  transfers between devices with their start and end apart: 104 -> 104, of which waited for: 43 -> 42; matrix products, arithmetic and copies ran while one was open for 11% -> 11% of each run, Pallas kernels for 44% -> 44%
where the time goes in v5:
time: 843 us; the launch traced here: 834 us
  Pallas kernels  366 us (43%)
  waiting for transfers between devices  253 us (30%)
  starting transfers between devices  82.3 us (10%)
  other arithmetic  71.9 us (9%)
  local copies, waits for them, and re-layouts  44.3 us (5%)
  between operations  15.7 us (2%)
    pallas_call x24, Pallas kernels, call(): pl.pallas_call(kernel, grid_spec=pltpu.PrefetchScalarGridSpec(num_scalar_...  245 us
    ppermute x91, waiting for transfers between devices, hop(): return lax.ppermute(value, axis, [(i, i ^ distance) for i in range(size)])  230 us
    ppermute x91, starting transfers between devices, hop(): return lax.ppermute(value, axis, [(i, i ^ distance) for i in range(size)])  74.7 us
    pallas_call x2, Pallas kernels, ff_weights(): pl.pallas_call(functools.partial(ff_weights_kernel, chunks, split), grid=...  33.9 us
    convert_element_type x6, other arithmetic, add_low(): return (left.astype(FULL) + right.astype(FULL)).astype(LOW)  27.8 us
    unnamed x190, local copies, waits for them, and re-layouts  25.6 us
    pallas_call x2, Pallas kernels, role_sums(): pl.pallas_call(role_sum_kernel, grid_spec=pltpu.PrefetchScalarGridSpec(nu...  21.3 us
    pallas_call x2, Pallas kernels, in_weights(): pl.pallas_call(functools.partial(in_weights_kernel, chunks), grid=(1,), i...  19.6 us
  transfers between devices with their start and end apart: 104, of which 42 were waited for; matrix products, arithmetic and copies ran while one was open for 11% of the time, Pallas kernels for 44%

profile of v5, /device:TPU:0, one launch (start us, length us, event | category | flops | bytes accessed | tf_op | source)
XLA Modules:
  0.0 833.5 jit_solution(15655129839443133462)
XLA Ops:
  39.8 9.5 %collective-permute-done = bf16[256,768]{1,0:T(8,128)(2,1)S(1)} collective-permute-done((bf16[256,768]{1,0:T(8,128)(2,1)}, bf16[256,768]{1,0:T(8,128)(2,1)S(1)}, u32[]{:S(2)}, u32[]{:S(2)}) %collective-permute-start) | collective-permute-done | bytes 393248 | tf_op jit(solution)/shard_map/ppermute | solution.py:27
  49.3 9.1 %collective-permute-done.6.refs_0_ = bf16[288,768]{1,0:T(8,128)(2,1)S(1)} collective-permute-done((bf16[288,768]{1,0:T(8,128)(2,1)S(1)}, bf16[288,768]{1,0:T(8,128)(2,1)S(1)}, u32[]{:S(2)}, u32[]{:S(2)}) %collective-permute-start.6) | collective-permute-done | bytes 442400 | tf_op jit(solution)/shard_map/ppermute | solution.py:27
  62.2 8.1 collective-permute-done.8.refs_1_
  74.6 17.0 %collective-permute-done.11 = bf16[192,1024]{1,0:T(8,128)(2,1)S(1)} collective-permute-done((bf16[192,1024]{1,0:T(8,128)(2,1)}, bf16[192,1024]{1,0:T(8,128)(2,1)S(1)}, u32[]{:S(2)}, u32[]{:S(2)}) %collective-permute-start.11) | collective-permute-done | bytes 393248 | tf_op jit(solution)/shard_map/ppermute | solution.py:27
  102.5 12.6 %collective-permute-done.14 = bf16[192,1024]{1,0:T(8,128)(2,1)S(1)} collective-permute-done((bf16[192,1024]{1,0:T(8,128)(2,1)}, bf16[192,1024]{1,0:T(8,128)(2,1)S(1)}, u32[]{:S(2)}, u32[]{:S(2)}) %collective-permute-start.14) | collective-permute-done | bytes 393248 | tf_op jit(solution)/shard_map/ppermute | solution.py:27
  115.1 6.0 project.4
  125.1 5.9 project.5
  131.9 6.8 attend.4
  142.7 18.7 %attend.5 = (bf16[256,768]{1,0:T(8,128)(2,1)}, f32[8,256]{1,0:T(8,128)}, bf16[256,1536]{1,0:T(8,128)(2,1)}) custom-call(s32[1]{0:T(128)} %bitcast.3.refs_0_, bf16[256,768]{1,0:T(8,128)(2,1)} %get-tuple-element.360.refs_1_.refs_11_, bf16[256,768]{1,0:T(8,128)(2,1)} %get-tuple-element.346.refs_2_.refs_13_, bf16[256,768]{1,0:T(8,128)(2,1)} %copy-done.81, ...), custom_call_target="tpu_custom_call" | custom-call | flops 82543902720 | bytes 129761280 | tf_op jit(solution)/shard_map/attend/pallas_call | solution.py:249
  167.7 8.7 %collective-permute-done.24.refs_1_ = bf16[192,1024]{1,0:T(8,128)(2,1)S(1)} collective-permute-done((bf16[192,1024]{1,0:T(8,128)(2,1)}, bf16[192,1024]{1,0:T(8,128)(2,1)S(1)}, u32[]{:S(2)}, u32[]{:S(2)}) %collective-permute-start.24) | collective-permute-done | bytes 393248 | tf_op jit(solution)/shard_map/ppermute | solution.py:27
  176.4 8.2 collective-permute-done.25.refs_2_
  184.6 6.2 collective-permute-done.22.refs_2_
  199.1 11.7 %feed_forward.4 = (f32[256,1536]{1,0:T(8,128)}, f32[256,1]{1,0:T(8,128)}, bf16[256,1536]{1,0:T(8,128)(2,1)}, bf16[256,2048]{1,0:T(8,128)(2,1)}, bf16[256,2048]{1...) custom-call(f32[256,1536]{1,0:T(8,128)} %get-tuple-element.369.refs_0_, ...), custom_call_target="tpu_custom_call" | custom-call | flops 144955146240 | bytes 637102080 | tf_op jit(solution)/shard_map/feed_forward/pallas_call | solution.py:249
  210.9 11.5 %feed_forward.5 = (f32[256,1536]{1,0:T(8,128)}, f32[256,1]{1,0:T(8,128)}, bf16[256,1536]{1,0:T(8,128)(2,1)}, bf16[256,2048]{1,0:T(8,128)(2,1)}, bf16[256,2048]{1...) custom-call(f32[256,1536]{1,0:T(8,128)} %get-tuple-element.377.refs_0_, ...), custom_call_target="tpu_custom_call" | custom-call | flops 144955146240 | bytes 637102080 | tf_op jit(solution)/shard_map/feed_forward/pallas_call | solution.py:249
  235.2 6.6 project.6
  242.1 15.6 %collective-permute-done.33 = bf16[192,1024]{1,0:T(8,128)(2,1)S(1)} collective-permute-done((bf16[192,1024]{1,0:T(8,128)(2,1)}, bf16[192,1024]{1,0:T(8,128)(2,1)S(1)}, u32[]{:S(2)}, u32[]{:S(2)}) %collective-permute-start.33) | collective-permute-done | bytes 393248 | tf_op jit(solution)/shard_map/ppermute | solution.py:27
  261.0 6.6 project.7
  268.6 6.9 attend.6
  283.5 9.2 %attend.7 = (bf16[256,768]{1,0:T(8,128)(2,1)}, f32[8,256]{1,0:T(8,128)}, bf16[256,1536]{1,0:T(8,128)(2,1)}) custom-call(s32[1]{0:T(128)} %bitcast.3.refs_0_, bf16[256,768]{1,0:T(8,128)(2,1)} %get-tuple-element.407.refs_1_.refs_11_, bf16[256,768]{1,0:T(8,128)(2,1)} %get-tuple-element.393.refs_2_.refs_13_, bf16[256,768]{1,0:T(8,128)(2,1)} %copy-done.85, ...), custom_call_target="tpu_custom_call" | custom-call | flops 82543902720 | bytes 129761280 | tf_op jit(solution)/shard_map/attend/pallas_call | solution.py:249
  292.8 10.5 %collective-permute-done.39 = bf16[256,768]{1,0:T(8,128)(2,1)S(1)} collective-permute-done((bf16[256,768]{1,0:T(8,128)(2,1)S(1)}, bf16[256,768]{1,0:T(8,128)(2,1)S(1)}, u32[]{:S(2)}, u32[]{:S(2)}) %collective-permute-start.39) | collective-permute-done | bytes 393248 | tf_op jit(solution)/shard_map/ppermute | solution.py:27
  318.6 11.6 %feed_forward.6 = (f32[256,1536]{1,0:T(8,128)}, f32[256,1]{1,0:T(8,128)}, bf16[256,1536]{1,0:T(8,128)(2,1)}, bf16[256,2048]{1,0:T(8,128)(2,1)}, bf16[256,2048]{1...) custom-call(f32[256,1536]{1,0:T(8,128)} %get-tuple-element.416.refs_0_.refs_3_, ...), custom_call_target="tpu_custom_call" | custom-call | flops 144955146240 | bytes 637102080 | tf_op jit(solution)/shard_map/feed_forward/pallas_call | solution.py:249
  331.9 11.5 %feed_forward.7 = (f32[256,1536]{1,0:T(8,128)}, f32[256,1]{1,0:T(8,128)}, bf16[256,1536]{1,0:T(8,128)(2,1)}, bf16[256,2048]{1,0:T(8,128)(2,1)}, bf16[256,2048]{1...) custom-call(f32[256,1536]{1,0:T(8,128)} %get-tuple-element.426.refs_0_.refs_3_, ...), custom_call_target="tpu_custom_call" | custom-call | flops 144955146240 | bytes 637102080 | tf_op jit(solution)/shard_map/feed_forward/pallas_call | solution.py:249
  347.3 13.6 %feed_back.4 = (bf16[256,4096]{1,0:T(8,128)(2,1)}, bf16[256,1536]{1,0:T(8,128)(2,1)}) custom-call(bf16[256,1536]{1,0:T(8,128)(2,1)} %pad_maximum_fusion.6.refs_0_.refs_3_, bf16[256,2048]{1,0:T(8,128)(2,1)} %get-tuple-element.433.refs_1_, bf16[256,2048]{1,0:T(8,128)(2,1)} %get-tuple-element.434.refs_2_, bf16[2,1024,768]{2,1,0:T(8,128)(2,1)} %refs_8_.7, ...), custom_call_target="tpu_custom_call" | custom-call | flops 144955146240 | bytes 652738560 | tf_op jit(solution)/shard_map/feed_back/pallas_call | solution.py:249
  367.9 13.2 %feed_back.5 = (bf16[256,4096]{1,0:T(8,128)(2,1)}, bf16[256,1536]{1,0:T(8,128)(2,1)}) custom-call(bf16[256,1536]{1,0:T(8,128)(2,1)} %pad_maximum_fusion.7.refs_0_.refs_2_, bf16[256,2048]{1,0:T(8,128)(2,1)} %get-tuple-element.421.refs_1_, bf16[256,2048]{1,0:T(8,128)(2,1)} %get-tuple-element.422.refs_2_, bf16[2,1024,768]{2,1,0:T(8,128)(2,1)} %refs_8_.7, ...), custom_call_target="tpu_custom_call" | custom-call | flops 144955146240 | bytes 652738560 | tf_op jit(solution)/shard_map/feed_back/pallas_call | solution.py:249
  382.0 16.9 %ff_weights.2 = (bf16[768,6144]{1,0:T(8,128)(2,1)}, bf16[768,6144]{1,0:T(8,128)(2,1)}) custom-call(bf16[256,1536]{1,0:T(8,128)(2,1)} %get-tuple-element.448.refs_0_, bf16[256,1536]{1,0:T(8,128)(2,1)} %get-tuple-element.449.refs_1_, bf16[256,1536]{1,0:T(8,128)(2,1)} %pad_maximum_fusion.7.refs_0_.refs_2_, bf16[256,1536]{1,0:T(8,128)(2,1)} %pad_maximum_fusion.6.refs_0_.refs_3_, ...), custom_call_target="tpu_custom_call" | custom-call | flops 289910292480 | bytes 754974720 | tf_op jit(solution)/shard_map/ff_weights/pallas_call | solution.py:616
  400.2 14.5 %attend_back.4 = (f32[256,1536]{1,0:T(8,128)}, bf16[256,1536]{1,0:T(8,128)(2,1)}, f32[1,1536]{1,0:T(1,128)}, f32[256,768]{1,0:T(8,128)}, f32[256,768]{1,0:T(8,12...) custom-call(s32[1]{0:T(128)} %bitcast.3.refs_0_, ...), custom_call_target="tpu_custom_call" | custom-call | flops 179180666880 | bytes 224363520 | tf_op jit(solution)/shard_map/attend_back/pallas_call | solution.py:249
  415.3 12.3 %add_convert_fusion = bf16[768,6144]{1,0:T(8,128)(2,1)} fusion(bf16[768,6144]{1,0:T(8,128)(2,1)} %collective-permute-done.52, bf16[768,6144]{1,0:T(8,128)(2,1)} %get-tuple-element.462), kind=kLoop, calls=%fused_computation | loop fusion | flops 18874368 | bytes 28311552 | tf_op jit(solution)/shard_map/convert_element_type | solution.py:81
  428.2 10.9 %attend_back.5 = (f32[256,1536]{1,0:T(8,128)}, bf16[256,1536]{1,0:T(8,128)(2,1)}, f32[1,1536]{1,0:T(1,128)}, f32[256,768]{1,0:T(8,128)}, f32[256,768]{1,0:T(8,128)}, /*index=5*/bf16[256,768]{1,0:T(8,128)(2,1)}) custom-call(s32[1]{0:T(128)} %bitcast.3.refs_0_, f32[256,1536]{1,0:T(8,128)} %convert_element_type.220.refs_1_, ...), custom_call_target="tpu_custom_call" | custom-call | flops 98650030080 | bytes 224363520 | tf_op jit(solution)/shard_map/attend_back/pallas_call | solution.py:249
  439.1 6.1 project_back.4
  454.0 10.0 %in_weights.2 = (bf16[768,2304]{1,0:T(8,128)(2,1)}, bf16[768,2304]{1,0:T(8,128)(2,1)}) custom-call(bf16[256,1536]{1,0:T(8,128)(2,1)} %get-tuple-element.476.refs_0_, bf16[256,1536]{1,0:T(8,128)(2,1)} %get-tuple-element.477.refs_1_, bf16[256,1536]{1,0:T(8,128)(2,1)} %get-tuple-element.466.refs_2_, bf16[256,1536]{1,0:T(8,128)(2,1)} %get-tuple-element.454.refs_3_, ...), custom_call_target="tpu_custom_call" | custom-call | flops 108716359680 | bytes 306708480 | tf_op jit(solution)/shard_map/in_weights/pallas_call | solution.py:656
  466.0 15.2 %feed_back.6 = (f32[256,1536]{1,0:T(8,128)}, bf16[256,1536]{1,0:T(8,128)(2,1)}, f32[1,1536]{1,0:T(1,128)}, bf16[256,4096]{1,0:T(8,128)(2,1)}, bf16[256,1536]{1,0:T(8,128)(2,1)}) custom-call(f32[256,1536]{1,0:T(8,128)} %get-tuple-element.480.refs_0_, bf16[256,1536]{1,0:T(8,128)(2,1)} %get-tuple-element.472.refs_1_, ...), custom_call_target="tpu_custom_call" | custom-call | flops 144955146240 | bytes 723624960 | tf_op jit(solution)/shard_map/feed_back/pallas_call | solution.py:249
  482.5 15.0 %feed_back.7 = (f32[256,1536]{1,0:T(8,128)}, bf16[256,1536]{1,0:T(8,128)(2,1)}, f32[1,1536]{1,0:T(1,128)}, bf16[256,4096]{1,0:T(8,128)(2,1)}, bf16[256,1536]{1,0:T(8,128)(2,1)}) custom-call(f32[256,1536]{1,0:T(8,128)} %get-tuple-element.486.refs_0_, bf16[256,1536]{1,0:T(8,128)(2,1)} %get-tuple-element.475.refs_1_, ...), custom_call_target="tpu_custom_call" | custom-call | flops 144955146240 | bytes 723624960 | tf_op jit(solution)/shard_map/feed_back/pallas_call | solution.py:249
  498.6 17.0 %ff_weights.3 = (bf16[768,6144]{1,0:T(8,128)(2,1)}, bf16[768,6144]{1,0:T(8,128)(2,1)}) custom-call(bf16[256,1536]{1,0:T(8,128)(2,1)} %get-tuple-element.492.refs_0_, bf16[256,1536]{1,0:T(8,128)(2,1)} %get-tuple-element.493.refs_1_, bf16[256,1536]{1,0:T(8,128)(2,1)} %get-tuple-element.488.refs_2_, bf16[256,1536]{1,0:T(8,128)(2,1)} %get-tuple-element.482.refs_3_, ...), custom_call_target="tpu_custom_call" | custom-call | flops 289910292480 | bytes 754974720 | tf_op jit(solution)/shard_map/ff_weights/pallas_call | solution.py:616
  515.6 6.2 reduce-scatter.3.cloned.1.call-done
  530.5 14.5 %attend_back.6 = (f32[256,1536]{1,0:T(8,128)}, bf16[256,1536]{1,0:T(8,128)(2,1)}, f32[1,1536]{1,0:T(1,128)}, f32[256,768]{1,0:T(8,128)}, f32[256,768]{1,0:T(8,12...) custom-call(s32[1]{0:T(128)} %bitcast.3.refs_0_, f32[256,1536]{1,0:T(8,128)} %get-tuple-element.499.refs_1_, ...), custom_call_target="tpu_custom_call" | custom-call | flops 179180666880 | bytes 224363520 | tf_op jit(solution)/shard_map/attend_back/pallas_call | solution.py:249
  548.0 13.1 %role_sums.2 = (bf16[384,3072]{1,0:T(8,128)(2,1)}, bf16[384,3072]{1,0:T(8,128)(2,1)}, bf16[384,3072]{1,0:T(8,128)(2,1)}, bf16[384,3072]{1,0:T(8,128)(2,1)}) custom-call(s32[8]{0:T(128)} %broadcast_xor_fusion.row_ref, s32[8]{0:T(128)} %constant.62.clone.side_ref, bf16[768,6144]{1,0:T(8,128)(2,1)} %get-tuple-element.509.left_ref, ...), custom_call_target="tpu_custom_call" | custom-call | bytes 424673280 | tf_op jit(solution)/shard_map/role_sums/pallas_call | solution.py:691
  563.1 11.3 %attend_back.7 = (f32[256,1536]{1,0:T(8,128)}, bf16[256,1536]{1,0:T(8,128)(2,1)}, f32[1,1536]{1,0:T(1,128)}, f32[256,768]{1,0:T(8,128)}, f32[256,768]{1,0:T(8,128)}, /*index=5*/bf16[256,768]{1,0:T(8,128)(2,1)}) custom-call(s32[1]{0:T(128)} %bitcast.3.refs_0_, f32[256,1536]{1,0:T(8,128)} %get-tuple-element.514.refs_1_, ...), custom_call_target="tpu_custom_call" | custom-call | flops 98650030080 | bytes 224363520 | tf_op jit(solution)/shard_map/attend_back/pallas_call | solution.py:249
  592.6 9.7 %in_weights.3 = (bf16[768,2304]{1,0:T(8,128)(2,1)}, bf16[768,2304]{1,0:T(8,128)(2,1)}) custom-call(bf16[256,1536]{1,0:T(8,128)(2,1)} %get-tuple-element.529.refs_0_, bf16[256,1536]{1,0:T(8,128)(2,1)} %get-tuple-element.530.refs_1_, bf16[256,1536]{1,0:T(8,128)(2,1)} %get-tuple-element.518.refs_2_, bf16[256,1536]{1,0:T(8,128)(2,1)} %get-tuple-element.501.refs_3_, ...), custom_call_target="tpu_custom_call" | custom-call | flops 108716359680 | bytes 306708480 | tf_op jit(solution)/shard_map/in_weights/pallas_call | solution.py:656
  608.4 8.4 %collective-permute-done.68 = bf16[256,1536]{1,0:T(8,128)(2,1)} collective-permute-done((bf16[256,1536]{1,0:T(8,128)(2,1)}, bf16[256,1536]{1,0:T(8,128)(2,1)}, u32[]{:S(2)}, u32[]{:S(2)}) %collective-permute-start.68) | collective-permute-done | bytes 786464 | tf_op jit(solution)/shard_map/ppermute | solution.py:62
  640.7 8.1 role_sums.3
  649.9 8.4 %collective-permute-done.73 = bf16[192,1152]{1,0:T(8,128)(2,1)S(1)} collective-permute-done((bf16[192,1152]{1,0:T(8,128)(2,1)}, bf16[192,1152]{1,0:T(8,128)(2,1)S(1)}, u32[]{:S(2)}, u32[]{:S(2)}) %collective-permute-start.73) | collective-permute-done | bytes 442400 | tf_op jit(solution)/shard_map/ppermute | solution.py:27
  660.9 18.3 %collective-permute-done.69 = bf16[192,3072]{1,0:T(8,128)(2,1)} collective-permute-done((bf16[192,3072]{1,0:T(8,128)(2,1)}, bf16[192,3072]{1,0:T(8,128)(2,1)}, u32[]{:S(2)}, u32[]{:S(2)}) %collective-permute-start.69) | collective-permute-done | bytes 1179680 | tf_op jit(solution)/shard_map/ppermute | solution.py:27
  687.0 28.4 %collective-permute-done.78 = bf16[384,1152]{1,0:T(8,128)(2,1)} collective-permute-done((bf16[384,1152]{1,0:T(8,128)(2,1)}, bf16[384,1152]{1,0:T(8,128)(2,1)}, u32[]{:S(2)}, u32[]{:S(2)}) %collective-permute-start.78) | collective-permute-done | bytes 884768 | tf_op jit(solution)/shard_map/ppermute | solution.py:27
  726.6 6.4 collective-permute-done.82
  743.7 6.4 spread_ff.2
  757.9 6.8 collective-permute-done.84
  775.3 18.7 %collective-permute-done.90.refs_4_.refs_6_.refs_12_.refs_14_.refs_20_.refs_22_ = bf16[192,3072]{1,0:T(8,128)(2,1)S(1)} collective-permute-done((bf16[192,3072]{1,0:T(8,128)(2,1)S(1)}, bf16[192,3072]{1,0:T(8,128)(2,1)S(1)}, u32[]{:S(2)}, u32[]{:S(2)}) %collective-permute-start.90) | collective-permute-done | bytes 1179680 | tf_op jit(solution)/shard_map/ppermute | solution.py:27
  800.7 6.8 spread_ff.3
  (485 shorter events, 283.1 us)
Async XLA Ops:
  7.2 160.5 %all-gather.9.cloned.1.call-start = ((), (), s32[]{:S(2)}) async-start(), calls=%async_computation.2 | async-start | bytes 1966080 | tf_op jit(solution)/shard_map/all_gather | solution.py:955
  7.2 28.8 %collective-permute-start.4 = (bf16[2,768,1024]{2,1,0:T(8,128)(2,1)}, bf16[2,768,1024]{2,1,0:T(8,128)(2,1)}, u32[]{:S(2)}, u32[]{:S(2)}) collective-permute-start(bf16[2,768,1024]{2,1,0:T(8,128)(2,1)} %refs_12_.11), channel_id=1, source_target_pairs={{0,4},{4,0},{1,5},{5,1},{2,6},{6,2},{3,7},{7,3},{8,12},{12,8},{9,1... | collective-permute-start | bytes 9437192 | tf_op jit(solution)/shard_map/ppermute | solution.py:27
  7.8 28.2 %collective-permute-start.5 = (bf16[2,768,1024]{2,1,0:T(8,128)(2,1)}, bf16[2,768,1024]{2,1,0:T(8,128)(2,1)}, u32[]{:S(2)}, u32[]{:S(2)}) collective-permute-start(bf16[2,768,1024]{2,1,0:T(8,128)(2,1)} %refs_13_.3), channel_id=1, source_target_pairs={{0,4},{4,0},{1,5},{5,1},{2,6},{6,2},{3,7},{7,3},{8,12},{12,8},{9,1... | collective-permute-start | bytes 9437192 | tf_op jit(solution)/shard_map/ppermute | solution.py:27
  17.5 31.8 %collective-permute-start = (bf16[256,768]{1,0:T(8,128)(2,1)}, bf16[256,768]{1,0:T(8,128)(2,1)S(1)}, u32[]{:S(2)}, u32[]{:S(2)}) collective-permute-start(bf16[256,768]{1,0:T(8,128)(2,1)} %get-tuple-element.312), channel_id=1, source_target_pairs={{0,2},{1,3},{2,0},{3,1},{4,6},{5,7},{6,4},{7,5},{8,10},{9,11},{10,... | collective-permute-start | bytes 1179656 | tf_op jit(solution)/shard_map/ppermute | solution.py:27
  21.2 79.5 %collective-permute-start.13 = (bf16[2,1024,768]{2,1,0:T(8,128)(2,1)}, bf16[2,1024,768]{2,1,0:T(8,128)(2,1)}, u32[]{:S(2)}, u32[]{:S(2)}) collective-permute-start(bf16[2,1024,768]{2,1,0:T(8,128)(2,1)} %refs_8_.7), channel_id=1, source_target_pairs={{0,4},{4,0},{1,5},{5,1},{2,6},{6,2},{3,7},{7,3},{8,12},{12,8},{9,1... | collective-permute-start | bytes 9437192 | tf_op jit(solution)/shard_map/ppermute | solution.py:27
  27.3 31.1 %collective-permute-start.6 = (bf16[288,768]{1,0:T(8,128)(2,1)S(1)}, bf16[288,768]{1,0:T(8,128)(2,1)S(1)}, u32[]{:S(2)}, u32[]{:S(2)}) collective-permute-start(bf16[288,768]{1,0:T(8,128)(2,1)S(1)} %copy-done.42), channel_id=1, source_target_pairs={{0,2},{1,3},{2,0},{3,1},{4,6},{5,7},{6,4},{7,5},{8,10},{9,11},{10,... | collective-permute-start | bytes 1327112 | tf_op jit(solution)/shard_map/ppermute | solution.py:27
  100.3 76.1 %all-gather.11.cloned.1.call-start = ((), (), s32[]{:S(2)}) async-start(), calls=%async_computation.3 | async-start | bytes 1966080 | tf_op jit(solution)/shard_map/all_gather | solution.py:955
  123.5 103.1 %all-gather.21.cloned.1.call-start = ((), (), s32[]{:S(2)}) async-start(), calls=%async_computation.10 | async-start | bytes 2211840 | tf_op jit(solution)/shard_map/all_gather | solution.py:957
  124.1 37.5 %collective-permute-start.16 = (bf16[192,1024]{1,0:T(8,128)(2,1)}, bf16[192,1024]{1,0:T(8,128)(2,1)}, u32[]{:S(2)}, u32[]{:S(2)}) collective-permute-start(bf16[192,1024]{1,0:T(8,128)(2,1)} %get-tuple-element.341), channel_id=1, source_target_pairs={{0,2},{1,3},{2,0},{3,1},{4,6},{5,7},{6,4},{7,5},{8,10},{9,11},{10,... | collective-permute-start | bytes 1179656 | tf_op jit(solution)/shard_map/ppermute | solution.py:27
  161.4 29.4 %collective-permute-start.22 = (bf16[256,1536]{1,0:T(8,128)(2,1)}, bf16[256,1536]{1,0:T(8,128)(2,1)S(1)}, u32[]{:S(2)}, u32[]{:S(2)}) collective-permute-start(bf16[256,1536]{1,0:T(8,128)(2,1)} %get-tuple-element.363.refs_1_), channel_id=1, source_target_pairs={{0,1},{1,0},{2,3},{3,2},{4,5},{5,4},{6,7},{7,6},{8,9},{9,8},{10,11... | collective-permute-start | bytes 2359304 | tf_op jit(solution)/shard_map/ppermute | solution.py:27
  162.5 28.3 %collective-permute-start.23 = (bf16[288,768]{1,0:T(8,128)(2,1)S(1)}, bf16[288,768]{1,0:T(8,128)(2,1)S(1)}, u32[]{:S(2)}, u32[]{:S(2)}) collective-permute-start(bf16[288,768]{1,0:T(8,128)(2,1)S(1)} %copy-done.41), channel_id=1, source_target_pairs={{0,2},{1,3},{2,0},{3,1},{4,6},{5,7},{6,4},{7,5},{8,10},{9,11},{10,... | collective-permute-start | bytes 1327112 | tf_op jit(solution)/shard_map/ppermute | solution.py:27
  194.3 34.9 %collective-permute-start.30 = (bf16[192,1024]{1,0:T(8,128)(2,1)}, bf16[192,1024]{1,0:T(8,128)(2,1)}, u32[]{:S(2)}, u32[]{:S(2)}) collective-permute-start(bf16[192,1024]{1,0:T(8,128)(2,1)} %get-tuple-element.385), channel_id=1, source_target_pairs={{0,2},{1,3},{2,0},{3,1},{4,6},{5,7},{6,4},{7,5},{8,10},{9,11},{10,... | collective-permute-start | bytes 1179656 | tf_op jit(solution)/shard_map/ppermute | solution.py:27
  194.9 97.9 %all-gather.13.cloned.1.call-start = ((), (), s32[]{:S(2)}) async-start(), calls=%async_computation.4 | async-start | bytes 1966080 | tf_op jit(solution)/shard_map/all_gather | solution.py:955
  231.4 28.5 %collective-permute-start.35 = (bf16[256,1536]{1,0:T(8,128)(2,1)S(1)}, bf16[256,1536]{1,0:T(8,128)(2,1)}, u32[]{:S(2)}, u32[]{:S(2)}) collective-permute-start(bf16[256,1536]{1,0:T(8,128)(2,1)S(1)} %copy-done.79), channel_id=1, source_target_pairs={{0,1},{1,0},{2,3},{3,2},{4,5},{5,4},{6,7},{7,6},{8,9},{9,8},{10,11... | collective-permute-start | bytes 2359304 | tf_op jit(solution)/shard_map/ppermute | solution.py:27
  234.3 77.3 %all-gather.15.cloned.1.call-start = ((), (), s32[]{:S(2)}) async-start(), calls=%async_computation.5 | async-start | bytes 1966080 | tf_op jit(solution)/shard_map/all_gather | solution.py:955
  241.9 26.0 %collective-permute-start.36 = (bf16[256,768]{1,0:T(8,128)(2,1)}, bf16[256,768]{1,0:T(8,128)(2,1)S(1)}, u32[]{:S(2)}, u32[]{:S(2)}) collective-permute-start(bf16[256,768]{1,0:T(8,128)(2,1)} %get-tuple-element.393.refs_2_.refs_13_), channel_id=1, source_target_pairs={{0,4},{4,0},{1,5},{5,1},{2,6},{6,2},{3,7},{7,3},{8,12},{12,8},{9,1... | collective-permute-start | bytes 1179656 | tf_op jit(solution)/shard_map/ppermute | solution.py:27
  267.8 254.0 %reduce-scatter.3.cloned.1.call-start = ((), (), s32[]{:S(2)}) async-start(), calls=%async_computation.6 | async-start | bytes 11796480 | tf_op jit(solution)/shard_map/reduce_scatter | solution.py:1024
  275.5 29.7 %collective-permute-start.38 = (bf16[256,1536]{1,0:T(8,128)(2,1)}, bf16[256,1536]{1,0:T(8,128)(2,1)S(1)}, u32[]{:S(2)}, u32[]{:S(2)}) collective-permute-start(bf16[256,1536]{1,0:T(8,128)(2,1)} %get-tuple-element.405.refs_1_), channel_id=1, source_target_pairs={{0,1},{1,0},{2,3},{3,2},{4,5},{5,4},{6,7},{7,6},{8,9},{9,8},{10,11... | collective-permute-start | bytes 2359304 | tf_op jit(solution)/shard_map/ppermute | solution.py:27
  280.0 26.2 %collective-permute-start.40 = (bf16[192,1024]{1,0:T(8,128)(2,1)S(1)}, bf16[192,1024]{1,0:T(8,128)(2,1)S(1)}, u32[]{:S(2)}, u32[]{:S(2)}) collective-permute-start(bf16[192,1024]{1,0:T(8,128)(2,1)S(1)} %collective-permute-done.34.refs_0_), channel_id=1, source_target_pairs={{0,8},{8,0},{16,24},{24,16},{1,9},{9,1},{17,25},{25,17},{2,10},{10... | collective-permute-start | bytes 1179656 | tf_op jit(solution)/shard_map/ppermute | solution.py:27
  281.8 26.4 %collective-permute-start.42 = (bf16[192,1024]{1,0:T(8,128)(2,1)S(1)}, bf16[192,1024]{1,0:T(8,128)(2,1)S(1)}, u32[]{:S(2)}, u32[]{:S(2)}) collective-permute-start(bf16[192,1024]{1,0:T(8,128)(2,1)S(1)} %collective-permute-done.34.refs_0_), channel_id=1, source_target_pairs={{0,24},{8,16},{16,8},{24,0},{1,25},{9,17},{17,9},{25,1},{2,26},{10... | collective-permute-start | bytes 1179656 | tf_op jit(solution)/shard_map/ppermute | solution.py:27
  364.4 35.9 %collective-permute-start.51 = (bf16[256,1536]{1,0:T(8,128)(2,1)}, bf16[256,1536]{1,0:T(8,128)(2,1)}, u32[]{:S(2)}, u32[]{:S(2)}) collective-permute-start(bf16[256,1536]{1,0:T(8,128)(2,1)} %get-tuple-element.441.refs_2_), channel_id=1, source_target_pairs={{0,1},{1,0},{2,3},{3,2},{4,5},{5,4},{6,7},{7,6},{8,9},{9,8},{10,11... | collective-permute-start | bytes 2359304 | tf_op jit(solution)/shard_map/ppermute | solution.py:27
  381.2 47.0 %collective-permute-start.54 = (bf16[256,1536]{1,0:T(8,128)(2,1)}, bf16[256,1536]{1,0:T(8,128)(2,1)}, u32[]{:S(2)}, u32[]{:S(2)}) collective-permute-start(bf16[256,1536]{1,0:T(8,128)(2,1)} %get-tuple-element.447.refs_2_), channel_id=1, source_target_pairs={{0,1},{1,0},{2,3},{3,2},{4,5},{5,4},{6,7},{7,6},{8,9},{9,8},{10,11... | collective-permute-start | bytes 2359304 | tf_op jit(solution)/shard_map/ppermute | solution.py:27
  427.7 162.8 %reduce-scatter.5.cloned.1.call-start = ((), (), s32[]{:S(2)}) async-start(), calls=%async_computation.7 | async-start | bytes 4423680 | tf_op jit(solution)/shard_map/reduce_scatter | solution.py:1024
  453.0 29.5 %collective-permute-start.57 = (bf16[256,1536]{1,0:T(8,128)(2,1)}, bf16[256,1536]{1,0:T(8,128)(2,1)}, u32[]{:S(2)}, u32[]{:S(2)}) collective-permute-start(bf16[256,1536]{1,0:T(8,128)(2,1)} %get-tuple-element.475.refs_1_), channel_id=1, source_target_pairs={{0,1},{1,0},{2,3},{3,2},{4,5},{5,4},{6,7},{7,6},{8,9},{9,8},{10,11... | collective-permute-start | bytes 2359304 | tf_op jit(solution)/shard_map/ppermute | solution.py:27
  481.2 49.3 %collective-permute-start.59 = (bf16[256,1536]{1,0:T(8,128)(2,1)}, bf16[256,1536]{1,0:T(8,128)(2,1)}, u32[]{:S(2)}, u32[]{:S(2)}) collective-permute-start(bf16[256,1536]{1,0:T(8,128)(2,1)} %get-tuple-element.485.refs_2_), channel_id=1, source_target_pairs={{0,1},{1,0},{2,3},{3,2},{4,5},{5,4},{6,7},{7,6},{8,9},{9,8},{10,11... | collective-permute-start | bytes 2359304 | tf_op jit(solution)/shard_map/ppermute | solution.py:27
  497.5 65.7 %collective-permute-start.63 = (bf16[256,1536]{1,0:T(8,128)(2,1)}, bf16[256,1536]{1,0:T(8,128)(2,1)}, u32[]{:S(2)}, u32[]{:S(2)}) collective-permute-start(bf16[256,1536]{1,0:T(8,128)(2,1)} %get-tuple-element.491.refs_2_), channel_id=1, source_target_pairs={{0,1},{1,0},{2,3},{3,2},{4,5},{5,4},{6,7},{7,6},{8,9},{9,8},{10,11... | collective-permute-start | bytes 2359304 | tf_op jit(solution)/shard_map/ppermute | solution.py:27
  498.6 26.6 %collective-permute-start.58 = (bf16[768,2304]{1,0:T(8,128)(2,1)}, bf16[768,2304]{1,0:T(8,128)(2,1)}, u32[]{:S(2)}, u32[]{:S(2)}) collective-permute-start(bf16[768,2304]{1,0:T(8,128)(2,1)} %get-tuple-element.497), channel_id=1, source_target_pairs={{0,4},{4,0},{1,5},{5,1},{2,6},{6,2},{3,7},{7,3},{8,12},{12,8},{9,1... | collective-permute-start | bytes 10616840 | tf_op jit(solution)/shard_map/ppermute | solution.py:27
  530.0 213.7 %all-gather.17.cloned.1.call-start = ((), (), s32[]{:S(2)}) async-start(), calls=%async_computation.8 | async-start | bytes 5898240 | tf_op jit(solution)/shard_map/all_gather | solution.py:1065
  545.0 29.5 %collective-permute-start.65 = (bf16[256,768]{1,0:T(8,128)(2,1)}, bf16[256,768]{1,0:T(8,128)(2,1)S(1)}, u32[]{:S(2)}, u32[]{:S(2)}) collective-permute-start(bf16[256,768]{1,0:T(8,128)(2,1)} %get-tuple-element.507), channel_id=1, source_target_pairs={{0,4},{4,0},{1,5},{5,1},{2,6},{6,2},{3,7},{7,3},{8,12},{12,8},{9,1... | collective-permute-start | bytes 1179656 | tf_op jit(solution)/shard_map/ppermute | solution.py:27
  545.5 56.7 %collective-permute-start.64 = (bf16[192,3072]{1,0:T(8,128)(2,1)}, bf16[192,3072]{1,0:T(8,128)(2,1)}, u32[]{:S(2)}, u32[]{:S(2)}) collective-permute-start(bf16[192,3072]{1,0:T(8,128)(2,1)} %get-tuple-element.516), channel_id=1, source_target_pairs={{0,2},{1,3},{2,0},{3,1},{4,6},{5,7},{6,4},{7,5},{8,10},{9,11},{10,... | collective-permute-start | bytes 3538952 | tf_op jit(solution)/shard_map/ppermute | solution.py:27
  561.1 63.3 %collective-permute-start.61 = (bf16[384,3072]{1,0:T(8,128)(2,1)}, bf16[384,3072]{1,0:T(8,128)(2,1)}, u32[]{:S(2)}, u32[]{:S(2)}) collective-permute-start(bf16[384,3072]{1,0:T(8,128)(2,1)} %get-tuple-element.512), channel_id=1, source_target_pairs={{0,8},{8,0},{16,24},{24,16},{1,9},{9,1},{17,25},{25,17},{2,10},{10... | collective-permute-start | bytes 7077896 | tf_op jit(solution)/shard_map/ppermute | solution.py:27
  562.5 62.4 %collective-permute-start.62 = (bf16[384,3072]{1,0:T(8,128)(2,1)}, bf16[384,3072]{1,0:T(8,128)(2,1)}, u32[]{:S(2)}, u32[]{:S(2)}) collective-permute-start(bf16[384,3072]{1,0:T(8,128)(2,1)} %get-tuple-element.513), channel_id=1, source_target_pairs={{0,16},{8,24},{16,0},{24,8},{1,17},{9,25},{17,1},{25,9},{2,18},{10... | collective-permute-start | bytes 7077896 | tf_op jit(solution)/shard_map/ppermute | solution.py:27
  581.1 27.3 %collective-permute-start.67 = (bf16[256,1536]{1,0:T(8,128)(2,1)}, bf16[256,1536]{1,0:T(8,128)(2,1)}, u32[]{:S(2)}, u32[]{:S(2)}) collective-permute-start(bf16[256,1536]{1,0:T(8,128)(2,1)} %get-tuple-element.524), channel_id=1, source_target_pairs={{1,0},{3,2},{4,5},{6,7},{9,8},{11,10},{12,13},{14,15},{17,16},{19,... | collective-permute-start | bytes 2359304 | tf_op jit(solution)/shard_map/ppermute | solution.py:62
  588.9 27.9 %collective-permute-start.68 = (bf16[256,1536]{1,0:T(8,128)(2,1)}, bf16[256,1536]{1,0:T(8,128)(2,1)}, u32[]{:S(2)}, u32[]{:S(2)}) collective-permute-start(bf16[256,1536]{1,0:T(8,128)(2,1)} %get-tuple-element.527), channel_id=1, source_target_pairs={{1,0},{3,2},{4,5},{6,7},{9,8},{11,10},{12,13},{14,15},{17,16},{19,... | collective-permute-start | bytes 2359304 | tf_op jit(solution)/shard_map/ppermute | solution.py:62
  629.1 167.9 %all-gather.19.cloned.1.call-start = ((), (), s32[]{:S(2)}) async-start(), calls=%async_computation.9 | async-start | bytes 2211840 | tf_op jit(solution)/shard_map/all_gather | solution.py:1065
  634.3 44.8 %collective-permute-start.69 = (bf16[192,3072]{1,0:T(8,128)(2,1)}, bf16[192,3072]{1,0:T(8,128)(2,1)}, u32[]{:S(2)}, u32[]{:S(2)}) collective-permute-start(bf16[192,3072]{1,0:T(8,128)(2,1)} %get-tuple-element.642), channel_id=1, source_target_pairs={{0,8},{8,0},{16,24},{24,16},{1,9},{9,1},{17,25},{25,17},{2,10},{10... | collective-permute-start | bytes 3538952 | tf_op jit(solution)/shard_map/ppermute | solution.py:27
  635.3 45.2 %collective-permute-start.75 = (bf16[192,3072]{1,0:T(8,128)(2,1)S(1)}, bf16[192,3072]{1,0:T(8,128)(2,1)}, u32[]{:S(2)}, u32[]{:S(2)}) collective-permute-start(bf16[192,3072]{1,0:T(8,128)(2,1)S(1)} %get-tuple-element.643), channel_id=1, source_target_pairs={{0,16},{8,24},{16,0},{24,8},{1,17},{9,25},{17,1},{25,9},{2,18},{10... | collective-permute-start | bytes 3538952 | tf_op jit(solution)/shard_map/ppermute | solution.py:27
  648.9 66.5 %collective-permute-start.78 = (bf16[384,1152]{1,0:T(8,128)(2,1)}, bf16[384,1152]{1,0:T(8,128)(2,1)}, u32[]{:S(2)}, u32[]{:S(2)}) collective-permute-start(bf16[384,1152]{1,0:T(8,128)(2,1)} %get-tuple-element.546), channel_id=1, source_target_pairs={{0,8},{8,0},{16,24},{24,16},{1,9},{9,1},{17,25},{25,17},{2,10},{10... | collective-permute-start | bytes 2654216 | tf_op jit(solution)/shard_map/ppermute | solution.py:27
  658.3 58.2 %collective-permute-start.79 = (bf16[384,1152]{1,0:T(8,128)(2,1)}, bf16[384,1152]{1,0:T(8,128)(2,1)}, u32[]{:S(2)}, u32[]{:S(2)}) collective-permute-start(bf16[384,1152]{1,0:T(8,128)(2,1)} %get-tuple-element.547), channel_id=1, source_target_pairs={{0,16},{8,24},{16,0},{24,8},{1,17},{9,25},{17,1},{25,9},{2,18},{10... | collective-permute-start | bytes 2654216 | tf_op jit(solution)/shard_map/ppermute | solution.py:27
  682.4 38.9 %collective-permute-start.76 = (bf16[256,1536]{1,0:T(8,128)(2,1)S(1)}, bf16[256,1536]{1,0:T(8,128)(2,1)S(1)}, u32[]{:S(2)}, u32[]{:S(2)}) collective-permute-start(bf16[256,1536]{1,0:T(8,128)(2,1)S(1)} %copy-done.38), channel_id=1, source_target_pairs={{1,0},{3,2},{4,5},{6,7},{9,8},{11,10},{12,13},{14,15},{17,16},{19,... | collective-permute-start | bytes 2359304 | tf_op jit(solution)/shard_map/ppermute | solution.py:62
  683.8 37.9 %collective-permute-start.77 = (bf16[256,1536]{1,0:T(8,128)(2,1)S(1)}, bf16[256,1536]{1,0:T(8,128)(2,1)S(1)}, u32[]{:S(2)}, u32[]{:S(2)}) collective-permute-start(bf16[256,1536]{1,0:T(8,128)(2,1)S(1)} %copy-done.39), channel_id=1, source_target_pairs={{1,0},{3,2},{4,5},{6,7},{9,8},{11,10},{12,13},{14,15},{17,16},{19,... | collective-permute-start | bytes 2359304 | tf_op jit(solution)/shard_map/ppermute | solution.py:62
  685.4 47.6 %collective-permute-start.82 = (bf16[192,3072]{1,0:T(8,128)(2,1)S(1)}, bf16[192,3072]{1,0:T(8,128)(2,1)S(1)}, u32[]{:S(2)}, u32[]{:S(2)}) collective-permute-start(bf16[192,3072]{1,0:T(8,128)(2,1)S(1)} %add_convert_fusion.4), channel_id=1, source_target_pairs={{0,2},{1,3},{2,0},{3,1},{4,6},{5,7},{6,4},{7,5},{8,10},{9,11},{10,... | collective-permute-start | bytes 3538952 | tf_op jit(solution)/shard_map/ppermute | solution.py:27
  737.1 29.0 %collective-permute-start.80 = (bf16[1024,768]{1,0:T(8,128)(2,1)}, bf16[1024,768]{1,0:T(8,128)(2,1)}, u32[]{:S(2)}, u32[]{:S(2)}) collective-permute-start(bf16[1024,768]{1,0:T(8,128)(2,1)} %pad_maximum_fusion.2), channel_id=1, source_target_pairs={{0,4},{4,0},{1,5},{5,1},{2,6},{6,2},{3,7},{7,3},{8,12},{12,8},{9,1... | collective-permute-start | bytes 4718600 | tf_op jit(solution)/shard_map/ppermute | solution.py:27
  755.5 38.5 %collective-permute-start.90 = (bf16[192,3072]{1,0:T(8,128)(2,1)S(1)}, bf16[192,3072]{1,0:T(8,128)(2,1)S(1)}, u32[]{:S(2)}, u32[]{:S(2)}) collective-permute-start(bf16[192,3072]{1,0:T(8,128)(2,1)S(1)} %pad_maximum_fusion.4), channel_id=1, source_target_pairs={{0,16},{8,24},{16,0},{24,8},{1,17},{9,25},{17,1},{25,9},{2,18},{10... | collective-permute-start | bytes 3538952 | tf_op jit(solution)/shard_map/ppermute | solution.py:27
  756.6 38.9 %collective-permute-start.89 = (bf16[192,3072]{1,0:T(8,128)(2,1)S(1)}, bf16[192,3072]{1,0:T(8,128)(2,1)S(1)}, u32[]{:S(2)}, u32[]{:S(2)}) collective-permute-start(bf16[192,3072]{1,0:T(8,128)(2,1)S(1)} %pad_maximum_fusion.3), channel_id=1, source_target_pairs={{0,8},{8,0},{16,24},{24,16},{1,9},{9,1},{17,25},{25,17},{2,10},{10... | collective-permute-start | bytes 3538952 | tf_op jit(solution)/shard_map/ppermute | solution.py:27
  773.2 47.1 %collective-permute-start.88 = (bf16[512,768]{1,0:T(8,128)(2,1)}, bf16[512,768]{1,0:T(8,128)(2,1)}, u32[]{:S(2)}, u32[]{:S(2)}) collective-permute-start(bf16[512,768]{1,0:T(8,128)(2,1)} %pad_maximum_fusion.8), channel_id=1, source_target_pairs={{0,2},{1,3},{2,0},{3,1},{4,6},{5,7},{6,4},{7,5},{8,10},{9,11},{10,... | collective-permute-start | bytes 2359304 | tf_op jit(solution)/shard_map/ppermute | solution.py:27
  773.2 34.2 %collective-permute-start.91 = (bf16[192,1152]{1,0:T(8,128)(2,1)S(1)}, bf16[192,1152]{1,0:T(8,128)(2,1)S(1)}, u32[]{:S(2)}, u32[]{:S(2)}) collective-permute-start(bf16[192,1152]{1,0:T(8,128)(2,1)S(1)} %add_convert_fusion.9.refs_0_), channel_id=1, source_target_pairs={{0,8},{8,0},{16,24},{24,16},{1,9},{9,1},{17,25},{25,17},{2,10},{10... | collective-permute-start | bytes 1327112 | tf_op jit(solution)/shard_map/ppermute | solution.py:27
  774.5 33.0 %collective-permute-start.92 = (bf16[192,1152]{1,0:T(8,128)(2,1)S(1)}, bf16[192,1152]{1,0:T(8,128)(2,1)}, u32[]{:S(2)}, u32[]{:S(2)}) collective-permute-start(bf16[192,1152]{1,0:T(8,128)(2,1)S(1)} %add_convert_fusion.9.refs_0_), channel_id=1, source_target_pairs={{0,16},{8,24},{16,0},{24,8},{1,17},{9,25},{17,1},{25,9},{2,18},{10... | collective-permute-start | bytes 1327112 | tf_op jit(solution)/shard_map/ppermute | solution.py:27
  (149 other events, 1519.2 us)
Sparse Core Ops, SparseCore 0:
  100.4 30.4 all-gather.8
  133.4 30.9 all-gather.10
  195.0 31.5 all-gather.20
  234.4 29.0 all-gather.12
  267.9 41.1 all-gather.14
  427.8 93.9 reduce-scatter.2
  530.1 56.7 reduce-scatter.4
  629.2 91.1 all-gather.16
  737.2 41.3 all-gather.18
